TPU v7x, 128 devices: a whole 4x4x4 slice. The times are simulated.
128 devices in a mesh: prow: 8 (over y, core), pcol: 16 (over x, z).
Axes of the slice: x: 4, y: 4, z: 4, core: 2. Of those that a mesh axis runs over, the one named last changes fastest.
Arguments:
- front: float32 [4, 8, 512, 2, 16, 512], P(None, 'prow', None, None, 'pcol'), as said below
- child_blocks: bfloat16 [8, 16, 16, 3, 256, 256], P('prow', 'pcol'), may hold values from -0.015625 to 0.015625
- row_map: int32 [2, 60], replicated, may hold values from 0 to 63, as said below
- slot_table: int32 [8, 16, 16, 3], replicated, may hold values from -1 to 7199, as said below
- struct_mask: int32 [64, 64], replicated, may hold values 0 or 1
Outputs:
- factored: float32 [4, 8, 512, 2, 16, 512], P(None, 'prow', None, None, 'pcol')
Inputs may be any that keep to these rules, and one draw needn't show every extreme that they name: `front`: with the children's blocks added, the lower triangle of the leading 2 * 512 rows and columns defines a symmetric positive definite matrix; diagonal entries are of order one, the others far smaller. Each row of row_map is strictly increasing. `slot_table`: every code c * 60 * 60 + i * 60 + j with c in 0..1 and i >= j appears in exactly one slot; a slot [p, s, q, k] holds a block whose front row lies in panel-wide block rows of grid row p and whose front column lies in panel-wide block columns of grid column q; the other slots hold -1; some grid row p and grid column q receive 3 blocks from every s.
All inputs are finite; a program needn't handle non-finite values.
Results may differ from a plain program's by a relative error of at most 0.00089.
Values may be sent and summed in bfloat16 or wider, within the bound.
No kernel may reach another device: no remote copies, remote signals or barrier semaphores. Data moves between devices by JAX's collectives and lax.ppermute only.
A program may use at most 192 MiB of HBM per device.

v0:
```python
import jax
import jax.numpy as jnp
import numpy as np
from jax import lax
from jax.sharding import PartitionSpec as P

CNB = 60
NPAN = 2


def from_root(block, axis, holder):
    block = jnp.where(lax.axis_index(axis) == holder, block, jnp.zeros_like(block))
    return lax.psum(block, axis)


def apply_update(front_here, row_panel, col_panel, weight, col_list):
    rows_here = row_panel.shape[0]
    panel_width = row_panel.shape[1]
    block_size = panel_width // 2
    count = len(col_list)
    col_array = np.array(col_list, dtype=np.int32)
    product = jnp.einsum(
        "rit,cjt->ricj", row_panel, col_panel[col_array], preferred_element_type=jnp.float32
    )
    chosen = weight[:, :, col_array, :]
    product = (
        product.reshape(rows_here, 2, block_size, count, 2, block_size)
        * chosen[:, :, None, :, :, None]
    )
    product = product.reshape(rows_here, panel_width, count, panel_width)
    return front_here - product


def factor_panel(front_here, panel_num, row_blocks):
    rows_count = lax.axis_size("prow")
    cols_count = lax.axis_size("pcol")
    grid_col = lax.axis_index("pcol")
    rows_here = front_here.shape[0]
    panel_width = front_here.shape[1]
    cols_here = front_here.shape[2]
    local_row = panel_num // rows_count
    local_col = panel_num // cols_count
    diag_block = from_root(front_here[local_row, :, local_col, :], "prow", panel_num % rows_count)
    symmetric = jnp.tril(diag_block) + jnp.tril(diag_block, -1).T
    factor = jnp.linalg.cholesky(symmetric)
    column = front_here[:, :, local_col, :]
    right_side = column.transpose(2, 0, 1).reshape(panel_width, rows_here * panel_width)
    solved = jax.scipy.linalg.solve_triangular(factor, right_side, lower=True)
    solved = solved.reshape(panel_width, rows_here, panel_width).transpose(1, 2, 0)
    below = (row_blocks > panel_num)[:, None, None]
    on_diag = (row_blocks == panel_num)[:, None, None]
    new_column = jnp.where(below, solved, jnp.where(on_diag, factor[None], column))
    is_owner = grid_col == panel_num % cols_count
    front_here = front_here.at[:, :, local_col, :].set(jnp.where(is_owner, new_column, column))
    row_panel = jnp.where(below, solved, jnp.float32(0.0)).astype(jnp.bfloat16)
    row_panel = from_root(row_panel, "pcol", panel_num % cols_count)
    ratio = cols_count // rows_count
    picked_rows = jnp.arange(cols_here, dtype=jnp.int32) * ratio + grid_col // rows_count
    picked = jnp.take(row_panel, picked_rows, axis=0)
    col_panel = from_root(picked, "prow", grid_col % rows_count)
    return (front_here, row_panel, col_panel)


def local(front, child_blocks, row_map, slot_table, struct_mask):
    rows_count = lax.axis_size("prow")
    cols_count = lax.axis_size("pcol")
    grid_row = lax.axis_index("prow")
    grid_col = lax.axis_index("pcol")
    rows_here = front.shape[0]
    panel_width = front.shape[2]
    cols_here = front.shape[3]
    block_size = panel_width // 2
    front_here = front.reshape(rows_here, panel_width, cols_here, panel_width)
    outgoing = child_blocks[0, 0]
    arrived = lax.all_to_all(outgoing, "pcol", split_axis=0, concat_axis=0, tiled=True)
    row_slots = lax.dynamic_index_in_dim(slot_table, grid_row, 0, False)
    slot_codes = lax.dynamic_index_in_dim(row_slots, grid_col, 1, False).reshape(-1)
    is_live = slot_codes >= 0
    code_value = jnp.maximum(slot_codes, 0)
    child_id = code_value // (CNB * CNB)
    child_row = code_value // CNB % CNB
    child_col = code_value % CNB
    flat_map = row_map.reshape(-1)
    map_keys = jnp.arange(2 * CNB, dtype=jnp.int32)
    parent_row = jnp.sum(
        jnp.where((child_id * CNB + child_row)[:, None] == map_keys[None, :], flat_map[None, :], 0),
        axis=1,
    )
    parent_col = jnp.sum(
        jnp.where((child_id * CNB + child_col)[:, None] == map_keys[None, :], flat_map[None, :], 0),
        axis=1,
    )
    target_row = jnp.where(is_live, parent_row // 2 // rows_count * 2 + parent_row % 2, 0)
    target_col = jnp.where(is_live, parent_col // 2 // cols_count * 2 + parent_col % 2, 0)
    pieces = jnp.where(
        is_live[:, None, None],
        arrived.reshape(-1, block_size, block_size),
        jnp.zeros((), jnp.bfloat16),
    )
    quarters = front_here.reshape(rows_here * 2, block_size, cols_here * 2, block_size)
    quarters = quarters.at[target_row, :, target_col, :].add(pieces.astype(jnp.float32))
    front_here = quarters.reshape(rows_here, panel_width, cols_here, panel_width)
    row_blocks = jnp.arange(rows_here, dtype=jnp.int32) * rows_count + grid_row
    col_blocks = jnp.arange(cols_here, dtype=jnp.int32) * cols_count + grid_col
    pair_index = jnp.arange(2, dtype=jnp.int32)
    sub_rows = ((2 * row_blocks)[:, None] + pair_index[None, :]).reshape(-1)
    sub_cols = ((2 * col_blocks)[:, None] + pair_index[None, :]).reshape(-1)
    local_mask = struct_mask[sub_rows][:, sub_cols].reshape(rows_here, 2, cols_here, 2)
    lower_part = row_blocks[:, None] >= col_blocks[None, :]
    base_weight = jnp.where(
        (local_mask > 0) & lower_part[:, None, :, None], jnp.float32(1.0), jnp.float32(0.0)
    )
    all_cols = list(range(cols_here))
    for panel_num in range(NPAN):
        front_here, row_panel, col_panel = factor_panel(front_here, panel_num, row_blocks)
        trailing = (row_blocks > panel_num)[:, None] & (col_blocks > panel_num)[None, :]
        front_here = apply_update(
            front_here,
            row_panel,
            col_panel,
            base_weight * jnp.where(trailing, jnp.float32(1.0), jnp.float32(0.0))[:, None, :, None],
            all_cols,
        )
    keep_blocks = jnp.where(lower_part, jnp.float32(1.0), jnp.float32(0.0))
    front_here = front_here * keep_blocks[:, None, :, None]
    return front_here.reshape(front.shape)


def solution(mesh):
    in_specs = (
        P(None, "prow", None, None, "pcol", None),
        P("prow", "pcol", None, None, None, None),
        P(),
        P(),
        P(),
    )
    out_specs = P(None, "prow", None, None, "pcol", None)
    return jax.shard_map(local, mesh=mesh, in_specs=in_specs, out_specs=out_specs, check_vma=False)
```

profile of v0, /device:TPU:1, one launch (start us, length us, event | category | flops | bytes accessed | tf_op | source)
XLA Modules:
  0.0 1026.9 jit_solution(5676959027340533628)
XLA Ops:
  16.8 29.4 %reduce.20 = f32[4,512,2,512]{3,2,1,0:T(2,128)} reduce(f32[4,1,512,2,1,512]{5,4,3,2,1,0:T(1,128)} %param.20, f32[]{:T(128)} %constant.385), dimensions={1,4}, to_apply=%param.20.reduce_sub_computation | reduce | bytes 16777220 | tf_op args[0]
  46.2 12.5 %reshape.811 = f32[8,256,4,256]{3,2,1,0:T(4,128)} reshape(f32[4,512,2,512]{3,2,1,0:T(2,128)} %reduce.20) | data formatting | bytes 16777216 | tf_op jit(solution)/shard_map/reshape;reshape | solution.py:100
  67.4 48.6 %all-to-all-done = bf16[16,3,256,256]{3,2,1,0:T(8,128)(2,1)} async-done(((bf16[16,3,256,256]{3,2,1,0:T(8,128)(2,1)}), bf16[16,3,256,256]{3,2,1,0:T(8,128)(2,1)}, u32[]{:S(2)}, u32[]{:S(2)}) %all-to-all-start) | async-done | bytes 6291488 | tf_op jit(solution)/shard_map/all_to_all | solution.py:75
  124.2 27.8 %scatter_fusion = f32[8,256,4,256]{3,1,2,0:T(8,128)} fusion(f32[8,256,4,256]{3,1,2,0:T(8,128)} %copy.112, s32[48]{0:T(128)S(1)} %fusion.90, f32[48,256,256]{2,1,0:T(8,128)} %fusion), kind=kCustom, calls=%fused_computation.8 | custom fusion | flops 3145728 | bytes 37749120 | tf_op jit(solution)/shard_map/scatter-add | solution.py:101
  152.0 10.4 %copy.113 = f32[8,256,4,256]{1,0,3,2:T(8,128)} copy(f32[8,256,4,256]{3,1,2,0:T(8,128)} %scatter_fusion) | data formatting | bytes 16777216 | tf_op jit(solution)/shard_map/scatter-add | solution.py:101
  162.4 10.5 %reshape.701 = f32[4,512,2,512]{1,0,3,2:T(4,128)} reshape(f32[8,256,4,256]{1,0,3,2:T(8,128)} %copy.113) | data formatting | bytes 16777216 | tf_op jit(solution)/shard_map/reshape | solution.py:102
  172.9 9.9 copy.123
  202.9 54.5 %all-reduce.8.cloned.1.call-done = f32[512,512]{1,0:T(8,128)} async-done(((f32[512,512]{1,0:T(8,128)}), f32[512,512]{1,0:T(8,128)}) %all-reduce.8.cloned.1.call-update) | async-done | bytes 1048592 | tf_op jit(solution)/shard_map/psum | solution.py:13
  261.9 11.7 %cholesky.286 = f32[128,128]{1,0:T(8,128)S(1)} custom-call(f32[128,128]{1,0:T(8,128)S(1)} %cholesky.426), custom_call_target="Cholesky" | custom-call | tf_op jit(solution)/shard_map/jit(cholesky)/cholesky | solution.py:45
  273.8 9.8 custom-call.29
  286.1 12.1 %cholesky.305 = f32[128,128]{1,0:T(8,128)S(1)} custom-call(f32[128,128]{1,0:T(8,128)S(1)} %cholesky.430), custom_call_target="Cholesky" | custom-call | tf_op jit(solution)/shard_map/jit(cholesky)/cholesky | solution.py:45
  298.3 9.8 custom-call.30
  309.7 11.7 %cholesky.326 = f32[128,128]{1,0:T(8,128)S(1)} custom-call(f32[128,128]{1,0:T(8,128)S(1)} %cholesky.435), custom_call_target="Cholesky" | custom-call | tf_op jit(solution)/shard_map/jit(cholesky)/cholesky | solution.py:45
  322.1 9.8 custom-call.31
  333.4 11.9 %cholesky.343 = f32[128,128]{1,0:T(8,128)S(1)} custom-call(f32[128,128]{1,0:T(8,128)S(1)} %convolution_subtract_fusion.9), custom_call_target="Cholesky" | custom-call | tf_op jit(solution)/shard_map/jit(cholesky)/cholesky | solution.py:45
  351.3 14.3 %while.6 = (s32[]{:T(128)}, f32[512,512]{1,0:T(8,128)}, s32[4,2]{0,1:T(2,128)S(1)}, f32[4,128,128]{2,1,0:T(8,128)}, s32[]{:T(128)}) while((s32[]{:T(128)}, f32[512,512]{1,0:T(8,128)}, s32[4,2]{0,1:T(2,128)S(1)}, f32[4,128,128]{2,1,0:T(8,128)}, s32[]{:T(128)}) %tuple.78), condition=%wide.while_cond.2, body=%wide.while_body.2.sunk | while | flops 2 | bytes 132705 | solution.py:48
  365.6 40.7 %custom-call.32 = f32[4,128,128]{1,2,0:T(8,128)} custom-call(f32[4,128,128]{2,1,0:T(8,128)} %get-tuple-element.46), custom_call_target="InvertDiagBlocksLowerTriangular" | custom-call | tf_op jit(solution)/shard_map/jit(_solve_triangular)/triangular_solve | solution.py:48
  439.6 11.6 %mul.152 = f32[4,512,2,512]{3,1,2,0:T(8,128)} reshape(f32[4,2,256,2,2,256]{5,4,2,1,3,0:T(2,128)} %mul.151) | data formatting | bytes 16777216 | tf_op jit(solution)/shard_map/mul | solution.py:27
  452.3 69.3 %all-reduce.10.cloned.1.call-done = bf16[4,512,512]{2,1,0:T(8,128)(2,1)} async-done(((bf16[4,512,512]{2,1,0:T(8,128)(2,1)}), bf16[4,512,512]{2,1,0:T(8,128)(2,1)}) %all-reduce.10.cloned.1.call-update) | async-done | bytes 2097168 | tf_op jit(solution)/shard_map/psum | solution.py:13
  532.0 54.0 %all-reduce.12.cloned.1.call-done = bf16[2,512,512]{2,1,0:T(8,128)(2,1)} async-done(((bf16[2,512,512]{2,1,0:T(8,128)(2,1)}), bf16[2,512,512]{2,1,0:T(8,128)(2,1)}) %all-reduce.12.cloned.1.call-update) | async-done | bytes 1048592 | tf_op jit(solution)/shard_map/psum | solution.py:13
  609.6 54.1 %all-reduce.14.cloned.1.call-done = f32[512,512]{1,0:T(8,128)} async-done(((f32[512,512]{1,0:T(8,128)}), f32[512,512]{1,0:T(8,128)}) %all-reduce.14.cloned.1.call-update) | async-done | bytes 1048592 | tf_op jit(solution)/shard_map/psum | solution.py:13
  669.6 11.7 %cholesky.358 = f32[128,128]{1,0:T(8,128)S(1)} custom-call(f32[128,128]{1,0:T(8,128)S(1)} %cholesky.439), custom_call_target="Cholesky" | custom-call | tf_op jit(solution)/shard_map/jit(cholesky)/cholesky | solution.py:45
  681.5 9.8 custom-call.33
  693.8 11.8 %cholesky.377 = f32[128,128]{1,0:T(8,128)S(1)} custom-call(f32[128,128]{1,0:T(8,128)S(1)} %cholesky.443), custom_call_target="Cholesky" | custom-call | tf_op jit(solution)/shard_map/jit(cholesky)/cholesky | solution.py:45
  718.4 11.7 %cholesky.398 = f32[128,128]{1,0:T(8,128)S(1)} custom-call(f32[128,128]{1,0:T(8,128)S(1)} %cholesky.448), custom_call_target="Cholesky" | custom-call | tf_op jit(solution)/shard_map/jit(cholesky)/cholesky | solution.py:45
  742.0 11.9 %cholesky.415 = f32[128,128]{1,0:T(8,128)S(1)} custom-call(f32[128,128]{1,0:T(8,128)S(1)} %convolution_subtract_fusion.8), custom_call_target="Cholesky" | custom-call | tf_op jit(solution)/shard_map/jit(cholesky)/cholesky | solution.py:45
  759.1 13.8 %while.7 = (s32[]{:T(128)}, f32[512,512]{1,0:T(8,128)}, s32[4,2]{0,1:T(2,128)S(1)}, f32[4,128,128]{2,1,0:T(8,128)}, s32[]{:T(128)}) while((s32[]{:T(128)}, f32[512,512]{1,0:T(8,128)}, s32[4,2]{0,1:T(2,128)S(1)}, f32[4,128,128]{2,1,0:T(8,128)}, s32[]{:T(128)}) %tuple.96), condition=%wide.while_cond.2.clone, body=%wide.while_body.2.clone.sunk | while | flops 2 | bytes 132705 | solution.py:48
  772.9 40.7 %custom-call.36 = f32[4,128,128]{1,2,0:T(8,128)} custom-call(f32[4,128,128]{2,1,0:T(8,128)} %get-tuple-element.47), custom_call_target="InvertDiagBlocksLowerTriangular" | custom-call | tf_op jit(solution)/shard_map/jit(_solve_triangular)/triangular_solve | solution.py:48
  844.6 11.6 %mul.157 = f32[4,512,2,512]{3,1,2,0:T(8,128)} reshape(f32[4,2,256,2,2,256]{5,4,2,1,3,0:T(2,128)} %mul.156) | data formatting | bytes 16777216 | tf_op jit(solution)/shard_map/mul | solution.py:27
  856.2 72.7 %all-reduce.16.cloned.1.call-done = bf16[4,512,512]{2,1,0:T(8,128)(2,1)} async-done(((bf16[4,512,512]{2,1,0:T(8,128)(2,1)}), bf16[4,512,512]{2,1,0:T(8,128)(2,1)}) %all-reduce.16.cloned.1.call-update) | async-done | bytes 2097168 | tf_op jit(solution)/shard_map/psum | solution.py:13
  939.3 54.0 %all-reduce.18.cloned.1.call-done = bf16[2,512,512]{2,1,0:T(8,128)(2,1)} async-done(((bf16[2,512,512]{2,1,0:T(8,128)(2,1)}), bf16[2,512,512]{2,1,0:T(8,128)(2,1)}) %all-reduce.18.cloned.1.call-update) | async-done | bytes 1048592 | tf_op jit(solution)/shard_map/psum | solution.py:13
  1003.4 16.3 %copy.139 = f32[4,1,512,2,1,512]{5,4,3,2,1,0:T(1,128)} copy(f32[4,1,512,2,1,512]{5,2,3,0,4,1:T(8,128)S(1)} %multiply_bitcast_fusion) | data formatting | bytes 16777216 | tf_op jit(solution)/shard_map/reshape | solution.py:126
  (227 shorter events, 244.7 us)
Async XLA Ops:
  6.5 8.7 copy-start
  6.5 10.1 copy-start.15
  6.5 109.4 %all-to-all-start = ((bf16[16,3,256,256]{3,2,1,0:T(8,128)(2,1)}), bf16[16,3,256,256]{3,2,1,0:T(8,128)(2,1)}, u32[]{:S(2)}, u32[]{:S(2)}) async-start(bf16[16,3,256,256]{3,2,1,0:T(8,128)(2,1)} %bitcast.260), calls=%async_computation | async-start | bytes 12582912 | tf_op jit(solution)/shard_map/all_to_all | solution.py:75
  15.2 242.2 %all-reduce.8.cloned.1.call-start = ((), (), s32[]{:S(2)}) async-start(), calls=%async_computation.1 | async-start | bytes 2097152 | tf_op jit(solution)/shard_map/psum | solution.py:13
  190.0 331.5 %all-reduce.10.cloned.1.call-start = ((), (), s32[]{:S(2)}) async-start(), calls=%async_computation.2 | async-start | bytes 4194304 | tf_op jit(solution)/shard_map/psum | solution.py:13
  260.9 1.0 copy-start.11
  351.3 60.3 %copy-start.8 = (f32[128,2048]{1,0:T(8,128)S(1)}, f32[128,2048]{1,0:T(8,128)}, u32[]{:S(2)}) copy-start(f32[128,2048]{1,0:T(8,128)} %copy.147) | copy-start | bytes 3145732
  406.3 4.2 copy-start.12
  410.6 4.3 copy-start.7
  426.7 5.1 copy-start.14
  430.9 155.1 %all-reduce.12.cloned.1.call-start = ((), (), s32[]{:S(2)}) async-start(), calls=%async_computation.3 | async-start | bytes 2097152 | tf_op jit(solution)/shard_map/psum | solution.py:13
  525.0 138.8 %all-reduce.14.cloned.1.call-start = ((), (), s32[]{:S(2)}) async-start(), calls=%async_computation.4 | async-start | bytes 2097152 | tf_op jit(solution)/shard_map/psum | solution.py:13
  525.0 62.8 %copy-start.3 = (bf16[4,512,512]{2,1,0:T(8,128)(2,1)S(1)}, bf16[4,512,512]{2,1,0:T(8,128)(2,1)}, u32[]{:S(2)}) copy-start(bf16[4,512,512]{2,1,0:T(8,128)(2,1)} %all-reduce.10.cloned.1.call-done) | copy-start | bytes 6291460
  596.0 4.7 copy-start.2
  601.8 327.1 %all-reduce.16.cloned.1.call-start = ((), (), s32[]{:S(2)}) async-start(), calls=%async_computation.5 | async-start | bytes 4194304 | tf_op jit(solution)/shard_map/psum | solution.py:13
  663.7 2.9 copy-start.9
  668.6 1.0 copy-start.10
  759.1 59.9 %copy-start.6 = (f32[128,2048]{1,0:T(8,128)S(1)}, f32[128,2048]{1,0:T(8,128)}, u32[]{:S(2)}) copy-start(f32[128,2048]{1,0:T(8,128)} %copy.151) | copy-start | bytes 3145732
  813.7 4.2 copy-start.13
  817.9 4.3 copy-start.5
  838.2 155.1 %all-reduce.18.cloned.1.call-start = ((), (), s32[]{:S(2)}) async-start(), calls=%async_computation.6 | async-start | bytes 2097152 | tf_op jit(solution)/shard_map/psum | solution.py:13
  932.3 62.8 %copy-start.4 = (bf16[4,512,512]{2,1,0:T(8,128)(2,1)S(1)}, bf16[4,512,512]{2,1,0:T(8,128)(2,1)}, u32[]{:S(2)}) copy-start(bf16[4,512,512]{2,1,0:T(8,128)(2,1)} %all-reduce.16.cloned.1.call-done) | copy-start | bytes 6291460
  1003.4 16.3 %copy-start.1 = (s32[8,16,16,3]{2,1,3,0:T(8,128)S(1)}, s32[8,16,16,3]{2,1,3,0:T(8,128)}, u32[]{:S(2)}) copy-start(s32[8,16,16,3]{2,1,3,0:T(8,128)} %param.23) | copy-start | bytes 73732
Sparse Core Ops, SparseCore 0:
  190.2 67.1 all-reduce.7
  431.0 90.5 all-reduce.9
  525.1 60.8 all-reduce.11
  601.9 61.7 all-reduce.13
  838.3 90.5 all-reduce.15
  932.4 60.8 all-reduce.17
where the time goes:
time: 1030 us
  waiting for transfers between devices  407 us (40%)
  other arithmetic  346 us (34%)
  local copies, waits for them, and re-layouts  192 us (19%)
  matrix products  52.3 us (5%)
  between operations  19.7 us (2%)
    psum x6, waiting for transfers between devices, from_root(): return lax.psum(block, axis)  359 us
    another operation x29, other arithmetic, factor_panel(): factor = jnp.linalg.cholesky(symmetric)  159 us
    another operation x7, other arithmetic, factor_panel(): solved = jax.scipy.linalg.solve_triangular(factor, right_side, lower=True)  88.9 us
    all_to_all x1, waiting for transfers between devices, local(): lax.all_to_all(outgoing, 'pcol', split_axis=0, concat_axis=0, tiled=True)  48.6 us
    another operation x31, local copies, waits for them, and re-layouts, factor_panel(): solved = jax.scipy.linalg.solve_triangular(factor, right_side, lower=True)  46.4 us
    mul x4, local copies, waits for them, and re-layouts, apply_update(): product.reshape(rows_here, 2, block_size, count, 2, block_size)  34.2 us
    unnamed x1, other arithmetic  29.4 us
    scatter-add x1, other arithmetic, local(): quarters.at[target_row, :, target_col, :].add(pieces.astype(jnp.float32))  27.8 us
  transfers between devices with their start and end apart: 7, of which 7 were waited for; matrix products, arithmetic and copies ran while one was open for 12% of the time, Pallas kernels for 0%

commit v1 on v0

v1 whole, which is shorter than its diff:
```python
import functools

import jax
import jax.numpy as jnp
from jax import lax
from jax.experimental import pallas as pl
from jax.experimental.pallas import tpu as pltpu
from jax.sharding import PartitionSpec as P

F32 = jnp.float32
BF16 = jnp.bfloat16
CNB = 60
NN = (((1,), (0,)), ((), ()))
NT = (((1,), (1,)), ((), ()))
MIB = 2**20
VMEM = pl.BlockSpec(memory_space=pltpu.VMEM)
SMEM = pl.BlockSpec(memory_space=pltpu.SMEM)


def split(x):
    high = x.astype(BF16)
    return high, (x - high.astype(F32)).astype(BF16)


def dot1(a, b, dims):
    return lax.dot_general(a, b, dims, preferred_element_type=F32)


def dot3(a, b, dims):
    ah, al = split(a)
    bh, bl = split(b)
    return dot1(ah, bh, dims) + (dot1(al, bh, dims) + dot1(ah, bl, dims))


def factor_base(S):
    n = S.shape[0]
    wide = 2 * n // 128
    lane = lax.broadcasted_iota(jnp.int32, (n, n), 1)
    sub = lax.broadcasted_iota(jnp.int32, (n, n), 0)
    M = jnp.concatenate([S, jnp.where(lane == sub, F32(1), F32(0))], axis=1)
    row = lax.broadcasted_iota(jnp.int32, (8, 1), 0)
    across = lambda v: jnp.concatenate([v] * wide, axis=1)
    done = []
    for o in range(0, n, 8):
        R = M[0:8]
        cols = [jnp.broadcast_to(R[:, o + j : o + j + 1], (8, 128)) for j in range(8)]
        D = [[jnp.broadcast_to(cols[j][i : i + 1], (8, 128)) for j in range(i + 1)] for i in range(8)]
        Y = [jnp.broadcast_to(R[i : i + 1], (8, 2 * n)) for i in range(8)]
        low = [[None] * 8 for _ in range(8)]
        inv = [None] * 8
        for j in range(8):
            inv[j] = 1.0 / D[j][j]
            for i in range(j + 1, 8):
                low[i][j] = D[i][j] * inv[j]
            for i in range(j + 1, 8):
                for m in range(j + 1, i + 1):
                    D[i][m] = D[i][m] - low[i][j] * D[m][j]
                Y[i] = Y[i] - across(low[i][j]) * Y[j]
        out = None
        for j in range(8):
            scaled = Y[j] * across(lax.rsqrt(D[j][j]))
            out = scaled if out is None else jnp.where(row == j, scaled, out)
        done.append(out)
        if o + 8 == n:
            break
        Z = [None] * 8
        for i in range(7, -1, -1):
            Z[i] = Y[i] * across(inv[i])
            for m in range(i + 1, 8):
                Z[i] = Z[i] - across(low[m][i]) * Z[m]
        step = Z[0]
        for i in range(1, 8):
            step = jnp.where(row == i, Z[i], step)
        parts = [jnp.zeros((o, 2 * n), F32)] if o else []
        parts += [step, jnp.zeros((n - o - 8, 2 * n), F32)]
        M = M[8:] - dot3(M[8:, :n], jnp.concatenate(parts, axis=0), NN)
    done = jnp.concatenate(done, axis=0)
    return jnp.where(lane >= sub, done[:, :n], F32(0)), jnp.where(lane <= sub, done[:, n:], F32(0))


def factor_whole(a_ref, l_ref, w_ref):
    n = a_ref.shape[0]
    b = 128
    w_ref[...] = jnp.zeros((n, n), F32)
    l_ref[...] = jnp.zeros((n, n), F32)
    lane = lax.broadcasted_iota(jnp.int32, (b, b), 1)
    sub = lax.broadcasted_iota(jnp.int32, (b, b), 0)
    for k in range(0, n, b):
        s = slice(k, k + b)
        D = a_ref[s, s]
        U, W = factor_base(jnp.where(sub >= lane, D, D.T))
        l_ref[s, s] = U.T
        w_ref[s, s] = W
        if k:
            T = dot3(l_ref[s, :k], w_ref[:k, :k], NN)
            w_ref[s, :k] = -dot3(W, T, NN)
        if k + b < n:
            L = dot3(a_ref[k + b :, s], W, NT)
            l_ref[k + b :, s] = L
            for j in range(k + b, n, b):
                off = j - k - b
                a_ref[j:, j : j + b] = a_ref[j:, j : j + b] - dot3(L[off:], L[off : off + b], NT)


def factor_first_kernel(d_ref, l_ref, w_ref, a_ref):
    a_ref[...] = d_ref[...]
    factor_whole(a_ref, l_ref, w_ref)


def factor_second_kernel(mask_ref, below_ref, d_ref, w0_ref, p_ref, l_ref, w_ref, a_ref):
    panel = dot3(below_ref[...], w0_ref[...], NT).astype(BF16)
    p_ref[...] = panel
    n = panel.shape[0]
    h = n // 2
    for i in range(2):
        for j in range(i + 1):
            r, c = slice(i * h, (i + 1) * h), slice(j * h, (j + 1) * h)
            product = dot1(panel[r], panel[c], NT)
            a_ref[r, c] = d_ref[r, c] - jnp.where(mask_ref[i * 2 + j] > 0, product, F32(0))
    factor_whole(a_ref, l_ref, w_ref)


CHOL_COST = pl.CostEstimate(flops=20_000_000_000, bytes_accessed=3 * MIB, transcendentals=1024)


def factor_first(D):
    n = D.shape[0]
    return pl.pallas_call(
        factor_first_kernel,
        out_shape=[jax.ShapeDtypeStruct((n, n), F32)] * 2,
        in_specs=[VMEM],
        out_specs=[VMEM] * 2,
        scratch_shapes=[pltpu.VMEM((n, n), F32)],
        cost_estimate=CHOL_COST,
        compiler_params=pltpu.CompilerParams(vmem_limit_bytes=40 * MIB),
    )(D)


def factor_second(mask, below, D, W0):
    n = D.shape[0]
    return pl.pallas_call(
        factor_second_kernel,
        out_shape=[jax.ShapeDtypeStruct((n, n), BF16)] + [jax.ShapeDtypeStruct((n, n), F32)] * 2,
        in_specs=[SMEM, VMEM, VMEM, VMEM],
        out_specs=[VMEM] * 3,
        scratch_shapes=[pltpu.VMEM((n, n), F32)],
        cost_estimate=CHOL_COST,
        compiler_params=pltpu.CompilerParams(vmem_limit_bytes=40 * MIB),
    )(mask, below, D, W0)


def cut_kernel(x_ref, o_ref):
    strips, _, rows, width = o_ref.shape
    for c in range(width // 128):
        tile = x_ref[pl.ds(c, strips * rows, stride=8), :]
        o_ref[:, 0, :, c * 128 : (c + 1) * 128] = tile.reshape(strips, rows, 128)


def cut_strips(front_rows, first, count, strips):
    return pl.pallas_call(
        cut_kernel,
        grid=(count,),
        out_shape=jax.ShapeDtypeStruct((strips, count, 16, 512), F32),
        in_specs=[pl.BlockSpec((2048, 128), lambda i: (i + first, 0))],
        out_specs=pl.BlockSpec((strips, 1, 16, 512), lambda i: (0, i, 0, 0)),
        cost_estimate=pl.CostEstimate(flops=0, bytes_accessed=count * 2 * MIB, transcendentals=0),
    )(front_rows)


def join_kernel(first, slot_ref, f_ref, c_ref, o_ref):
    count = o_ref.shape[0]
    for i in range(count):
        for j in range(4):
            value = f_ref[j // 2, i, :, (j % 2) * 256 : (j % 2 + 1) * 256]
            for child in range(2):
                slot = slot_ref[((i + first) * 4 + j) * 2 + child]
                piece = c_ref[jnp.maximum(slot, 0)].astype(F32)
                value = value + jnp.where(slot >= 0, piece, F32(0))
            o_ref[i, :, j * 256 : (j + 1) * 256] = value


def join_strips(slots, front_strips, child_strips, first, count):
    return pl.pallas_call(
        functools.partial(join_kernel, first),
        out_shape=jax.ShapeDtypeStruct((count, 16, 1024), F32),
        in_specs=[SMEM, VMEM, VMEM],
        out_specs=VMEM,
        cost_estimate=pl.CostEstimate(flops=0, bytes_accessed=3 * MIB, transcendentals=0),
    )(slots, front_strips, child_strips)


def solve_first_kernel(keep_ref, d_ref, r_ref, w_ref, o_ref):
    width = w_ref.shape[0]
    b = jnp.concatenate(
        [d_ref[:, :, :width].reshape(32, width), r_ref[:, :, :width].reshape(96, width)], axis=0
    )
    x = dot3(b, w_ref[...], NT).reshape(8, 16, width)
    for i in range(8):
        o_ref[i] = jnp.where(keep_ref[i] > 0, x[i], F32(0)).astype(BF16)


def solve_second_kernel(keep_ref, d_ref, r_ref, p_ref, p10_ref, w_ref, o_ref):
    width = w_ref.shape[0]
    half = width // 2
    b = jnp.concatenate(
        [d_ref[:, :, width:].reshape(32, width), r_ref[:, :, width:].reshape(96, width)], axis=0
    )
    u = dot1(p_ref[...].reshape(128, width), p10_ref[...], NT)
    rows = []
    for i in range(8):
        s = slice(16 * i, 16 * i + 16)
        parts = []
        for j in range(2):
            c = slice(j * half, (j + 1) * half)
            parts.append(b[s, c] - jnp.where(keep_ref[8 + 2 * i + j] > 0, u[s, c], F32(0)))
        rows.append(jnp.concatenate(parts, axis=1))
    x = dot3(jnp.concatenate(rows, axis=0), w_ref[...], NT).reshape(8, 16, width)
    for i in range(8):
        o_ref[i] = jnp.where(keep_ref[i] > 0, x[i], F32(0)).astype(BF16)


def solve_strips(kernel, *operands):
    return pl.pallas_call(
        kernel,
        out_shape=jax.ShapeDtypeStruct((8, 16, 512), BF16),
        in_specs=[SMEM] + [VMEM] * (len(operands) - 1),
        out_specs=VMEM,
        cost_estimate=pl.CostEstimate(flops=400_000_000, bytes_accessed=2 * MIB, transcendentals=0),
    )(*operands)


def finish_kernel(slot_ref, flag_ref, f_ref, *refs):
    child = refs[:8]
    row_refs = refs[8:10]
    col_refs = refs[10:12]
    l_ref, w_ref, o_ref = refs[12:15]
    i = pl.program_id(0)
    rows = jnp.concatenate([ref[:, 0].reshape(256, 512) for ref in row_refs], axis=1)
    for lc in range(2):
        state = flag_ref[32 + i * 2 + lc]

        @pl.when(state > 0)
        def _():
            blocks = []
            for sc in range(2):
                j = lc * 2 + sc
                cols = jnp.concatenate([ref[sc, :, lc].reshape(256, 512) for ref in col_refs], axis=1)
                value = jnp.concatenate(
                    [f_ref[pl.ds(lc * 4 + sc * 2 + c, 256, stride=8), :] for c in range(2)], axis=1
                )
                for ch in range(2):
                    live = slot_ref[(i * 4 + j) * 2 + ch] >= 0
                    value = value + jnp.where(live, child[j * 2 + ch][0].astype(F32), F32(0))
                product = dot1(rows, cols, NT)
                blocks.append(value - jnp.where(flag_ref[i * 4 + j] > 0, product, F32(0)))
            block = jnp.concatenate(blocks, axis=1)

            def put(value):
                for c in range(4):
                    o_ref[pl.ds(lc * 4 + c, 256, stride=8), :] = value[:, c * 128 : (c + 1) * 128]

            @pl.when(state == 1)
            def _():
                put(block)

            if lc == 0:

                @pl.when(state == 2)
                def _():
                    put(dot3(block, w_ref[...], NT))

                @pl.when(state == 3)
                def _():
                    put(l_ref[pl.ds(pl.multiple_of(lax.rem(i, 2) * 256, 256), 256), :])

        @pl.when(state == 0)
        def _():
            for c in range(4):
                o_ref[pl.ds(lc * 4 + c, 256, stride=8), :] = jnp.zeros((256, 128), F32)


def finish(slots, flags, front_rows, arrived, row_panels, col_panels, L, W):
    def child_spec(k):
        return pl.BlockSpec((1, 256, 256), lambda i, s, f: (jnp.maximum(s[i * 8 + k], 0), 0, 0))

    whole = lambda shape: pl.BlockSpec(shape, lambda i, s, f: (0,) * len(shape))
    return pl.pallas_call(
        finish_kernel,
        grid_spec=pltpu.PrefetchScalarGridSpec(
            num_scalar_prefetch=2,
            grid=(8,),
            in_specs=[pl.BlockSpec((2048, 128), lambda i, s, f: (i, 0))]
            + [child_spec(k) for k in range(8)]
            + [pl.BlockSpec((16, 1, 16, 512), lambda i, s, f: (0, i, 0, 0))] * 2
            + [whole((2, 16, 2, 16, 512))] * 2
            + [whole((512, 512))] * 2,
            out_specs=pl.BlockSpec((2048, 128), lambda i, s, f: (i, 0)),
        ),
        out_shape=jax.ShapeDtypeStruct(front_rows.shape, F32),
        cost_estimate=pl.CostEstimate(flops=5_000_000_000, bytes_accessed=28 * MIB, transcendentals=0),
        compiler_params=pltpu.CompilerParams(vmem_limit_bytes=48 * MIB),
    )(slots, flags, front_rows, *([arrived] * 8), *row_panels, *col_panels, L, W)


def slot_of_targets(codes, row_map, rows, cols):
    index = jnp.arange(CNB, dtype=jnp.int32)

    def place(blocks):
        hit = row_map[None] == blocks[:, None, None]
        return jnp.sum(jnp.where(hit, index + 1, 0), axis=-1) - 1

    pi, pj = place(rows), place(cols)
    child = jnp.arange(2, dtype=jnp.int32) * (CNB * CNB)
    wanted = child + pi[:, None, :] * CNB + pj[None, :, :]
    known = (pi[:, None, :] >= 0) & (pj[None, :, :] >= 0)
    wanted = jnp.where(known, wanted, -2).reshape(-1)
    number = jnp.arange(codes.shape[0], dtype=jnp.int32)
    return jnp.sum(jnp.where(wanted[:, None] == codes[None, :], number + 1, 0), axis=-1) - 1


def spread(x, axis, count):
    return lax.all_to_all(jnp.broadcast_to(x[None], (count,) + x.shape), axis, 0, 0, tiled=True)


def local(front, child_blocks, row_map, slot_table, struct_mask):
    prow, pcol = lax.axis_size("prow"), lax.axis_size("pcol")
    p, q = lax.axis_index("prow"), lax.axis_index("pcol")
    core = p % 2
    front_rows = front.reshape(16384, 128)
    child = child_blocks[0, 0]

    pair = jnp.arange(2, dtype=jnp.int32)
    row_blocks = jnp.arange(4, dtype=jnp.int32) * prow + p
    col_blocks = jnp.arange(2, dtype=jnp.int32) * pcol + q
    sub_rows = (2 * row_blocks[:, None] + pair).reshape(-1)
    sub_cols = (2 * col_blocks[:, None] + pair).reshape(-1)

    cut_child = child[:2].reshape(6, 16, 16, 256).transpose(1, 0, 2, 3)
    got_child = lax.all_to_all(cut_child, "pcol", 0, 0, tiled=True).reshape(96, 16, 256)
    cut_top = cut_strips(front_rows, 0, 2, pcol)
    got_top = lax.all_to_all(cut_top, "pcol", 0, 0, tiled=True)[:2]

    my_codes = lax.dynamic_index_in_dim(slot_table, p, 0, False)
    strip_slots = slot_of_targets(my_codes[:, :2].reshape(-1), row_map, sub_rows, jnp.arange(4, dtype=jnp.int32))
    slots = slot_of_targets(
        lax.dynamic_index_in_dim(my_codes, q, 1, False).reshape(-1), row_map, sub_rows, sub_cols
    )
    row_mask = struct_mask[sub_rows]
    lower = row_blocks[:, None] >= col_blocks[None, :]
    mask = row_mask[:, sub_cols]
    state = jnp.where(lower, 1, 0)
    owner = (q < 2) & (jnp.arange(2) == 0)
    state = jnp.where(owner[None, :] & lower, jnp.where(row_blocks[:, None] == q, 3, 2), state)
    flags = jnp.concatenate([mask.reshape(-1), jnp.repeat(state, 2, axis=0).reshape(-1)]).astype(jnp.int32)
    keep0 = (sub_rows >= 2).astype(jnp.int32)
    keep1 = jnp.concatenate([(sub_rows >= 4).astype(jnp.int32), row_mask[:, 2:4].reshape(-1)])

    top = join_strips(strip_slots, got_top, got_child, 0, 2)

    half_top = lax.all_to_all(jnp.tile(top, (prow // 2, 1, 1)), "prow", 0, 0, tiled=True)
    swap = [(i, i ^ 1) for i in range(prow)]

    def assemble(strip):
        mine = spread(strip, "pcol", pcol).reshape(256, -1)
        other = lax.ppermute(mine, "prow", swap)
        return jnp.concatenate(
            [jnp.where(core == 0, mine, other), jnp.where(core == 0, other, mine)], axis=0
        )

    D0 = assemble(half_top[0, :, :512])
    half_rest, front_rest, D0 = lax.optimization_barrier((half_top[1], front_rows, D0))
    L0, W0 = factor_first(D0)
    rest1 = assemble(half_rest)
    cut_low = cut_strips(front_rows, 2, 6, pcol)
    cut_low, rest1 = lax.optimization_barrier((cut_low, rest1))
    got_low = lax.all_to_all(cut_low, "pcol", 0, 0, tiled=True)[:2]
    child, got_low = lax.optimization_barrier((child, got_low))
    arrived = lax.all_to_all(child, "pcol", 0, 0, tiled=True).reshape(48, 256, 256)

    P10, L1, W1 = factor_second(struct_mask[2:4, 2:4].reshape(-1), rest1[:, :512], rest1[:, 512:], W0)
    low = join_strips(strip_slots, got_low, got_child, 2, 6)
    P0 = solve_strips(solve_first_kernel, keep0, top, low, W0)
    row0 = lax.all_gather(P0, "pcol")
    P1 = solve_strips(solve_second_kernel, keep1, top, low, P0, P10, W1)
    row1 = lax.all_gather(P1, "pcol")

    both = jnp.stack([P0, P1]).reshape(2, 4, 2, 16, 512).transpose(2, 0, 1, 3, 4)
    both = lax.all_to_all(jnp.tile(both, (prow // 2, 1, 1, 1, 1)), "prow", 0, 0, tiled=True)
    both = both.reshape(8, 2, 2, 2, 16, 512).transpose(3, 0, 1, 2, 4, 5).reshape(16, 2, 2, 16, 512)
    mine = lax.all_to_all(both, "pcol", 0, 0, tiled=True)
    other = lax.ppermute(mine, "prow", swap)
    ordered = jnp.stack([jnp.where(core == 0, mine, other), jnp.where(core == 0, other, mine)])

    L = jnp.where(q == 0, L0, L1)
    W = jnp.where(q == 0, W0, W1)
    out = finish(
        slots, flags, front_rows, arrived, (row0, row1), (ordered[:, :, 0], ordered[:, :, 1]), L, W
    )
    return out.reshape(front.shape)


def solution(mesh):
    in_specs = (
        P(None, "prow", None, None, "pcol", None),
        P("prow", "pcol", None, None, None, None),
        P(),
        P(),
        P(),
    )
    out_specs = P(None, "prow", None, None, "pcol", None)
    return jax.shard_map(local, mesh=mesh, in_specs=in_specs, out_specs=out_specs, check_vma=False)
```

time: 1030 us -> 373 us (0.36)
  other arithmetic: 346 us -> 6.27 us
  waiting for transfers between devices: 407 us -> 116 us
  local copies, waits for them, and re-layouts: 192 us -> 14.2 us
  blocking collectives: 0 us -> 96.2 us
  Pallas kernels: 0 us -> 90.9 us
  matrix products: 52.3 us -> 0 us
  starting transfers between devices: 9.72 us -> 30.6 us
    psum x6 -> x0, waiting for transfers between devices: 359 us -> none  [from_root(): return lax.psum(block, axis)]
    another operation x36 -> x1, other arithmetic: 247 us -> 0.14 us  [local(): jnp.stack([jnp.where(core == 0, mine, other), jnp.where(core == 0, other,...]
    all_to_all x0 -> x5, blocking collectives: none -> 96.2 us  [the longest x2 31.1 us: spread(): lax.all_to_all(jnp.broadcast_to(x[None], (count,) + x.shape), axis, 0, 0,...]
    pallas_call x0 -> x9, Pallas kernels: none -> 90.9 us  [the longest x1 28 us: factor_second(): pl.pallas_call(factor_second_kernel, out_shape=[jax.ShapeDtypeStruct((n,...]
    all_gather x0 -> x2, waiting for transfers between devices: none -> 90 us  [the longest x1 90 us: local(): row1 = lax.all_gather(P1, 'pcol')]
    another operation x42 -> x3, local copies, waits for them, and re-layouts: 67.4 us -> 1.15 us  [the longest x1 0.95 us: local(): jnp.tile(top, (prow // 2, 1, 1))]
    another operation x26 -> x0, matrix products: 35.9 us -> none  [the longest x14 24.9 us: factor_panel(): solved = jax.scipy.linalg.solve_triangular(factor, right_side, lower=True)]
    reshape x3 -> x4, local copies, waits for them, and re-layouts: 36.7 us -> 1.24 us  [the longest x1 1 us: local(): cut_child = child[:2].reshape(6, 16, 16, 256).transpose(1, 0, 2, 3)]
  transfers between devices with their start and end apart: 7 -> 9, of which waited for: 7 -> 5; matrix products, arithmetic and copies ran while one was open for 12% -> 3% of each run, Pallas kernels for 0% -> 17%
where the time goes in v1:
time: 373 us; the launch traced here: 368 us
  waiting for transfers between devices  116 us (31%)
  blocking collectives  96.2 us (26%)
  Pallas kernels  90.9 us (24%)
  starting transfers between devices  30.6 us (8%)
  between operations  14.3 us (4%)
  local copies, waits for them, and re-layouts  14.2 us (4%)
  other arithmetic  6.27 us (2%)
    all_gather x1, waiting for transfers between devices, local(): row1 = lax.all_gather(P1, 'pcol')  90 us
    all_to_all x2, blocking collectives, spread(): lax.all_to_all(jnp.broadcast_to(x[None], (count,) + x.shape), axis, 0, 0,...  31.1 us
    all_to_all x1, blocking collectives, local(): mine = lax.all_to_all(both, 'pcol', 0, 0, tiled=True)  29.2 us
    pallas_call x1, Pallas kernels, factor_second(): pl.pallas_call(factor_second_kernel, out_shape=[jax.ShapeDtypeStruct((n,...  28 us
    pallas_call x1, Pallas kernels, factor_first(): pl.pallas_call(factor_first_kernel, out_shape=[jax.ShapeDtypeStruct((n, n...  26.2 us
    all_to_all x1, blocking collectives, local(): lax.all_to_all(jnp.tile(top, (prow // 2, 1, 1)), 'prow', 0, 0, tiled=True)  18.4 us
    pallas_call x1, Pallas kernels, finish(): pl.pallas_call(finish_kernel, grid_spec=pltpu.PrefetchScalarGridSpec(num_...  18.2 us
    all_to_all x1, blocking collectives, local(): lax.all_to_all(jnp.tile(both, (prow // 2, 1, 1, 1, 1)), 'prow', 0, 0, til...  17.5 us
  transfers between devices with their start and end apart: 9, of which 5 were waited for; matrix products, arithmetic and copies ran while one was open for 3% of the time, Pallas kernels for 17%

profile of v1, /device:TPU:1, one launch (start us, length us, event | category | flops | bytes accessed | tf_op | source)
XLA Modules:
  0.0 368.0 jit_solution(12114131084787198382)
XLA Ops:
  6.5 2.5 shard_map.56
  9.0 8.6 %all-to-all-start = ((f32[16,2,16,512]{3,2,1,0:T(8,128)}), f32[16,2,16,512]{3,2,1,0:T(8,128)S(1)}, u32[]{:S(2)}, u32[]{:S(2)}) async-start(f32[16,2,16,512]{3,2,1,0:T(8,128)} %shard_map.56), calls=%async_computation | async-start | bytes 2097152 | tf_op jit(solution)/shard_map/all_to_all | solution.py:341
  19.0 1.0 copy.67
  20.0 13.1 %all-to-all-done = f32[16,2,16,512]{3,2,1,0:T(8,128)S(1)} async-done(((f32[16,2,16,512]{3,2,1,0:T(8,128)}), f32[16,2,16,512]{3,2,1,0:T(8,128)S(1)}, u32[]{:S(2)}, u32[]{:S(2)}) %all-to-all-start) | async-done | bytes 1048608 | tf_op jit(solution)/shard_map/all_to_all | solution.py:341
  33.1 4.0 %all-to-all-start.1 = ((bf16[16,6,16,256]{3,2,1,0:T(8,128)(2,1)}), bf16[16,6,16,256]{3,2,1,0:T(8,128)(2,1)S(1)}, u32[]{:S(2)}, u32[]{:S(2)}) async-start(bf16[16,6,16,256]{3,2,1,0:T(8,128)(2,1)} %bitcast.51), calls=%async_computation.1 | async-start | bytes 1572864 | tf_op jit(solution)/shard_map/all_to_all | solution.py:339
  38.9 8.7 %all-to-all-done.1 = bf16[16,6,16,256]{3,2,1,0:T(8,128)(2,1)S(1)} async-done(((bf16[16,6,16,256]{3,2,1,0:T(8,128)(2,1)}), bf16[16,6,16,256]{3,2,1,0:T(8,128)(2,1)S(1)}, u32[]{:S(2)}, u32[]{:S(2)}) %all-to-all-start.1) | async-done | bytes 786464 | tf_op jit(solution)/shard_map/all_to_all | solution.py:339
  48.5 1.9 shard_map.57.d_ref
  50.4 0.9 tile.8
  51.4 18.4 %all_to_all.45 = f32[8,16,1024]{2,1,0:T(8,128)S(1)} all-to-all(f32[8,16,1024]{2,1,0:T(8,128)S(1)} %bitcast.67), channel_id=1, replica_groups=mesh['prow'=8,'pcol'=16] {'prow'}, dimensions={0} | all-to-all | bytes 1048576 | tf_op jit(solution)/shard_map/all_to_all | solution.py:360
  69.8 12.1 %all_to_all.46 = f32[16,16,512]{2,1,0:T(8,128)S(1)} all-to-all(f32[16,16,512]{2,1,0:T(8,128)S(1)} %broadcast_in_dim.115), channel_id=1, replica_groups=mesh['prow'=8,'pcol'=16] {'pcol'}, dimensions={0} | all-to-all | bytes 1048576 | tf_op jit(solution)/shard_map/all_to_all | solution.py:322
  81.9 3.4 collective-permute-start
  85.3 1.5 collective-permute-done
  87.2 19.0 %all_to_all.47 = f32[16,16,1024]{2,1,0:T(8,128)S(1)} all-to-all(f32[16,16,1024]{2,1,0:T(8,128)S(1)} %broadcast_in_dim.116), channel_id=1, replica_groups=mesh['prow'=8,'pcol'=16] {'pcol'}, dimensions={0} | all-to-all | bytes 2097152 | tf_op jit(solution)/shard_map/all_to_all | solution.py:322
  106.2 2.1 collective-permute-start.1
  108.4 6.1 %shard_map.55 = f32[16,6,16,512]{3,2,1,0:T(8,128)} custom-call(f32[16384,128]{1,0:T(8,128)} %bitcast.54), custom_call_target="tpu_custom_call" | custom-call | bytes 12582912 | tf_op jit(solution)/shard_map/pallas_call | solution.py:160
  117.2 4.5 %all-to-all-start.5 = ((f32[16,6,16,512]{3,2,1,0:T(8,128)}), f32[16,6,16,512]{3,2,1,0:T(8,128)}, u32[]{:S(2)}, u32[]{:S(2)}) async-start(f32[16,6,16,512]{3,2,1,0:T(8,128)} %shard_map.55), calls=%async_computation.5 | async-start | bytes 6291456 | tf_op jit(solution)/shard_map/all_to_all | solution.py:376
  121.9 26.2 %shard_map.59 = (f32[512,512]{1,0:T(8,128)S(1)}, f32[512,512]{1,0:T(8,128)S(1)}) custom-call(f32[512,512]{1,0:T(8,128)S(1)} %pad_maximum_fusion.2.d_ref), custom_call_target="tpu_custom_call" | custom-call | flops 20000000000 | bytes 3145728 | tf_op jit(solution)/shard_map/pallas_call | solution.py:128
  149.5 28.0 %shard_map.61 = (bf16[512,512]{1,0:T(8,128)(2,1)S(1)}, f32[512,512]{1,0:T(8,128)S(1)}, f32[512,512]{1,0:T(8,128)S(1)}) custom-call(s32[4]{0:T(128)S(1)} %reshape.291.mask_ref, f32[512,512]{1,0:T(8,128)S(1)} %get-tuple-element.34.below_ref, f32[512,512]{1,0:T(8,128)S(1)} %get-tuple-element.33.d_ref, f32[512,512]{1,0:T(8,128)S(1)} %get-tuple-element.21.w_ref.w0_ref), custom_call_target="tpu_custom_call" | custom-call | flops 20000000000 | bytes 3145728 | tf_op jit(solution)/shard_map/pallas_call | solution.py:141
  177.5 1.0 copy-done.4
  179.4 2.0 slice.57.f_ref
  181.4 2.1 shard_map.58.r_ref
  183.5 2.7 shard_map.60.p_ref
  186.3 3.1 shard_map.62
  190.5 17.5 %all_to_all.48 = bf16[8,2,4,16,512]{4,3,2,1,0:T(8,128)(2,1)S(1)} all-to-all(bf16[8,2,4,16,512]{4,3,2,1,0:T(8,128)(2,1)S(1)} %bitcast.61), channel_id=1, replica_groups=mesh['prow'=8,'pcol'=16] {'prow'}, dimensions={0} | all-to-all | bytes 2097152 | tf_op jit(solution)/shard_map/all_to_all | solution.py:388
  208.1 29.2 %all_to_all.49 = bf16[16,2,2,16,512]{4,3,2,1,0:T(8,128)(2,1)S(1)} all-to-all(bf16[16,2,2,16,512]{4,3,2,1,0:T(8,128)(2,1)S(1)} %bitcast.63), channel_id=1, replica_groups=mesh['prow'=8,'pcol'=16] {'pcol'}, dimensions={0} | all-to-all | bytes 2097152 | tf_op jit(solution)/shard_map/all_to_all | solution.py:390
  237.3 4.7 %all-to-all-start.6 = ((bf16[16,3,256,256]{3,2,1,0:T(8,128)(2,1)}), bf16[16,3,256,256]{3,2,1,0:T(8,128)(2,1)}, u32[]{:S(2)}, u32[]{:S(2)}) async-start(bf16[16,3,256,256]{3,2,1,0:T(8,128)(2,1)} %bitcast.56), calls=%async_computation.6 | async-start | bytes 12582912 | tf_op jit(solution)/shard_map/all_to_all | solution.py:378
  244.6 3.1 collective-permute-start.2
  248.4 1.6 collective-permute-done.2
  250.2 1.2 fusion.2
  251.3 90.0 %all-gather.7.cloned.1.call-done = bf16[128,16,512]{2,1,0:T(8,128)(2,1)} async-done(((bf16[8,16,512]{2,1,0:T(8,128)(2,1)}), bf16[128,16,512]{2,1,0:T(8,128)(2,1)}) %all-gather.7.cloned.1.call-update) | async-done | bytes 2097168 | tf_op jit(solution)/shard_map/all_gather | solution.py:385
  341.3 1.2 copy-done.1
  342.5 18.2 %shard_map.63 = f32[16384,128]{1,0:T(8,128)} custom-call(s32[64]{0:T(128)S(1)} %broadcast_add_fusion.3.slot_ref, s32[48]{0:T(128)S(1)} %pad_add_fusion.flag_ref, f32[16384,128]{1,0:T(8,128)} %bitcast.55, bf16[48,256,256]{2,1,0:T(8,128)(2,1)} %bitcast.14.refs_0_.refs_1_.refs_2_.refs_3_.refs_4_.refs_5_.refs_6_.refs_7_, ...), custom_call_target="tpu_custom_call" | custom-call | flops 5000000000 | bytes 29360128 | tf_op jit(solution)/shard_map/pallas_call | solution.py:287
  (121 shorter events, 14.1 us)
Async XLA Ops:
  6.5 30.7 %copy-start = (s32[8,16,16,3]{2,1,3,0:T(8,128)S(1)}, s32[8,16,16,3]{2,1,3,0:T(8,128)}, u32[]{:S(2)}) copy-start(s32[8,16,16,3]{2,1,3,0:T(8,128)} %param.8) | copy-start | bytes 73732
  9.0 8.9 %copy-start.16 = (s32[2,60]{1,0:T(2,128)S(1)}, s32[2,60]{1,0:T(2,128)}, u32[]{:S(2)}) copy-start(s32[2,60]{1,0:T(2,128)} %param.7) | copy-start | bytes 1444
  9.0 10.0 %slice-start = ((bf16[1,1,16,3,256,256]{5,4,3,2,1,0:T(8,128)(2,1)}), bf16[1,1,2,3,256,256]{5,4,3,2,1,0:T(8,128)(2,1)S(1)}, s32[]{:S(2)}) async-start(bf16[1,1,16,3,256,256]{5,4,3,2,1,0:T(8,128)(2,1)} %param.6), calls=%async_computation.11 | async-start | bytes 1572864 | tf_op jit(solution)/shard_map/slice | solution.py:338
  9.0 24.1 %all-to-all-start = ((f32[16,2,16,512]{3,2,1,0:T(8,128)}), f32[16,2,16,512]{3,2,1,0:T(8,128)S(1)}, u32[]{:S(2)}, u32[]{:S(2)}) async-start(f32[16,2,16,512]{3,2,1,0:T(8,128)} %shard_map.56), calls=%async_computation | async-start | bytes 2097152 | tf_op jit(solution)/shard_map/all_to_all | solution.py:341
  33.1 14.5 %all-to-all-start.1 = ((bf16[16,6,16,256]{3,2,1,0:T(8,128)(2,1)}), bf16[16,6,16,256]{3,2,1,0:T(8,128)(2,1)S(1)}, u32[]{:S(2)}, u32[]{:S(2)}) async-start(bf16[16,6,16,256]{3,2,1,0:T(8,128)(2,1)} %bitcast.51), calls=%async_computation.1 | async-start | bytes 1572864 | tf_op jit(solution)/shard_map/all_to_all | solution.py:339
  47.6 0.9 copy-start.13
  81.9 5.0 %collective-permute-start = (f32[256,512]{1,0:T(8,128)S(1)}, f32[256,512]{1,0:T(8,128)S(1)}, u32[]{:S(2)}, u32[]{:S(2)}) collective-permute-start(f32[256,512]{1,0:T(8,128)S(1)} %bitcast.66), channel_id=1, source_target_pairs={{0,16},{16,0},{32,48},{48,32},{64,80},{80,64},{96,112},{112,96},{1... | collective-permute-start | bytes 1572872 | tf_op jit(solution)/shard_map/ppermute | solution.py:365
  106.2 10.4 %collective-permute-start.1 = (f32[256,1024]{1,0:T(8,128)S(1)}, f32[256,1024]{1,0:T(8,128)S(1)}, u32[]{:S(2)}, u32[]{:S(2)}) collective-permute-start(f32[256,1024]{1,0:T(8,128)S(1)} %bitcast.60), channel_id=1, source_target_pairs={{0,16},{16,0},{32,48},{48,32},{64,80},{80,64},{96,112},{112,96},{1... | collective-permute-start | bytes 3145736 | tf_op jit(solution)/shard_map/ppermute | solution.py:365
  108.4 6.1 %copy-start.15 = (s32[64,64]{1,0:T(8,128)S(1)}, s32[64,64]{1,0:T(8,128)}, u32[]{:S(2)}) copy-start(s32[64,64]{1,0:T(8,128)} %param.9) | copy-start | bytes 49156
  117.2 62.2 %all-to-all-start.5 = ((f32[16,6,16,512]{3,2,1,0:T(8,128)}), f32[16,6,16,512]{3,2,1,0:T(8,128)}, u32[]{:S(2)}, u32[]{:S(2)}) async-start(f32[16,6,16,512]{3,2,1,0:T(8,128)} %shard_map.55), calls=%async_computation.5 | async-start | bytes 6291456 | tf_op jit(solution)/shard_map/all_to_all | solution.py:376
  121.7 129.7 %all-gather.5.cloned.1.call-start = ((), (), s32[]{:S(2)}) async-start(), calls=%async_computation.9 | async-start | bytes 2228224 | tf_op jit(solution)/shard_map/all_gather | solution.py:383
  148.1 1.0 copy-start.6
  148.1 1.4 copy-start.2
  177.5 1.0 copy-start.4
  178.5 0.8 copy-start.10
  179.3 6.9 %copy-start.8 = (f32[512,512]{1,0:T(8,128)}, f32[512,512]{1,0:T(8,128)S(1)}, u32[]{:S(2)}) copy-start(f32[512,512]{1,0:T(8,128)S(1)} %get-tuple-element.26) | copy-start | bytes 3145732
  186.2 3.2 copy-start.14
  237.3 7.2 %copy-start.11 = (bf16[16,2,2,16,512]{4,3,2,1,0:T(8,128)(2,1)}, bf16[16,2,2,16,512]{4,3,2,1,0:T(8,128)(2,1)S(1)}, u32[]{:S(2)}) copy-start(bf16[16,2,2,16,512]{4,3,2,1,0:T(8,128)(2,1)S(1)} %all_to_all.49) | copy-start | bytes 3145732
  237.3 104.0 %all-to-all-start.6 = ((bf16[16,3,256,256]{3,2,1,0:T(8,128)(2,1)}), bf16[16,3,256,256]{3,2,1,0:T(8,128)(2,1)}, u32[]{:S(2)}, u32[]{:S(2)}) async-start(bf16[16,3,256,256]{3,2,1,0:T(8,128)(2,1)} %bitcast.56), calls=%async_computation.6 | async-start | bytes 12582912 | tf_op jit(solution)/shard_map/all_to_all | solution.py:378
  242.0 5.9 %copy-start.3 = (f32[512,512]{1,0:T(8,128)S(1)}, f32[512,512]{1,0:T(8,128)}, u32[]{:S(2)}) copy-start(f32[512,512]{1,0:T(8,128)} %copy-done.2) | copy-start | bytes 3145732
  242.0 5.9 %copy-start.5 = (f32[512,512]{1,0:T(8,128)S(1)}, f32[512,512]{1,0:T(8,128)}, u32[]{:S(2)}) copy-start(f32[512,512]{1,0:T(8,128)} %copy-done.4) | copy-start | bytes 3145732
  242.1 99.2 %all-gather.7.cloned.1.call-start = ((), (), s32[]{:S(2)}) async-start(), calls=%async_computation.10 | async-start | bytes 2228224 | tf_op jit(solution)/shard_map/all_gather | solution.py:385
  244.6 3.5 copy-start.7
  244.6 3.5 copy-start.9
  244.6 5.4 %collective-permute-start.2 = (bf16[16,2,2,16,512]{4,3,2,0,1:T(8,128)(2,1)S(1)}, bf16[16,2,2,16,512]{4,3,2,0,1:T(8,128)(2,1)S(1)}, u32[]{:S(2)}, u32[]{:S(2)}) collective-permute-start(bf16[16,2,2,16,512]{4,3,2,0,1:T(8,128)(2,1)S(1)} %copy.60), channel_id=1, source_target_pairs={{0,16},{16,0},{32,48},{48,32},{64,80},{80,64},{96,112},{112,96},{1... | collective-permute-start | bytes 3145736 | tf_op jit(solution)/shard_map/ppermute | solution.py:391
  248.1 1.9 copy-start.12
  341.3 1.2 copy-start.1
Sparse Core Ops, SparseCore 0:
  186.4 52.3 all-gather.4
  245.0 96.1 all-gather.6

commit v2 on v1

--- a/solution.py
+++ b/solution.py
@@ -102,51 +102,69 @@
                 a_ref[j:, j : j + b] = a_ref[j:, j : j + b] - dot3(L[off:], L[off : off + b], NT)
 
 
-def factor_first_kernel(d_ref, l_ref, w_ref, a_ref):
-    a_ref[...] = d_ref[...]
+def place_rows(at_ref, pieces, put):
+    core, x, z = at_ref[0], at_ref[1], at_ref[2]
+    for ref, sub in zip(pieces, (core, 1 - core)):
+        for i in range(4):
+            for j in range(4):
+                strip = lax.rem(x + i, 4) * 4 + lax.rem(z + j, 4)
+                put(pl.ds(pl.multiple_of(sub * 256 + strip * 16, 16), 16), ref[i, j])
+
+
+def factor_first_kernel(at_ref, mine_ref, other_ref, l_ref, w_ref, a_ref):
+    def put(rows, value):
+        a_ref[rows, :] = value
+
+    place_rows(at_ref, (mine_ref, other_ref), put)
     factor_whole(a_ref, l_ref, w_ref)
 
 
-def factor_second_kernel(mask_ref, below_ref, d_ref, w0_ref, p_ref, l_ref, w_ref, a_ref):
-    panel = dot3(below_ref[...], w0_ref[...], NT).astype(BF16)
+def factor_second_kernel(at_ref, mask_ref, mine_ref, other_ref, w0_ref, p_ref, l_ref, w_ref, a_ref, b_ref):
+    n = a_ref.shape[0]
+
+    def put(rows, value):
+        b_ref[rows, :] = value[:, :n]
+        a_ref[rows, :] = value[:, n:]
+
+    place_rows(at_ref, (mine_ref, other_ref), put)
+    panel = dot3(b_ref[...], w0_ref[...], NT).astype(BF16)
     p_ref[...] = panel
-    n = panel.shape[0]
     h = n // 2
     for i in range(2):
         for j in range(i + 1):
             r, c = slice(i * h, (i + 1) * h), slice(j * h, (j + 1) * h)
             product = dot1(panel[r], panel[c], NT)
-            a_ref[r, c] = d_ref[r, c] - jnp.where(mask_ref[i * 2 + j] > 0, product, F32(0))
+            a_ref[r, c] = a_ref[r, c] - jnp.where(mask_ref[i * 2 + j] > 0, product, F32(0))
     factor_whole(a_ref, l_ref, w_ref)
 
 
 CHOL_COST = pl.CostEstimate(flops=20_000_000_000, bytes_accessed=3 * MIB, transcendentals=1024)
 
 
-def factor_first(D):
-    n = D.shape[0]
+def factor_first(at, mine, other):
+    n = mine.shape[-1]
     return pl.pallas_call(
         factor_first_kernel,
         out_shape=[jax.ShapeDtypeStruct((n, n), F32)] * 2,
-        in_specs=[VMEM],
+        in_specs=[SMEM, VMEM, VMEM],
         out_specs=[VMEM] * 2,
         scratch_shapes=[pltpu.VMEM((n, n), F32)],
         cost_estimate=CHOL_COST,
         compiler_params=pltpu.CompilerParams(vmem_limit_bytes=40 * MIB),
-    )(D)
-
-
-def factor_second(mask, below, D, W0):
-    n = D.shape[0]
+    )(at, mine, other)
+
+
+def factor_second(at, mask, mine, other, W0):
+    n = W0.shape[0]
     return pl.pallas_call(
         factor_second_kernel,
         out_shape=[jax.ShapeDtypeStruct((n, n), BF16)] + [jax.ShapeDtypeStruct((n, n), F32)] * 2,
-        in_specs=[SMEM, VMEM, VMEM, VMEM],
+        in_specs=[SMEM, SMEM, VMEM, VMEM, VMEM],
         out_specs=[VMEM] * 3,
-        scratch_shapes=[pltpu.VMEM((n, n), F32)],
+        scratch_shapes=[pltpu.VMEM((n, n), F32)] * 2,
         cost_estimate=CHOL_COST,
         compiler_params=pltpu.CompilerParams(vmem_limit_bytes=40 * MIB),
-    )(mask, below, D, W0)
+    )(at, mask, mine, other, W0)
 
 
 def cut_kernel(x_ref, o_ref):
@@ -229,6 +247,26 @@
     )(*operands)
 
 
+def deal_kernel(y_ref, *refs):
+    o_ref = refs[-1]
+    for panel in range(2):
+        for k in range(4):
+            row = lax.rem(y_ref[0] + k, 4) * 2
+            for c in range(2):
+                for lr in range(4):
+                    o_ref[(lr % 2) * 8 + row + c, panel, lr // 2] = refs[panel * 4 + k][c, lr]
+
+
+def deal(y, first, second):
+    return pl.pallas_call(
+        deal_kernel,
+        out_shape=jax.ShapeDtypeStruct((16, 2, 2, 16, 512), BF16),
+        in_specs=[SMEM] + [VMEM] * 8,
+        out_specs=VMEM,
+        cost_estimate=pl.CostEstimate(flops=0, bytes_accessed=4 * MIB, transcendentals=0),
+    )(y, *first, *second)
+
+
 def finish_kernel(slot_ref, flag_ref, f_ref, *refs):
     child = refs[:8]
     row_refs = refs[8:10]
@@ -318,10 +356,6 @@
     return jnp.sum(jnp.where(wanted[:, None] == codes[None, :], number + 1, 0), axis=-1) - 1
 
 
-def spread(x, axis, count):
-    return lax.all_to_all(jnp.broadcast_to(x[None], (count,) + x.shape), axis, 0, 0, tiled=True)
-
-
 def local(front, child_blocks, row_map, slot_table, struct_mask):
     prow, pcol = lax.axis_size("prow"), lax.axis_size("pcol")
     p, q = lax.axis_index("prow"), lax.axis_index("pcol")
@@ -357,37 +391,56 @@
 
     top = join_strips(strip_slots, got_top, got_child, 0, 2)
 
-    half_top = lax.all_to_all(jnp.tile(top, (prow // 2, 1, 1)), "prow", 0, 0, tiled=True)
-    swap = [(i, i ^ 1) for i in range(prow)]
+    y, x, z = p // 2, q // 4, q % 4
+    at = jnp.stack([core, x, z]).astype(jnp.int32)
+    swap = [(i, i ^ 1) for i in range(8)]
+    along_y = lambda k: [(2 * ((i + k) % 4) + c, 2 * i + c) for i in range(4) for c in range(2)]
+    along_x = lambda k: [(4 * ((i + k) % 4) + j, 4 * i + j) for i in range(4) for j in range(4)]
+    along_z = lambda k: [(4 * j + (i + k) % 4, 4 * j + i) for i in range(4) for j in range(4)]
+    got = lax.ppermute(jnp.where(core == 0, top[1], top[0]), "prow", swap)
+    kept = jnp.where(core == 0, top[0], top[1])
+    first = jnp.where(core == 0, kept, got)[:, :512]
+    rest = jnp.where(core == 0, got, kept)
+    both = jnp.concatenate([first, rest], axis=1)
+    sent = [lax.ppermute(both, "prow", [(c, 2 * k + c) for c in range(2)]) for k in range(1, 4)]
+    both = jnp.where(y == 0, both, sent[0] + sent[1] + sent[2])
 
     def assemble(strip):
-        mine = spread(strip, "pcol", pcol).reshape(256, -1)
-        other = lax.ppermute(mine, "prow", swap)
-        return jnp.concatenate(
-            [jnp.where(core == 0, mine, other), jnp.where(core == 0, other, mine)], axis=0
-        )
-
-    D0 = assemble(half_top[0, :, :512])
-    half_rest, front_rest, D0 = lax.optimization_barrier((half_top[1], front_rows, D0))
-    L0, W0 = factor_first(D0)
-    rest1 = assemble(half_rest)
+        ring = jnp.stack([strip] + [lax.ppermute(strip, "pcol", along_z(k)) for k in range(1, 4)])
+        mine = jnp.stack([ring] + [lax.ppermute(ring, "pcol", along_x(k)) for k in range(1, 4)])
+        return mine, lax.ppermute(mine, "prow", swap)
+
+    def gather_columns(strips):
+        halves = strips.reshape(4, 2, 16, 512)
+        even, odd = halves[:, 0], halves[:, 1]
+        got = lax.ppermute(jnp.where(core == 0, odd, even), "prow", swap)
+        kept = jnp.where(core == 0, even, odd)
+        chip = jnp.where(core == 0, jnp.stack([kept, got]), jnp.stack([got, kept]))
+        return [chip] + [lax.ppermute(chip, "prow", along_y(k)) for k in range(1, 4)]
+
+    top0 = assemble(both[:, :512])
+    top1 = assemble(both[:, 512:])
+
     cut_low = cut_strips(front_rows, 2, 6, pcol)
-    cut_low, rest1 = lax.optimization_barrier((cut_low, rest1))
+    cut_low, top = lax.optimization_barrier((cut_low, top))
     got_low = lax.all_to_all(cut_low, "pcol", 0, 0, tiled=True)[:2]
     child, got_low = lax.optimization_barrier((child, got_low))
     arrived = lax.all_to_all(child, "pcol", 0, 0, tiled=True).reshape(48, 256, 256)
 
-    P10, L1, W1 = factor_second(struct_mask[2:4, 2:4].reshape(-1), rest1[:, :512], rest1[:, 512:], W0)
+    L0, W0 = factor_first(at, *top0)
     low = join_strips(strip_slots, got_low, got_child, 2, 6)
     P0 = solve_strips(solve_first_kernel, keep0, top, low, W0)
     row0 = lax.all_gather(P0, "pcol")
+    P0, top1 = lax.optimization_barrier((P0, top1))
+    cols0 = gather_columns(P0)
+    P10, L1, W1 = factor_second(at, struct_mask[2:4, 2:4].reshape(-1), *top1, W0)
     P1 = solve_strips(solve_second_kernel, keep1, top, low, P0, P10, W1)
     row1 = lax.all_gather(P1, "pcol")
-
-    both = jnp.stack([P0, P1]).reshape(2, 4, 2, 16, 512).transpose(2, 0, 1, 3, 4)
-    both = lax.all_to_all(jnp.tile(both, (prow // 2, 1, 1, 1, 1)), "prow", 0, 0, tiled=True)
-    both = both.reshape(8, 2, 2, 2, 16, 512).transpose(3, 0, 1, 2, 4, 5).reshape(16, 2, 2, 16, 512)
-    mine = lax.all_to_all(both, "pcol", 0, 0, tiled=True)
+    cols1 = gather_columns(P1)
+
+    dealt = deal(y.reshape(1).astype(jnp.int32), cols0, cols1)
+    dealt, arrived = lax.optimization_barrier((dealt, arrived))
+    mine = lax.all_to_all(dealt, "pcol", 0, 0, tiled=True)
     other = lax.ppermute(mine, "prow", swap)
     ordered = jnp.stack([jnp.where(core == 0, mine, other), jnp.where(core == 0, other, mine)])
 

time: 373 us -> 361 us (0.968)
  blocking collectives: 96.2 us -> 0 us
  starting transfers between devices: 30.6 us -> 99 us
  waiting for transfers between devices: 116 us -> 125 us
    all_to_all x5 -> x0, blocking collectives: 96.2 us -> none  [the longest x2 31.1 us: spread(): lax.all_to_all(jnp.broadcast_to(x[None], (count,) + x.shape), axis, 0, 0,...]
    ppermute x2 -> x26, waiting for transfers between devices: 1.53 us -> 94.2 us  [the longest x6 45 us: assemble(): lax.ppermute(strip, 'pcol', along_z(k))]
    all_gather x1, waiting for transfers between devices: 90 us -> 0.01 us  [local(): row1 = lax.all_gather(P1, 'pcol')]
    ppermute x2 -> x26, starting transfers between devices: 5.53 us -> 59 us  [the longest x6 24.2 us: assemble(): lax.ppermute(ring, 'pcol', along_x(k))]
    all_to_all x0 -> x1, waiting for transfers between devices: none -> 14.7 us  [local(): mine = lax.all_to_all(dealt, 'pcol', 0, 0, tiled=True)]
    all_to_all x0 -> x1, starting transfers between devices: none -> 11.2 us  [local(): mine = lax.all_to_all(dealt, 'pcol', 0, 0, tiled=True)]
    all_to_all x1, waiting for transfers between devices: 13.1 us -> 6.92 us  [local(): got_top = lax.all_to_all(cut_top, 'pcol', 0, 0, tiled=True)[:2]]
    unnamed x34 -> x48, local copies, waits for them, and re-layouts: 5.14 us -> 7.59 us
  transfers between devices with their start and end apart: 9 -> 34, of which waited for: 5 -> 20; matrix products, arithmetic and copies ran while one was open for 3% -> 4% of each run, Pallas kernels for 17% -> 20%
where the time goes in v2:
time: 361 us; the launch traced here: 354 us
  waiting for transfers between devices  125 us (35%)
  starting transfers between devices  99 us (27%)
  Pallas kernels  94.3 us (26%)
  local copies, waits for them, and re-layouts  14.9 us (4%)
  between operations  14.1 us (4%)
  other arithmetic  7.01 us (2%)
    ppermute x6, waiting for transfers between devices, assemble(): lax.ppermute(strip, 'pcol', along_z(k))  45 us
    ppermute x6, waiting for transfers between devices, assemble(): lax.ppermute(ring, 'pcol', along_x(k))  37.6 us
    pallas_call x1, Pallas kernels, factor_second(): pl.pallas_call(factor_second_kernel, out_shape=[jax.ShapeDtypeStruct((n,...  28 us
    pallas_call x1, Pallas kernels, factor_first(): pl.pallas_call(factor_first_kernel, out_shape=[jax.ShapeDtypeStruct((n, n...  27 us
    ppermute x6, starting transfers between devices, assemble(): lax.ppermute(ring, 'pcol', along_x(k))  24.2 us
    pallas_call x1, Pallas kernels, finish(): pl.pallas_call(finish_kernel, grid_spec=pltpu.PrefetchScalarGridSpec(num_...  18.1 us
    all_to_all x1, waiting for transfers between devices, local(): mine = lax.all_to_all(dealt, 'pcol', 0, 0, tiled=True)  14.7 us
    all_to_all x1, starting transfers between devices, local(): mine = lax.all_to_all(dealt, 'pcol', 0, 0, tiled=True)  11.2 us
  transfers between devices with their start and end apart: 34, of which 20 were waited for; matrix products, arithmetic and copies ran while one was open for 4% of the time, Pallas kernels for 20%

profile of v2, /device:TPU:1, one launch (start us, length us, event | category | flops | bytes accessed | tf_op | source)
XLA Modules:
  0.0 354.3 jit_solution(15818480347404266676)
XLA Ops:
  6.5 2.5 shard_map.56
  9.1 8.4 %all-to-all-start = ((f32[16,2,16,512]{3,2,1,0:T(8,128)}), f32[16,2,16,512]{3,2,1,0:T(8,128)S(1)}, u32[]{:S(2)}, u32[]{:S(2)}) async-start(f32[16,2,16,512]{3,2,1,0:T(8,128)} %shard_map.56), calls=%async_computation | async-start | bytes 2097152 | tf_op jit(solution)/shard_map/all_to_all | solution.py:375
  17.5 6.2 %shard_map.55 = f32[16,6,16,512]{3,2,1,0:T(8,128)} custom-call(f32[16384,128]{1,0:T(8,128)} %bitcast.99), custom_call_target="tpu_custom_call" | custom-call | bytes 12582912 | tf_op jit(solution)/shard_map/pallas_call | solution.py:178
  26.1 6.9 %all-to-all-done = f32[16,2,16,512]{3,2,1,0:T(8,128)S(1)} async-done(((f32[16,2,16,512]{3,2,1,0:T(8,128)}), f32[16,2,16,512]{3,2,1,0:T(8,128)S(1)}, u32[]{:S(2)}, u32[]{:S(2)}) %all-to-all-start) | async-done | bytes 1048608 | tf_op jit(solution)/shard_map/all_to_all | solution.py:375
  33.0 4.0 %all-to-all-start.1 = ((bf16[16,6,16,256]{3,2,1,0:T(8,128)(2,1)}), bf16[16,6,16,256]{3,2,1,0:T(8,128)(2,1)S(1)}, u32[]{:S(2)}, u32[]{:S(2)}) async-start(bf16[16,6,16,256]{3,2,1,0:T(8,128)(2,1)} %bitcast.96), calls=%async_computation.1 | async-start | bytes 1572864 | tf_op jit(solution)/shard_map/all_to_all | solution.py:373
  38.8 8.7 %all-to-all-done.1 = bf16[16,6,16,256]{3,2,1,0:T(8,128)(2,1)S(1)} async-done(((bf16[16,6,16,256]{3,2,1,0:T(8,128)(2,1)}), bf16[16,6,16,256]{3,2,1,0:T(8,128)(2,1)S(1)}, u32[]{:S(2)}, u32[]{:S(2)}) %all-to-all-start.1) | async-done | bytes 786464 | tf_op jit(solution)/shard_map/all_to_all | solution.py:373
  50.3 4.6 %all-to-all-start.2 = ((f32[16,6,16,512]{3,2,1,0:T(8,128)}), f32[16,6,16,512]{3,2,1,0:T(8,128)}, u32[]{:S(2)}, u32[]{:S(2)}) async-start(f32[16,6,16,512]{3,2,1,0:T(8,128)} %shard_map.55), calls=%async_computation.2 | async-start | bytes 6291456 | tf_op jit(solution)/shard_map/all_to_all | solution.py:426
  55.0 4.8 %collective-permute-start = (f32[16,1024]{1,0:T(8,128)S(1)}, f32[16,1024]{1,0:T(8,128)S(1)}, u32[]{:S(2)}, u32[]{:S(2)}) collective-permute-start(f32[16,1024]{1,0:T(8,128)S(1)} %select_bitcast_fusion.6), channel_id=1, source_target_pairs={{0,16},{16,0},{32,48},{48,32},{64,80},{80,64},{96,112},{112,96},{1... | collective-permute-start | bytes 196616 | tf_op jit(solution)/shard_map/ppermute | solution.py:400
  60.7 4.6 %collective-permute-start.3 = (f32[16,1536]{1,0:T(8,128)S(1)}, f32[16,1536]{1,0:T(8,128)S(1)}, u32[]{:S(2)}, u32[]{:S(2)}) collective-permute-start(f32[16,1536]{1,0:T(8,128)S(1)} %pad_maximum_fusion.5), channel_id=1, source_target_pairs={{0,96},{16,112},{1,97},{17,113},{2,98},{18,114},{3,99},{19,115},{4... | collective-permute-start | bytes 294920 | tf_op jit(solution)/shard_map/ppermute | solution.py:405
  70.6 3.0 collective-permute-start.5
  75.2 12.1 %collective-permute-done.5 = f32[16,512]{1,0:T(8,128)S(1)} collective-permute-done((f32[16,512]{1,0:T(8,128)S(1)}, f32[16,512]{1,0:T(8,128)S(1)}, u32[]{:S(2)}, u32[]{:S(2)}) %collective-permute-start.5) | collective-permute-done | bytes 32800 | tf_op jit(solution)/shard_map/ppermute | solution.py:409
  89.4 2.6 collective-permute-start.8
  92.0 3.7 %collective-permute-start.7 = (f32[4,16,512]{2,1,0:T(8,128)S(1)}, f32[4,16,512]{2,1,0:T(8,128)S(1)}, u32[]{:S(2)}, u32[]{:S(2)}) collective-permute-start(f32[4,16,512]{2,1,0:T(8,128)S(1)} %get-tuple-element.48), channel_id=1, source_target_pairs={{4,0},{5,1},{6,2},{7,3},{8,4},{9,5},{10,6},{11,7},{12,8},{13,9},{1... | collective-permute-start | bytes 393224 | tf_op jit(solution)/shard_map/ppermute | solution.py:410
  96.3 2.5 collective-permute-done.7
  98.8 2.8 collective-permute-done.9
  101.6 4.6 %collective-permute-start.10 = (f32[4,4,16,512]{3,2,1,0:T(8,128)S(1)}, f32[4,4,16,512]{3,2,1,0:T(8,128)S(1)}, u32[]{:S(2)}, u32[]{:S(2)}) collective-permute-start(f32[4,4,16,512]{3,2,1,0:T(8,128)S(1)} %pad_maximum_fusion.2.mine_ref), channel_id=1, source_target_pairs={{0,16},{16,0},{32,48},{48,32},{64,80},{80,64},{96,112},{112,96},{1... | collective-permute-start | bytes 1572872 | tf_op jit(solution)/shard_map/ppermute | solution.py:411
  108.6 5.3 %all-to-all-start.3 = ((bf16[16,3,256,256]{3,2,1,0:T(8,128)(2,1)}), bf16[16,3,256,256]{3,2,1,0:T(8,128)(2,1)}, u32[]{:S(2)}, u32[]{:S(2)}) async-start(bf16[16,3,256,256]{3,2,1,0:T(8,128)(2,1)} %bitcast.101), calls=%async_computation.3 | async-start | bytes 12582912 | tf_op jit(solution)/shard_map/all_to_all | solution.py:428
  114.1 27.0 %shard_map.59 = (f32[512,512]{1,0:T(8,128)S(1)}, f32[512,512]{1,0:T(8,128)S(1)}) custom-call(s32[3]{0:T(128)S(1)} %pad_add_fusion.1.at_ref, f32[4,4,16,512]{3,2,1,0:T(8,128)S(1)} %pad_maximum_fusion.2.mine_ref, f32[4,4,16,512]{3,2,1,0:T(8,128)S(1)} %collective-permute-done.10.other_ref), custom_call_target="tpu_custom_call" | custom-call | flops 20000000000 | bytes 3145728 | tf_op jit(solution)/shard_map/pallas_call | solution.py:146
  145.3 2.8 shard_map.60.p_ref
  148.2 3.1 collective-permute-start.12
  152.8 19.0 %collective-permute-done.12 = f32[16,1024]{1,0:T(8,128)S(1)} collective-permute-done((f32[16,1024]{1,0:T(8,128)S(1)}, f32[16,1024]{1,0:T(8,128)S(1)}, u32[]{:S(2)}, u32[]{:S(2)}) %collective-permute-start.12) | collective-permute-done | bytes 65568 | tf_op jit(solution)/shard_map/ppermute | solution.py:409
  171.8 11.7 %collective-permute-done.11 = f32[16,1024]{1,0:T(8,128)S(1)} collective-permute-done((f32[16,1024]{1,0:T(8,128)S(1)}, f32[16,1024]{1,0:T(8,128)S(1)}, u32[]{:S(2)}, u32[]{:S(2)}) %collective-permute-start.11) | collective-permute-done | bytes 65568 | tf_op jit(solution)/shard_map/ppermute | solution.py:409
  183.6 17.3 %collective-permute-start.14 = (f32[4,16,1024]{2,1,0:T(8,128)S(1)}, f32[4,16,1024]{2,1,0:T(8,128)S(1)}, u32[]{:S(2)}, u32[]{:S(2)}) collective-permute-start(f32[4,16,1024]{2,1,0:T(8,128)S(1)} %get-tuple-element.42), channel_id=1, source_target_pairs={{4,0},{5,1},{6,2},{7,3},{8,4},{9,5},{10,6},{11,7},{12,8},{13,9},{1... | collective-permute-start | bytes 786440 | tf_op jit(solution)/shard_map/ppermute | solution.py:410
  201.5 25.9 %collective-permute-done.15 = f32[4,16,1024]{2,1,0:T(8,128)S(1)} collective-permute-done((f32[4,16,1024]{2,1,0:T(8,128)S(1)}, f32[4,16,1024]{2,1,0:T(8,128)S(1)}, u32[]{:S(2)}, u32[]{:S(2)}) %collective-permute-start.15) | collective-permute-done | bytes 262176 | tf_op jit(solution)/shard_map/ppermute | solution.py:410
  227.4 5.8 %collective-permute-done.16 = f32[4,16,1024]{2,1,0:T(8,128)S(1)} collective-permute-done((f32[4,16,1024]{2,1,0:T(8,128)S(1)}, f32[4,16,1024]{2,1,0:T(8,128)S(1)}, u32[]{:S(2)}, u32[]{:S(2)}) %collective-permute-start.16) | collective-permute-done | bytes 262176 | tf_op jit(solution)/shard_map/ppermute | solution.py:410
  236.5 28.0 %shard_map.61 = (bf16[512,512]{1,0:T(8,128)(2,1)S(1)}, f32[512,512]{1,0:T(8,128)S(1)}, f32[512,512]{1,0:T(8,128)S(1)}) custom-call(s32[3]{0:T(128)S(1)} %pad_add_fusion.1.at_ref, s32[4]{0:T(128)S(1)} %reshape.319.mask_ref, f32[4,4,16,1024]{3,2,1,0:T(8,128)S(1)} %pad_maximum_fusion.1.mine_ref, f32[4,4,16,1024]{3,2,1,0:T(8,128)S(1)} %collective-permute-done.17.other_ref, ...), custom_call_target="tpu_custom_call" | custom-call | flops 20000000000 | bytes 3145728 | tf_op jit(solution)/shard_map/pallas_call | solution.py:159
  267.4 3.1 shard_map.62
  281.7 3.8 %collective-permute-done.25.refs_7_ = bf16[2,4,16,512]{3,2,1,0:T(8,128)(2,1)S(1)} collective-permute-done((bf16[2,4,16,512]{3,2,1,0:T(8,128)(2,1)S(1)}, bf16[2,4,16,512]{3,2,1,0:T(8,128)(2,1)S(1)}, u32[]{:S(2)}, u32[]{:S(2)}) %collective-permute-start.25) | collective-permute-done | bytes 131104 | tf_op jit(solution)/shard_map/ppermute | solution.py:419
  290.5 11.2 %all-to-all-start.4 = ((bf16[16,2,2,16,512]{4,3,2,1,0:T(8,128)(2,1)}), bf16[16,2,2,16,512]{4,3,2,1,0:T(8,128)(2,1)S(1)}, u32[]{:S(2)}, u32[]{:S(2)}) async-start(bf16[16,2,2,16,512]{4,3,2,1,0:T(8,128)(2,1)} %shard_map.63), calls=%async_computation.4 | async-start | bytes 2097152 | tf_op jit(solution)/shard_map/all_to_all | solution.py:443
  303.2 14.7 %all-to-all-done.4 = bf16[16,2,2,16,512]{4,3,2,1,0:T(8,128)(2,1)S(1)} async-done(((bf16[16,2,2,16,512]{4,3,2,1,0:T(8,128)(2,1)}), bf16[16,2,2,16,512]{4,3,2,1,0:T(8,128)(2,1)S(1)}, u32[]{:S(2)}, u32[]{:S(2)}) %all-to-all-start.4) | async-done | bytes 1048608 | tf_op jit(solution)/shard_map/all_to_all | solution.py:443
  318.0 6.2 %collective-permute-start.26 = (bf16[16,2,2,16,512]{4,3,2,0,1:T(8,128)(2,1)S(1)}, bf16[16,2,2,16,512]{4,3,2,0,1:T(8,128)(2,1)S(1)}, u32[]{:S(2)}, u32[]{:S(2)}) collective-permute-start(bf16[16,2,2,16,512]{4,3,2,0,1:T(8,128)(2,1)S(1)} %copy.56), channel_id=1, source_target_pairs={{0,16},{16,0},{32,48},{48,32},{64,80},{80,64},{96,112},{112,96},{1... | collective-permute-start | bytes 3145736 | tf_op jit(solution)/shard_map/ppermute | solution.py:444
  329.1 18.1 %shard_map.64 = f32[16384,128]{1,0:T(8,128)} custom-call(s32[64]{0:T(128)S(1)} %broadcast_add_fusion.3.slot_ref, s32[48]{0:T(128)S(1)} %pad_add_fusion.flag_ref, f32[16384,128]{1,0:T(8,128)} %bitcast.100, bf16[48,256,256]{2,1,0:T(8,128)(2,1)} %bitcast.39.refs_0_.refs_1_.refs_2_.refs_3_.refs_4_.refs_5_.refs_6_.refs_7_, ...), custom_call_target="tpu_custom_call" | custom-call | flops 5000000000 | bytes 29360128 | tf_op jit(solution)/shard_map/pallas_call | solution.py:325
  (183 shorter events, 54.8 us)
Async XLA Ops:
  9.1 23.9 %all-to-all-start = ((f32[16,2,16,512]{3,2,1,0:T(8,128)}), f32[16,2,16,512]{3,2,1,0:T(8,128)S(1)}, u32[]{:S(2)}, u32[]{:S(2)}) async-start(f32[16,2,16,512]{3,2,1,0:T(8,128)} %shard_map.56), calls=%async_computation | async-start | bytes 2097152 | tf_op jit(solution)/shard_map/all_to_all | solution.py:375
  33.0 14.5 %all-to-all-start.1 = ((bf16[16,6,16,256]{3,2,1,0:T(8,128)(2,1)}), bf16[16,6,16,256]{3,2,1,0:T(8,128)(2,1)S(1)}, u32[]{:S(2)}, u32[]{:S(2)}) async-start(bf16[16,6,16,256]{3,2,1,0:T(8,128)(2,1)} %bitcast.96), calls=%async_computation.1 | async-start | bytes 1572864 | tf_op jit(solution)/shard_map/all_to_all | solution.py:373
  50.3 56.4 %all-to-all-start.2 = ((f32[16,6,16,512]{3,2,1,0:T(8,128)}), f32[16,6,16,512]{3,2,1,0:T(8,128)}, u32[]{:S(2)}, u32[]{:S(2)}) async-start(f32[16,6,16,512]{3,2,1,0:T(8,128)} %shard_map.55), calls=%async_computation.2 | async-start | bytes 6291456 | tf_op jit(solution)/shard_map/all_to_all | solution.py:426
  55.0 5.7 %collective-permute-start = (f32[16,1024]{1,0:T(8,128)S(1)}, f32[16,1024]{1,0:T(8,128)S(1)}, u32[]{:S(2)}, u32[]{:S(2)}) collective-permute-start(f32[16,1024]{1,0:T(8,128)S(1)} %select_bitcast_fusion.6), channel_id=1, source_target_pairs={{0,16},{16,0},{32,48},{48,32},{64,80},{80,64},{96,112},{112,96},{1... | collective-permute-start | bytes 196616 | tf_op jit(solution)/shard_map/ppermute | solution.py:400
  60.7 7.3 %collective-permute-start.3 = (f32[16,1536]{1,0:T(8,128)S(1)}, f32[16,1536]{1,0:T(8,128)S(1)}, u32[]{:S(2)}, u32[]{:S(2)}) collective-permute-start(f32[16,1536]{1,0:T(8,128)S(1)} %pad_maximum_fusion.5), channel_id=1, source_target_pairs={{0,96},{16,112},{1,97},{17,113},{2,98},{18,114},{3,99},{19,115},{4... | collective-permute-start | bytes 294920 | tf_op jit(solution)/shard_map/ppermute | solution.py:405
  66.7 3.9 %collective-permute-start.1 = (f32[16,1536]{1,0:T(8,128)S(1)}, f32[16,1536]{1,0:T(8,128)S(1)}, u32[]{:S(2)}, u32[]{:S(2)}) collective-permute-start(f32[16,1536]{1,0:T(8,128)S(1)} %pad_maximum_fusion.5), channel_id=1, source_target_pairs={{0,32},{16,48},{1,33},{17,49},{2,34},{18,50},{3,35},{19,51},{4,36}... | collective-permute-start | bytes 294920 | tf_op jit(solution)/shard_map/ppermute | solution.py:405
  70.6 16.6 %collective-permute-start.5 = (f32[16,512]{1,0:T(8,128)S(1)}, f32[16,512]{1,0:T(8,128)S(1)}, u32[]{:S(2)}, u32[]{:S(2)}) collective-permute-start(f32[16,512]{1,0:T(8,128)S(1)} %get-tuple-element.52), channel_id=1, source_target_pairs={{2,0},{6,4},{10,8},{14,12},{3,1},{7,5},{11,9},{15,13},{0,2},{4,6},... | collective-permute-start | bytes 98312 | tf_op jit(solution)/shard_map/ppermute | solution.py:409
  73.7 15.7 %collective-permute-start.4 = (f32[16,512]{1,0:T(8,128)S(1)}, f32[16,512]{1,0:T(8,128)S(1)}, u32[]{:S(2)}, u32[]{:S(2)}) collective-permute-start(f32[16,512]{1,0:T(8,128)S(1)} %get-tuple-element.52), channel_id=1, source_target_pairs={{1,0},{5,4},{9,8},{13,12},{2,1},{6,5},{10,9},{14,13},{3,2},{7,6},{... | collective-permute-start | bytes 98312 | tf_op jit(solution)/shard_map/ppermute | solution.py:409
  74.6 14.9 %collective-permute-start.6 = (f32[16,512]{1,0:T(8,128)S(1)}, f32[16,512]{1,0:T(8,128)S(1)}, u32[]{:S(2)}, u32[]{:S(2)}) collective-permute-start(f32[16,512]{1,0:T(8,128)S(1)} %get-tuple-element.52), channel_id=1, source_target_pairs={{3,0},{7,4},{11,8},{15,12},{0,1},{4,5},{8,9},{12,13},{1,2},{5,6},{... | collective-permute-start | bytes 98312 | tf_op jit(solution)/shard_map/ppermute | solution.py:409
  89.4 6.9 %collective-permute-start.8 = (f32[4,16,512]{2,1,0:T(8,128)S(1)}, f32[4,16,512]{2,1,0:T(8,128)S(1)}, u32[]{:S(2)}, u32[]{:S(2)}) collective-permute-start(f32[4,16,512]{2,1,0:T(8,128)S(1)} %get-tuple-element.48), channel_id=1, source_target_pairs={{8,0},{9,1},{10,2},{11,3},{12,4},{13,5},{14,6},{15,7},{0,8},{1,9},... | collective-permute-start | bytes 393224 | tf_op jit(solution)/shard_map/ppermute | solution.py:410
  92.0 6.8 %collective-permute-start.7 = (f32[4,16,512]{2,1,0:T(8,128)S(1)}, f32[4,16,512]{2,1,0:T(8,128)S(1)}, u32[]{:S(2)}, u32[]{:S(2)}) collective-permute-start(f32[4,16,512]{2,1,0:T(8,128)S(1)} %get-tuple-element.48), channel_id=1, source_target_pairs={{4,0},{5,1},{6,2},{7,3},{8,4},{9,5},{10,6},{11,7},{12,8},{13,9},{1... | collective-permute-start | bytes 393224 | tf_op jit(solution)/shard_map/ppermute | solution.py:410
  95.7 5.8 %collective-permute-start.9 = (f32[4,16,512]{2,1,0:T(8,128)S(1)}, f32[4,16,512]{2,1,0:T(8,128)S(1)}, u32[]{:S(2)}, u32[]{:S(2)}) collective-permute-start(f32[4,16,512]{2,1,0:T(8,128)S(1)} %get-tuple-element.48), channel_id=1, source_target_pairs={{12,0},{13,1},{14,2},{15,3},{0,4},{1,5},{2,6},{3,7},{4,8},{5,9},{6... | collective-permute-start | bytes 393224 | tf_op jit(solution)/shard_map/ppermute | solution.py:410
  101.6 12.5 %collective-permute-start.10 = (f32[4,4,16,512]{3,2,1,0:T(8,128)S(1)}, f32[4,4,16,512]{3,2,1,0:T(8,128)S(1)}, u32[]{:S(2)}, u32[]{:S(2)}) collective-permute-start(f32[4,4,16,512]{3,2,1,0:T(8,128)S(1)} %pad_maximum_fusion.2.mine_ref), channel_id=1, source_target_pairs={{0,16},{16,0},{32,48},{48,32},{64,80},{80,64},{96,112},{112,96},{1... | collective-permute-start | bytes 1572872 | tf_op jit(solution)/shard_map/ppermute | solution.py:411
  108.6 181.9 %all-to-all-start.3 = ((bf16[16,3,256,256]{3,2,1,0:T(8,128)(2,1)}), bf16[16,3,256,256]{3,2,1,0:T(8,128)(2,1)}, u32[]{:S(2)}, u32[]{:S(2)}) async-start(bf16[16,3,256,256]{3,2,1,0:T(8,128)(2,1)} %bitcast.101), calls=%async_computation.3 | async-start | bytes 12582912 | tf_op jit(solution)/shard_map/all_to_all | solution.py:428
  113.9 214.0 %all-gather.5.cloned.1.call-start = ((), (), s32[]{:S(2)}) async-start(), calls=%async_computation.5 | async-start | bytes 2228224 | tf_op jit(solution)/shard_map/all_gather | solution.py:433
  148.1 179.8 %all-gather.7.cloned.1.call-start = ((), (), s32[]{:S(2)}) async-start(), calls=%async_computation.6 | async-start | bytes 2228224 | tf_op jit(solution)/shard_map/all_gather | solution.py:438
  148.2 23.6 %collective-permute-start.12 = (f32[16,1024]{1,0:T(8,128)S(1)}, f32[16,1024]{1,0:T(8,128)S(1)}, u32[]{:S(2)}, u32[]{:S(2)}) collective-permute-start(f32[16,1024]{1,0:T(8,128)S(1)} %get-tuple-element.50), channel_id=1, source_target_pairs={{2,0},{6,4},{10,8},{14,12},{3,1},{7,5},{11,9},{15,13},{0,2},{4,6},... | collective-permute-start | bytes 196616 | tf_op jit(solution)/shard_map/ppermute | solution.py:409
  151.3 32.2 %collective-permute-start.11 = (f32[16,1024]{1,0:T(8,128)S(1)}, f32[16,1024]{1,0:T(8,128)S(1)}, u32[]{:S(2)}, u32[]{:S(2)}) collective-permute-start(f32[16,1024]{1,0:T(8,128)S(1)} %get-tuple-element.50), channel_id=1, source_target_pairs={{1,0},{5,4},{9,8},{13,12},{2,1},{6,5},{10,9},{14,13},{3,2},{7,6},{... | collective-permute-start | bytes 196616 | tf_op jit(solution)/shard_map/ppermute | solution.py:409
  152.0 31.5 %collective-permute-start.13 = (f32[16,1024]{1,0:T(8,128)S(1)}, f32[16,1024]{1,0:T(8,128)S(1)}, u32[]{:S(2)}, u32[]{:S(2)}) collective-permute-start(f32[16,1024]{1,0:T(8,128)S(1)} %get-tuple-element.50), channel_id=1, source_target_pairs={{3,0},{7,4},{11,8},{15,12},{0,1},{4,5},{8,9},{12,13},{1,2},{5,6},{... | collective-permute-start | bytes 196616 | tf_op jit(solution)/shard_map/ppermute | solution.py:409
  183.5 43.9 %collective-permute-start.15 = (f32[4,16,1024]{2,1,0:T(8,128)S(1)}, f32[4,16,1024]{2,1,0:T(8,128)S(1)}, u32[]{:S(2)}, u32[]{:S(2)}) collective-permute-start(f32[4,16,1024]{2,1,0:T(8,128)S(1)} %get-tuple-element.42), channel_id=1, source_target_pairs={{8,0},{9,1},{10,2},{11,3},{12,4},{13,5},{14,6},{15,7},{0,8},{1,9},... | collective-permute-start | bytes 786440 | tf_op jit(solution)/shard_map/ppermute | solution.py:410
  183.6 43.8 %collective-permute-start.14 = (f32[4,16,1024]{2,1,0:T(8,128)S(1)}, f32[4,16,1024]{2,1,0:T(8,128)S(1)}, u32[]{:S(2)}, u32[]{:S(2)}) collective-permute-start(f32[4,16,1024]{2,1,0:T(8,128)S(1)} %get-tuple-element.42), channel_id=1, source_target_pairs={{4,0},{5,1},{6,2},{7,3},{8,4},{9,5},{10,6},{11,7},{12,8},{13,9},{1... | collective-permute-start | bytes 786440 | tf_op jit(solution)/shard_map/ppermute | solution.py:410
  201.0 32.3 %collective-permute-start.16 = (f32[4,16,1024]{2,1,0:T(8,128)S(1)}, f32[4,16,1024]{2,1,0:T(8,128)S(1)}, u32[]{:S(2)}, u32[]{:S(2)}) collective-permute-start(f32[4,16,1024]{2,1,0:T(8,128)S(1)} %get-tuple-element.42), channel_id=1, source_target_pairs={{12,0},{13,1},{14,2},{15,3},{0,4},{1,5},{2,6},{3,7},{4,8},{5,9},{6... | collective-permute-start | bytes 786440 | tf_op jit(solution)/shard_map/ppermute | solution.py:410
  233.3 3.2 collective-permute-start.17
  271.9 4.8 %collective-permute-start.22 = (bf16[4,16,512]{2,1,0:T(8,128)(2,1)S(1)}, bf16[4,16,512]{2,1,0:T(8,128)(2,1)S(1)}, u32[]{:S(2)}, u32[]{:S(2)}) collective-permute-start(bf16[4,16,512]{2,1,0:T(8,128)(2,1)S(1)} %get-tuple-element.44), channel_id=1, source_target_pairs={{0,16},{16,0},{32,48},{48,32},{64,80},{80,64},{96,112},{112,96},{1... | collective-permute-start | bytes 196616 | tf_op jit(solution)/shard_map/ppermute | solution.py:416
  272.1 6.0 %collective-permute-start.21 = (bf16[2,4,16,512]{3,2,1,0:T(8,128)(2,1)S(1)}, bf16[2,4,16,512]{3,2,1,0:T(8,128)(2,1)S(1)}, u32[]{:S(2)}, u32[]{:S(2)}) collective-permute-start(bf16[2,4,16,512]{3,2,1,0:T(8,128)(2,1)S(1)} %maximum_select_fusion.refs_0_), channel_id=1, source_target_pairs={{96,0},{112,16},{0,32},{16,48},{32,64},{48,80},{64,96},{80,112},{9... | collective-permute-start | bytes 393224 | tf_op jit(solution)/shard_map/ppermute | solution.py:419
  273.6 8.2 %collective-permute-start.20 = (bf16[2,4,16,512]{3,2,1,0:T(8,128)(2,1)S(1)}, bf16[2,4,16,512]{3,2,1,0:T(8,128)(2,1)S(1)}, u32[]{:S(2)}, u32[]{:S(2)}) collective-permute-start(bf16[2,4,16,512]{3,2,1,0:T(8,128)(2,1)S(1)} %maximum_select_fusion.refs_0_), channel_id=1, source_target_pairs={{64,0},{80,16},{96,32},{112,48},{0,64},{16,80},{32,96},{48,112},{6... | collective-permute-start | bytes 393224 | tf_op jit(solution)/shard_map/ppermute | solution.py:419
  275.7 6.1 %collective-permute-start.19 = (bf16[2,4,16,512]{3,2,1,0:T(8,128)(2,1)S(1)}, bf16[2,4,16,512]{3,2,1,0:T(8,128)(2,1)S(1)}, u32[]{:S(2)}, u32[]{:S(2)}) collective-permute-start(bf16[2,4,16,512]{3,2,1,0:T(8,128)(2,1)S(1)} %maximum_select_fusion.refs_0_), channel_id=1, source_target_pairs={{32,0},{48,16},{64,32},{80,48},{96,64},{112,80},{0,96},{16,112},{3... | collective-permute-start | bytes 393224 | tf_op jit(solution)/shard_map/ppermute | solution.py:419
  276.7 8.8 %collective-permute-start.25 = (bf16[2,4,16,512]{3,2,1,0:T(8,128)(2,1)S(1)}, bf16[2,4,16,512]{3,2,1,0:T(8,128)(2,1)S(1)}, u32[]{:S(2)}, u32[]{:S(2)}) collective-permute-start(bf16[2,4,16,512]{3,2,1,0:T(8,128)(2,1)S(1)} %maximum_select_fusion.1.refs_4_), channel_id=1, source_target_pairs={{96,0},{112,16},{0,32},{16,48},{32,64},{48,80},{64,96},{80,112},{9... | collective-permute-start | bytes 393224 | tf_op jit(solution)/shard_map/ppermute | solution.py:419
  277.3 10.1 %collective-permute-start.24 = (bf16[2,4,16,512]{3,2,1,0:T(8,128)(2,1)S(1)}, bf16[2,4,16,512]{3,2,1,0:T(8,128)(2,1)S(1)}, u32[]{:S(2)}, u32[]{:S(2)}) collective-permute-start(bf16[2,4,16,512]{3,2,1,0:T(8,128)(2,1)S(1)} %maximum_select_fusion.1.refs_4_), channel_id=1, source_target_pairs={{64,0},{80,16},{96,32},{112,48},{0,64},{16,80},{32,96},{48,112},{6... | collective-permute-start | bytes 393224 | tf_op jit(solution)/shard_map/ppermute | solution.py:419
  278.1 9.2 %collective-permute-start.23 = (bf16[2,4,16,512]{3,2,1,0:T(8,128)(2,1)S(1)}, bf16[2,4,16,512]{3,2,1,0:T(8,128)(2,1)S(1)}, u32[]{:S(2)}, u32[]{:S(2)}) collective-permute-start(bf16[2,4,16,512]{3,2,1,0:T(8,128)(2,1)S(1)} %maximum_select_fusion.1.refs_4_), channel_id=1, source_target_pairs={{32,0},{48,16},{64,32},{80,48},{96,64},{112,80},{0,96},{16,112},{3... | collective-permute-start | bytes 393224 | tf_op jit(solution)/shard_map/ppermute | solution.py:419
  290.5 27.4 %all-to-all-start.4 = ((bf16[16,2,2,16,512]{4,3,2,1,0:T(8,128)(2,1)}), bf16[16,2,2,16,512]{4,3,2,1,0:T(8,128)(2,1)S(1)}, u32[]{:S(2)}, u32[]{:S(2)}) async-start(bf16[16,2,2,16,512]{4,3,2,1,0:T(8,128)(2,1)} %shard_map.63), calls=%async_computation.4 | async-start | bytes 2097152 | tf_op jit(solution)/shard_map/all_to_all | solution.py:443
  318.0 8.5 %collective-permute-start.26 = (bf16[16,2,2,16,512]{4,3,2,0,1:T(8,128)(2,1)S(1)}, bf16[16,2,2,16,512]{4,3,2,0,1:T(8,128)(2,1)S(1)}, u32[]{:S(2)}, u32[]{:S(2)}) collective-permute-start(bf16[16,2,2,16,512]{4,3,2,0,1:T(8,128)(2,1)S(1)} %copy.56), channel_id=1, source_target_pairs={{0,16},{16,0},{32,48},{48,32},{64,80},{80,64},{96,112},{112,96},{1... | collective-permute-start | bytes 3145736 | tf_op jit(solution)/shard_map/ppermute | solution.py:444
  (27 other events, 372.7 us)
Sparse Core Ops, SparseCore 0:
  148.2 81.6 all-gather.4
  270.6 56.1 all-gather.6

commit v3 on v2

--- a/solution.py
+++ b/solution.py
@@ -112,8 +112,10 @@
 
 
 def factor_first_kernel(at_ref, mine_ref, other_ref, l_ref, w_ref, a_ref):
+    n = a_ref.shape[0]
+
     def put(rows, value):
-        a_ref[rows, :] = value
+        a_ref[rows, :] = value[:, :n]
 
     place_rows(at_ref, (mine_ref, other_ref), put)
     factor_whole(a_ref, l_ref, w_ref)
@@ -123,8 +125,8 @@
     n = a_ref.shape[0]
 
     def put(rows, value):
-        b_ref[rows, :] = value[:, :n]
-        a_ref[rows, :] = value[:, n:]
+        b_ref[rows, :] = value[:, n : 2 * n]
+        a_ref[rows, :] = value[:, 2 * n :]
 
     place_rows(at_ref, (mine_ref, other_ref), put)
     panel = dot3(b_ref[...], w0_ref[...], NT).astype(BF16)
@@ -142,7 +144,7 @@
 
 
 def factor_first(at, mine, other):
-    n = mine.shape[-1]
+    n = mine.shape[-1] // 3
     return pl.pallas_call(
         factor_first_kernel,
         out_shape=[jax.ShapeDtypeStruct((n, n), F32)] * 2,
@@ -371,8 +373,16 @@
 
     cut_child = child[:2].reshape(6, 16, 16, 256).transpose(1, 0, 2, 3)
     got_child = lax.all_to_all(cut_child, "pcol", 0, 0, tiled=True).reshape(96, 16, 256)
-    cut_top = cut_strips(front_rows, 0, 2, pcol)
-    got_top = lax.all_to_all(cut_top, "pcol", 0, 0, tiled=True)[:2]
+    cut = cut_strips(front_rows, 0, 8, pcol)
+    from_first = jnp.where(q == 0, cut[0], F32(0))
+    from_second = jnp.where(q == 1, cut[1], F32(0))
+    for k in range(1, 16):
+        after = (k + 1) % 16
+        piece = lax.dynamic_index_in_dim(cut, jnp.where(q == 0, k, after), 0, False)
+        piece = lax.ppermute(piece, "pcol", [(0, k), (1, after)])
+        from_first = from_first + jnp.where(q == k, piece, F32(0))
+        from_second = from_second + jnp.where(q == after, piece, F32(0))
+    fronts = jnp.stack([from_first, from_second])
 
     my_codes = lax.dynamic_index_in_dim(slot_table, p, 0, False)
     strip_slots = slot_of_targets(my_codes[:, :2].reshape(-1), row_map, sub_rows, jnp.arange(4, dtype=jnp.int32))
@@ -389,7 +399,8 @@
     keep0 = (sub_rows >= 2).astype(jnp.int32)
     keep1 = jnp.concatenate([(sub_rows >= 4).astype(jnp.int32), row_mask[:, 2:4].reshape(-1)])
 
-    top = join_strips(strip_slots, got_top, got_child, 0, 2)
+    top = join_strips(strip_slots, fronts[:, :2], got_child, 0, 2)
+    low = join_strips(strip_slots, fronts[:, 2:], got_child, 2, 6)
 
     y, x, z = p // 2, q // 4, q % 4
     at = jnp.stack([core, x, z]).astype(jnp.int32)
@@ -418,22 +429,16 @@
         chip = jnp.where(core == 0, jnp.stack([kept, got]), jnp.stack([got, kept]))
         return [chip] + [lax.ppermute(chip, "prow", along_y(k)) for k in range(1, 4)]
 
-    top0 = assemble(both[:, :512])
-    top1 = assemble(both[:, 512:])
-
-    cut_low = cut_strips(front_rows, 2, 6, pcol)
-    cut_low, top = lax.optimization_barrier((cut_low, top))
-    got_low = lax.all_to_all(cut_low, "pcol", 0, 0, tiled=True)[:2]
-    child, got_low = lax.optimization_barrier((child, got_low))
+    diag = assemble(both)
+    child, diag = lax.optimization_barrier((child, diag))
     arrived = lax.all_to_all(child, "pcol", 0, 0, tiled=True).reshape(48, 256, 256)
 
-    L0, W0 = factor_first(at, *top0)
-    low = join_strips(strip_slots, got_low, got_child, 2, 6)
+    L0, W0 = factor_first(at, *diag)
     P0 = solve_strips(solve_first_kernel, keep0, top, low, W0)
     row0 = lax.all_gather(P0, "pcol")
-    P0, top1 = lax.optimization_barrier((P0, top1))
+    P0, diag = lax.optimization_barrier((P0, diag))
     cols0 = gather_columns(P0)
-    P10, L1, W1 = factor_second(at, struct_mask[2:4, 2:4].reshape(-1), *top1, W0)
+    P10, L1, W1 = factor_second(at, struct_mask[2:4, 2:4].reshape(-1), *diag, W0)
     P1 = solve_strips(solve_second_kernel, keep1, top, low, P0, P10, W1)
     row1 = lax.all_gather(P1, "pcol")
     cols1 = gather_columns(P1)

time: 361 us -> 378 us (1.047)
  waiting for transfers between devices: 125 us -> 134 us
  other arithmetic: 7.01 us -> 13 us
  local copies, waits for them, and re-layouts: 14.9 us -> 20.1 us
    all_gather x1, waiting for transfers between devices: 0.01 us -> 44.6 us  [local(): row0 = lax.all_gather(P0, 'pcol')]
    ppermute x6 -> x3, waiting for transfers between devices: 45 us -> 2.49 us  [assemble(): lax.ppermute(strip, 'pcol', along_z(k))]
    ppermute x0 -> x15, waiting for transfers between devices: none -> 30.7 us  [local(): piece = lax.ppermute(piece, 'pcol', [(0, k), (1, after)])]
    ppermute x0 -> x15, starting transfers between devices: none -> 28.3 us  [local(): piece = lax.ppermute(piece, 'pcol', [(0, k), (1, after)])]
    ppermute x6 -> x3, waiting for transfers between devices: 37.6 us -> 14.6 us  [assemble(): lax.ppermute(ring, 'pcol', along_x(k))]
    ppermute x6 -> x3, starting transfers between devices: 24.2 us -> 7.05 us  [assemble(): lax.ppermute(ring, 'pcol', along_x(k))]
    all_to_all x1, waiting for transfers between devices: 0.01 us -> 14.4 us  [local(): lax.all_to_all(child, 'pcol', 0, 0, tiled=True).reshape(48, 256, 256)]
    all_to_all x2 -> x0, starting transfers between devices: 13 us -> none  [the longest x1 8.43 us: local(): got_top = lax.all_to_all(cut_top, 'pcol', 0, 0, tiled=True)[:2]]
  transfers between devices with their start and end apart: 34 -> 40, of which waited for: 20 -> 22; matrix products, arithmetic and copies ran while one was open for 4% -> 5% of each run, Pallas kernels for 20% -> 20%
where the time goes in v3:
time: 378 us; the launch traced here: 371 us
  waiting for transfers between devices  134 us (35%)
  starting transfers between devices  95.6 us (25%)
  Pallas kernels  93.6 us (25%)
  local copies, waits for them, and re-layouts  20.1 us (5%)
  between operations  14.5 us (4%)
  other arithmetic  13 us (3%)
    all_gather x1, waiting for transfers between devices, local(): row0 = lax.all_gather(P0, 'pcol')  44.6 us
    ppermute x15, waiting for transfers between devices, local(): piece = lax.ppermute(piece, 'pcol', [(0, k), (1, after)])  30.7 us
    ppermute x15, starting transfers between devices, local(): piece = lax.ppermute(piece, 'pcol', [(0, k), (1, after)])  28.3 us
    pallas_call x1, Pallas kernels, factor_second(): pl.pallas_call(factor_second_kernel, out_shape=[jax.ShapeDtypeStruct((n,...  28.1 us
    pallas_call x1, Pallas kernels, factor_first(): pl.pallas_call(factor_first_kernel, out_shape=[jax.ShapeDtypeStruct((n, n...  26.8 us
    pallas_call x1, Pallas kernels, finish(): pl.pallas_call(finish_kernel, grid_spec=pltpu.PrefetchScalarGridSpec(num_...  18.4 us
    ppermute x3, waiting for transfers between devices, assemble(): lax.ppermute(ring, 'pcol', along_x(k))  14.6 us
    all_to_all x1, waiting for transfers between devices, local(): lax.all_to_all(child, 'pcol', 0, 0, tiled=True).reshape(48, 256, 256)  14.4 us
  transfers between devices with their start and end apart: 40, of which 22 were waited for; matrix products, arithmetic and copies ran while one was open for 5% of the time, Pallas kernels for 20%

profile of v3, /device:TPU:1, one launch (start us, length us, event | category | flops | bytes accessed | tf_op | source)
XLA Modules:
  0.0 370.9 jit_solution(15666584395768413829)
XLA Ops:
  8.8 8.4 %all-to-all-start = ((bf16[16,6,16,256]{3,2,1,0:T(8,128)(2,1)}), bf16[16,6,16,256]{3,2,1,0:T(8,128)(2,1)S(1)}, u32[]{:S(2)}, u32[]{:S(2)}) async-start(bf16[16,6,16,256]{3,2,1,0:T(8,128)(2,1)} %bitcast.187), calls=%async_computation | async-start | bytes 1572864 | tf_op jit(solution)/shard_map/all_to_all | solution.py:375
  17.3 7.9 %shard_map.55 = f32[16,8,16,512]{3,2,1,0:T(8,128)} custom-call(f32[16384,128]{1,0:T(8,128)} %bitcast.189), custom_call_target="tpu_custom_call" | custom-call | bytes 16777216 | tf_op jit(solution)/shard_map/pallas_call | solution.py:180
  25.2 3.7 dynamic-slice_bitcast_fusion.14
  28.9 3.2 collective-permute-start
  32.1 4.0 %collective-permute-start.14 = (f32[8,16,512]{2,1,0:T(8,128)S(1)}, f32[8,16,512]{2,1,0:T(8,128)S(1)}, u32[]{:S(2)}, u32[]{:S(2)}) collective-permute-start(f32[8,16,512]{2,1,0:T(8,128)S(1)} %get-tuple-element.36), channel_id=1, source_target_pairs={{0,15},{1,0},{16,31},{17,16},{32,47},{33,32},{48,63},{49,48},{64,7... | collective-permute-start | bytes 786440 | tf_op jit(solution)/shard_map/ppermute | solution.py:382
  47.4 5.3 %collective-permute-done.12 = f32[8,16,512]{2,1,0:T(8,128)S(1)} collective-permute-done((f32[8,16,512]{2,1,0:T(8,128)S(1)}, f32[8,16,512]{2,1,0:T(8,128)S(1)}, u32[]{:S(2)}, u32[]{:S(2)}) %collective-permute-start.12) | collective-permute-done | bytes 262176 | tf_op jit(solution)/shard_map/ppermute | solution.py:382
  54.0 4.4 %collective-permute-done.11 = f32[8,16,512]{2,1,0:T(8,128)S(1)} collective-permute-done((f32[8,16,512]{2,1,0:T(8,128)}, f32[8,16,512]{2,1,0:T(8,128)S(1)}, u32[]{:S(2)}, u32[]{:S(2)}) %collective-permute-start.11) | collective-permute-done | bytes 262176 | tf_op jit(solution)/shard_map/ppermute | solution.py:382
  68.9 4.0 %collective-permute-done.6 = f32[8,16,512]{2,1,0:T(8,128)} collective-permute-done((f32[8,16,512]{2,1,0:T(8,128)}, f32[8,16,512]{2,1,0:T(8,128)}, u32[]{:S(2)}, u32[]{:S(2)}) %collective-permute-start.6) | collective-permute-done | bytes 262176 | tf_op jit(solution)/shard_map/ppermute | solution.py:382
  75.6 3.1 collective-permute-done.5
  78.8 6.1 %collective-permute-done.4 = f32[8,16,512]{2,1,0:T(8,128)} collective-permute-done((f32[8,16,512]{2,1,0:T(8,128)}, f32[8,16,512]{2,1,0:T(8,128)}, u32[]{:S(2)}, u32[]{:S(2)}) %collective-permute-start.4) | collective-permute-done | bytes 262176 | tf_op jit(solution)/shard_map/ppermute | solution.py:382
  84.9 5.6 %collective-permute-done.3 = f32[8,16,512]{2,1,0:T(8,128)} collective-permute-done((f32[8,16,512]{2,1,0:T(8,128)}, f32[8,16,512]{2,1,0:T(8,128)}, u32[]{:S(2)}, u32[]{:S(2)}) %collective-permute-start.3) | collective-permute-done | bytes 262176 | tf_op jit(solution)/shard_map/ppermute | solution.py:382
  102.7 4.6 %collective-permute-start.18 = (f32[16,1536]{1,0:T(8,128)S(1)}, f32[16,1536]{1,0:T(8,128)S(1)}, u32[]{:S(2)}, u32[]{:S(2)}) collective-permute-start(f32[16,1536]{1,0:T(8,128)S(1)} %pad_maximum_fusion.5), channel_id=1, source_target_pairs={{0,96},{16,112},{1,97},{17,113},{2,98},{18,114},{3,99},{19,115},{4... | collective-permute-start | bytes 294920 | tf_op jit(solution)/shard_map/ppermute | solution.py:416
  112.6 3.9 %collective-permute-start.21 = (f32[16,1536]{1,0:T(8,128)S(1)}, f32[16,1536]{1,0:T(8,128)S(1)}, u32[]{:S(2)}, u32[]{:S(2)}) collective-permute-start(f32[16,1536]{1,0:T(8,128)S(1)} %add_select_fusion), channel_id=1, source_target_pairs={{3,0},{7,4},{11,8},{15,12},{0,1},{4,5},{8,9},{12,13},{1,2},{5,6},{... | collective-permute-start | bytes 294920 | tf_op jit(solution)/shard_map/ppermute | solution.py:420
  116.4 2.5 collective-permute-start.19
  118.9 2.5 collective-permute-done.20
  121.6 7.0 %collective-permute-start.22 = (f32[4,16,1536]{2,1,0:T(8,128)S(1)}, f32[4,16,1536]{2,1,0:T(8,128)S(1)}, u32[]{:S(2)}, u32[]{:S(2)}) collective-permute-start(f32[4,16,1536]{2,1,0:T(8,128)S(1)} %get-tuple-element.55), channel_id=1, source_target_pairs={{4,0},{5,1},{6,2},{7,3},{8,4},{9,5},{10,6},{11,7},{12,8},{13,9},{1... | collective-permute-start | bytes 1179656 | tf_op jit(solution)/shard_map/ppermute | solution.py:421
  128.5 2.5 collective-permute-done.23
  131.0 12.1 %collective-permute-done.22 = f32[4,16,1536]{2,1,0:T(8,128)S(1)} collective-permute-done((f32[4,16,1536]{2,1,0:T(8,128)S(1)}, f32[4,16,1536]{2,1,0:T(8,128)S(1)}, u32[]{:S(2)}, u32[]{:S(2)}) %collective-permute-start.22) | collective-permute-done | bytes 393248 | tf_op jit(solution)/shard_map/ppermute | solution.py:421
  151.1 6.0 %all-to-all-start.1 = ((bf16[16,3,256,256]{3,2,1,0:T(8,128)(2,1)}), bf16[16,3,256,256]{3,2,1,0:T(8,128)(2,1)}, u32[]{:S(2)}, u32[]{:S(2)}) async-start(bf16[16,3,256,256]{3,2,1,0:T(8,128)(2,1)} %bitcast.191), calls=%async_computation.1 | async-start | bytes 12582912 | tf_op jit(solution)/shard_map/all_to_all | solution.py:434
  157.4 26.8 %shard_map.58 = (f32[512,512]{1,0:T(8,128)S(1)}, f32[512,512]{1,0:T(8,128)S(1)}) custom-call(s32[3]{0:T(128)S(1)} %pad_add_fusion.1.at_ref, f32[4,4,16,1536]{3,2,1,0:T(8,128)S(1)} %pad_maximum_fusion.mine_ref, f32[4,4,16,1536]{3,2,1,0:T(8,128)S(1)} %collective-permute-done.25.other_ref), custom_call_target="tpu_custom_call" | custom-call | flops 20000000000 | bytes 3145728 | tf_op jit(solution)/shard_map/pallas_call | solution.py:148
  186.2 2.7 shard_map.59.p_ref
  190.2 28.1 %shard_map.60 = (bf16[512,512]{1,0:T(8,128)(2,1)S(1)}, f32[512,512]{1,0:T(8,128)S(1)}, f32[512,512]{1,0:T(8,128)S(1)}) custom-call(s32[3]{0:T(128)S(1)} %pad_add_fusion.1.at_ref, s32[4]{0:T(128)S(1)} %reshape.325.mask_ref, f32[4,4,16,1536]{3,2,1,0:T(8,128)S(1)} %pad_maximum_fusion.mine_ref, f32[4,4,16,1536]{3,2,1,0:T(8,128)S(1)} %collective-permute-done.25.other_ref, ...), custom_call_target="tpu_custom_call" | custom-call | flops 20000000000 | bytes 3145728 | tf_op jit(solution)/shard_map/pallas_call | solution.py:161
  221.1 3.1 shard_map.61
  229.0 2.5 collective-permute-start.27
  235.9 3.2 collective-permute-done.33.refs_7_
  242.4 2.3 shard_map.62
  244.7 14.4 %all-to-all-done.1 = bf16[16,3,256,256]{3,2,1,0:T(8,128)(2,1)} async-done(((bf16[16,3,256,256]{3,2,1,0:T(8,128)(2,1)}), bf16[16,3,256,256]{3,2,1,0:T(8,128)(2,1)}, u32[]{:S(2)}, u32[]{:S(2)}) %all-to-all-start.1) | async-done | bytes 6291488 | tf_op jit(solution)/shard_map/all_to_all | solution.py:434
  259.1 13.9 %all-to-all-start.2 = ((bf16[16,2,2,16,512]{4,3,2,1,0:T(8,128)(2,1)}), bf16[16,2,2,16,512]{4,3,2,1,0:T(8,128)(2,1)S(1)}, u32[]{:S(2)}, u32[]{:S(2)}) async-start(bf16[16,2,2,16,512]{4,3,2,1,0:T(8,128)(2,1)} %shard_map.62), calls=%async_computation.2 | async-start | bytes 2097152 | tf_op jit(solution)/shard_map/all_to_all | solution.py:448
  274.6 14.3 %all-to-all-done.2 = bf16[16,2,2,16,512]{4,3,2,1,0:T(8,128)(2,1)S(1)} async-done(((bf16[16,2,2,16,512]{4,3,2,1,0:T(8,128)(2,1)}), bf16[16,2,2,16,512]{4,3,2,1,0:T(8,128)(2,1)S(1)}, u32[]{:S(2)}, u32[]{:S(2)}) %all-to-all-start.2) | async-done | bytes 1048608 | tf_op jit(solution)/shard_map/all_to_all | solution.py:448
  289.9 5.9 %collective-permute-start.34 = (bf16[16,2,2,16,512]{4,3,2,0,1:T(8,128)(2,1)S(1)}, bf16[16,2,2,16,512]{4,3,2,0,1:T(8,128)(2,1)S(1)}, u32[]{:S(2)}, u32[]{:S(2)}) collective-permute-start(bf16[16,2,2,16,512]{4,3,2,0,1:T(8,128)(2,1)S(1)} %copy.56), channel_id=1, source_target_pairs={{0,16},{16,0},{32,48},{48,32},{64,80},{80,64},{96,112},{112,96},{1... | collective-permute-start | bytes 3145736 | tf_op jit(solution)/shard_map/ppermute | solution.py:449
  299.4 44.6 %all-gather.5.cloned.1.call-done = bf16[128,16,512]{2,1,0:T(8,128)(2,1)} async-done(((bf16[8,16,512]{2,1,0:T(8,128)(2,1)}), bf16[128,16,512]{2,1,0:T(8,128)(2,1)}) %all-gather.5.cloned.1.call-update) | async-done | bytes 2097168 | tf_op jit(solution)/shard_map/all_gather | solution.py:438
  345.2 18.4 %shard_map.63 = f32[16384,128]{1,0:T(8,128)} custom-call(s32[64]{0:T(128)S(1)} %broadcast_add_fusion.3.slot_ref, s32[48]{0:T(128)S(1)} %pad_add_fusion.flag_ref, f32[16384,128]{1,0:T(8,128)} %bitcast.190, bf16[48,256,256]{2,1,0:T(8,128)(2,1)} %bitcast.50.refs_0_.refs_1_.refs_2_.refs_3_.refs_4_.refs_5_.refs_6_.refs_7_, ...), custom_call_target="tpu_custom_call" | custom-call | flops 5000000000 | bytes 29360128 | tf_op jit(solution)/shard_map/pallas_call | solution.py:327
  (200 shorter events, 79.0 us)
Async XLA Ops:
  8.8 86.1 %all-to-all-start = ((bf16[16,6,16,256]{3,2,1,0:T(8,128)(2,1)}), bf16[16,6,16,256]{3,2,1,0:T(8,128)(2,1)S(1)}, u32[]{:S(2)}, u32[]{:S(2)}) async-start(bf16[16,6,16,256]{3,2,1,0:T(8,128)(2,1)} %bitcast.187), calls=%async_computation | async-start | bytes 1572864 | tf_op jit(solution)/shard_map/all_to_all | solution.py:375
  28.9 12.6 %collective-permute-start = (f32[8,16,512]{2,1,0:T(8,128)S(1)}, f32[8,16,512]{2,1,0:T(8,128)S(1)}, u32[]{:S(2)}, u32[]{:S(2)}) collective-permute-start(f32[8,16,512]{2,1,0:T(8,128)S(1)} %get-tuple-element.35), channel_id=1, source_target_pairs={{0,1},{1,2},{16,17},{17,18},{32,33},{33,34},{48,49},{49,50},{64,65... | collective-permute-start | bytes 786440 | tf_op jit(solution)/shard_map/ppermute | solution.py:382
  32.1 10.7 %collective-permute-start.14 = (f32[8,16,512]{2,1,0:T(8,128)S(1)}, f32[8,16,512]{2,1,0:T(8,128)S(1)}, u32[]{:S(2)}, u32[]{:S(2)}) collective-permute-start(f32[8,16,512]{2,1,0:T(8,128)S(1)} %get-tuple-element.36), channel_id=1, source_target_pairs={{0,15},{1,0},{16,31},{17,16},{32,47},{33,32},{48,63},{49,48},{64,7... | collective-permute-start | bytes 786440 | tf_op jit(solution)/shard_map/ppermute | solution.py:382
  36.1 10.0 %collective-permute-start.13 = (f32[8,16,512]{2,1,0:T(8,128)S(1)}, f32[8,16,512]{2,1,0:T(8,128)S(1)}, u32[]{:S(2)}, u32[]{:S(2)}) collective-permute-start(f32[8,16,512]{2,1,0:T(8,128)S(1)} %get-tuple-element.37), channel_id=1, source_target_pairs={{0,14},{1,15},{16,30},{17,31},{32,46},{33,47},{48,62},{49,63},{64,... | collective-permute-start | bytes 786440 | tf_op jit(solution)/shard_map/ppermute | solution.py:382
  37.4 15.3 %collective-permute-start.12 = (f32[8,16,512]{2,1,0:T(8,128)S(1)}, f32[8,16,512]{2,1,0:T(8,128)S(1)}, u32[]{:S(2)}, u32[]{:S(2)}) collective-permute-start(f32[8,16,512]{2,1,0:T(8,128)S(1)} %get-tuple-element.38), channel_id=1, source_target_pairs={{0,13},{1,14},{16,29},{17,30},{32,45},{33,46},{48,61},{49,62},{64,... | collective-permute-start | bytes 786440 | tf_op jit(solution)/shard_map/ppermute | solution.py:382
  38.7 19.7 %collective-permute-start.11 = (f32[8,16,512]{2,1,0:T(8,128)}, f32[8,16,512]{2,1,0:T(8,128)S(1)}, u32[]{:S(2)}, u32[]{:S(2)}) collective-permute-start(f32[8,16,512]{2,1,0:T(8,128)} %get-tuple-element.39), channel_id=1, source_target_pairs={{0,12},{1,13},{16,28},{17,29},{32,44},{33,45},{48,60},{49,61},{64,... | collective-permute-start | bytes 786440 | tf_op jit(solution)/shard_map/ppermute | solution.py:382
  41.5 19.4 %collective-permute-start.10 = (f32[8,16,512]{2,1,0:T(8,128)}, f32[8,16,512]{2,1,0:T(8,128)S(1)}, u32[]{:S(2)}, u32[]{:S(2)}) collective-permute-start(f32[8,16,512]{2,1,0:T(8,128)} %get-tuple-element.40), channel_id=1, source_target_pairs={{0,11},{1,12},{16,27},{17,28},{32,43},{33,44},{48,59},{49,60},{64,... | collective-permute-start | bytes 786440 | tf_op jit(solution)/shard_map/ppermute | solution.py:382
  42.8 20.1 %collective-permute-start.9 = (f32[8,16,512]{2,1,0:T(8,128)}, f32[8,16,512]{2,1,0:T(8,128)S(1)}, u32[]{:S(2)}, u32[]{:S(2)}) collective-permute-start(f32[8,16,512]{2,1,0:T(8,128)} %get-tuple-element.41), channel_id=1, source_target_pairs={{0,10},{1,11},{16,26},{17,27},{32,42},{33,43},{48,58},{49,59},{64,... | collective-permute-start | bytes 786440 | tf_op jit(solution)/shard_map/ppermute | solution.py:382
  46.1 18.8 %collective-permute-start.8 = (f32[8,16,512]{2,1,0:T(8,128)}, f32[8,16,512]{2,1,0:T(8,128)S(1)}, u32[]{:S(2)}, u32[]{:S(2)}) collective-permute-start(f32[8,16,512]{2,1,0:T(8,128)} %get-tuple-element.42), channel_id=1, source_target_pairs={{0,9},{1,10},{16,25},{17,26},{32,41},{33,42},{48,57},{49,58},{64,7... | collective-permute-start | bytes 786440 | tf_op jit(solution)/shard_map/ppermute | solution.py:382
  52.7 14.2 %collective-permute-start.7 = (f32[8,16,512]{2,1,0:T(8,128)}, f32[8,16,512]{2,1,0:T(8,128)S(1)}, u32[]{:S(2)}, u32[]{:S(2)}) collective-permute-start(f32[8,16,512]{2,1,0:T(8,128)} %get-tuple-element.43), channel_id=1, source_target_pairs={{0,8},{1,9},{16,24},{17,25},{32,40},{33,41},{48,56},{49,57},{64,72... | collective-permute-start | bytes 786440 | tf_op jit(solution)/shard_map/ppermute | solution.py:382
  58.4 14.5 %collective-permute-start.6 = (f32[8,16,512]{2,1,0:T(8,128)}, f32[8,16,512]{2,1,0:T(8,128)}, u32[]{:S(2)}, u32[]{:S(2)}) collective-permute-start(f32[8,16,512]{2,1,0:T(8,128)} %get-tuple-element.44), channel_id=1, source_target_pairs={{0,7},{1,8},{16,23},{17,24},{32,39},{33,40},{48,55},{49,56},{64,71... | collective-permute-start | bytes 786440 | tf_op jit(solution)/shard_map/ppermute | solution.py:382
  60.9 17.9 %collective-permute-start.5 = (f32[8,16,512]{2,1,0:T(8,128)}, f32[8,16,512]{2,1,0:T(8,128)}, u32[]{:S(2)}, u32[]{:S(2)}) collective-permute-start(f32[8,16,512]{2,1,0:T(8,128)} %get-tuple-element.45), channel_id=1, source_target_pairs={{0,6},{1,7},{16,22},{17,23},{32,38},{33,39},{48,54},{49,55},{64,70... | collective-permute-start | bytes 786440 | tf_op jit(solution)/shard_map/ppermute | solution.py:382
  62.9 22.0 %collective-permute-start.4 = (f32[8,16,512]{2,1,0:T(8,128)}, f32[8,16,512]{2,1,0:T(8,128)}, u32[]{:S(2)}, u32[]{:S(2)}) collective-permute-start(f32[8,16,512]{2,1,0:T(8,128)} %get-tuple-element.46), channel_id=1, source_target_pairs={{0,5},{1,6},{16,21},{17,22},{32,37},{33,38},{48,53},{49,54},{64,69... | collective-permute-start | bytes 786440 | tf_op jit(solution)/shard_map/ppermute | solution.py:382
  64.9 25.6 %collective-permute-start.3 = (f32[8,16,512]{2,1,0:T(8,128)}, f32[8,16,512]{2,1,0:T(8,128)}, u32[]{:S(2)}, u32[]{:S(2)}) collective-permute-start(f32[8,16,512]{2,1,0:T(8,128)} %get-tuple-element.47), channel_id=1, source_target_pairs={{0,4},{1,5},{16,20},{17,21},{32,36},{33,37},{48,52},{49,53},{64,68... | collective-permute-start | bytes 786440 | tf_op jit(solution)/shard_map/ppermute | solution.py:382
  66.9 23.6 %collective-permute-start.2 = (f32[8,16,512]{2,1,0:T(8,128)}, f32[8,16,512]{2,1,0:T(8,128)}, u32[]{:S(2)}, u32[]{:S(2)}) collective-permute-start(f32[8,16,512]{2,1,0:T(8,128)} %get-tuple-element.48), channel_id=1, source_target_pairs={{0,3},{1,4},{16,19},{17,20},{32,35},{33,36},{48,51},{49,52},{64,67... | collective-permute-start | bytes 786440 | tf_op jit(solution)/shard_map/ppermute | solution.py:382
  72.9 17.6 %collective-permute-start.1 = (f32[8,16,512]{2,1,0:T(8,128)}, f32[8,16,512]{2,1,0:T(8,128)}, u32[]{:S(2)}, u32[]{:S(2)}) collective-permute-start(f32[8,16,512]{2,1,0:T(8,128)} %get-tuple-element.49), channel_id=1, source_target_pairs={{0,2},{1,3},{16,18},{17,19},{32,34},{33,35},{48,50},{49,51},{64,66... | collective-permute-start | bytes 786440 | tf_op jit(solution)/shard_map/ppermute | solution.py:382
  102.7 7.3 %collective-permute-start.18 = (f32[16,1536]{1,0:T(8,128)S(1)}, f32[16,1536]{1,0:T(8,128)S(1)}, u32[]{:S(2)}, u32[]{:S(2)}) collective-permute-start(f32[16,1536]{1,0:T(8,128)S(1)} %pad_maximum_fusion.5), channel_id=1, source_target_pairs={{0,96},{16,112},{1,97},{17,113},{2,98},{18,114},{3,99},{19,115},{4... | collective-permute-start | bytes 294920 | tf_op jit(solution)/shard_map/ppermute | solution.py:416
  112.6 6.4 %collective-permute-start.21 = (f32[16,1536]{1,0:T(8,128)S(1)}, f32[16,1536]{1,0:T(8,128)S(1)}, u32[]{:S(2)}, u32[]{:S(2)}) collective-permute-start(f32[16,1536]{1,0:T(8,128)S(1)} %add_select_fusion), channel_id=1, source_target_pairs={{3,0},{7,4},{11,8},{15,12},{0,1},{4,5},{8,9},{12,13},{1,2},{5,6},{... | collective-permute-start | bytes 294920 | tf_op jit(solution)/shard_map/ppermute | solution.py:420
  121.5 9.6 %collective-permute-start.23 = (f32[4,16,1536]{2,1,0:T(8,128)S(1)}, f32[4,16,1536]{2,1,0:T(8,128)S(1)}, u32[]{:S(2)}, u32[]{:S(2)}) collective-permute-start(f32[4,16,1536]{2,1,0:T(8,128)S(1)} %get-tuple-element.55), channel_id=1, source_target_pairs={{8,0},{9,1},{10,2},{11,3},{12,4},{13,5},{14,6},{15,7},{0,8},{1,9},... | collective-permute-start | bytes 1179656 | tf_op jit(solution)/shard_map/ppermute | solution.py:421
  121.6 21.6 %collective-permute-start.22 = (f32[4,16,1536]{2,1,0:T(8,128)S(1)}, f32[4,16,1536]{2,1,0:T(8,128)S(1)}, u32[]{:S(2)}, u32[]{:S(2)}) collective-permute-start(f32[4,16,1536]{2,1,0:T(8,128)S(1)} %get-tuple-element.55), channel_id=1, source_target_pairs={{4,0},{5,1},{6,2},{7,3},{8,4},{9,5},{10,6},{11,7},{12,8},{13,9},{1... | collective-permute-start | bytes 1179656 | tf_op jit(solution)/shard_map/ppermute | solution.py:421
  128.5 14.6 %collective-permute-start.24 = (f32[4,16,1536]{2,1,0:T(8,128)S(1)}, f32[4,16,1536]{2,1,0:T(8,128)S(1)}, u32[]{:S(2)}, u32[]{:S(2)}) collective-permute-start(f32[4,16,1536]{2,1,0:T(8,128)S(1)} %get-tuple-element.55), channel_id=1, source_target_pairs={{12,0},{13,1},{14,2},{15,3},{0,4},{1,5},{2,6},{3,7},{4,8},{5,9},{6... | collective-permute-start | bytes 1179656 | tf_op jit(solution)/shard_map/ppermute | solution.py:421
  143.3 7.9 %collective-permute-start.25 = (f32[4,4,16,1536]{3,2,1,0:T(8,128)S(1)}, f32[4,4,16,1536]{3,2,1,0:T(8,128)S(1)}, u32[]{:S(2)}, u32[]{:S(2)}) collective-permute-start(f32[4,4,16,1536]{3,2,1,0:T(8,128)S(1)} %pad_maximum_fusion.mine_ref), channel_id=1, source_target_pairs={{0,16},{16,0},{32,48},{48,32},{64,80},{80,64},{96,112},{112,96},{1... | collective-permute-start | bytes 4718600 | tf_op jit(solution)/shard_map/ppermute | solution.py:422
  151.1 108.0 %all-to-all-start.1 = ((bf16[16,3,256,256]{3,2,1,0:T(8,128)(2,1)}), bf16[16,3,256,256]{3,2,1,0:T(8,128)(2,1)}, u32[]{:S(2)}, u32[]{:S(2)}) async-start(bf16[16,3,256,256]{3,2,1,0:T(8,128)(2,1)} %bitcast.191), calls=%async_computation.1 | async-start | bytes 12582912 | tf_op jit(solution)/shard_map/all_to_all | solution.py:434
  157.2 142.2 %all-gather.7.cloned.1.call-start = ((), (), s32[]{:S(2)}) async-start(), calls=%async_computation.4 | async-start | bytes 2228224 | tf_op jit(solution)/shard_map/all_gather | solution.py:443
  224.3 119.7 %all-gather.5.cloned.1.call-start = ((), (), s32[]{:S(2)}) async-start(), calls=%async_computation.3 | async-start | bytes 2228224 | tf_op jit(solution)/shard_map/all_gather | solution.py:438
  226.7 6.8 %collective-permute-start.29 = (bf16[2,4,16,512]{3,2,1,0:T(8,128)(2,1)S(1)}, bf16[2,4,16,512]{3,2,1,0:T(8,128)(2,1)S(1)}, u32[]{:S(2)}, u32[]{:S(2)}) collective-permute-start(bf16[2,4,16,512]{3,2,1,0:T(8,128)(2,1)S(1)} %maximum_select_fusion.refs_0_), channel_id=1, source_target_pairs={{96,0},{112,16},{0,32},{16,48},{32,64},{48,80},{64,96},{80,112},{9... | collective-permute-start | bytes 393224 | tf_op jit(solution)/shard_map/ppermute | solution.py:430
  229.0 7.0 %collective-permute-start.27 = (bf16[2,4,16,512]{3,2,1,0:T(8,128)(2,1)S(1)}, bf16[2,4,16,512]{3,2,1,0:T(8,128)(2,1)S(1)}, u32[]{:S(2)}, u32[]{:S(2)}) collective-permute-start(bf16[2,4,16,512]{3,2,1,0:T(8,128)(2,1)S(1)} %maximum_select_fusion.refs_0_), channel_id=1, source_target_pairs={{32,0},{48,16},{64,32},{80,48},{96,64},{112,80},{0,96},{16,112},{3... | collective-permute-start | bytes 393224 | tf_op jit(solution)/shard_map/ppermute | solution.py:430
  231.5 7.7 %collective-permute-start.33 = (bf16[2,4,16,512]{3,2,1,0:T(8,128)(2,1)S(1)}, bf16[2,4,16,512]{3,2,1,0:T(8,128)(2,1)S(1)}, u32[]{:S(2)}, u32[]{:S(2)}) collective-permute-start(bf16[2,4,16,512]{3,2,1,0:T(8,128)(2,1)S(1)} %maximum_select_fusion.1.refs_4_), channel_id=1, source_target_pairs={{96,0},{112,16},{0,32},{16,48},{32,64},{48,80},{64,96},{80,112},{9... | collective-permute-start | bytes 393224 | tf_op jit(solution)/shard_map/ppermute | solution.py:430
  231.5 9.2 %collective-permute-start.32 = (bf16[2,4,16,512]{3,2,1,0:T(8,128)(2,1)S(1)}, bf16[2,4,16,512]{3,2,1,0:T(8,128)(2,1)S(1)}, u32[]{:S(2)}, u32[]{:S(2)}) collective-permute-start(bf16[2,4,16,512]{3,2,1,0:T(8,128)(2,1)S(1)} %maximum_select_fusion.1.refs_4_), channel_id=1, source_target_pairs={{64,0},{80,16},{96,32},{112,48},{0,64},{16,80},{32,96},{48,112},{6... | collective-permute-start | bytes 393224 | tf_op jit(solution)/shard_map/ppermute | solution.py:430
  233.5 8.2 %collective-permute-start.31 = (bf16[2,4,16,512]{3,2,1,0:T(8,128)(2,1)S(1)}, bf16[2,4,16,512]{3,2,1,0:T(8,128)(2,1)S(1)}, u32[]{:S(2)}, u32[]{:S(2)}) collective-permute-start(bf16[2,4,16,512]{3,2,1,0:T(8,128)(2,1)S(1)} %maximum_select_fusion.1.refs_4_), channel_id=1, source_target_pairs={{32,0},{48,16},{64,32},{80,48},{96,64},{112,80},{0,96},{16,112},{3... | collective-permute-start | bytes 393224 | tf_op jit(solution)/shard_map/ppermute | solution.py:430
  259.1 29.7 %all-to-all-start.2 = ((bf16[16,2,2,16,512]{4,3,2,1,0:T(8,128)(2,1)}), bf16[16,2,2,16,512]{4,3,2,1,0:T(8,128)(2,1)S(1)}, u32[]{:S(2)}, u32[]{:S(2)}) async-start(bf16[16,2,2,16,512]{4,3,2,1,0:T(8,128)(2,1)} %shard_map.62), calls=%async_computation.2 | async-start | bytes 2097152 | tf_op jit(solution)/shard_map/all_to_all | solution.py:448
  289.9 8.2 %collective-permute-start.34 = (bf16[16,2,2,16,512]{4,3,2,0,1:T(8,128)(2,1)S(1)}, bf16[16,2,2,16,512]{4,3,2,0,1:T(8,128)(2,1)S(1)}, u32[]{:S(2)}, u32[]{:S(2)}) collective-permute-start(bf16[16,2,2,16,512]{4,3,2,0,1:T(8,128)(2,1)S(1)} %copy.56), channel_id=1, source_target_pairs={{0,16},{16,0},{32,48},{48,32},{64,80},{80,64},{96,112},{112,96},{1... | collective-permute-start | bytes 3145736 | tf_op jit(solution)/shard_map/ppermute | solution.py:449
  (37 other events, 280.7 us)
Sparse Core Ops, SparseCore 0:
  224.4 73.8 all-gather.6
  300.4 43.5 all-gather.4

commit v4 on v2

--- a/solution.py
+++ b/solution.py
@@ -102,31 +102,18 @@
                 a_ref[j:, j : j + b] = a_ref[j:, j : j + b] - dot3(L[off:], L[off : off + b], NT)
 
 
-def place_rows(at_ref, pieces, put):
-    core, x, z = at_ref[0], at_ref[1], at_ref[2]
-    for ref, sub in zip(pieces, (core, 1 - core)):
-        for i in range(4):
-            for j in range(4):
-                strip = lax.rem(x + i, 4) * 4 + lax.rem(z + j, 4)
-                put(pl.ds(pl.multiple_of(sub * 256 + strip * 16, 16), 16), ref[i, j])
-
-
 def factor_first_kernel(at_ref, mine_ref, other_ref, l_ref, w_ref, a_ref):
-    def put(rows, value):
-        a_ref[rows, :] = value
-
-    place_rows(at_ref, (mine_ref, other_ref), put)
+    for ref, sub in ((mine_ref, at_ref[0]), (other_ref, 1 - at_ref[0])):
+        a_ref[pl.ds(pl.multiple_of(sub * 256, 256), 256), :] = ref[...].reshape(256, -1)
     factor_whole(a_ref, l_ref, w_ref)
 
 
 def factor_second_kernel(at_ref, mask_ref, mine_ref, other_ref, w0_ref, p_ref, l_ref, w_ref, a_ref, b_ref):
     n = a_ref.shape[0]
-
-    def put(rows, value):
-        b_ref[rows, :] = value[:, :n]
-        a_ref[rows, :] = value[:, n:]
-
-    place_rows(at_ref, (mine_ref, other_ref), put)
+    for ref, sub in ((mine_ref, at_ref[0]), (other_ref, 1 - at_ref[0])):
+        rows = pl.ds(pl.multiple_of(sub * 256, 256), 256)
+        b_ref[rows, :] = ref[:, :, :n].reshape(256, n)
+        a_ref[rows, :] = ref[:, :, n:].reshape(256, n)
     panel = dot3(b_ref[...], w0_ref[...], NT).astype(BF16)
     p_ref[...] = panel
     h = n // 2
@@ -167,44 +154,88 @@
     )(at, mask, mine, other, W0)
 
 
-def cut_kernel(x_ref, o_ref):
-    strips, _, rows, width = o_ref.shape
-    for c in range(width // 128):
-        tile = x_ref[pl.ds(c, strips * rows, stride=8), :]
-        o_ref[:, 0, :, c * 128 : (c + 1) * 128] = tile.reshape(strips, rows, 128)
-
-
-def cut_strips(front_rows, first, count, strips):
-    return pl.pallas_call(
-        cut_kernel,
-        grid=(count,),
-        out_shape=jax.ShapeDtypeStruct((strips, count, 16, 512), F32),
-        in_specs=[pl.BlockSpec((2048, 128), lambda i: (i + first, 0))],
-        out_specs=pl.BlockSpec((strips, 1, 16, 512), lambda i: (0, i, 0, 0)),
-        cost_estimate=pl.CostEstimate(flops=0, bytes_accessed=count * 2 * MIB, transcendentals=0),
-    )(front_rows)
-
-
-def join_kernel(first, slot_ref, f_ref, c_ref, o_ref):
-    count = o_ref.shape[0]
-    for i in range(count):
+def cut_top_kernel(x_ref, c_ref, o_ref):
+    for k in range(6):
+        o_ref[:, k] = c_ref[k].reshape(16, 16, 256)
+    for i in range(2):
+        for c in range(4):
+            high, low = split(x_ref[pl.ds(i * 2048 + c, 256, stride=8), :])
+            at = 6 + i * 4 + c // 2 * 2
+            lanes = slice(c % 2 * 128, c % 2 * 128 + 128)
+            o_ref[:, at, :, lanes] = high.reshape(16, 16, 128)
+            o_ref[:, at + 1, :, lanes] = low.reshape(16, 16, 128)
+
+
+def cut_top(front_rows, child):
+    return pl.pallas_call(
+        cut_top_kernel,
+        grid=(1,),
+        out_shape=jax.ShapeDtypeStruct((16, 14, 16, 256), BF16),
+        in_specs=[
+            pl.BlockSpec((4096, 128), lambda i: (0, 0)),
+            pl.BlockSpec((6, 256, 256), lambda i: (0, 0, 0)),
+        ],
+        out_specs=pl.BlockSpec((16, 14, 16, 256), lambda i: (0, 0, 0, 0)),
+        cost_estimate=pl.CostEstimate(flops=0, bytes_accessed=5 * MIB, transcendentals=0),
+        compiler_params=pltpu.CompilerParams(vmem_limit_bytes=40 * MIB),
+    )(front_rows, child)
+
+
+def cut_low_kernel(at_ref, x_ref, o_ref):
+    q = at_ref[1]
+    o_ref[...] = jnp.zeros(o_ref.shape, F32)
+    for owner in range(2):
+
+        @pl.when(q == owner)
+        def _():
+            for c in range(4):
+                tile = x_ref[pl.ds(c, 256, stride=8), :]
+                o_ref[:, 0, :, owner * 512 + c * 128 : owner * 512 + c * 128 + 128] = tile.reshape(16, 16, 128)
+
+
+def cut_low(at, front_rows):
+    return pl.pallas_call(
+        cut_low_kernel,
+        grid=(6,),
+        out_shape=jax.ShapeDtypeStruct((16, 6, 16, 1024), F32),
+        in_specs=[SMEM, pl.BlockSpec((2048, 128), lambda i: (i + 2, 0))],
+        out_specs=pl.BlockSpec((16, 1, 16, 1024), lambda i: (0, i, 0, 0)),
+        cost_estimate=pl.CostEstimate(flops=0, bytes_accessed=12 * MIB, transcendentals=0),
+    )(at, front_rows)
+
+
+def add_pieces(value, slot_ref, c_ref, row, j):
+    for child in range(2):
+        slot = slot_ref[(row * 4 + j) * 2 + child]
+        known = jnp.maximum(slot, 0)
+        piece = c_ref[known // 6, lax.rem(known, 6)].astype(F32)
+        value = value + jnp.where(slot >= 0, piece, F32(0))
+    return value
+
+
+def join_top_kernel(slot_ref, c_ref, o_ref):
+    for i in range(2):
         for j in range(4):
-            value = f_ref[j // 2, i, :, (j % 2) * 256 : (j % 2 + 1) * 256]
-            for child in range(2):
-                slot = slot_ref[((i + first) * 4 + j) * 2 + child]
-                piece = c_ref[jnp.maximum(slot, 0)].astype(F32)
-                value = value + jnp.where(slot >= 0, piece, F32(0))
-            o_ref[i, :, j * 256 : (j + 1) * 256] = value
-
-
-def join_strips(slots, front_strips, child_strips, first, count):
-    return pl.pallas_call(
-        functools.partial(join_kernel, first),
+            at = 6 + i * 4 + j % 2 * 2
+            value = c_ref[j // 2, at].astype(F32) + c_ref[j // 2, at + 1].astype(F32)
+            o_ref[i, :, j * 256 : (j + 1) * 256] = add_pieces(value, slot_ref, c_ref, i, j)
+
+
+def join_low_kernel(slot_ref, c_ref, f_ref, o_ref):
+    for i in range(6):
+        for j in range(4):
+            lanes = slice(j * 256, (j + 1) * 256)
+            o_ref[i, :, lanes] = add_pieces(f_ref[i, :, lanes], slot_ref, c_ref, i + 2, j)
+
+
+def join_strips(kernel, count, slots, *operands):
+    return pl.pallas_call(
+        kernel,
         out_shape=jax.ShapeDtypeStruct((count, 16, 1024), F32),
-        in_specs=[SMEM, VMEM, VMEM],
+        in_specs=[SMEM] + [VMEM] * len(operands),
         out_specs=VMEM,
         cost_estimate=pl.CostEstimate(flops=0, bytes_accessed=3 * MIB, transcendentals=0),
-    )(slots, front_strips, child_strips)
+    )(slots, *operands)
 
 
 def solve_first_kernel(keep_ref, d_ref, r_ref, w_ref, o_ref):
@@ -247,33 +278,43 @@
     )(*operands)
 
 
-def deal_kernel(y_ref, *refs):
+def deal_kernel(at_ref, p_ref, *refs):
     o_ref = refs[-1]
+    for q in range(16):
+        o_ref[q, 0:8] = p_ref[...]
     for panel in range(2):
         for k in range(4):
-            row = lax.rem(y_ref[0] + k, 4) * 2
+            row = lax.rem(at_ref[2] + k, 4) * 2
             for c in range(2):
                 for lr in range(4):
-                    o_ref[(lr % 2) * 8 + row + c, panel, lr // 2] = refs[panel * 4 + k][c, lr]
-
-
-def deal(y, first, second):
+                    o_ref[(lr % 2) * 8 + row + c, 8 + panel * 2 + lr // 2] = refs[panel * 4 + k][c, lr]
+
+
+def deal(at, P1, first, second):
     return pl.pallas_call(
         deal_kernel,
-        out_shape=jax.ShapeDtypeStruct((16, 2, 2, 16, 512), BF16),
-        in_specs=[SMEM] + [VMEM] * 8,
+        out_shape=jax.ShapeDtypeStruct((16, 12, 16, 512), BF16),
+        in_specs=[SMEM] + [VMEM] * 9,
         out_specs=VMEM,
-        cost_estimate=pl.CostEstimate(flops=0, bytes_accessed=4 * MIB, transcendentals=0),
-    )(y, *first, *second)
+        cost_estimate=pl.CostEstimate(flops=0, bytes_accessed=6 * MIB, transcendentals=0),
+    )(at, P1, *first, *second)
 
 
 def finish_kernel(slot_ref, flag_ref, f_ref, *refs):
     child = refs[:8]
-    row_refs = refs[8:10]
-    col_refs = refs[10:12]
-    l_ref, w_ref, o_ref = refs[12:15]
+    row0_ref, row1_ref, mine_ref, other_ref, l_ref, w_ref, o_ref, cols_ref = refs[8:]
     i = pl.program_id(0)
-    rows = jnp.concatenate([ref[:, 0].reshape(256, 512) for ref in row_refs], axis=1)
+
+    @pl.when(i == 0)
+    def _():
+        core = flag_ref[48]
+        for ref, sub in ((mine_ref, core), (other_ref, 1 - core)):
+            for panel in range(2):
+                for lc in range(2):
+                    strips = ref[:, panel * 2 + lc].reshape(256, 512)
+                    cols_ref[lc * 2 + sub, :, panel * 512 : (panel + 1) * 512] = strips
+
+    rows = jnp.concatenate([ref[:, 0].reshape(256, 512) for ref in (row0_ref, row1_ref)], axis=1)
     for lc in range(2):
         state = flag_ref[32 + i * 2 + lc]
 
@@ -282,14 +323,13 @@
             blocks = []
             for sc in range(2):
                 j = lc * 2 + sc
-                cols = jnp.concatenate([ref[sc, :, lc].reshape(256, 512) for ref in col_refs], axis=1)
                 value = jnp.concatenate(
                     [f_ref[pl.ds(lc * 4 + sc * 2 + c, 256, stride=8), :] for c in range(2)], axis=1
                 )
                 for ch in range(2):
                     live = slot_ref[(i * 4 + j) * 2 + ch] >= 0
                     value = value + jnp.where(live, child[j * 2 + ch][0].astype(F32), F32(0))
-                product = dot1(rows, cols, NT)
+                product = dot1(rows, cols_ref[j], NT)
                 blocks.append(value - jnp.where(flag_ref[i * 4 + j] > 0, product, F32(0)))
             block = jnp.concatenate(blocks, axis=1)
 
@@ -317,11 +357,14 @@
                 o_ref[pl.ds(lc * 4 + c, 256, stride=8), :] = jnp.zeros((256, 128), F32)
 
 
-def finish(slots, flags, front_rows, arrived, row_panels, col_panels, L, W):
+def finish(slots, flags, front_rows, arrived, row0, dealt, other, L, W):
     def child_spec(k):
         return pl.BlockSpec((1, 256, 256), lambda i, s, f: (jnp.maximum(s[i * 8 + k], 0), 0, 0))
 
-    whole = lambda shape: pl.BlockSpec(shape, lambda i, s, f: (0,) * len(shape))
+    def whole(shape, *at):
+        return pl.BlockSpec(shape, lambda i, s, f: at)
+
+    rows = pl.BlockSpec((16, 1, 16, 512), lambda i, s, f: (0, i, 0, 0))
     return pl.pallas_call(
         finish_kernel,
         grid_spec=pltpu.PrefetchScalarGridSpec(
@@ -329,15 +372,16 @@
             grid=(8,),
             in_specs=[pl.BlockSpec((2048, 128), lambda i, s, f: (i, 0))]
             + [child_spec(k) for k in range(8)]
-            + [pl.BlockSpec((16, 1, 16, 512), lambda i, s, f: (0, i, 0, 0))] * 2
-            + [whole((2, 16, 2, 16, 512))] * 2
-            + [whole((512, 512))] * 2,
+            + [rows, rows]
+            + [whole((16, 4, 16, 512), 0, 2, 0, 0), whole((16, 4, 16, 512), 0, 0, 0, 0)]
+            + [whole((512, 512), 0, 0)] * 2,
             out_specs=pl.BlockSpec((2048, 128), lambda i, s, f: (i, 0)),
+            scratch_shapes=[pltpu.VMEM((4, 256, 1024), BF16)],
         ),
         out_shape=jax.ShapeDtypeStruct(front_rows.shape, F32),
         cost_estimate=pl.CostEstimate(flops=5_000_000_000, bytes_accessed=28 * MIB, transcendentals=0),
         compiler_params=pltpu.CompilerParams(vmem_limit_bytes=48 * MIB),
-    )(slots, flags, front_rows, *([arrived] * 8), *row_panels, *col_panels, L, W)
+    )(slots, flags, front_rows, *([arrived] * 8), row0, dealt, dealt, other, L, W)
 
 
 def slot_of_targets(codes, row_map, rows, cols):
@@ -356,10 +400,16 @@
     return jnp.sum(jnp.where(wanted[:, None] == codes[None, :], number + 1, 0), axis=-1) - 1
 
 
+def spread(x, axis, count):
+    return lax.all_to_all(jnp.broadcast_to(x[None], (count,) + x.shape), axis, 0, 0, tiled=True)
+
+
 def local(front, child_blocks, row_map, slot_table, struct_mask):
     prow, pcol = lax.axis_size("prow"), lax.axis_size("pcol")
     p, q = lax.axis_index("prow"), lax.axis_index("pcol")
-    core = p % 2
+    core, y = p % 2, p // 2
+    at = jnp.stack([core, q, y]).astype(jnp.int32)
+    swap = [(i, i ^ 1) for i in range(8)]
     front_rows = front.reshape(16384, 128)
     child = child_blocks[0, 0]
 
@@ -369,10 +419,10 @@
     sub_rows = (2 * row_blocks[:, None] + pair).reshape(-1)
     sub_cols = (2 * col_blocks[:, None] + pair).reshape(-1)
 
-    cut_child = child[:2].reshape(6, 16, 16, 256).transpose(1, 0, 2, 3)
-    got_child = lax.all_to_all(cut_child, "pcol", 0, 0, tiled=True).reshape(96, 16, 256)
-    cut_top = cut_strips(front_rows, 0, 2, pcol)
-    got_top = lax.all_to_all(cut_top, "pcol", 0, 0, tiled=True)[:2]
+    got = lax.all_to_all(cut_top(front_rows, child.reshape(48, 256, 256)), "pcol", 0, 0, tiled=True)
+    low_front = lax.psum_scatter(
+        cut_low(at, front_rows).reshape(96, 16, 1024), "pcol", scatter_dimension=0, tiled=True
+    )
 
     my_codes = lax.dynamic_index_in_dim(slot_table, p, 0, False)
     strip_slots = slot_of_targets(my_codes[:, :2].reshape(-1), row_map, sub_rows, jnp.arange(4, dtype=jnp.int32))
@@ -385,70 +435,49 @@
     state = jnp.where(lower, 1, 0)
     owner = (q < 2) & (jnp.arange(2) == 0)
     state = jnp.where(owner[None, :] & lower, jnp.where(row_blocks[:, None] == q, 3, 2), state)
-    flags = jnp.concatenate([mask.reshape(-1), jnp.repeat(state, 2, axis=0).reshape(-1)]).astype(jnp.int32)
+    flags = jnp.concatenate([mask.reshape(-1), jnp.repeat(state, 2, axis=0).reshape(-1), core.reshape(1)])
+    flags = flags.astype(jnp.int32)
     keep0 = (sub_rows >= 2).astype(jnp.int32)
     keep1 = jnp.concatenate([(sub_rows >= 4).astype(jnp.int32), row_mask[:, 2:4].reshape(-1)])
 
-    top = join_strips(strip_slots, got_top, got_child, 0, 2)
-
-    y, x, z = p // 2, q // 4, q % 4
-    at = jnp.stack([core, x, z]).astype(jnp.int32)
-    swap = [(i, i ^ 1) for i in range(8)]
-    along_y = lambda k: [(2 * ((i + k) % 4) + c, 2 * i + c) for i in range(4) for c in range(2)]
-    along_x = lambda k: [(4 * ((i + k) % 4) + j, 4 * i + j) for i in range(4) for j in range(4)]
-    along_z = lambda k: [(4 * j + (i + k) % 4, 4 * j + i) for i in range(4) for j in range(4)]
-    got = lax.ppermute(jnp.where(core == 0, top[1], top[0]), "prow", swap)
-    kept = jnp.where(core == 0, top[0], top[1])
-    first = jnp.where(core == 0, kept, got)[:, :512]
-    rest = jnp.where(core == 0, got, kept)
-    both = jnp.concatenate([first, rest], axis=1)
-    sent = [lax.ppermute(both, "prow", [(c, 2 * k + c) for c in range(2)]) for k in range(1, 4)]
-    both = jnp.where(y == 0, both, sent[0] + sent[1] + sent[2])
-
-    def assemble(strip):
-        ring = jnp.stack([strip] + [lax.ppermute(strip, "pcol", along_z(k)) for k in range(1, 4)])
-        mine = jnp.stack([ring] + [lax.ppermute(ring, "pcol", along_x(k)) for k in range(1, 4)])
-        return mine, lax.ppermute(mine, "prow", swap)
+    top = join_strips(join_top_kernel, 2, strip_slots, got)
+
+    half_top = lax.all_to_all(jnp.tile(top, (prow // 2, 1, 1)), "prow", 0, 0, tiled=True)
+    first = spread(half_top[0, :, :512], "pcol", pcol)
+    diag0 = (first, lax.ppermute(first, "prow", swap))
+    half_rest, diag0 = lax.optimization_barrier((half_top[1], diag0))
+    rest = spread(half_rest, "pcol", pcol)
+    diag1 = (rest, lax.ppermute(rest, "prow", swap))
+    child, diag0, diag1 = lax.optimization_barrier((child, diag0, diag1))
+    arrived = lax.all_to_all(child, "pcol", 0, 0, tiled=True).reshape(48, 256, 256)
 
     def gather_columns(strips):
         halves = strips.reshape(4, 2, 16, 512)
         even, odd = halves[:, 0], halves[:, 1]
-        got = lax.ppermute(jnp.where(core == 0, odd, even), "prow", swap)
+        sent = lax.ppermute(jnp.where(core == 0, odd, even), "prow", swap)
         kept = jnp.where(core == 0, even, odd)
-        chip = jnp.where(core == 0, jnp.stack([kept, got]), jnp.stack([got, kept]))
-        return [chip] + [lax.ppermute(chip, "prow", along_y(k)) for k in range(1, 4)]
-
-    top0 = assemble(both[:, :512])
-    top1 = assemble(both[:, 512:])
-
-    cut_low = cut_strips(front_rows, 2, 6, pcol)
-    cut_low, top = lax.optimization_barrier((cut_low, top))
-    got_low = lax.all_to_all(cut_low, "pcol", 0, 0, tiled=True)[:2]
-    child, got_low = lax.optimization_barrier((child, got_low))
-    arrived = lax.all_to_all(child, "pcol", 0, 0, tiled=True).reshape(48, 256, 256)
-
-    L0, W0 = factor_first(at, *top0)
-    low = join_strips(strip_slots, got_low, got_child, 2, 6)
+        chip = jnp.where(core == 0, jnp.stack([kept, sent]), jnp.stack([sent, kept]))
+        along = lambda k: [(2 * ((i + k) % 4) + c, 2 * i + c) for i in range(4) for c in range(2)]
+        return [chip] + [lax.ppermute(chip, "prow", along(k)) for k in range(1, 4)]
+
+    L0, W0 = factor_first(at, *diag0)
+    low = join_strips(join_low_kernel, 6, strip_slots, got, low_front)
     P0 = solve_strips(solve_first_kernel, keep0, top, low, W0)
     row0 = lax.all_gather(P0, "pcol")
-    P0, top1 = lax.optimization_barrier((P0, top1))
+    P0, diag1 = lax.optimization_barrier((P0, diag1))
     cols0 = gather_columns(P0)
-    P10, L1, W1 = factor_second(at, struct_mask[2:4, 2:4].reshape(-1), *top1, W0)
+    P10, L1, W1 = factor_second(at, struct_mask[2:4, 2:4].reshape(-1), *diag1, W0)
     P1 = solve_strips(solve_second_kernel, keep1, top, low, P0, P10, W1)
-    row1 = lax.all_gather(P1, "pcol")
     cols1 = gather_columns(P1)
 
-    dealt = deal(y.reshape(1).astype(jnp.int32), cols0, cols1)
-    dealt, arrived = lax.optimization_barrier((dealt, arrived))
-    mine = lax.all_to_all(dealt, "pcol", 0, 0, tiled=True)
-    other = lax.ppermute(mine, "prow", swap)
-    ordered = jnp.stack([jnp.where(core == 0, mine, other), jnp.where(core == 0, other, mine)])
+    dealt = deal(at, P1, cols0, cols1)
+    dealt, arrived, row0 = lax.optimization_barrier((dealt, arrived, row0))
+    dealt = lax.all_to_all(dealt, "pcol", 0, 0, tiled=True)
+    other = lax.ppermute(dealt[:, 8:], "prow", swap)
 
     L = jnp.where(q == 0, L0, L1)
     W = jnp.where(q == 0, W0, W1)
-    out = finish(
-        slots, flags, front_rows, arrived, (row0, row1), (ordered[:, :, 0], ordered[:, :, 1]), L, W
-    )
+    out = finish(slots, flags, front_rows, arrived, row0, dealt, other, L, W)
     return out.reshape(front.shape)
 
 

time: 361 us -> 338 us (0.936)
  blocking collectives: 0 us -> 56.6 us
  starting transfers between devices: 99 us -> 46.9 us
  waiting for transfers between devices: 125 us -> 94.8 us
    ppermute x27 -> x11, waiting for transfers between devices: 94.5 us -> 13.6 us  [the longest x6 8.09 us: gather_columns(): return [chip] + [lax.ppermute(chip, 'prow', along(k)) for k in range(1, 4)]]
    all_to_all x0 -> x3, blocking collectives: none -> 56.6 us  [the longest x2 37 us: spread(): lax.all_to_all(jnp.broadcast_to(x[None], (count,) + x.shape), axis, 0, 0,...]
    ppermute x27 -> x11, starting transfers between devices: 65.3 us -> 17.2 us  [the longest x6 6.01 us: gather_columns(): return [chip] + [lax.ppermute(chip, 'prow', along(k)) for k in range(1, 4)]]
    all_to_all x4 -> x2, waiting for transfers between devices: 30.3 us -> 62.9 us  [the longest x1 38.4 us: local(): dealt = lax.all_to_all(dealt, 'pcol', 0, 0, tiled=True)]
    all_to_all x1, waiting for transfers between devices: 0.01 us -> 18.1 us  [local(): lax.all_to_all(child, 'pcol', 0, 0, tiled=True).reshape(48, 256, 256)]
    unnamed x48 -> x46, local copies, waits for them, and re-layouts: 7.59 us -> 11.9 us
    all_to_all x4 -> x2, starting transfers between devices: 28.2 us -> 24.7 us  [the longest x1 16.5 us: local(): dealt = lax.all_to_all(dealt, 'pcol', 0, 0, tiled=True)]
  transfers between devices with their start and end apart: 34 -> 16, of which waited for: 20 -> 13; matrix products, arithmetic and copies ran while one was open for 4% -> 3% of each run, Pallas kernels for 20% -> 22%
where the time goes in v4:
time: 338 us; the launch traced here: 334 us
  Pallas kernels  97.6 us (29%)
  waiting for transfers between devices  94.8 us (28%)
  blocking collectives  56.6 us (17%)
  starting transfers between devices  46.9 us (14%)
  local copies, waits for them, and re-layouts  18.2 us (5%)
  between operations  13.9 us (4%)
  other arithmetic  5.62 us (2%)
    all_to_all x1, waiting for transfers between devices, local(): dealt = lax.all_to_all(dealt, 'pcol', 0, 0, tiled=True)  38.4 us
    all_to_all x2, blocking collectives, spread(): lax.all_to_all(jnp.broadcast_to(x[None], (count,) + x.shape), axis, 0, 0,...  37 us
    pallas_call x1, Pallas kernels, factor_second(): pl.pallas_call(factor_second_kernel, out_shape=[jax.ShapeDtypeStruct((n,...  28 us
    pallas_call x1, Pallas kernels, factor_first(): pl.pallas_call(factor_first_kernel, out_shape=[jax.ShapeDtypeStruct((n, n...  27 us
    all_to_all x1, waiting for transfers between devices, local(): lax.all_to_all(cut_top(front_rows, child.reshape(48, 256, 256)), 'pcol',...  24.4 us
    all_to_all x1, blocking collectives, local(): lax.all_to_all(jnp.tile(top, (prow // 2, 1, 1)), 'prow', 0, 0, tiled=True)  19.6 us
    pallas_call x1, Pallas kernels, finish(): pl.pallas_call(finish_kernel, grid_spec=pltpu.PrefetchScalarGridSpec(num_...  18.3 us
    all_to_all x1, waiting for transfers between devices, local(): lax.all_to_all(child, 'pcol', 0, 0, tiled=True).reshape(48, 256, 256)  18.1 us
  transfers between devices with their start and end apart: 16, of which 13 were waited for; matrix products, arithmetic and copies ran while one was open for 3% of the time, Pallas kernels for 22%

profile of v4, /device:TPU:1, one launch (start us, length us, event | category | flops | bytes accessed | tf_op | source)
XLA Modules:
  0.0 333.6 jit_solution(9776965894157006248)
XLA Ops:
  7.1 7.1 %shard_map.57 = f32[16,6,16,1024]{3,2,1,0:T(8,128)} custom-call(s32[3]{0:T(128)} %pad_add_fusion.1.at_ref, f32[16384,128]{1,0:T(8,128)} %bitcast.66), custom_call_target="tpu_custom_call" | custom-call | bytes 12582912 | tf_op jit(solution)/shard_map/pallas_call | solution.py:197
  14.3 2.8 copy-done.1
  17.0 3.2 shard_map.55
  20.3 8.2 %all-to-all-start = ((bf16[16,14,16,256]{3,2,1,0:T(8,128)(2,1)}), bf16[16,14,16,256]{3,2,1,0:T(8,128)(2,1)S(1)}, u32[]{:S(2)}, u32[]{:S(2)}) async-start(bf16[16,14,16,256]{3,2,1,0:T(8,128)(2,1)} %shard_map.55), calls=%async_computation | async-start | bytes 3670016 | tf_op jit(solution)/shard_map/all_to_all | solution.py:422
  31.1 24.4 %all-to-all-done.c_ref = bf16[16,14,16,256]{3,2,1,0:T(8,128)(2,1)S(1)} async-done(((bf16[16,14,16,256]{3,2,1,0:T(8,128)(2,1)}), bf16[16,14,16,256]{3,2,1,0:T(8,128)(2,1)S(1)}, u32[]{:S(2)}, u32[]{:S(2)}) %all-to-all-start) | async-done | bytes 1835040 | tf_op jit(solution)/shard_map/all_to_all | solution.py:422
  55.6 1.3 copy-done.13
  56.9 2.3 shard_map.56.d_ref
  60.1 19.6 %all_to_all.30 = f32[8,16,1024]{2,1,0:T(8,128)S(1)} all-to-all(f32[8,16,1024]{2,1,0:T(8,128)S(1)} %bitcast.71), channel_id=1, replica_groups=mesh['prow'=8,'pcol'=16] {'prow'}, dimensions={0} | all-to-all | bytes 1048576 | tf_op jit(solution)/shard_map/all_to_all | solution.py:445
  79.7 13.9 %all_to_all.31.mine_ref = f32[16,16,512]{2,1,0:T(8,128)S(1)} all-to-all(f32[16,16,512]{2,1,0:T(8,128)S(1)} %broadcast_in_dim.115), channel_id=1, replica_groups=mesh['prow'=8,'pcol'=16] {'pcol'}, dimensions={0} | all-to-all | bytes 1048576 | tf_op jit(solution)/shard_map/all_to_all | solution.py:404
  93.6 2.7 collective-permute-start
  96.3 1.5 collective-permute-done.other_ref
  98.0 23.1 %all_to_all.32.mine_ref = f32[16,16,1024]{2,1,0:T(8,128)S(1)} all-to-all(f32[16,16,1024]{2,1,0:T(8,128)S(1)} %broadcast_in_dim.116), channel_id=1, replica_groups=mesh['prow'=8,'pcol'=16] {'pcol'}, dimensions={0} | all-to-all | bytes 2097152 | tf_op jit(solution)/shard_map/all_to_all | solution.py:404
  121.1 3.7 %collective-permute-start.1 = (f32[16,16,1024]{2,1,0:T(8,128)S(1)}, f32[16,16,1024]{2,1,0:T(8,128)S(1)}, u32[]{:S(2)}, u32[]{:S(2)}) collective-permute-start(f32[16,16,1024]{2,1,0:T(8,128)S(1)} %all_to_all.32.mine_ref), channel_id=1, source_target_pairs={{0,16},{16,0},{32,48},{48,32},{64,80},{80,64},{96,112},{112,96},{1... | collective-permute-start | bytes 3145736 | tf_op jit(solution)/shard_map/ppermute | solution.py:450
  124.8 2.3 collective-permute-done.1.other_ref
  128.1 4.8 %all-to-all-start.4 = ((bf16[16,3,256,256]{3,2,1,0:T(8,128)(2,1)}), bf16[16,3,256,256]{3,2,1,0:T(8,128)(2,1)}, u32[]{:S(2)}, u32[]{:S(2)}) async-start(bf16[16,3,256,256]{3,2,1,0:T(8,128)(2,1)} %bitcast.63), calls=%async_computation.5 | async-start | bytes 12582912 | tf_op jit(solution)/shard_map/all_to_all | solution.py:452
  133.7 27.0 %shard_map.59 = (f32[512,512]{1,0:T(8,128)S(1)}, f32[512,512]{1,0:T(8,128)S(1)}) custom-call(s32[3]{0:T(128)S(1)} %copy-done.10, f32[16,16,512]{2,1,0:T(8,128)S(1)} %all_to_all.31.mine_ref, f32[16,16,512]{2,1,0:T(8,128)S(1)} %collective-permute-done.other_ref), custom_call_target="tpu_custom_call" | custom-call | flops 20000000000 | bytes 3145728 | tf_op jit(solution)/shard_map/pallas_call | solution.py:133
  161.7 2.6 shard_map.58.r_ref
  164.2 2.7 shard_map.60.p_ref
  172.4 28.0 %shard_map.61 = (bf16[512,512]{1,0:T(8,128)(2,1)S(1)}, f32[512,512]{1,0:T(8,128)S(1)}, f32[512,512]{1,0:T(8,128)S(1)}) custom-call(s32[3]{0:T(128)S(1)} %copy-done.10, s32[4]{0:T(128)S(1)} %reshape.313.mask_ref, f32[16,16,1024]{2,1,0:T(8,128)S(1)} %all_to_all.32.mine_ref, f32[16,16,1024]{2,1,0:T(8,128)S(1)} %copy-done.12, f32[512,512]{1,0:T(8,128)S(1)} %copy-done.3), custom_call_target="tpu_custom_call" | custom-call | flops 20000000000 | bytes 3145728 | tf_op jit(solution)/shard_map/pallas_call | solution.py:146
  203.2 3.1 shard_map.62.p_ref
  207.5 2.2 collective-permute-start.4
  211.3 1.5 collective-permute-start.8
  216.7 3.2 collective-permute-done.9.refs_7_
  219.9 1.5 collective-permute-done.8.refs_6_
  222.3 3.2 shard_map.63
  225.5 18.1 %all-to-all-done.4 = bf16[16,3,256,256]{3,2,1,0:T(8,128)(2,1)} async-done(((bf16[16,3,256,256]{3,2,1,0:T(8,128)(2,1)}), bf16[16,3,256,256]{3,2,1,0:T(8,128)(2,1)}, u32[]{:S(2)}, u32[]{:S(2)}) %all-to-all-start.4) | async-done | bytes 6291488 | tf_op jit(solution)/shard_map/all_to_all | solution.py:452
  243.8 16.5 %all-to-all-start.5 = ((bf16[16,12,16,512]{3,2,1,0:T(8,128)(2,1)}), bf16[16,12,16,512]{3,2,1,0:T(8,128)(2,1)}, u32[]{:S(2)}, u32[]{:S(2)}) async-start(bf16[16,12,16,512]{3,2,1,0:T(8,128)(2,1)} %shard_map.63), calls=%async_computation.6 | async-start | bytes 6291456 | tf_op jit(solution)/shard_map/all_to_all | solution.py:475
  262.0 38.4 %all-to-all-done.5.refs_9_.refs_10_ = bf16[16,12,16,512]{3,2,1,0:T(8,128)(2,1)} async-done(((bf16[16,12,16,512]{3,2,1,0:T(8,128)(2,1)}), bf16[16,12,16,512]{3,2,1,0:T(8,128)(2,1)}, u32[]{:S(2)}, u32[]{:S(2)}) %all-to-all-start.5) | async-done | bytes 3145760 | tf_op jit(solution)/shard_map/all_to_all | solution.py:475
  300.4 1.5 slice.51
  301.9 4.1 %collective-permute-start.10 = (bf16[16,4,16,512]{3,2,1,0:T(8,128)(2,1)S(1)}, bf16[16,4,16,512]{3,2,1,0:T(8,128)(2,1)S(1)}, u32[]{:S(2)}, u32[]{:S(2)}) collective-permute-start(bf16[16,4,16,512]{3,2,1,0:T(8,128)(2,1)S(1)} %slice.51), channel_id=1, source_target_pairs={{0,16},{16,0},{32,48},{48,32},{64,80},{80,64},{96,112},{112,96},{1... | collective-permute-start | bytes 3145736 | tf_op jit(solution)/shard_map/ppermute | solution.py:476
  306.6 1.6 collective-permute-done.10.refs_11_
  308.3 18.3 %shard_map.64 = f32[16384,128]{1,0:T(8,128)} custom-call(s32[64]{0:T(128)S(1)} %broadcast_add_fusion.3.slot_ref, s32[49]{0:T(128)S(1)} %pad_add_fusion.flag_ref, f32[16384,128]{1,0:T(8,128)} %bitcast.68, bf16[48,256,256]{2,1,0:T(8,128)(2,1)} %bitcast.22.refs_0_.refs_1_.refs_2_.refs_3_.refs_4_.refs_5_.refs_6_.refs_7_, ...), custom_call_target="tpu_custom_call" | custom-call | flops 5000000000 | bytes 29360128 | tf_op jit(solution)/shard_map/pallas_call | solution.py:368
  (135 shorter events, 25.2 us)
Async XLA Ops:
  6.5 23.5 %copy-start = (s32[8,16,16,3]{2,1,3,0:T(8,128)S(1)}, s32[8,16,16,3]{2,1,3,0:T(8,128)}, u32[]{:S(2)}) copy-start(s32[8,16,16,3]{2,1,3,0:T(8,128)} %param.8) | copy-start | bytes 73732
  6.5 155.1 %reduce-scatter.2.cloned.1.call-start = ((), (), s32[]{:S(2)}) async-start(), calls=%async_computation.7 | async-start | bytes 6684672 | tf_op jit(solution)/shard_map/reduce_scatter | solution.py:423
  14.2 2.8 copy-start.1
  17.0 11.8 %copy-start.22 = (s32[2,60]{1,0:T(2,128)S(1)}, s32[2,60]{1,0:T(2,128)}, u32[]{:S(2)}) copy-start(s32[2,60]{1,0:T(2,128)} %param.7) | copy-start | bytes 1444
  20.3 35.3 %all-to-all-start = ((bf16[16,14,16,256]{3,2,1,0:T(8,128)(2,1)}), bf16[16,14,16,256]{3,2,1,0:T(8,128)(2,1)S(1)}, u32[]{:S(2)}, u32[]{:S(2)}) async-start(bf16[16,14,16,256]{3,2,1,0:T(8,128)(2,1)} %shard_map.55), calls=%async_computation | async-start | bytes 3670016 | tf_op jit(solution)/shard_map/all_to_all | solution.py:422
  55.6 1.3 copy-start.13
  93.6 4.2 %collective-permute-start = (f32[16,16,512]{2,1,0:T(8,128)S(1)}, f32[16,16,512]{2,1,0:T(8,128)S(1)}, u32[]{:S(2)}, u32[]{:S(2)}) collective-permute-start(f32[16,16,512]{2,1,0:T(8,128)S(1)} %all_to_all.31.mine_ref), channel_id=1, source_target_pairs={{0,16},{16,0},{32,48},{48,32},{64,80},{80,64},{96,112},{112,96},{1... | collective-permute-start | bytes 1572872 | tf_op jit(solution)/shard_map/ppermute | solution.py:447
  121.1 6.0 %collective-permute-start.1 = (f32[16,16,1024]{2,1,0:T(8,128)S(1)}, f32[16,16,1024]{2,1,0:T(8,128)S(1)}, u32[]{:S(2)}, u32[]{:S(2)}) collective-permute-start(f32[16,16,1024]{2,1,0:T(8,128)S(1)} %all_to_all.32.mine_ref), channel_id=1, source_target_pairs={{0,16},{16,0},{32,48},{48,32},{64,80},{80,64},{96,112},{112,96},{1... | collective-permute-start | bytes 3145736 | tf_op jit(solution)/shard_map/ppermute | solution.py:450
  128.1 5.5 %copy-start.10 = (s32[3]{0:T(128)S(1)}, s32[3]{0:T(128)}, u32[]{:S(2)}) copy-start(s32[3]{0:T(128)} %pad_add_fusion.1.at_ref) | copy-start | bytes 40
  128.1 115.4 %all-to-all-start.4 = ((bf16[16,3,256,256]{3,2,1,0:T(8,128)(2,1)}), bf16[16,3,256,256]{3,2,1,0:T(8,128)(2,1)}, u32[]{:S(2)}, u32[]{:S(2)}) async-start(bf16[16,3,256,256]{3,2,1,0:T(8,128)(2,1)} %bitcast.63), calls=%async_computation.5 | async-start | bytes 12582912 | tf_op jit(solution)/shard_map/all_to_all | solution.py:452
  132.9 110.9 %all-gather.3.cloned.1.call-start = ((), (), s32[]{:S(2)}) async-start(), calls=%async_computation.8 | async-start | bytes 2228224 | tf_op jit(solution)/shard_map/all_gather | solution.py:466
  133.7 33.4 %copy-start.21 = (s32[64,64]{1,0:T(8,128)S(1)}, s32[64,64]{1,0:T(8,128)}, u32[]{:S(2)}) copy-start(s32[64,64]{1,0:T(8,128)} %param.9) | copy-start | bytes 49156
  169.5 37.9 %collective-permute-start.2 = (bf16[4,16,512]{2,1,0:T(8,128)(2,1)S(1)}, bf16[4,16,512]{2,1,0:T(8,128)(2,1)S(1)}, u32[]{:S(2)}, u32[]{:S(2)}) collective-permute-start(bf16[4,16,512]{2,1,0:T(8,128)(2,1)S(1)} %get-tuple-element.48), channel_id=1, source_target_pairs={{0,16},{16,0},{32,48},{48,32},{64,80},{80,64},{96,112},{112,96},{1... | collective-permute-start | bytes 196616 | tf_op jit(solution)/shard_map/ppermute | solution.py:457
  169.9 1.2 copy-start.3
  207.2 3.0 collective-permute-start.6
  207.4 14.9 %copy-start.14 = (bf16[2,4,16,512]{3,2,1,0:T(8,128)(2,1)}, bf16[2,4,16,512]{3,2,1,0:T(8,128)(2,1)S(1)}, u32[]{:S(2)}) copy-start(bf16[2,4,16,512]{3,2,1,0:T(8,128)(2,1)S(1)} %maximum_select_fusion.refs_0_) | copy-start | bytes 393220
  207.4 6.6 %collective-permute-start.5 = (bf16[2,4,16,512]{3,2,1,0:T(8,128)(2,1)S(1)}, bf16[2,4,16,512]{3,2,1,0:T(8,128)(2,1)S(1)}, u32[]{:S(2)}, u32[]{:S(2)}) collective-permute-start(bf16[2,4,16,512]{3,2,1,0:T(8,128)(2,1)S(1)} %maximum_select_fusion.refs_0_), channel_id=1, source_target_pairs={{96,0},{112,16},{0,32},{16,48},{32,64},{48,80},{64,96},{80,112},{9... | collective-permute-start | bytes 393224 | tf_op jit(solution)/shard_map/ppermute | solution.py:461
  207.5 8.4 %collective-permute-start.4 = (bf16[2,4,16,512]{3,2,1,0:T(8,128)(2,1)S(1)}, bf16[2,4,16,512]{3,2,1,0:T(8,128)(2,1)S(1)}, u32[]{:S(2)}, u32[]{:S(2)}) collective-permute-start(bf16[2,4,16,512]{3,2,1,0:T(8,128)(2,1)S(1)} %maximum_select_fusion.refs_0_), channel_id=1, source_target_pairs={{64,0},{80,16},{96,32},{112,48},{0,64},{16,80},{32,96},{48,112},{6... | collective-permute-start | bytes 393224 | tf_op jit(solution)/shard_map/ppermute | solution.py:461
  209.7 7.0 %collective-permute-start.3 = (bf16[2,4,16,512]{3,2,1,0:T(8,128)(2,1)S(1)}, bf16[2,4,16,512]{3,2,1,0:T(8,128)(2,1)S(1)}, u32[]{:S(2)}, u32[]{:S(2)}) collective-permute-start(bf16[2,4,16,512]{3,2,1,0:T(8,128)(2,1)S(1)} %maximum_select_fusion.refs_0_), channel_id=1, source_target_pairs={{32,0},{48,16},{64,32},{80,48},{96,64},{112,80},{0,96},{16,112},{3... | collective-permute-start | bytes 393224 | tf_op jit(solution)/shard_map/ppermute | solution.py:461
  210.2 6.5 %copy-start.15 = (bf16[2,4,16,512]{3,2,1,0:T(8,128)(2,1)}, bf16[2,4,16,512]{3,2,1,0:T(8,128)(2,1)S(1)}, u32[]{:S(2)}) copy-start(bf16[2,4,16,512]{3,2,1,0:T(8,128)(2,1)S(1)} %maximum_select_fusion.1.refs_4_) | copy-start | bytes 393220
  210.2 96.0 %copy-start.4 = (f32[512,512]{1,0:T(8,128)S(1)}, f32[512,512]{1,0:T(8,128)}, u32[]{:S(2)}) copy-start(f32[512,512]{1,0:T(8,128)} %copy-done.2) | copy-start | bytes 3145732
  210.2 96.0 %copy-start.6 = (f32[512,512]{1,0:T(8,128)S(1)}, f32[512,512]{1,0:T(8,128)}, u32[]{:S(2)}) copy-start(f32[512,512]{1,0:T(8,128)} %copy-done.5) | copy-start | bytes 3145732
  210.2 9.7 %collective-permute-start.9 = (bf16[2,4,16,512]{3,2,1,0:T(8,128)(2,1)S(1)}, bf16[2,4,16,512]{3,2,1,0:T(8,128)(2,1)S(1)}, u32[]{:S(2)}, u32[]{:S(2)}) collective-permute-start(bf16[2,4,16,512]{3,2,1,0:T(8,128)(2,1)S(1)} %maximum_select_fusion.1.refs_4_), channel_id=1, source_target_pairs={{96,0},{112,16},{0,32},{16,48},{32,64},{48,80},{64,96},{80,112},{9... | collective-permute-start | bytes 393224 | tf_op jit(solution)/shard_map/ppermute | solution.py:461
  211.3 10.2 %collective-permute-start.8 = (bf16[2,4,16,512]{3,2,1,0:T(8,128)(2,1)S(1)}, bf16[2,4,16,512]{3,2,1,0:T(8,128)(2,1)S(1)}, u32[]{:S(2)}, u32[]{:S(2)}) collective-permute-start(bf16[2,4,16,512]{3,2,1,0:T(8,128)(2,1)S(1)} %maximum_select_fusion.1.refs_4_), channel_id=1, source_target_pairs={{64,0},{80,16},{96,32},{112,48},{0,64},{16,80},{32,96},{48,112},{6... | collective-permute-start | bytes 393224 | tf_op jit(solution)/shard_map/ppermute | solution.py:461
  214.0 7.4 %copy-start.16 = (bf16[2,4,16,512]{3,2,1,0:T(8,128)(2,1)}, bf16[2,4,16,512]{3,2,1,0:T(8,128)(2,1)S(1)}, u32[]{:S(2)}) copy-start(bf16[2,4,16,512]{3,2,1,0:T(8,128)(2,1)S(1)} %collective-permute-done.5.refs_3_) | copy-start | bytes 393220
  214.0 8.3 %collective-permute-start.7 = (bf16[2,4,16,512]{3,2,1,0:T(8,128)(2,1)S(1)}, bf16[2,4,16,512]{3,2,1,0:T(8,128)(2,1)}, u32[]{:S(2)}, u32[]{:S(2)}) collective-permute-start(bf16[2,4,16,512]{3,2,1,0:T(8,128)(2,1)S(1)} %maximum_select_fusion.1.refs_4_), channel_id=1, source_target_pairs={{32,0},{48,16},{64,32},{80,48},{96,64},{112,80},{0,96},{16,112},{3... | collective-permute-start | bytes 393224 | tf_op jit(solution)/shard_map/ppermute | solution.py:461
  215.9 5.6 %copy-start.17 = (bf16[2,4,16,512]{3,2,1,0:T(8,128)(2,1)}, bf16[2,4,16,512]{3,2,1,0:T(8,128)(2,1)S(1)}, u32[]{:S(2)}) copy-start(bf16[2,4,16,512]{3,2,1,0:T(8,128)(2,1)S(1)} %collective-permute-done.4.refs_2_) | copy-start | bytes 393220
  216.7 4.8 %copy-start.18 = (bf16[2,4,16,512]{3,2,1,0:T(8,128)(2,1)}, bf16[2,4,16,512]{3,2,1,0:T(8,128)(2,1)S(1)}, u32[]{:S(2)}) copy-start(bf16[2,4,16,512]{3,2,1,0:T(8,128)(2,1)S(1)} %collective-permute-done.3.refs_1_) | copy-start | bytes 393220
  219.9 1.5 copy-start.19
  243.8 56.6 %all-to-all-start.5 = ((bf16[16,12,16,512]{3,2,1,0:T(8,128)(2,1)}), bf16[16,12,16,512]{3,2,1,0:T(8,128)(2,1)}, u32[]{:S(2)}, u32[]{:S(2)}) async-start(bf16[16,12,16,512]{3,2,1,0:T(8,128)(2,1)} %shard_map.63), calls=%async_computation.6 | async-start | bytes 6291456 | tf_op jit(solution)/shard_map/all_to_all | solution.py:475
  300.4 7.9 %copy-start.7 = (bf16[128,16,512]{2,1,0:T(8,128)(2,1)S(1)}, bf16[128,16,512]{2,1,0:T(8,128)(2,1)}, u32[]{:S(2)}) copy-start(bf16[128,16,512]{2,1,0:T(8,128)(2,1)} %all-gather.3.cloned.1.call-done) | copy-start | bytes 6291460
  301.9 6.4 %collective-permute-start.10 = (bf16[16,4,16,512]{3,2,1,0:T(8,128)(2,1)S(1)}, bf16[16,4,16,512]{3,2,1,0:T(8,128)(2,1)S(1)}, u32[]{:S(2)}, u32[]{:S(2)}) collective-permute-start(bf16[16,4,16,512]{3,2,1,0:T(8,128)(2,1)S(1)} %slice.51), channel_id=1, source_target_pairs={{0,16},{16,0},{32,48},{48,32},{64,80},{80,64},{96,112},{112,96},{1... | collective-permute-start | bytes 3145736 | tf_op jit(solution)/shard_map/ppermute | solution.py:476
  (7 other events, 6.6 us)
Sparse Core Ops, SparseCore 0:
  14.4 111.1 reduce-scatter.1
  167.1 76.6 all-gather.2

commit v5 on v4

--- a/solution.py
+++ b/solution.py
@@ -32,53 +32,62 @@
     return dot1(ah, bh, dims) + (dot1(al, bh, dims) + dot1(ah, bl, dims))
 
 
-def factor_base(S):
-    n = S.shape[0]
-    wide = 2 * n // 128
-    lane = lax.broadcasted_iota(jnp.int32, (n, n), 1)
-    sub = lax.broadcasted_iota(jnp.int32, (n, n), 0)
-    M = jnp.concatenate([S, jnp.where(lane == sub, F32(1), F32(0))], axis=1)
+GROUPS = 4
+
+
+def eliminate(R, n):
     row = lax.broadcasted_iota(jnp.int32, (8, 1), 0)
-    across = lambda v: jnp.concatenate([v] * wide, axis=1)
+    across = lambda v: jnp.concatenate([v, v], axis=1)
+    over = lambda x, lane: jnp.broadcast_to(x[:, lane : lane + 1], (8, 128))
     done = []
-    for o in range(0, n, 8):
-        R = M[0:8]
-        cols = [jnp.broadcast_to(R[:, o + j : o + j + 1], (8, 128)) for j in range(8)]
+    for g in range(len(R)):
+        base = 8 * g
+        later = range(g + 1, len(R))
+        cols = [over(R[g], base + j) for j in range(8)]
+        below = {h: [over(R[h], base + j) for j in range(8)] for h in later}
         D = [[jnp.broadcast_to(cols[j][i : i + 1], (8, 128)) for j in range(i + 1)] for i in range(8)]
-        Y = [jnp.broadcast_to(R[i : i + 1], (8, 2 * n)) for i in range(8)]
-        low = [[None] * 8 for _ in range(8)]
-        inv = [None] * 8
-        for j in range(8):
-            inv[j] = 1.0 / D[j][j]
-            for i in range(j + 1, 8):
-                low[i][j] = D[i][j] * inv[j]
-            for i in range(j + 1, 8):
-                for m in range(j + 1, i + 1):
-                    D[i][m] = D[i][m] - low[i][j] * D[m][j]
-                Y[i] = Y[i] - across(low[i][j]) * Y[j]
+        Y = [jnp.broadcast_to(R[g][i : i + 1], (8, 2 * n)) for i in range(8)]
         out = None
         for j in range(8):
-            scaled = Y[j] * across(lax.rsqrt(D[j][j]))
+            scale = lax.rsqrt(D[j][j])
+            inverse = scale * scale
+            for i in range(j + 1, 8):
+                factor = D[i][j] * inverse
+                for m in range(j + 1, i):
+                    D[i][m] = D[i][m] - factor * D[m][j]
+                D[i][i] = D[i][i] - (D[i][j] * D[i][j]) * inverse
+                Y[i] = Y[i] - across(factor) * Y[j]
+            for h in later:
+                factor = below[h][j] * inverse
+                for m in range(j + 1, 8):
+                    below[h][m] = below[h][m] - factor * D[m][j]
+                R[h] = R[h] - across(factor) * Y[j]
+            scaled = Y[j] * across(scale)
             out = scaled if out is None else jnp.where(row == j, scaled, out)
         done.append(out)
-        if o + 8 == n:
-            break
-        Z = [None] * 8
-        for i in range(7, -1, -1):
-            Z[i] = Y[i] * across(inv[i])
-            for m in range(i + 1, 8):
-                Z[i] = Z[i] - across(low[m][i]) * Z[m]
-        step = Z[0]
-        for i in range(1, 8):
-            step = jnp.where(row == i, Z[i], step)
-        parts = [jnp.zeros((o, 2 * n), F32)] if o else []
-        parts += [step, jnp.zeros((n - o - 8, 2 * n), F32)]
-        M = M[8:] - dot3(M[8:, :n], jnp.concatenate(parts, axis=0), NN)
-    done = jnp.concatenate(done, axis=0)
-    return jnp.where(lane >= sub, done[:, :n], F32(0)), jnp.where(lane <= sub, done[:, n:], F32(0))
-
-
-def factor_whole(a_ref, l_ref, w_ref):
+    return jnp.concatenate(done, axis=0)
+
+
+def factor_base(m_ref, o_ref):
+    n = m_ref.shape[0]
+    step = 8 * GROUPS
+
+    def body(k, _):
+        at = k * step
+        rows = pl.ds(pl.multiple_of(at, step), step)
+        X = m_ref[rows, :]
+        A = pltpu.roll(X[:, :n], jnp.where(k == 0, 0, n - at), 1)
+        X = jnp.concatenate([A, X[:, n:]], axis=1)
+        out = eliminate([X[8 * g : 8 * g + 8] for g in range(GROUPS)], n)
+        out = jnp.concatenate([pltpu.roll(out[:, :n], at, 1), out[:, n:]], axis=1)
+        o_ref[rows, :] = out
+        m_ref[...] = m_ref[...] - dot3(out[:, :n].T, out, NN)
+        return 0
+
+    lax.fori_loop(0, n // step, body, 0)
+
+
+def factor_whole(a_ref, l_ref, w_ref, m_ref, o_ref):
     n = a_ref.shape[0]
     b = 128
     w_ref[...] = jnp.zeros((n, n), F32)
@@ -88,8 +97,11 @@
     for k in range(0, n, b):
         s = slice(k, k + b)
         D = a_ref[s, s]
-        U, W = factor_base(jnp.where(sub >= lane, D, D.T))
-        l_ref[s, s] = U.T
+        m_ref[:, :b] = jnp.where(sub >= lane, D, D.T)
+        m_ref[:, b:] = jnp.where(lane == sub, F32(1), F32(0))
+        factor_base(m_ref, o_ref)
+        W = jnp.where(lane <= sub, o_ref[:, b:], F32(0))
+        l_ref[s, s] = jnp.where(lane >= sub, o_ref[:, :b], F32(0)).T
         w_ref[s, s] = W
         if k:
             T = dot3(l_ref[s, :k], w_ref[:k, :k], NN)
@@ -102,18 +114,21 @@
                 a_ref[j:, j : j + b] = a_ref[j:, j : j + b] - dot3(L[off:], L[off : off + b], NT)
 
 
-def factor_first_kernel(at_ref, mine_ref, other_ref, l_ref, w_ref, a_ref):
+def factor_first_kernel(at_ref, mine_ref, other_ref, l_ref, w_ref, a_ref, m_ref, o_ref):
+    n = a_ref.shape[0]
     for ref, sub in ((mine_ref, at_ref[0]), (other_ref, 1 - at_ref[0])):
-        a_ref[pl.ds(pl.multiple_of(sub * 256, 256), 256), :] = ref[...].reshape(256, -1)
-    factor_whole(a_ref, l_ref, w_ref)
-
-
-def factor_second_kernel(at_ref, mask_ref, mine_ref, other_ref, w0_ref, p_ref, l_ref, w_ref, a_ref, b_ref):
+        a_ref[pl.ds(pl.multiple_of(sub * 256, 256), 256), :] = ref[:, :, :n].reshape(256, n)
+    factor_whole(a_ref, l_ref, w_ref, m_ref, o_ref)
+
+
+def factor_second_kernel(
+    at_ref, mask_ref, mine_ref, other_ref, w0_ref, p_ref, l_ref, w_ref, a_ref, m_ref, o_ref, b_ref
+):
     n = a_ref.shape[0]
     for ref, sub in ((mine_ref, at_ref[0]), (other_ref, 1 - at_ref[0])):
         rows = pl.ds(pl.multiple_of(sub * 256, 256), 256)
-        b_ref[rows, :] = ref[:, :, :n].reshape(256, n)
-        a_ref[rows, :] = ref[:, :, n:].reshape(256, n)
+        b_ref[rows, :] = ref[:, :, n : 2 * n].reshape(256, n)
+        a_ref[rows, :] = ref[:, :, 2 * n :].reshape(256, n)
     panel = dot3(b_ref[...], w0_ref[...], NT).astype(BF16)
     p_ref[...] = panel
     h = n // 2
@@ -122,20 +137,20 @@
             r, c = slice(i * h, (i + 1) * h), slice(j * h, (j + 1) * h)
             product = dot1(panel[r], panel[c], NT)
             a_ref[r, c] = a_ref[r, c] - jnp.where(mask_ref[i * 2 + j] > 0, product, F32(0))
-    factor_whole(a_ref, l_ref, w_ref)
+    factor_whole(a_ref, l_ref, w_ref, m_ref, o_ref)
 
 
 CHOL_COST = pl.CostEstimate(flops=20_000_000_000, bytes_accessed=3 * MIB, transcendentals=1024)
 
 
 def factor_first(at, mine, other):
-    n = mine.shape[-1]
+    n = mine.shape[-1] // 3
     return pl.pallas_call(
         factor_first_kernel,
         out_shape=[jax.ShapeDtypeStruct((n, n), F32)] * 2,
         in_specs=[SMEM, VMEM, VMEM],
         out_specs=[VMEM] * 2,
-        scratch_shapes=[pltpu.VMEM((n, n), F32)],
+        scratch_shapes=[pltpu.VMEM((n, n), F32)] + [pltpu.VMEM((128, 256), F32)] * 2,
         cost_estimate=CHOL_COST,
         compiler_params=pltpu.CompilerParams(vmem_limit_bytes=40 * MIB),
     )(at, mine, other)
@@ -148,7 +163,9 @@
         out_shape=[jax.ShapeDtypeStruct((n, n), BF16)] + [jax.ShapeDtypeStruct((n, n), F32)] * 2,
         in_specs=[SMEM, SMEM, VMEM, VMEM, VMEM],
         out_specs=[VMEM] * 3,
-        scratch_shapes=[pltpu.VMEM((n, n), F32)] * 2,
+        scratch_shapes=[pltpu.VMEM((n, n), F32)]
+        + [pltpu.VMEM((128, 256), F32)] * 2
+        + [pltpu.VMEM((n, n), F32)],
         cost_estimate=CHOL_COST,
         compiler_params=pltpu.CompilerParams(vmem_limit_bytes=40 * MIB),
     )(at, mask, mine, other, W0)
@@ -278,31 +295,64 @@
     )(*operands)
 
 
-def deal_kernel(at_ref, p_ref, *refs):
+def deal_kernel(at_ref, p0_ref, p1_ref, *refs):
     o_ref = refs[-1]
     for q in range(16):
-        o_ref[q, 0:8] = p_ref[...]
+        o_ref[q, 0:8] = p0_ref[...]
+        o_ref[q, 8:16] = p1_ref[...]
     for panel in range(2):
         for k in range(4):
             row = lax.rem(at_ref[2] + k, 4) * 2
             for c in range(2):
                 for lr in range(4):
-                    o_ref[(lr % 2) * 8 + row + c, 8 + panel * 2 + lr // 2] = refs[panel * 4 + k][c, lr]
-
-
-def deal(at, P1, first, second):
+                    o_ref[(lr % 2) * 8 + row + c, 16 + panel * 2 + lr // 2] = refs[panel * 4 + k][c, lr]
+
+
+def deal(at, P0, P1, first, second):
     return pl.pallas_call(
         deal_kernel,
-        out_shape=jax.ShapeDtypeStruct((16, 12, 16, 512), BF16),
-        in_specs=[SMEM] + [VMEM] * 9,
+        out_shape=jax.ShapeDtypeStruct((16, 20, 16, 512), BF16),
+        in_specs=[SMEM] + [VMEM] * 10,
         out_specs=VMEM,
-        cost_estimate=pl.CostEstimate(flops=0, bytes_accessed=6 * MIB, transcendentals=0),
-    )(at, P1, *first, *second)
-
-
-def finish_kernel(slot_ref, flag_ref, f_ref, *refs):
-    child = refs[:8]
-    row0_ref, row1_ref, mine_ref, other_ref, l_ref, w_ref, o_ref, cols_ref = refs[8:]
+        cost_estimate=pl.CostEstimate(flops=0, bytes_accessed=8 * MIB, transcendentals=0),
+        compiler_params=pltpu.CompilerParams(vmem_limit_bytes=24 * MIB),
+    )(at, P0, P1, *first, *second)
+
+
+def extend_kernel(slot_ref, f_ref, *refs):
+    child, o_ref = refs[:8], refs[8]
+    i = pl.program_id(0)
+    for j in range(4):
+        live = [slot_ref[(i * 4 + j) * 2 + ch] >= 0 for ch in range(2)]
+        pieces = [child[j * 2 + ch] for ch in range(2)]
+        for c in range(2):
+            lanes = slice(c * 128, (c + 1) * 128)
+            rows = pl.ds(j * 2 + c, 256, stride=8)
+            value = f_ref[rows, :]
+            for ch in range(2):
+                value = value + jnp.where(live[ch], pieces[ch][0, :, lanes].astype(F32), F32(0))
+            o_ref[rows, :] = value
+
+
+def extend(slots, front_rows, arrived):
+    def child_spec(k):
+        return pl.BlockSpec((1, 256, 256), lambda i, s: (jnp.maximum(s[i * 8 + k], 0), 0, 0))
+
+    return pl.pallas_call(
+        extend_kernel,
+        grid_spec=pltpu.PrefetchScalarGridSpec(
+            num_scalar_prefetch=1,
+            grid=(8,),
+            in_specs=[pl.BlockSpec((2048, 128), lambda i, s: (i, 0))] + [child_spec(k) for k in range(8)],
+            out_specs=pl.BlockSpec((2048, 128), lambda i, s: (i, 0)),
+        ),
+        out_shape=jax.ShapeDtypeStruct(front_rows.shape, F32),
+        cost_estimate=pl.CostEstimate(flops=0, bytes_accessed=24 * MIB, transcendentals=0),
+        compiler_params=pltpu.CompilerParams(vmem_limit_bytes=24 * MIB),
+    )(slots, front_rows, *([arrived] * 8))
+
+
+def finish_kernel(flag_ref, f_ref, row0_ref, row1_ref, mine_ref, other_ref, l_ref, w_ref, o_ref, cols_ref):
     i = pl.program_id(0)
 
     @pl.when(i == 0)
@@ -326,9 +376,6 @@
                 value = jnp.concatenate(
                     [f_ref[pl.ds(lc * 4 + sc * 2 + c, 256, stride=8), :] for c in range(2)], axis=1
                 )
-                for ch in range(2):
-                    live = slot_ref[(i * 4 + j) * 2 + ch] >= 0
-                    value = value + jnp.where(live, child[j * 2 + ch][0].astype(F32), F32(0))
                 product = dot1(rows, cols_ref[j], NT)
                 blocks.append(value - jnp.where(flag_ref[i * 4 + j] > 0, product, F32(0)))
             block = jnp.concatenate(blocks, axis=1)
@@ -357,31 +404,27 @@
                 o_ref[pl.ds(lc * 4 + c, 256, stride=8), :] = jnp.zeros((256, 128), F32)
 
 
-def finish(slots, flags, front_rows, arrived, row0, dealt, other, L, W):
-    def child_spec(k):
-        return pl.BlockSpec((1, 256, 256), lambda i, s, f: (jnp.maximum(s[i * 8 + k], 0), 0, 0))
-
+def finish(flags, extended, dealt, other, L, W):
     def whole(shape, *at):
-        return pl.BlockSpec(shape, lambda i, s, f: at)
-
-    rows = pl.BlockSpec((16, 1, 16, 512), lambda i, s, f: (0, i, 0, 0))
+        return pl.BlockSpec(shape, lambda i, f: at)
+
     return pl.pallas_call(
         finish_kernel,
         grid_spec=pltpu.PrefetchScalarGridSpec(
-            num_scalar_prefetch=2,
+            num_scalar_prefetch=1,
             grid=(8,),
-            in_specs=[pl.BlockSpec((2048, 128), lambda i, s, f: (i, 0))]
-            + [child_spec(k) for k in range(8)]
-            + [rows, rows]
-            + [whole((16, 4, 16, 512), 0, 2, 0, 0), whole((16, 4, 16, 512), 0, 0, 0, 0)]
+            in_specs=[pl.BlockSpec((2048, 128), lambda i, f: (i, 0))]
+            + [pl.BlockSpec((16, 1, 16, 512), lambda i, f: (0, i, 0, 0))]
+            + [pl.BlockSpec((16, 1, 16, 512), lambda i, f: (0, i + 8, 0, 0))]
+            + [whole((16, 4, 16, 512), 0, 4, 0, 0), whole((16, 4, 16, 512), 0, 0, 0, 0)]
             + [whole((512, 512), 0, 0)] * 2,
-            out_specs=pl.BlockSpec((2048, 128), lambda i, s, f: (i, 0)),
+            out_specs=pl.BlockSpec((2048, 128), lambda i, f: (i, 0)),
             scratch_shapes=[pltpu.VMEM((4, 256, 1024), BF16)],
         ),
-        out_shape=jax.ShapeDtypeStruct(front_rows.shape, F32),
-        cost_estimate=pl.CostEstimate(flops=5_000_000_000, bytes_accessed=28 * MIB, transcendentals=0),
+        out_shape=jax.ShapeDtypeStruct(extended.shape, F32),
+        cost_estimate=pl.CostEstimate(flops=5_000_000_000, bytes_accessed=24 * MIB, transcendentals=0),
         compiler_params=pltpu.CompilerParams(vmem_limit_bytes=48 * MIB),
-    )(slots, flags, front_rows, *([arrived] * 8), row0, dealt, dealt, other, L, W)
+    )(flags, extended, dealt, dealt, dealt, other, L, W)
 
 
 def slot_of_targets(codes, row_map, rows, cols):
@@ -419,7 +462,9 @@
     sub_rows = (2 * row_blocks[:, None] + pair).reshape(-1)
     sub_cols = (2 * col_blocks[:, None] + pair).reshape(-1)
 
-    got = lax.all_to_all(cut_top(front_rows, child.reshape(48, 256, 256)), "pcol", 0, 0, tiled=True)
+    cut = cut_top(front_rows, child.reshape(48, 256, 256))
+    got = lax.all_to_all(cut, "pcol", 0, 0, tiled=True)
+    front_rows, _ = lax.optimization_barrier((front_rows, cut))
     low_front = lax.psum_scatter(
         cut_low(at, front_rows).reshape(96, 16, 1024), "pcol", scatter_dimension=0, tiled=True
     )
@@ -443,12 +488,9 @@
     top = join_strips(join_top_kernel, 2, strip_slots, got)
 
     half_top = lax.all_to_all(jnp.tile(top, (prow // 2, 1, 1)), "prow", 0, 0, tiled=True)
-    first = spread(half_top[0, :, :512], "pcol", pcol)
-    diag0 = (first, lax.ppermute(first, "prow", swap))
-    half_rest, diag0 = lax.optimization_barrier((half_top[1], diag0))
-    rest = spread(half_rest, "pcol", pcol)
-    diag1 = (rest, lax.ppermute(rest, "prow", swap))
-    child, diag0, diag1 = lax.optimization_barrier((child, diag0, diag1))
+    first = spread(jnp.concatenate([half_top[0, :, :512], half_top[1]], axis=1), "pcol", pcol)
+    diag = (first, lax.ppermute(first, "prow", swap))
+    child, diag = lax.optimization_barrier((child, diag))
     arrived = lax.all_to_all(child, "pcol", 0, 0, tiled=True).reshape(48, 256, 256)
 
     def gather_columns(strips):
@@ -460,24 +502,26 @@
         along = lambda k: [(2 * ((i + k) % 4) + c, 2 * i + c) for i in range(4) for c in range(2)]
         return [chip] + [lax.ppermute(chip, "prow", along(k)) for k in range(1, 4)]
 
-    L0, W0 = factor_first(at, *diag0)
+    L0, W0 = factor_first(at, *diag)
     low = join_strips(join_low_kernel, 6, strip_slots, got, low_front)
     P0 = solve_strips(solve_first_kernel, keep0, top, low, W0)
-    row0 = lax.all_gather(P0, "pcol")
-    P0, diag1 = lax.optimization_barrier((P0, diag1))
+    P0, diag = lax.optimization_barrier((P0, diag))
     cols0 = gather_columns(P0)
-    P10, L1, W1 = factor_second(at, struct_mask[2:4, 2:4].reshape(-1), *diag1, W0)
+    P10, L1, W1 = factor_second(at, struct_mask[2:4, 2:4].reshape(-1), *diag, W0)
+    W1, cols0 = lax.optimization_barrier((W1, cols0))
     P1 = solve_strips(solve_second_kernel, keep1, top, low, P0, P10, W1)
     cols1 = gather_columns(P1)
 
-    dealt = deal(at, P1, cols0, cols1)
-    dealt, arrived, row0 = lax.optimization_barrier((dealt, arrived, row0))
+    dealt = deal(at, P0, P1, cols0, cols1)
+    dealt, arrived = lax.optimization_barrier((dealt, arrived))
     dealt = lax.all_to_all(dealt, "pcol", 0, 0, tiled=True)
-    other = lax.ppermute(dealt[:, 8:], "prow", swap)
+    extended = extend(slots, front_rows, arrived)
+    dealt, extended = lax.optimization_barrier((dealt, extended))
+    other = lax.ppermute(dealt[:, 16:], "prow", swap)
 
     L = jnp.where(q == 0, L0, L1)
     W = jnp.where(q == 0, W0, W1)
-    out = finish(slots, flags, front_rows, arrived, row0, dealt, other, L, W)
+    out = finish(flags, extended, dealt, other, L, W)
     return out.reshape(front.shape)
 
 

time: 338 us -> 365 us (1.080)
  the two profiles are of different devices: /device:TPU:1 before, /device:TPU:77 now
where the time goes in v5:
time: 365 us; the launch traced here: 363 us
  waiting for transfers between devices  117 us (32%)
  Pallas kernels  90 us (25%)
  starting transfers between devices  60.1 us (16%)
  blocking collectives  45 us (12%)
  local copies, waits for them, and re-layouts  31.2 us (9%)
  between operations  13.7 us (4%)
  other arithmetic  6.81 us (2%)
    all_to_all x1, waiting for transfers between devices, local(): dealt = lax.all_to_all(dealt, 'pcol', 0, 0, tiled=True)  66.9 us
    all_to_all x1, blocking collectives, spread(): lax.all_to_all(jnp.broadcast_to(x[None], (count,) + x.shape), axis, 0, 0,...  29.2 us
    all_to_all x1, waiting for transfers between devices, local(): got = lax.all_to_all(cut, 'pcol', 0, 0, tiled=True)  24.2 us
    unnamed x44, local copies, waits for them, and re-layouts  24 us
    pallas_call x1, Pallas kernels, factor_second(): pl.pallas_call(factor_second_kernel, out_shape=[jax.ShapeDtypeStruct((n,...  23.9 us
    ppermute x2, starting transfers between devices, gather_columns(): sent = lax.ppermute(jnp.where(core == 0, odd, even), 'prow', swap)  23.6 us
    pallas_call x1, Pallas kernels, factor_first(): pl.pallas_call(factor_first_kernel, out_shape=[jax.ShapeDtypeStruct((n, n...  22.7 us
    all_to_all x1, blocking collectives, local(): lax.all_to_all(jnp.tile(top, (prow // 2, 1, 1)), 'prow', 0, 0, tiled=True)  15.8 us
  transfers between devices with their start and end apart: 14, of which 9 were waited for; matrix products, arithmetic and copies ran while one was open for 3% of the time, Pallas kernels for 18%

profile of v5, /device:TPU:77, one launch (start us, length us, event | category | flops | bytes accessed | tf_op | source)
XLA Modules:
  0.0 363.4 jit_solution(18106329035384696391)
XLA Ops:
  6.5 2.8 copy-done.3
  9.4 3.2 shard_map.55
  13.2 6.9 %shard_map.57 = f32[16,6,16,1024]{3,2,1,0:T(8,128)} custom-call(s32[3]{0:T(128)} %pad_add_fusion.1.at_ref, f32[16384,128]{1,0:T(8,128)} %bitcast.63), custom_call_target="tpu_custom_call" | custom-call | bytes 12582912 | tf_op jit(solution)/shard_map/pallas_call | solution.py:214
  20.1 6.8 %all-to-all-start = ((bf16[16,14,16,256]{3,2,1,0:T(8,128)(2,1)}), bf16[16,14,16,256]{3,2,1,0:T(8,128)(2,1)S(1)}, u32[]{:S(2)}, u32[]{:S(2)}) async-start(bf16[16,14,16,256]{3,2,1,0:T(8,128)(2,1)} %shard_map.55), calls=%async_computation | async-start | bytes 3670016 | tf_op jit(solution)/shard_map/all_to_all | solution.py:466
  29.6 24.2 %all-to-all-done.c_ref = bf16[16,14,16,256]{3,2,1,0:T(8,128)(2,1)S(1)} async-done(((bf16[16,14,16,256]{3,2,1,0:T(8,128)(2,1)}), bf16[16,14,16,256]{3,2,1,0:T(8,128)(2,1)S(1)}, u32[]{:S(2)}, u32[]{:S(2)}) %all-to-all-start) | async-done | bytes 1835040 | tf_op jit(solution)/shard_map/all_to_all | solution.py:466
  55.0 2.3 shard_map.56.d_ref
  58.2 15.8 %all_to_all.25 = f32[8,16,1024]{2,1,0:T(8,128)S(1)} all-to-all(f32[8,16,1024]{2,1,0:T(8,128)S(1)} %bitcast.70), channel_id=1, replica_groups=mesh['prow'=8,'pcol'=16] {'prow'}, dimensions={0} | all-to-all | bytes 1048576 | tf_op jit(solution)/shard_map/all_to_all | solution.py:490
  74.2 29.2 %all_to_all.26.mine_ref = f32[16,16,1536]{2,1,0:T(8,128)S(1)} all-to-all(f32[16,16,1536]{2,1,0:T(8,128)S(1)} %broadcast_in_dim.111), channel_id=1, replica_groups=mesh['prow'=8,'pcol'=16] {'pcol'}, dimensions={0} | all-to-all | bytes 3145728 | tf_op jit(solution)/shard_map/all_to_all | solution.py:447
  104.6 3.0 collective-permute-done.other_ref
  108.8 8.2 %all-to-all-start.3 = ((bf16[16,3,256,256]{3,2,1,0:T(8,128)(2,1)}), bf16[16,3,256,256]{3,2,1,0:T(8,128)(2,1)}, u32[]{:S(2)}, u32[]{:S(2)}) async-start(bf16[16,3,256,256]{3,2,1,0:T(8,128)(2,1)} %bitcast.65), calls=%async_computation.4 | async-start | bytes 12582912 | tf_op jit(solution)/shard_map/all_to_all | solution.py:494
  119.9 22.7 %shard_map.59 = (f32[512,512]{1,0:T(8,128)S(1)}, f32[512,512]{1,0:T(8,128)S(1)}) custom-call(s32[3]{0:T(128)S(1)} %copy-done.15, f32[16,16,1536]{2,1,0:T(8,128)S(1)} %all_to_all.26.mine_ref, f32[16,16,1536]{2,1,0:T(8,128)S(1)} %copy-done.17), custom_call_target="tpu_custom_call" | custom-call | flops 20000000000 | bytes 3145728 | tf_op jit(solution)/shard_map/pallas_call | solution.py:148
  144.7 14.8 %reduce-scatter.2.cloned.1.call-done.f_ref = f32[6,16,1024]{2,1,0:T(8,128)} async-done(((f32[96,16,1024]{2,1,0:T(8,128)}), f32[6,16,1024]{2,1,0:T(8,128)}) %reduce-scatter.2.cloned.1.call-update) | async-done | bytes 393232 | tf_op jit(solution)/shard_map/reduce_scatter | solution.py:468
  159.5 2.6 shard_map.58.r_ref
  162.1 2.7 shard_map.60.p_ref.p0_ref
  165.8 22.3 %collective-permute-start.1 = (bf16[4,16,512]{2,1,0:T(8,128)(2,1)S(1)}, bf16[4,16,512]{2,1,0:T(8,128)(2,1)S(1)}, u32[]{:S(2)}, u32[]{:S(2)}) collective-permute-start(bf16[4,16,512]{2,1,0:T(8,128)(2,1)S(1)} %get-tuple-element.52), channel_id=1, source_target_pairs={{0,16},{16,0},{32,48},{48,32},{64,80},{80,64},{96,112},{112,96},{1... | collective-permute-start | bytes 196616 | tf_op jit(solution)/shard_map/ppermute | solution.py:499
  191.3 1.6 collective-permute-start.2
  195.5 23.9 %shard_map.61 = (bf16[512,512]{1,0:T(8,128)(2,1)S(1)}, f32[512,512]{1,0:T(8,128)S(1)}, f32[512,512]{1,0:T(8,128)S(1)}) custom-call(s32[3]{0:T(128)S(1)} %copy-done.15, s32[4]{0:T(128)S(1)} %reshape.313.mask_ref, f32[16,16,1536]{2,1,0:T(8,128)S(1)} %all_to_all.26.mine_ref, f32[16,16,1536]{2,1,0:T(8,128)S(1)} %copy-done.18, f32[512,512]{1,0:T(8,128)S(1)} %copy-done.6), custom_call_target="tpu_custom_call" | custom-call | flops 20000000000 | bytes 3145728 | tf_op jit(solution)/shard_map/pallas_call | solution.py:161
  222.2 3.1 shard_map.62.p1_ref
  228.5 3.0 collective-permute-start.7
  231.6 1.7 collective-permute-done.8.refs_7_
  233.2 1.5 collective-permute-done.7.refs_6_
  234.8 3.2 collective-permute-done.6.refs_5_
  239.8 2.3 copy-done.4
  242.1 11.5 %all-to-all-start.4 = ((bf16[16,20,16,512]{3,2,1,0:T(8,128)(2,1)}), bf16[16,20,16,512]{3,2,1,0:T(8,128)(2,1)}, u32[]{:S(2)}, u32[]{:S(2)}) async-start(bf16[16,20,16,512]{3,2,1,0:T(8,128)(2,1)} %copy-done.4), calls=%async_computation.5 | async-start | bytes 10485760 | tf_op jit(solution)/shard_map/all_to_all | solution.py:517
  254.7 3.4 copy-done.1
  258.1 8.0 %shard_map.64.f_ref = f32[16384,128]{1,0:T(8,128)S(1)} custom-call(s32[64]{0:T(128)S(1)} %broadcast_add_fusion.2.slot_ref, f32[16384,128]{1,0:T(8,128)S(1)} %bitcast.64, bf16[48,256,256]{2,1,0:T(8,128)(2,1)} %bitcast.22.refs_0_.refs_1_.refs_2_.refs_3_.refs_4_.refs_5_.refs_6_.refs_7_, ...), custom_call_target="tpu_custom_call" | custom-call | bytes 25165824 | tf_op jit(solution)/shard_map/pallas_call | solution.py:341
  266.0 3.3 copy-done.2
  269.3 66.9 %all-to-all-done.4.row0_ref.row1_ref.mine_ref = bf16[16,20,16,512]{3,2,1,0:T(8,128)(2,1)} async-done(((bf16[16,20,16,512]{3,2,1,0:T(8,128)(2,1)}), bf16[16,20,16,512]{3,2,1,0:T(8,128)(2,1)}, u32[]{:S(2)}, u32[]{:S(2)}) %all-to-all-start.4) | async-done | bytes 5242912 | tf_op jit(solution)/shard_map/all_to_all | solution.py:517
  336.2 2.3 slice.39
  338.5 1.9 collective-permute-start.9
  341.3 1.4 broadcast_select_fusion.1.l_ref
  342.9 13.6 %shard_map.65 = f32[16384,128]{1,0:T(8,128)} custom-call(s32[49]{0:T(128)S(1)} %pad_add_fusion.flag_ref, f32[16384,128]{1,0:T(8,128)} %copy-done.2, bf16[16,20,16,512]{3,2,1,0:T(8,128)(2,1)} %all-to-all-done.4.row0_ref.row1_ref.mine_ref, bf16[16,20,16,512]{3,2,1,0:T(8,128)(2,1)} %all-to-all-done.4.row0_ref.row1_ref.mine_ref, ...), custom_call_target="tpu_custom_call" | custom-call | flops 5000000000 | bytes 25165824 | tf_op jit(solution)/shard_map/pallas_call | solution.py:411
  (128 shorter events, 29.3 us)
Async XLA Ops:
  6.5 22.0 %copy-start = (s32[8,16,16,3]{2,1,3,0:T(8,128)S(1)}, s32[8,16,16,3]{2,1,3,0:T(8,128)}, u32[]{:S(2)}) copy-start(s32[8,16,16,3]{2,1,3,0:T(8,128)} %param.8) | copy-start | bytes 73732
  6.5 153.0 %reduce-scatter.2.cloned.1.call-start = ((), (), s32[]{:S(2)}) async-start(), calls=%async_computation.6 | async-start | bytes 6684672 | tf_op jit(solution)/shard_map/reduce_scatter | solution.py:468
  6.5 2.8 copy-start.3
  20.1 7.2 %copy-start.21 = (s32[2,60]{1,0:T(2,128)S(1)}, s32[2,60]{1,0:T(2,128)}, u32[]{:S(2)}) copy-start(s32[2,60]{1,0:T(2,128)} %param.7) | copy-start | bytes 1444
  20.1 33.6 %all-to-all-start = ((bf16[16,14,16,256]{3,2,1,0:T(8,128)(2,1)}), bf16[16,14,16,256]{3,2,1,0:T(8,128)(2,1)S(1)}, u32[]{:S(2)}, u32[]{:S(2)}) async-start(bf16[16,14,16,256]{3,2,1,0:T(8,128)(2,1)} %shard_map.55), calls=%async_computation | async-start | bytes 3670016 | tf_op jit(solution)/shard_map/all_to_all | solution.py:466
  53.7 1.3 copy-start.19
  103.4 4.2 %collective-permute-start = (f32[16,16,1536]{2,1,0:T(8,128)S(1)}, f32[16,16,1536]{2,1,0:T(8,128)S(1)}, u32[]{:S(2)}, u32[]{:S(2)}) collective-permute-start(f32[16,16,1536]{2,1,0:T(8,128)S(1)} %all_to_all.26.mine_ref), channel_id=1, source_target_pairs={{0,16},{16,0},{32,48},{48,32},{64,80},{80,64},{96,112},{112,96},{1... | collective-permute-start | bytes 4718600 | tf_op jit(solution)/shard_map/ppermute | solution.py:492
  107.6 1.2 copy-start.16
  108.8 8.3 %copy-start.20 = (s32[64,64]{1,0:T(8,128)S(1)}, s32[64,64]{1,0:T(8,128)}, u32[]{:S(2)}) copy-start(s32[64,64]{1,0:T(8,128)} %param.9) | copy-start | bytes 49156
  108.8 9.7 %copy-start.15 = (s32[3]{0:T(128)S(1)}, s32[3]{0:T(128)}, u32[]{:S(2)}) copy-start(s32[3]{0:T(128)} %pad_add_fusion.1.at_ref) | copy-start | bytes 40
  108.8 133.3 %all-to-all-start.3 = ((bf16[16,3,256,256]{3,2,1,0:T(8,128)(2,1)}), bf16[16,3,256,256]{3,2,1,0:T(8,128)(2,1)}, u32[]{:S(2)}, u32[]{:S(2)}) async-start(bf16[16,3,256,256]{3,2,1,0:T(8,128)(2,1)} %bitcast.65), calls=%async_computation.4 | async-start | bytes 12582912 | tf_op jit(solution)/shard_map/all_to_all | solution.py:494
  118.5 1.4 copy-start.17
  142.7 1.0 copy-start.5
  143.7 1.0 copy-start.12
  165.8 23.2 %collective-permute-start.1 = (bf16[4,16,512]{2,1,0:T(8,128)(2,1)S(1)}, bf16[4,16,512]{2,1,0:T(8,128)(2,1)S(1)}, u32[]{:S(2)}, u32[]{:S(2)}) collective-permute-start(bf16[4,16,512]{2,1,0:T(8,128)(2,1)S(1)} %get-tuple-element.52), channel_id=1, source_target_pairs={{0,16},{16,0},{32,48},{48,32},{64,80},{80,64},{96,112},{112,96},{1... | collective-permute-start | bytes 196616 | tf_op jit(solution)/shard_map/ppermute | solution.py:499
  189.0 49.0 %copy-start.10 = (bf16[8,16,512]{2,1,0:T(8,128)(2,1)S(1)}, bf16[8,16,512]{2,1,0:T(8,128)(2,1)}, u32[]{:S(2)}) copy-start(bf16[8,16,512]{2,1,0:T(8,128)(2,1)} %shard_map.60.p_ref.p0_ref) | copy-start | bytes 393220
  189.0 33.2 %collective-permute-start.4 = (bf16[2,4,16,512]{3,2,1,0:T(8,128)(2,1)S(1)}, bf16[2,4,16,512]{3,2,1,0:T(8,128)(2,1)S(1)}, u32[]{:S(2)}, u32[]{:S(2)}) collective-permute-start(bf16[2,4,16,512]{3,2,1,0:T(8,128)(2,1)S(1)} %maximum_select_fusion.refs_0_), channel_id=1, source_target_pairs={{96,0},{112,16},{0,32},{16,48},{32,64},{48,80},{64,96},{80,112},{9... | collective-permute-start | bytes 393224 | tf_op jit(solution)/shard_map/ppermute | solution.py:503
  190.3 31.9 %collective-permute-start.3 = (bf16[2,4,16,512]{3,2,1,0:T(8,128)(2,1)S(1)}, bf16[2,4,16,512]{3,2,1,0:T(8,128)(2,1)S(1)}, u32[]{:S(2)}, u32[]{:S(2)}) collective-permute-start(bf16[2,4,16,512]{3,2,1,0:T(8,128)(2,1)S(1)} %maximum_select_fusion.refs_0_), channel_id=1, source_target_pairs={{64,0},{80,16},{96,32},{112,48},{0,64},{16,80},{32,96},{48,112},{6... | collective-permute-start | bytes 393224 | tf_op jit(solution)/shard_map/ppermute | solution.py:503
  191.3 30.9 %collective-permute-start.2 = (bf16[2,4,16,512]{3,2,1,0:T(8,128)(2,1)S(1)}, bf16[2,4,16,512]{3,2,1,0:T(8,128)(2,1)S(1)}, u32[]{:S(2)}, u32[]{:S(2)}) collective-permute-start(bf16[2,4,16,512]{3,2,1,0:T(8,128)(2,1)S(1)} %maximum_select_fusion.refs_0_), channel_id=1, source_target_pairs={{32,0},{48,16},{64,32},{80,48},{96,64},{112,80},{0,96},{16,112},{3... | collective-permute-start | bytes 393224 | tf_op jit(solution)/shard_map/ppermute | solution.py:503
  192.9 1.2 copy-start.6
  194.1 1.4 copy-start.18
  226.3 2.2 collective-permute-start.5
  228.4 4.8 %collective-permute-start.8 = (bf16[2,4,16,512]{3,2,1,0:T(8,128)(2,1)S(1)}, bf16[2,4,16,512]{3,2,1,0:T(8,128)(2,1)S(1)}, u32[]{:S(2)}, u32[]{:S(2)}) collective-permute-start(bf16[2,4,16,512]{3,2,1,0:T(8,128)(2,1)S(1)} %maximum_select_fusion.1.refs_4_), channel_id=1, source_target_pairs={{96,0},{112,16},{0,32},{16,48},{32,64},{48,80},{64,96},{80,112},{9... | collective-permute-start | bytes 393224 | tf_op jit(solution)/shard_map/ppermute | solution.py:503
  228.5 6.3 %collective-permute-start.7 = (bf16[2,4,16,512]{3,2,1,0:T(8,128)(2,1)S(1)}, bf16[2,4,16,512]{3,2,1,0:T(8,128)(2,1)S(1)}, u32[]{:S(2)}, u32[]{:S(2)}) collective-permute-start(bf16[2,4,16,512]{3,2,1,0:T(8,128)(2,1)S(1)} %maximum_select_fusion.1.refs_4_), channel_id=1, source_target_pairs={{64,0},{80,16},{96,32},{112,48},{0,64},{16,80},{32,96},{48,112},{6... | collective-permute-start | bytes 393224 | tf_op jit(solution)/shard_map/ppermute | solution.py:503
  231.6 6.4 %collective-permute-start.6 = (bf16[2,4,16,512]{3,2,1,0:T(8,128)(2,1)S(1)}, bf16[2,4,16,512]{3,2,1,0:T(8,128)(2,1)S(1)}, u32[]{:S(2)}, u32[]{:S(2)}) collective-permute-start(bf16[2,4,16,512]{3,2,1,0:T(8,128)(2,1)S(1)} %maximum_select_fusion.1.refs_4_), channel_id=1, source_target_pairs={{32,0},{48,16},{64,32},{80,48},{96,64},{112,80},{0,96},{16,112},{3... | collective-permute-start | bytes 393224 | tf_op jit(solution)/shard_map/ppermute | solution.py:503
  239.8 2.4 copy-start.4
  242.1 94.1 %all-to-all-start.4 = ((bf16[16,20,16,512]{3,2,1,0:T(8,128)(2,1)}), bf16[16,20,16,512]{3,2,1,0:T(8,128)(2,1)}, u32[]{:S(2)}, u32[]{:S(2)}) async-start(bf16[16,20,16,512]{3,2,1,0:T(8,128)(2,1)} %copy-done.4), calls=%async_computation.5 | async-start | bytes 10485760 | tf_op jit(solution)/shard_map/all_to_all | solution.py:517
  254.7 3.4 copy-start.1
  266.0 3.3 copy-start.2
  269.3 73.4 %copy-start.7 = (f32[512,512]{1,0:T(8,128)S(1)}, f32[512,512]{1,0:T(8,128)}, u32[]{:S(2)}) copy-start(f32[512,512]{1,0:T(8,128)} %copy-done.5) | copy-start | bytes 3145732
  269.3 73.4 %copy-start.9 = (f32[512,512]{1,0:T(8,128)S(1)}, f32[512,512]{1,0:T(8,128)}, u32[]{:S(2)}) copy-start(f32[512,512]{1,0:T(8,128)} %copy-done.8) | copy-start | bytes 3145732
  338.5 4.4 %collective-permute-start.9 = (bf16[16,4,16,512]{3,2,1,0:T(8,128)(2,1)}, bf16[16,4,16,512]{3,2,1,0:T(8,128)(2,1)S(1)}, u32[]{:S(2)}, u32[]{:S(2)}) collective-permute-start(bf16[16,4,16,512]{3,2,1,0:T(8,128)(2,1)} %slice.39), channel_id=1, source_target_pairs={{0,16},{16,0},{32,48},{48,32},{64,80},{80,64},{96,112},{112,96},{1... | collective-permute-start | bytes 3145736 | tf_op jit(solution)/shard_map/ppermute | solution.py:520
  (4 other events, 3.7 us)
Sparse Core Ops, SparseCore 0:
  20.2 139.2 reduce-scatter.1

commit v6 on v5

--- a/solution.py
+++ b/solution.py
@@ -490,7 +490,7 @@
     half_top = lax.all_to_all(jnp.tile(top, (prow // 2, 1, 1)), "prow", 0, 0, tiled=True)
     first = spread(jnp.concatenate([half_top[0, :, :512], half_top[1]], axis=1), "pcol", pcol)
     diag = (first, lax.ppermute(first, "prow", swap))
-    child, diag = lax.optimization_barrier((child, diag))
+    child, diag, low_front = lax.optimization_barrier((child, diag, low_front))
     arrived = lax.all_to_all(child, "pcol", 0, 0, tiled=True).reshape(48, 256, 256)
 
     def gather_columns(strips):

time: 365 us -> 335 us (0.918)
  the two profiles are of different devices: /device:TPU:77 before, /device:TPU:1 now
where the time goes in v6:
time: 335 us; the launch traced here: 333 us
  waiting for transfers between devices  96.7 us (29%)
  Pallas kernels  93.4 us (28%)
  blocking collectives  49.1 us (15%)
  starting transfers between devices  42.4 us (13%)
  local copies, waits for them, and re-layouts  31.1 us (9%)
  between operations  13.7 us (4%)
  other arithmetic  6.9 us (2%)
    all_to_all x1, waiting for transfers between devices, local(): dealt = lax.all_to_all(dealt, 'pcol', 0, 0, tiled=True)  43.4 us
    all_to_all x1, blocking collectives, spread(): lax.all_to_all(jnp.broadcast_to(x[None], (count,) + x.shape), axis, 0, 0,...  29.4 us
    unnamed x44, local copies, waits for them, and re-layouts  24 us
    pallas_call x1, Pallas kernels, factor_second(): pl.pallas_call(factor_second_kernel, out_shape=[jax.ShapeDtypeStruct((n,...  23.9 us
    all_to_all x1, waiting for transfers between devices, local(): got = lax.all_to_all(cut, 'pcol', 0, 0, tiled=True)  23.3 us
    pallas_call x1, Pallas kernels, factor_first(): pl.pallas_call(factor_first_kernel, out_shape=[jax.ShapeDtypeStruct((n, n...  22.7 us
    all_to_all x1, blocking collectives, local(): lax.all_to_all(jnp.tile(top, (prow // 2, 1, 1)), 'prow', 0, 0, tiled=True)  19.7 us
    pallas_call x1, Pallas kernels, finish(): pl.pallas_call(finish_kernel, grid_spec=pltpu.PrefetchScalarGridSpec(num_...  17 us
  transfers between devices with their start and end apart: 14, of which 9 were waited for; matrix products, arithmetic and copies ran while one was open for 3% of the time, Pallas kernels for 20%

profile of v6, /device:TPU:1, one launch (start us, length us, event | category | flops | bytes accessed | tf_op | source)
XLA Modules:
  0.0 333.3 jit_solution(15124858021508089607)
XLA Ops:
  6.5 2.8 copy-done.3
  9.4 3.2 shard_map.55
  13.2 7.1 %shard_map.57 = f32[16,6,16,1024]{3,2,1,0:T(8,128)} custom-call(s32[3]{0:T(128)} %pad_add_fusion.1.at_ref, f32[16384,128]{1,0:T(8,128)} %bitcast.63), custom_call_target="tpu_custom_call" | custom-call | bytes 12582912 | tf_op jit(solution)/shard_map/pallas_call | solution.py:214
  20.4 8.2 %all-to-all-start = ((bf16[16,14,16,256]{3,2,1,0:T(8,128)(2,1)}), bf16[16,14,16,256]{3,2,1,0:T(8,128)(2,1)S(1)}, u32[]{:S(2)}, u32[]{:S(2)}) async-start(bf16[16,14,16,256]{3,2,1,0:T(8,128)(2,1)} %shard_map.55), calls=%async_computation | async-start | bytes 3670016 | tf_op jit(solution)/shard_map/all_to_all | solution.py:466
  31.3 23.3 %all-to-all-done.c_ref = bf16[16,14,16,256]{3,2,1,0:T(8,128)(2,1)S(1)} async-done(((bf16[16,14,16,256]{3,2,1,0:T(8,128)(2,1)}), bf16[16,14,16,256]{3,2,1,0:T(8,128)(2,1)S(1)}, u32[]{:S(2)}, u32[]{:S(2)}) %all-to-all-start) | async-done | bytes 1835040 | tf_op jit(solution)/shard_map/all_to_all | solution.py:466
  55.9 2.3 shard_map.56.d_ref
  59.1 19.7 %all_to_all.25 = f32[8,16,1024]{2,1,0:T(8,128)S(1)} all-to-all(f32[8,16,1024]{2,1,0:T(8,128)S(1)} %bitcast.70), channel_id=1, replica_groups=mesh['prow'=8,'pcol'=16] {'prow'}, dimensions={0} | all-to-all | bytes 1048576 | tf_op jit(solution)/shard_map/all_to_all | solution.py:490
  78.9 29.4 %all_to_all.26.mine_ref = f32[16,16,1536]{2,1,0:T(8,128)S(1)} all-to-all(f32[16,16,1536]{2,1,0:T(8,128)S(1)} %broadcast_in_dim.111), channel_id=1, replica_groups=mesh['prow'=8,'pcol'=16] {'pcol'}, dimensions={0} | all-to-all | bytes 3145728 | tf_op jit(solution)/shard_map/all_to_all | solution.py:447
  108.3 1.7 collective-permute-start
  110.1 3.0 collective-permute-done.other_ref
  114.3 15.1 %reduce-scatter.2.cloned.1.call-done.f_ref = f32[6,16,1024]{2,1,0:T(8,128)} async-done(((f32[96,16,1024]{2,1,0:T(8,128)}), f32[6,16,1024]{2,1,0:T(8,128)}) %reduce-scatter.2.cloned.1.call-update) | async-done | bytes 393232 | tf_op jit(solution)/shard_map/reduce_scatter | solution.py:468
  129.4 4.8 %all-to-all-start.3 = ((bf16[16,3,256,256]{3,2,1,0:T(8,128)(2,1)}), bf16[16,3,256,256]{3,2,1,0:T(8,128)(2,1)}, u32[]{:S(2)}, u32[]{:S(2)}) async-start(bf16[16,3,256,256]{3,2,1,0:T(8,128)(2,1)} %bitcast.65), calls=%async_computation.4 | async-start | bytes 12582912 | tf_op jit(solution)/shard_map/all_to_all | solution.py:494
  135.8 2.6 shard_map.58.r_ref
  139.8 22.7 %shard_map.59 = (f32[512,512]{1,0:T(8,128)S(1)}, f32[512,512]{1,0:T(8,128)S(1)}) custom-call(s32[3]{0:T(128)S(1)} %copy-done.15, f32[16,16,1536]{2,1,0:T(8,128)S(1)} %all_to_all.26.mine_ref, f32[16,16,1536]{2,1,0:T(8,128)S(1)} %copy-done.17), custom_call_target="tpu_custom_call" | custom-call | flops 20000000000 | bytes 3145728 | tf_op jit(solution)/shard_map/pallas_call | solution.py:148
  164.5 2.7 shard_map.60.p_ref.p0_ref
  168.1 2.1 collective-permute-start.1
  172.4 2.5 collective-permute-start.3
  178.7 23.9 %shard_map.61 = (bf16[512,512]{1,0:T(8,128)(2,1)S(1)}, f32[512,512]{1,0:T(8,128)S(1)}, f32[512,512]{1,0:T(8,128)S(1)}) custom-call(s32[3]{0:T(128)S(1)} %copy-done.15, s32[4]{0:T(128)S(1)} %reshape.313.mask_ref, f32[16,16,1536]{2,1,0:T(8,128)S(1)} %all_to_all.26.mine_ref, f32[16,16,1536]{2,1,0:T(8,128)S(1)} %copy-done.18, f32[512,512]{1,0:T(8,128)S(1)} %copy-done.6), custom_call_target="tpu_custom_call" | custom-call | flops 20000000000 | bytes 3145728 | tf_op jit(solution)/shard_map/pallas_call | solution.py:161
  205.4 3.1 shard_map.62.p1_ref
  212.6 1.9 collective-permute-start.6
  214.5 6.1 %collective-permute-done.8.refs_7_ = bf16[2,4,16,512]{3,2,1,0:T(8,128)(2,1)S(1)} collective-permute-done((bf16[2,4,16,512]{3,2,1,0:T(8,128)(2,1)S(1)}, bf16[2,4,16,512]{3,2,1,0:T(8,128)(2,1)S(1)}, u32[]{:S(2)}, u32[]{:S(2)}) %collective-permute-start.8) | collective-permute-done | bytes 131104 | tf_op jit(solution)/shard_map/ppermute | solution.py:503
  222.7 2.3 copy-done.4
  225.0 4.2 %all-to-all-done.3 = bf16[16,3,256,256]{3,2,1,0:T(8,128)(2,1)} async-done(((bf16[16,3,256,256]{3,2,1,0:T(8,128)(2,1)}), bf16[16,3,256,256]{3,2,1,0:T(8,128)(2,1)}, u32[]{:S(2)}, u32[]{:S(2)}) %all-to-all-start.3) | async-done | bytes 6291488 | tf_op jit(solution)/shard_map/all_to_all | solution.py:494
  229.2 7.2 %all-to-all-start.4 = ((bf16[16,20,16,512]{3,2,1,0:T(8,128)(2,1)}), bf16[16,20,16,512]{3,2,1,0:T(8,128)(2,1)}, u32[]{:S(2)}, u32[]{:S(2)}) async-start(bf16[16,20,16,512]{3,2,1,0:T(8,128)(2,1)} %copy-done.4), calls=%async_computation.5 | async-start | bytes 10485760 | tf_op jit(solution)/shard_map/all_to_all | solution.py:517
  237.5 3.4 %copy-done.1 = f32[4,1,512,2,1,512]{5,4,3,2,1,0:T(1,128)S(1)} copy-done((f32[4,1,512,2,1,512]{5,4,3,2,1,0:T(1,128)S(1)}, f32[4,1,512,2,1,512]{5,4,3,2,1,0:T(1,128)}, u32[]{:S(2)}) %copy-start.1) | copy-done | bytes 8388632
  240.9 7.8 %shard_map.64.f_ref = f32[16384,128]{1,0:T(8,128)S(1)} custom-call(s32[64]{0:T(128)S(1)} %broadcast_add_fusion.2.slot_ref, f32[16384,128]{1,0:T(8,128)S(1)} %bitcast.64, bf16[48,256,256]{2,1,0:T(8,128)(2,1)} %bitcast.22.refs_0_.refs_1_.refs_2_.refs_3_.refs_4_.refs_5_.refs_6_.refs_7_, ...), custom_call_target="tpu_custom_call" | custom-call | bytes 25165824 | tf_op jit(solution)/shard_map/pallas_call | solution.py:341
  248.8 3.3 copy-done.2
  252.0 43.4 %all-to-all-done.4.row0_ref.row1_ref.mine_ref = bf16[16,20,16,512]{3,2,1,0:T(8,128)(2,1)} async-done(((bf16[16,20,16,512]{3,2,1,0:T(8,128)(2,1)}), bf16[16,20,16,512]{3,2,1,0:T(8,128)(2,1)}, u32[]{:S(2)}, u32[]{:S(2)}) %all-to-all-start.4) | async-done | bytes 5242912 | tf_op jit(solution)/shard_map/all_to_all | solution.py:517
  295.4 2.3 slice.39
  297.7 9.3 %collective-permute-start.9 = (bf16[16,4,16,512]{3,2,1,0:T(8,128)(2,1)}, bf16[16,4,16,512]{3,2,1,0:T(8,128)(2,1)S(1)}, u32[]{:S(2)}, u32[]{:S(2)}) collective-permute-start(bf16[16,4,16,512]{3,2,1,0:T(8,128)(2,1)} %slice.39), channel_id=1, source_target_pairs={{0,16},{16,0},{32,48},{48,32},{64,80},{80,64},{96,112},{112,96},{1... | collective-permute-start | bytes 3145736 | tf_op jit(solution)/shard_map/ppermute | solution.py:520
  307.8 1.4 broadcast_select_fusion.1.l_ref
  309.5 17.0 %shard_map.65 = f32[16384,128]{1,0:T(8,128)} custom-call(s32[49]{0:T(128)S(1)} %pad_add_fusion.flag_ref, f32[16384,128]{1,0:T(8,128)} %copy-done.2, bf16[16,20,16,512]{3,2,1,0:T(8,128)(2,1)} %all-to-all-done.4.row0_ref.row1_ref.mine_ref, bf16[16,20,16,512]{3,2,1,0:T(8,128)(2,1)} %all-to-all-done.4.row0_ref.row1_ref.mine_ref, ...), custom_call_target="tpu_custom_call" | custom-call | flops 5000000000 | bytes 25165824 | tf_op jit(solution)/shard_map/pallas_call | solution.py:411
  (128 shorter events, 29.6 us)
Async XLA Ops:
  6.5 23.7 %copy-start = (s32[8,16,16,3]{2,1,3,0:T(8,128)S(1)}, s32[8,16,16,3]{2,1,3,0:T(8,128)}, u32[]{:S(2)}) copy-start(s32[8,16,16,3]{2,1,3,0:T(8,128)} %param.8) | copy-start | bytes 73732
  6.5 122.9 %reduce-scatter.2.cloned.1.call-start = ((), (), s32[]{:S(2)}) async-start(), calls=%async_computation.6 | async-start | bytes 6684672 | tf_op jit(solution)/shard_map/reduce_scatter | solution.py:468
  6.5 2.8 copy-start.3
  20.4 8.6 %copy-start.21 = (s32[2,60]{1,0:T(2,128)S(1)}, s32[2,60]{1,0:T(2,128)}, u32[]{:S(2)}) copy-start(s32[2,60]{1,0:T(2,128)} %param.7) | copy-start | bytes 1444
  20.4 34.2 %all-to-all-start = ((bf16[16,14,16,256]{3,2,1,0:T(8,128)(2,1)}), bf16[16,14,16,256]{3,2,1,0:T(8,128)(2,1)S(1)}, u32[]{:S(2)}, u32[]{:S(2)}) async-start(bf16[16,14,16,256]{3,2,1,0:T(8,128)(2,1)} %shard_map.55), calls=%async_computation | async-start | bytes 3670016 | tf_op jit(solution)/shard_map/all_to_all | solution.py:466
  54.6 1.3 copy-start.19
  108.3 4.7 %collective-permute-start = (f32[16,16,1536]{2,1,0:T(8,128)S(1)}, f32[16,16,1536]{2,1,0:T(8,128)S(1)}, u32[]{:S(2)}, u32[]{:S(2)}) collective-permute-start(f32[16,16,1536]{2,1,0:T(8,128)S(1)} %all_to_all.26.mine_ref), channel_id=1, source_target_pairs={{0,16},{16,0},{32,48},{48,32},{64,80},{80,64},{96,112},{112,96},{1... | collective-permute-start | bytes 4718600 | tf_op jit(solution)/shard_map/ppermute | solution.py:492
  113.1 1.2 copy-start.16
  129.4 4.9 %copy-start.20 = (s32[64,64]{1,0:T(8,128)S(1)}, s32[64,64]{1,0:T(8,128)}, u32[]{:S(2)}) copy-start(s32[64,64]{1,0:T(8,128)} %param.9) | copy-start | bytes 49156
  129.4 8.9 %copy-start.15 = (s32[3]{0:T(128)S(1)}, s32[3]{0:T(128)}, u32[]{:S(2)}) copy-start(s32[3]{0:T(128)} %pad_add_fusion.1.at_ref) | copy-start | bytes 40
  129.4 99.8 %all-to-all-start.3 = ((bf16[16,3,256,256]{3,2,1,0:T(8,128)(2,1)}), bf16[16,3,256,256]{3,2,1,0:T(8,128)(2,1)}, u32[]{:S(2)}, u32[]{:S(2)}) async-start(bf16[16,3,256,256]{3,2,1,0:T(8,128)(2,1)} %bitcast.65), calls=%async_computation.4 | async-start | bytes 12582912 | tf_op jit(solution)/shard_map/all_to_all | solution.py:494
  138.3 1.4 copy-start.17
  162.5 1.0 copy-start.5
  163.5 1.0 copy-start.12
  168.1 3.0 collective-permute-start.1
  171.1 49.7 %copy-start.10 = (bf16[8,16,512]{2,1,0:T(8,128)(2,1)S(1)}, bf16[8,16,512]{2,1,0:T(8,128)(2,1)}, u32[]{:S(2)}) copy-start(bf16[8,16,512]{2,1,0:T(8,128)(2,1)} %shard_map.60.p_ref.p0_ref) | copy-start | bytes 393220
  171.2 34.2 %collective-permute-start.4 = (bf16[2,4,16,512]{3,2,1,0:T(8,128)(2,1)S(1)}, bf16[2,4,16,512]{3,2,1,0:T(8,128)(2,1)S(1)}, u32[]{:S(2)}, u32[]{:S(2)}) collective-permute-start(bf16[2,4,16,512]{3,2,1,0:T(8,128)(2,1)S(1)} %maximum_select_fusion.refs_0_), channel_id=1, source_target_pairs={{96,0},{112,16},{0,32},{16,48},{32,64},{48,80},{64,96},{80,112},{9... | collective-permute-start | bytes 393224 | tf_op jit(solution)/shard_map/ppermute | solution.py:503
  172.4 32.9 %collective-permute-start.3 = (bf16[2,4,16,512]{3,2,1,0:T(8,128)(2,1)S(1)}, bf16[2,4,16,512]{3,2,1,0:T(8,128)(2,1)S(1)}, u32[]{:S(2)}, u32[]{:S(2)}) collective-permute-start(bf16[2,4,16,512]{3,2,1,0:T(8,128)(2,1)S(1)} %maximum_select_fusion.refs_0_), channel_id=1, source_target_pairs={{64,0},{80,16},{96,32},{112,48},{0,64},{16,80},{32,96},{48,112},{6... | collective-permute-start | bytes 393224 | tf_op jit(solution)/shard_map/ppermute | solution.py:503
  174.9 30.5 %collective-permute-start.2 = (bf16[2,4,16,512]{3,2,1,0:T(8,128)(2,1)S(1)}, bf16[2,4,16,512]{3,2,1,0:T(8,128)(2,1)S(1)}, u32[]{:S(2)}, u32[]{:S(2)}) collective-permute-start(bf16[2,4,16,512]{3,2,1,0:T(8,128)(2,1)S(1)} %maximum_select_fusion.refs_0_), channel_id=1, source_target_pairs={{32,0},{48,16},{64,32},{80,48},{96,64},{112,80},{0,96},{16,112},{3... | collective-permute-start | bytes 393224 | tf_op jit(solution)/shard_map/ppermute | solution.py:503
  176.0 1.2 copy-start.6
  177.3 1.4 copy-start.18
  209.4 2.2 collective-permute-start.5
  211.6 9.0 %collective-permute-start.8 = (bf16[2,4,16,512]{3,2,1,0:T(8,128)(2,1)S(1)}, bf16[2,4,16,512]{3,2,1,0:T(8,128)(2,1)S(1)}, u32[]{:S(2)}, u32[]{:S(2)}) collective-permute-start(bf16[2,4,16,512]{3,2,1,0:T(8,128)(2,1)S(1)} %maximum_select_fusion.1.refs_4_), channel_id=1, source_target_pairs={{96,0},{112,16},{0,32},{16,48},{32,64},{48,80},{64,96},{80,112},{9... | collective-permute-start | bytes 393224 | tf_op jit(solution)/shard_map/ppermute | solution.py:503
  212.0 8.6 %collective-permute-start.7 = (bf16[2,4,16,512]{3,2,1,0:T(8,128)(2,1)S(1)}, bf16[2,4,16,512]{3,2,1,0:T(8,128)(2,1)S(1)}, u32[]{:S(2)}, u32[]{:S(2)}) collective-permute-start(bf16[2,4,16,512]{3,2,1,0:T(8,128)(2,1)S(1)} %maximum_select_fusion.1.refs_4_), channel_id=1, source_target_pairs={{64,0},{80,16},{96,32},{112,48},{0,64},{16,80},{32,96},{48,112},{6... | collective-permute-start | bytes 393224 | tf_op jit(solution)/shard_map/ppermute | solution.py:503
  212.6 8.3 %collective-permute-start.6 = (bf16[2,4,16,512]{3,2,1,0:T(8,128)(2,1)S(1)}, bf16[2,4,16,512]{3,2,1,0:T(8,128)(2,1)S(1)}, u32[]{:S(2)}, u32[]{:S(2)}) collective-permute-start(bf16[2,4,16,512]{3,2,1,0:T(8,128)(2,1)S(1)} %maximum_select_fusion.1.refs_4_), channel_id=1, source_target_pairs={{32,0},{48,16},{64,32},{80,48},{96,64},{112,80},{0,96},{16,112},{3... | collective-permute-start | bytes 393224 | tf_op jit(solution)/shard_map/ppermute | solution.py:503
  222.7 2.4 copy-start.4
  229.2 66.2 %all-to-all-start.4 = ((bf16[16,20,16,512]{3,2,1,0:T(8,128)(2,1)}), bf16[16,20,16,512]{3,2,1,0:T(8,128)(2,1)}, u32[]{:S(2)}, u32[]{:S(2)}) async-start(bf16[16,20,16,512]{3,2,1,0:T(8,128)(2,1)} %copy-done.4), calls=%async_computation.5 | async-start | bytes 10485760 | tf_op jit(solution)/shard_map/all_to_all | solution.py:517
  237.5 3.4 %copy-start.1 = (f32[4,1,512,2,1,512]{5,4,3,2,1,0:T(1,128)S(1)}, f32[4,1,512,2,1,512]{5,4,3,2,1,0:T(1,128)}, u32[]{:S(2)}) copy-start(f32[4,1,512,2,1,512]{5,4,3,2,1,0:T(1,128)} %param.5) | copy-start | bytes 25165828
  248.7 3.3 copy-start.2
  252.0 57.2 %copy-start.7 = (f32[512,512]{1,0:T(8,128)S(1)}, f32[512,512]{1,0:T(8,128)}, u32[]{:S(2)}) copy-start(f32[512,512]{1,0:T(8,128)} %copy-done.5) | copy-start | bytes 3145732
  252.0 57.2 %copy-start.9 = (f32[512,512]{1,0:T(8,128)S(1)}, f32[512,512]{1,0:T(8,128)}, u32[]{:S(2)}) copy-start(f32[512,512]{1,0:T(8,128)} %copy-done.8) | copy-start | bytes 3145732
  297.7 11.8 %collective-permute-start.9 = (bf16[16,4,16,512]{3,2,1,0:T(8,128)(2,1)}, bf16[16,4,16,512]{3,2,1,0:T(8,128)(2,1)S(1)}, u32[]{:S(2)}, u32[]{:S(2)}) collective-permute-start(bf16[16,4,16,512]{3,2,1,0:T(8,128)(2,1)} %slice.39), channel_id=1, source_target_pairs={{0,16},{16,0},{32,48},{48,32},{64,80},{80,64},{96,112},{112,96},{1... | collective-permute-start | bytes 3145736 | tf_op jit(solution)/shard_map/ppermute | solution.py:520
  (4 other events, 3.7 us)
Sparse Core Ops, SparseCore 0:
  20.5 108.8 reduce-scatter.1

commit v7 on v5

--- a/solution.py
+++ b/solution.py
@@ -171,54 +171,37 @@
     )(at, mask, mine, other, W0)
 
 
-def cut_top_kernel(x_ref, c_ref, o_ref):
-    for k in range(6):
-        o_ref[:, k] = c_ref[k].reshape(16, 16, 256)
-    for i in range(2):
-        for c in range(4):
-            high, low = split(x_ref[pl.ds(i * 2048 + c, 256, stride=8), :])
-            at = 6 + i * 4 + c // 2 * 2
-            lanes = slice(c % 2 * 128, c % 2 * 128 + 128)
-            o_ref[:, at, :, lanes] = high.reshape(16, 16, 128)
-            o_ref[:, at + 1, :, lanes] = low.reshape(16, 16, 128)
-
-
-def cut_top(front_rows, child):
-    return pl.pallas_call(
-        cut_top_kernel,
-        grid=(1,),
-        out_shape=jax.ShapeDtypeStruct((16, 14, 16, 256), BF16),
+def cut_kernel(x_ref, c_ref, o_ref):
+    i = pl.program_id(0)
+
+    @pl.when(i < 3)
+    def _():
+        for k in range(2):
+            o_ref[:, k] = c_ref[k].reshape(16, 16, 256)
+
+    for half in range(2):
+
+        @pl.when((i >= 3) & (lax.rem(i, 2) == 1 - half))
+        def _():
+            for c in range(2):
+                high, low = split(x_ref[pl.ds(half * 2 + c, 256, stride=8), :])
+                lanes = slice(c * 128, c * 128 + 128)
+                o_ref[:, 0, :, lanes] = high.reshape(16, 16, 128)
+                o_ref[:, 1, :, lanes] = low.reshape(16, 16, 128)
+
+
+def cut_strips(front_rows, child):
+    return pl.pallas_call(
+        cut_kernel,
+        grid=(19,),
+        out_shape=jax.ShapeDtypeStruct((16, 38, 16, 256), BF16),
         in_specs=[
-            pl.BlockSpec((4096, 128), lambda i: (0, 0)),
-            pl.BlockSpec((6, 256, 256), lambda i: (0, 0, 0)),
+            pl.BlockSpec((2048, 128), lambda i: (jnp.maximum(i - 3, 0) // 2, 0)),
+            pl.BlockSpec((2, 256, 256), lambda i: (jnp.minimum(i, 2), 0, 0)),
         ],
-        out_specs=pl.BlockSpec((16, 14, 16, 256), lambda i: (0, 0, 0, 0)),
-        cost_estimate=pl.CostEstimate(flops=0, bytes_accessed=5 * MIB, transcendentals=0),
-        compiler_params=pltpu.CompilerParams(vmem_limit_bytes=40 * MIB),
+        out_specs=pl.BlockSpec((16, 2, 16, 256), lambda i: (0, i, 0, 0)),
+        cost_estimate=pl.CostEstimate(flops=0, bytes_accessed=14 * MIB, transcendentals=0),
     )(front_rows, child)
-
-
-def cut_low_kernel(at_ref, x_ref, o_ref):
-    q = at_ref[1]
-    o_ref[...] = jnp.zeros(o_ref.shape, F32)
-    for owner in range(2):
-
-        @pl.when(q == owner)
-        def _():
-            for c in range(4):
-                tile = x_ref[pl.ds(c, 256, stride=8), :]
-                o_ref[:, 0, :, owner * 512 + c * 128 : owner * 512 + c * 128 + 128] = tile.reshape(16, 16, 128)
-
-
-def cut_low(at, front_rows):
-    return pl.pallas_call(
-        cut_low_kernel,
-        grid=(6,),
-        out_shape=jax.ShapeDtypeStruct((16, 6, 16, 1024), F32),
-        in_specs=[SMEM, pl.BlockSpec((2048, 128), lambda i: (i + 2, 0))],
-        out_specs=pl.BlockSpec((16, 1, 16, 1024), lambda i: (0, i, 0, 0)),
-        cost_estimate=pl.CostEstimate(flops=0, bytes_accessed=12 * MIB, transcendentals=0),
-    )(at, front_rows)
 
 
 def add_pieces(value, slot_ref, c_ref, row, j):
@@ -230,29 +213,27 @@
     return value
 
 
-def join_top_kernel(slot_ref, c_ref, o_ref):
-    for i in range(2):
+def join_kernel(first, slot_ref, c_ref, f_ref, o_ref):
+    for i in range(o_ref.shape[0]):
         for j in range(4):
-            at = 6 + i * 4 + j % 2 * 2
-            value = c_ref[j // 2, at].astype(F32) + c_ref[j // 2, at + 1].astype(F32)
-            o_ref[i, :, j * 256 : (j + 1) * 256] = add_pieces(value, slot_ref, c_ref, i, j)
-
-
-def join_low_kernel(slot_ref, c_ref, f_ref, o_ref):
-    for i in range(6):
-        for j in range(4):
-            lanes = slice(j * 256, (j + 1) * 256)
-            o_ref[i, :, lanes] = add_pieces(f_ref[i, :, lanes], slot_ref, c_ref, i + 2, j)
-
-
-def join_strips(kernel, count, slots, *operands):
-    return pl.pallas_call(
-        kernel,
+            at = 6 + (i + first) * 4 + j % 2 * 2
+            value = f_ref[j // 2, at].astype(F32) + f_ref[j // 2, at + 1].astype(F32)
+            o_ref[i, :, j * 256 : (j + 1) * 256] = add_pieces(value, slot_ref, c_ref, i + first, j)
+
+
+def join_strips(first, count, slots, got):
+    return pl.pallas_call(
+        functools.partial(join_kernel, first),
+        grid=(1,),
         out_shape=jax.ShapeDtypeStruct((count, 16, 1024), F32),
-        in_specs=[SMEM] + [VMEM] * len(operands),
-        out_specs=VMEM,
+        in_specs=[
+            SMEM,
+            pl.BlockSpec((16, 6, 16, 256), lambda i: (0, 0, 0, 0)),
+            pl.BlockSpec((2, 38, 16, 256), lambda i: (0, 0, 0, 0)),
+        ],
+        out_specs=pl.BlockSpec((count, 16, 1024), lambda i: (0, 0, 0)),
         cost_estimate=pl.CostEstimate(flops=0, bytes_accessed=3 * MIB, transcendentals=0),
-    )(slots, *operands)
+    )(slots, got, got)
 
 
 def solve_first_kernel(keep_ref, d_ref, r_ref, w_ref, o_ref):
@@ -462,12 +443,7 @@
     sub_rows = (2 * row_blocks[:, None] + pair).reshape(-1)
     sub_cols = (2 * col_blocks[:, None] + pair).reshape(-1)
 
-    cut = cut_top(front_rows, child.reshape(48, 256, 256))
-    got = lax.all_to_all(cut, "pcol", 0, 0, tiled=True)
-    front_rows, _ = lax.optimization_barrier((front_rows, cut))
-    low_front = lax.psum_scatter(
-        cut_low(at, front_rows).reshape(96, 16, 1024), "pcol", scatter_dimension=0, tiled=True
-    )
+    got = lax.all_to_all(cut_strips(front_rows, child.reshape(48, 256, 256)), "pcol", 0, 0, tiled=True)
 
     my_codes = lax.dynamic_index_in_dim(slot_table, p, 0, False)
     strip_slots = slot_of_targets(my_codes[:, :2].reshape(-1), row_map, sub_rows, jnp.arange(4, dtype=jnp.int32))
@@ -485,7 +461,7 @@
     keep0 = (sub_rows >= 2).astype(jnp.int32)
     keep1 = jnp.concatenate([(sub_rows >= 4).astype(jnp.int32), row_mask[:, 2:4].reshape(-1)])
 
-    top = join_strips(join_top_kernel, 2, strip_slots, got)
+    top = join_strips(0, 2, strip_slots, got)
 
     half_top = lax.all_to_all(jnp.tile(top, (prow // 2, 1, 1)), "prow", 0, 0, tiled=True)
     first = spread(jnp.concatenate([half_top[0, :, :512], half_top[1]], axis=1), "pcol", pcol)
@@ -503,7 +479,7 @@
         return [chip] + [lax.ppermute(chip, "prow", along(k)) for k in range(1, 4)]
 
     L0, W0 = factor_first(at, *diag)
-    low = join_strips(join_low_kernel, 6, strip_slots, got, low_front)
+    low = join_strips(2, 6, strip_slots, got)
     P0 = solve_strips(solve_first_kernel, keep0, top, low, W0)
     P0, diag = lax.optimization_barrier((P0, diag))
     cols0 = gather_columns(P0)
@@ -516,11 +492,11 @@
     dealt, arrived = lax.optimization_barrier((dealt, arrived))
     dealt = lax.all_to_all(dealt, "pcol", 0, 0, tiled=True)
     extended = extend(slots, front_rows, arrived)
-    dealt, extended = lax.optimization_barrier((dealt, extended))
-    other = lax.ppermute(dealt[:, 16:], "prow", swap)
-
     L = jnp.where(q == 0, L0, L1)
     W = jnp.where(q == 0, W0, W1)
+    dealt, extended, L, W = lax.optimization_barrier((dealt, extended, L, W))
+    other = lax.ppermute(dealt[:, 16:], "prow", swap)
+
     out = finish(flags, extended, dealt, other, L, W)
     return out.reshape(front.shape)
 

time: 365 us -> 383 us (1.049)
  the two profiles are of different devices: /device:TPU:77 before, /device:TPU:1 now
where the time goes in v7:
time: 383 us; the launch traced here: 381 us
  waiting for transfers between devices  161 us (42%)
  Pallas kernels  97.4 us (25%)
  blocking collectives  47.5 us (12%)
  starting transfers between devices  42.5 us (11%)
  local copies, waits for them, and re-layouts  27 us (7%)
  other arithmetic  5.17 us (1%)
    all_to_all x1, waiting for transfers between devices, local(): lax.all_to_all(cut_strips(front_rows, child.reshape(48, 256, 256)), 'pcol...  71.1 us
    all_to_all x1, waiting for transfers between devices, local(): dealt = lax.all_to_all(dealt, 'pcol', 0, 0, tiled=True)  62.1 us
    all_to_all x1, blocking collectives, spread(): lax.all_to_all(jnp.broadcast_to(x[None], (count,) + x.shape), axis, 0, 0,...  31.4 us
    pallas_call x1, Pallas kernels, factor_second(): pl.pallas_call(factor_second_kernel, out_shape=[jax.ShapeDtypeStruct((n,...  23.9 us
    pallas_call x1, Pallas kernels, factor_first(): pl.pallas_call(factor_first_kernel, out_shape=[jax.ShapeDtypeStruct((n, n...  22.7 us
    unnamed x38, local copies, waits for them, and re-layouts  19.9 us
    all_to_all x1, waiting for transfers between devices, local(): lax.all_to_all(child, 'pcol', 0, 0, tiled=True).reshape(48, 256, 256)  18.2 us
    pallas_call x1, Pallas kernels, finish(): pl.pallas_call(finish_kernel, grid_spec=pltpu.PrefetchScalarGridSpec(num_...  17 us
  transfers between devices with their start and end apart: 13, of which 9 were waited for; matrix products, arithmetic and copies ran while one was open for 2% of the time, Pallas kernels for 17%

profile of v7, /device:TPU:1, one launch (start us, length us, event | category | flops | bytes accessed | tf_op | source)
XLA Modules:
  0.0 381.2 jit_solution(13995472068981310469)
XLA Ops:
  0.0 14.6 %shard_map.55 = bf16[16,38,16,256]{3,2,1,0:T(8,128)(2,1)} custom-call(f32[16384,128]{1,0:T(8,128)} %bitcast.61, bf16[48,256,256]{2,1,0:T(8,128)(2,1)} %bitcast.65), custom_call_target="tpu_custom_call" | custom-call | bytes 14680064 | tf_op jit(solution)/shard_map/pallas_call | solution.py:194
  14.6 8.6 %all-to-all-start = ((bf16[16,38,16,256]{3,2,1,0:T(8,128)(2,1)}), bf16[16,38,16,256]{3,2,1,0:T(8,128)(2,1)}, u32[]{:S(2)}, u32[]{:S(2)}) async-start(bf16[16,38,16,256]{3,2,1,0:T(8,128)(2,1)} %shard_map.55), calls=%async_computation | async-start | bytes 9961472 | tf_op jit(solution)/shard_map/all_to_all | solution.py:446
  25.9 71.1 %all-to-all-done.c_ref.f_ref = bf16[16,38,16,256]{3,2,1,0:T(8,128)(2,1)} async-done(((bf16[16,38,16,256]{3,2,1,0:T(8,128)(2,1)}), bf16[16,38,16,256]{3,2,1,0:T(8,128)(2,1)}, u32[]{:S(2)}, u32[]{:S(2)}) %all-to-all-start) | async-done | bytes 4980768 | tf_op jit(solution)/shard_map/all_to_all | solution.py:446
  97.0 2.1 shard_map.56.d_ref
  100.0 16.1 %all_to_all.25 = f32[8,16,1024]{2,1,0:T(8,128)S(1)} all-to-all(f32[8,16,1024]{2,1,0:T(8,128)S(1)} %bitcast.67), channel_id=1, replica_groups=mesh['prow'=8,'pcol'=16] {'prow'}, dimensions={0} | all-to-all | bytes 1048576 | tf_op jit(solution)/shard_map/all_to_all | solution.py:466
  116.3 31.4 %all_to_all.26.mine_ref = f32[16,16,1536]{2,1,0:T(8,128)S(1)} all-to-all(f32[16,16,1536]{2,1,0:T(8,128)S(1)} %broadcast_in_dim.111), channel_id=1, replica_groups=mesh['prow'=8,'pcol'=16] {'pcol'}, dimensions={0} | all-to-all | bytes 3145728 | tf_op jit(solution)/shard_map/all_to_all | solution.py:428
  147.7 3.4 collective-permute-start
  151.1 3.0 collective-permute-done.other_ref
  155.3 4.8 %all-to-all-start.3 = ((bf16[16,3,256,256]{3,2,1,0:T(8,128)(2,1)}), bf16[16,3,256,256]{3,2,1,0:T(8,128)(2,1)}, u32[]{:S(2)}, u32[]{:S(2)}) async-start(bf16[16,3,256,256]{3,2,1,0:T(8,128)(2,1)} %bitcast.66), calls=%async_computation.3 | async-start | bytes 12582912 | tf_op jit(solution)/shard_map/all_to_all | solution.py:470
  161.6 2.3 shard_map.57.r_ref
  164.0 1.4 copy-done.15
  165.4 22.7 %shard_map.58 = (f32[512,512]{1,0:T(8,128)S(1)}, f32[512,512]{1,0:T(8,128)S(1)}) custom-call(s32[3]{0:T(128)S(1)} %pad_add_fusion.1.at_ref, f32[16,16,1536]{2,1,0:T(8,128)S(1)} %all_to_all.26.mine_ref, f32[16,16,1536]{2,1,0:T(8,128)S(1)} %copy-done.15), custom_call_target="tpu_custom_call" | custom-call | flops 20000000000 | bytes 3145728 | tf_op jit(solution)/shard_map/pallas_call | solution.py:148
  190.2 2.7 shard_map.59.p_ref.p0_ref
  195.5 1.8 collective-permute-start.3
  199.2 1.4 copy-done.16
  200.6 23.9 %shard_map.60 = (bf16[512,512]{1,0:T(8,128)(2,1)S(1)}, f32[512,512]{1,0:T(8,128)S(1)}, f32[512,512]{1,0:T(8,128)S(1)}) custom-call(s32[3]{0:T(128)S(1)} %pad_add_fusion.1.at_ref, s32[4]{0:T(128)S(1)} %reshape.309.mask_ref, f32[16,16,1536]{2,1,0:T(8,128)S(1)} %all_to_all.26.mine_ref, f32[16,16,1536]{2,1,0:T(8,128)S(1)} %copy-done.16, f32[512,512]{1,0:T(8,128)S(1)} %copy-done.5), custom_call_target="tpu_custom_call" | custom-call | flops 20000000000 | bytes 3145728 | tf_op jit(solution)/shard_map/pallas_call | solution.py:161
  227.4 3.1 shard_map.61.p1_ref
  234.4 1.6 collective-permute-start.7
  236.0 2.0 collective-permute-start.6
  238.0 1.4 collective-permute-done.8.refs_7_
  239.4 3.1 collective-permute-done.7.refs_6_
  244.3 2.3 copy-done.3
  246.6 18.2 %all-to-all-done.3 = bf16[16,3,256,256]{3,2,1,0:T(8,128)(2,1)} async-done(((bf16[16,3,256,256]{3,2,1,0:T(8,128)(2,1)}), bf16[16,3,256,256]{3,2,1,0:T(8,128)(2,1)}, u32[]{:S(2)}, u32[]{:S(2)}) %all-to-all-start.3) | async-done | bytes 6291488 | tf_op jit(solution)/shard_map/all_to_all | solution.py:470
  264.8 13.1 %all-to-all-start.4 = ((bf16[16,20,16,512]{3,2,1,0:T(8,128)(2,1)}), bf16[16,20,16,512]{3,2,1,0:T(8,128)(2,1)}, u32[]{:S(2)}, u32[]{:S(2)}) async-start(bf16[16,20,16,512]{3,2,1,0:T(8,128)(2,1)} %copy-done.3), calls=%async_computation.4 | async-start | bytes 10485760 | tf_op jit(solution)/shard_map/all_to_all | solution.py:493
  279.0 3.4 copy-done.1
  282.4 8.0 %shard_map.63.f_ref = f32[16384,128]{1,0:T(8,128)S(1)} custom-call(s32[64]{0:T(128)S(1)} %broadcast_add_fusion.2.slot_ref, f32[16384,128]{1,0:T(8,128)S(1)} %bitcast.62, bf16[48,256,256]{2,1,0:T(8,128)(2,1)} %bitcast.21.refs_0_.refs_1_.refs_2_.refs_3_.refs_4_.refs_5_.refs_6_.refs_7_, ...), custom_call_target="tpu_custom_call" | custom-call | bytes 25165824 | tf_op jit(solution)/shard_map/pallas_call | solution.py:322
  290.4 3.3 copy-done.2
  293.6 62.1 %all-to-all-done.4.row0_ref.row1_ref.mine_ref = bf16[16,20,16,512]{3,2,1,0:T(8,128)(2,1)} async-done(((bf16[16,20,16,512]{3,2,1,0:T(8,128)(2,1)}), bf16[16,20,16,512]{3,2,1,0:T(8,128)(2,1)}, u32[]{:S(2)}, u32[]{:S(2)}) %all-to-all-start.4) | async-done | bytes 5242912 | tf_op jit(solution)/shard_map/all_to_all | solution.py:493
  355.8 2.3 slice.39
  358.1 3.7 collective-permute-start.9
  363.0 1.2 collective-permute-done.9.other_ref
  364.2 17.0 %shard_map.64 = f32[16384,128]{1,0:T(8,128)} custom-call(s32[49]{0:T(128)S(1)} %pad_add_fusion.flag_ref, f32[16384,128]{1,0:T(8,128)} %copy-done.2, bf16[16,20,16,512]{3,2,1,0:T(8,128)(2,1)} %all-to-all-done.4.row0_ref.row1_ref.mine_ref, bf16[16,20,16,512]{3,2,1,0:T(8,128)(2,1)} %all-to-all-done.4.row0_ref.row1_ref.mine_ref, ...), custom_call_target="tpu_custom_call" | custom-call | flops 5000000000 | bytes 25165824 | tf_op jit(solution)/shard_map/pallas_call | solution.py:392
  (118 shorter events, 23.7 us)
Async XLA Ops:
  0.0 24.8 %copy-start = (s32[8,16,16,3]{2,1,3,0:T(8,128)S(1)}, s32[8,16,16,3]{2,1,3,0:T(8,128)}, u32[]{:S(2)}) copy-start(s32[8,16,16,3]{2,1,3,0:T(8,128)} %param.8) | copy-start | bytes 73732
  14.6 9.0 %copy-start.18 = (s32[2,60]{1,0:T(2,128)S(1)}, s32[2,60]{1,0:T(2,128)}, u32[]{:S(2)}) copy-start(s32[2,60]{1,0:T(2,128)} %param.7) | copy-start | bytes 1444
  14.6 82.4 %all-to-all-start = ((bf16[16,38,16,256]{3,2,1,0:T(8,128)(2,1)}), bf16[16,38,16,256]{3,2,1,0:T(8,128)(2,1)}, u32[]{:S(2)}, u32[]{:S(2)}) async-start(bf16[16,38,16,256]{3,2,1,0:T(8,128)(2,1)} %shard_map.55), calls=%async_computation | async-start | bytes 9961472 | tf_op jit(solution)/shard_map/all_to_all | solution.py:446
  147.7 6.5 %collective-permute-start = (f32[16,16,1536]{2,1,0:T(8,128)S(1)}, f32[16,16,1536]{2,1,0:T(8,128)S(1)}, u32[]{:S(2)}, u32[]{:S(2)}) collective-permute-start(f32[16,16,1536]{2,1,0:T(8,128)S(1)} %all_to_all.26.mine_ref), channel_id=1, source_target_pairs={{0,16},{16,0},{32,48},{48,32},{64,80},{80,64},{96,112},{112,96},{1... | collective-permute-start | bytes 4718600 | tf_op jit(solution)/shard_map/ppermute | solution.py:468
  154.1 1.1 copy-start.14
  155.3 4.9 %copy-start.17 = (s32[64,64]{1,0:T(8,128)S(1)}, s32[64,64]{1,0:T(8,128)}, u32[]{:S(2)}) copy-start(s32[64,64]{1,0:T(8,128)} %param.9) | copy-start | bytes 49156
  155.3 109.5 %all-to-all-start.3 = ((bf16[16,3,256,256]{3,2,1,0:T(8,128)(2,1)}), bf16[16,3,256,256]{3,2,1,0:T(8,128)(2,1)}, u32[]{:S(2)}, u32[]{:S(2)}) async-start(bf16[16,3,256,256]{3,2,1,0:T(8,128)(2,1)} %bitcast.66), calls=%async_computation.3 | async-start | bytes 12582912 | tf_op jit(solution)/shard_map/all_to_all | solution.py:470
  164.0 1.4 copy-start.15
  188.1 1.0 copy-start.4
  189.1 1.1 copy-start.10
  193.8 1.4 collective-permute-start.1
  195.1 47.3 %copy-start.8 = (bf16[8,16,512]{2,1,0:T(8,128)(2,1)S(1)}, bf16[8,16,512]{2,1,0:T(8,128)(2,1)}, u32[]{:S(2)}) copy-start(bf16[8,16,512]{2,1,0:T(8,128)(2,1)} %shard_map.59.p_ref.p0_ref) | copy-start | bytes 393220
  195.2 32.2 %collective-permute-start.4 = (bf16[2,4,16,512]{3,2,1,0:T(8,128)(2,1)S(1)}, bf16[2,4,16,512]{3,2,1,0:T(8,128)(2,1)S(1)}, u32[]{:S(2)}, u32[]{:S(2)}) collective-permute-start(bf16[2,4,16,512]{3,2,1,0:T(8,128)(2,1)S(1)} %maximum_select_fusion.refs_0_), channel_id=1, source_target_pairs={{96,0},{112,16},{0,32},{16,48},{32,64},{48,80},{64,96},{80,112},{9... | collective-permute-start | bytes 393224 | tf_op jit(solution)/shard_map/ppermute | solution.py:479
  195.5 31.8 %collective-permute-start.3 = (bf16[2,4,16,512]{3,2,1,0:T(8,128)(2,1)S(1)}, bf16[2,4,16,512]{3,2,1,0:T(8,128)(2,1)S(1)}, u32[]{:S(2)}, u32[]{:S(2)}) collective-permute-start(bf16[2,4,16,512]{3,2,1,0:T(8,128)(2,1)S(1)} %maximum_select_fusion.refs_0_), channel_id=1, source_target_pairs={{64,0},{80,16},{96,32},{112,48},{0,64},{16,80},{32,96},{48,112},{6... | collective-permute-start | bytes 393224 | tf_op jit(solution)/shard_map/ppermute | solution.py:479
  197.3 30.1 %collective-permute-start.2 = (bf16[2,4,16,512]{3,2,1,0:T(8,128)(2,1)S(1)}, bf16[2,4,16,512]{3,2,1,0:T(8,128)(2,1)S(1)}, u32[]{:S(2)}, u32[]{:S(2)}) collective-permute-start(bf16[2,4,16,512]{3,2,1,0:T(8,128)(2,1)S(1)} %maximum_select_fusion.refs_0_), channel_id=1, source_target_pairs={{32,0},{48,16},{64,32},{80,48},{96,64},{112,80},{0,96},{16,112},{3... | collective-permute-start | bytes 393224 | tf_op jit(solution)/shard_map/ppermute | solution.py:479
  198.0 1.2 copy-start.5
  199.2 1.4 copy-start.16
  224.6 1.0 copy-start.7
  225.6 1.0 copy-start.12
  226.6 0.8 copy-start.13
  231.4 1.9 collective-permute-start.5
  233.3 6.1 %collective-permute-start.8 = (bf16[2,4,16,512]{3,2,1,0:T(8,128)(2,1)S(1)}, bf16[2,4,16,512]{3,2,1,0:T(8,128)(2,1)S(1)}, u32[]{:S(2)}, u32[]{:S(2)}) collective-permute-start(bf16[2,4,16,512]{3,2,1,0:T(8,128)(2,1)S(1)} %maximum_select_fusion.1.refs_4_), channel_id=1, source_target_pairs={{96,0},{112,16},{0,32},{16,48},{32,64},{48,80},{64,96},{80,112},{9... | collective-permute-start | bytes 393224 | tf_op jit(solution)/shard_map/ppermute | solution.py:479
  234.4 8.1 %collective-permute-start.7 = (bf16[2,4,16,512]{3,2,1,0:T(8,128)(2,1)S(1)}, bf16[2,4,16,512]{3,2,1,0:T(8,128)(2,1)S(1)}, u32[]{:S(2)}, u32[]{:S(2)}) collective-permute-start(bf16[2,4,16,512]{3,2,1,0:T(8,128)(2,1)S(1)} %maximum_select_fusion.1.refs_4_), channel_id=1, source_target_pairs={{64,0},{80,16},{96,32},{112,48},{0,64},{16,80},{32,96},{48,112},{6... | collective-permute-start | bytes 393224 | tf_op jit(solution)/shard_map/ppermute | solution.py:479
  236.0 6.5 %collective-permute-start.6 = (bf16[2,4,16,512]{3,2,1,0:T(8,128)(2,1)S(1)}, bf16[2,4,16,512]{3,2,1,0:T(8,128)(2,1)S(1)}, u32[]{:S(2)}, u32[]{:S(2)}) collective-permute-start(bf16[2,4,16,512]{3,2,1,0:T(8,128)(2,1)S(1)} %maximum_select_fusion.1.refs_4_), channel_id=1, source_target_pairs={{32,0},{48,16},{64,32},{80,48},{96,64},{112,80},{0,96},{16,112},{3... | collective-permute-start | bytes 393224 | tf_op jit(solution)/shard_map/ppermute | solution.py:479
  242.5 0.9 copy-start.9
  244.3 2.4 copy-start.3
  264.8 13.7 %copy-start.11 = (f32[512,512]{1,0:T(8,128)S(1)}, f32[512,512]{1,0:T(8,128)}, u32[]{:S(2)}) copy-start(f32[512,512]{1,0:T(8,128)} %copy-done.10) | copy-start | bytes 3145732
  264.8 13.9 %copy-start.6 = (f32[512,512]{1,0:T(8,128)S(1)}, f32[512,512]{1,0:T(8,128)}, u32[]{:S(2)}) copy-start(f32[512,512]{1,0:T(8,128)} %copy-done.4) | copy-start | bytes 3145732
  264.8 91.0 %all-to-all-start.4 = ((bf16[16,20,16,512]{3,2,1,0:T(8,128)(2,1)}), bf16[16,20,16,512]{3,2,1,0:T(8,128)(2,1)}, u32[]{:S(2)}, u32[]{:S(2)}) async-start(bf16[16,20,16,512]{3,2,1,0:T(8,128)(2,1)} %copy-done.3), calls=%async_computation.4 | async-start | bytes 10485760 | tf_op jit(solution)/shard_map/all_to_all | solution.py:493
  279.0 3.4 copy-start.1
  290.4 3.3 copy-start.2
  358.1 6.2 %collective-permute-start.9 = (bf16[16,4,16,512]{3,2,1,0:T(8,128)(2,1)}, bf16[16,4,16,512]{3,2,1,0:T(8,128)(2,1)S(1)}, u32[]{:S(2)}, u32[]{:S(2)}) collective-permute-start(bf16[16,4,16,512]{3,2,1,0:T(8,128)(2,1)} %slice.39), channel_id=1, source_target_pairs={{0,16},{16,0},{32,48},{48,32},{64,80},{80,64},{96,112},{112,96},{1... | collective-permute-start | bytes 3145736 | tf_op jit(solution)/shard_map/ppermute | solution.py:498

commit v8 on v6

--- a/solution.py
+++ b/solution.py
@@ -352,7 +352,7 @@
     )(slots, front_rows, *([arrived] * 8))
 
 
-def finish_kernel(flag_ref, f_ref, row0_ref, row1_ref, mine_ref, other_ref, l_ref, w_ref, o_ref, cols_ref):
+def finish_kernel(flag_ref, f_ref, row0_ref, row1_ref, mine_ref, other_ref, l_ref, wh_ref, wl_ref, o_ref, cols_ref):
     i = pl.program_id(0)
 
     @pl.when(i == 0)
@@ -392,7 +392,9 @@
 
                 @pl.when(state == 2)
                 def _():
-                    put(dot3(block, w_ref[...], NT))
+                    high, low = split(block)
+                    wh = wh_ref[...]
+                    put(dot1(high, wh, NT) + (dot1(low, wh, NT) + dot1(high, wl_ref[...], NT)))
 
                 @pl.when(state == 3)
                 def _():
@@ -417,14 +419,14 @@
             + [pl.BlockSpec((16, 1, 16, 512), lambda i, f: (0, i, 0, 0))]
             + [pl.BlockSpec((16, 1, 16, 512), lambda i, f: (0, i + 8, 0, 0))]
             + [whole((16, 4, 16, 512), 0, 4, 0, 0), whole((16, 4, 16, 512), 0, 0, 0, 0)]
-            + [whole((512, 512), 0, 0)] * 2,
+            + [whole((512, 512), 0, 0)] * 3,
             out_specs=pl.BlockSpec((2048, 128), lambda i, f: (i, 0)),
             scratch_shapes=[pltpu.VMEM((4, 256, 1024), BF16)],
         ),
         out_shape=jax.ShapeDtypeStruct(extended.shape, F32),
         cost_estimate=pl.CostEstimate(flops=5_000_000_000, bytes_accessed=24 * MIB, transcendentals=0),
         compiler_params=pltpu.CompilerParams(vmem_limit_bytes=48 * MIB),
-    )(flags, extended, dealt, dealt, dealt, other, L, W)
+    )(flags, extended, dealt, dealt, dealt, other, L, *W)
 
 
 def slot_of_targets(codes, row_map, rows, cols):
@@ -462,12 +464,12 @@
     sub_rows = (2 * row_blocks[:, None] + pair).reshape(-1)
     sub_cols = (2 * col_blocks[:, None] + pair).reshape(-1)
 
-    cut = cut_top(front_rows, child.reshape(48, 256, 256))
-    got = lax.all_to_all(cut, "pcol", 0, 0, tiled=True)
-    front_rows, _ = lax.optimization_barrier((front_rows, cut))
+    low_cut = cut_low(at, front_rows)
     low_front = lax.psum_scatter(
-        cut_low(at, front_rows).reshape(96, 16, 1024), "pcol", scatter_dimension=0, tiled=True
+        low_cut.reshape(96, 16, 1024), "pcol", scatter_dimension=0, tiled=True
     )
+    front_top, _ = lax.optimization_barrier((front_rows, low_cut))
+    got = lax.all_to_all(cut_top(front_top, child.reshape(48, 256, 256)), "pcol", 0, 0, tiled=True)
 
     my_codes = lax.dynamic_index_in_dim(slot_table, p, 0, False)
     strip_slots = slot_of_targets(my_codes[:, :2].reshape(-1), row_map, sub_rows, jnp.arange(4, dtype=jnp.int32))
@@ -516,11 +518,10 @@
     dealt, arrived = lax.optimization_barrier((dealt, arrived))
     dealt = lax.all_to_all(dealt, "pcol", 0, 0, tiled=True)
     extended = extend(slots, front_rows, arrived)
-    dealt, extended = lax.optimization_barrier((dealt, extended))
+    L = jnp.where(q == 0, L0, L1)
+    W = split(jnp.where(q == 0, W0, W1))
+    dealt, extended, L, W = lax.optimization_barrier((dealt, extended, L, W))
     other = lax.ppermute(dealt[:, 16:], "prow", swap)
-
-    L = jnp.where(q == 0, L0, L1)
-    W = jnp.where(q == 0, W0, W1)
     out = finish(flags, extended, dealt, other, L, W)
     return out.reshape(front.shape)
 

time: 335 us -> 330 us (0.985)
  blocking collectives: 49.1 us -> 45.3 us
    all_to_all x1, blocking collectives: 29.4 us -> 25.8 us  [spread(): lax.all_to_all(jnp.broadcast_to(x[None], (count,) + x.shape), axis, 0, 0,...]
    unnamed x44 -> x48, local copies, waits for them, and re-layouts: 24 us -> 24 us
  transfers between devices with their start and end apart: 14 -> 14, of which waited for: 9 -> 10; matrix products, arithmetic and copies ran while one was open for 3% -> 4% of each run, Pallas kernels for 20% -> 21%
where the time goes in v8:
time: 330 us; the launch traced here: 329 us
  waiting for transfers between devices  93.4 us (28%)
  Pallas kernels  93.2 us (28%)
  blocking collectives  45.3 us (14%)
  starting transfers between devices  43.1 us (13%)
  local copies, waits for them, and re-layouts  31.1 us (9%)
  between operations  13.7 us (4%)
  other arithmetic  8.71 us (3%)
    all_to_all x1, waiting for transfers between devices, local(): dealt = lax.all_to_all(dealt, 'pcol', 0, 0, tiled=True)  40.4 us
    all_to_all x1, blocking collectives, spread(): lax.all_to_all(jnp.broadcast_to(x[None], (count,) + x.shape), axis, 0, 0,...  25.8 us
    all_to_all x1, waiting for transfers between devices, local(): lax.all_to_all(cut_top(front_top, child.reshape(48, 256, 256)), 'pcol', 0...  24.5 us
    unnamed x48, local copies, waits for them, and re-layouts  24 us
    pallas_call x1, Pallas kernels, factor_second(): pl.pallas_call(factor_second_kernel, out_shape=[jax.ShapeDtypeStruct((n,...  23.9 us
    pallas_call x1, Pallas kernels, factor_first(): pl.pallas_call(factor_first_kernel, out_shape=[jax.ShapeDtypeStruct((n, n...  22.7 us
    all_to_all x1, blocking collectives, local(): lax.all_to_all(jnp.tile(top, (prow // 2, 1, 1)), 'prow', 0, 0, tiled=True)  19.5 us
    pallas_call x1, Pallas kernels, finish(): pl.pallas_call(finish_kernel, grid_spec=pltpu.PrefetchScalarGridSpec(num_...  16.8 us
  transfers between devices with their start and end apart: 14, of which 10 were waited for; matrix products, arithmetic and copies ran while one was open for 4% of the time, Pallas kernels for 21%

profile of v8, /device:TPU:1, one launch (start us, length us, event | category | flops | bytes accessed | tf_op | source)
XLA Modules:
  0.0 328.5 jit_solution(1596591685528977694)
XLA Ops:
  7.2 7.1 %shard_map.55 = f32[16,6,16,1024]{3,2,1,0:T(8,128)} custom-call(s32[3]{0:T(128)} %pad_add_fusion.1.at_ref, f32[16384,128]{1,0:T(8,128)} %bitcast.62), custom_call_target="tpu_custom_call" | custom-call | bytes 12582912 | tf_op jit(solution)/shard_map/pallas_call | solution.py:214
  14.3 2.8 copy-done.3
  17.1 3.2 shard_map.56
  20.3 8.2 %all-to-all-start = ((bf16[16,14,16,256]{3,2,1,0:T(8,128)(2,1)}), bf16[16,14,16,256]{3,2,1,0:T(8,128)(2,1)S(1)}, u32[]{:S(2)}, u32[]{:S(2)}) async-start(bf16[16,14,16,256]{3,2,1,0:T(8,128)(2,1)} %shard_map.56), calls=%async_computation | async-start | bytes 3670016 | tf_op jit(solution)/shard_map/all_to_all | solution.py:472
  31.2 24.5 %all-to-all-done.c_ref = bf16[16,14,16,256]{3,2,1,0:T(8,128)(2,1)S(1)} async-done(((bf16[16,14,16,256]{3,2,1,0:T(8,128)(2,1)}), bf16[16,14,16,256]{3,2,1,0:T(8,128)(2,1)S(1)}, u32[]{:S(2)}, u32[]{:S(2)}) %all-to-all-start) | async-done | bytes 1835040 | tf_op jit(solution)/shard_map/all_to_all | solution.py:472
  57.0 2.3 shard_map.57.d_ref
  60.2 19.5 %all_to_all.25 = f32[8,16,1024]{2,1,0:T(8,128)S(1)} all-to-all(f32[8,16,1024]{2,1,0:T(8,128)S(1)} %bitcast.70), channel_id=1, replica_groups=mesh['prow'=8,'pcol'=16] {'prow'}, dimensions={0} | all-to-all | bytes 1048576 | tf_op jit(solution)/shard_map/all_to_all | solution.py:492
  80.0 25.8 %all_to_all.26.mine_ref = f32[16,16,1536]{2,1,0:T(8,128)S(1)} all-to-all(f32[16,16,1536]{2,1,0:T(8,128)S(1)} %broadcast_in_dim.111), channel_id=1, replica_groups=mesh['prow'=8,'pcol'=16] {'pcol'}, dimensions={0} | all-to-all | bytes 3145728 | tf_op jit(solution)/shard_map/all_to_all | solution.py:449
  105.7 2.3 collective-permute-start
  108.0 3.0 collective-permute-done.other_ref
  112.3 12.4 %reduce-scatter.2.cloned.1.call-done.f_ref = f32[6,16,1024]{2,1,0:T(8,128)} async-done(((f32[96,16,1024]{2,1,0:T(8,128)}), f32[6,16,1024]{2,1,0:T(8,128)}) %reduce-scatter.2.cloned.1.call-update) | async-done | bytes 393232 | tf_op jit(solution)/shard_map/reduce_scatter | solution.py:468
  124.7 4.8 %all-to-all-start.3 = ((bf16[16,3,256,256]{3,2,1,0:T(8,128)(2,1)}), bf16[16,3,256,256]{3,2,1,0:T(8,128)(2,1)}, u32[]{:S(2)}, u32[]{:S(2)}) async-start(bf16[16,3,256,256]{3,2,1,0:T(8,128)(2,1)} %bitcast.65), calls=%async_computation.4 | async-start | bytes 12582912 | tf_op jit(solution)/shard_map/all_to_all | solution.py:496
  131.0 2.6 shard_map.58.r_ref
  135.0 22.7 %shard_map.59 = (f32[512,512]{1,0:T(8,128)S(1)}, f32[512,512]{1,0:T(8,128)S(1)}) custom-call(s32[3]{0:T(128)S(1)} %copy-done.17, f32[16,16,1536]{2,1,0:T(8,128)S(1)} %all_to_all.26.mine_ref, f32[16,16,1536]{2,1,0:T(8,128)S(1)} %copy-done.19), custom_call_target="tpu_custom_call" | custom-call | flops 20000000000 | bytes 3145728 | tf_op jit(solution)/shard_map/pallas_call | solution.py:148
  159.7 2.7 shard_map.60.p_ref.p0_ref
  163.4 2.1 collective-permute-start.1
  167.7 2.4 collective-permute-start.3
  173.9 23.9 %shard_map.61 = (bf16[512,512]{1,0:T(8,128)(2,1)S(1)}, f32[512,512]{1,0:T(8,128)S(1)}, f32[512,512]{1,0:T(8,128)S(1)}) custom-call(s32[3]{0:T(128)S(1)} %copy-done.17, s32[4]{0:T(128)S(1)} %reshape.313.mask_ref, f32[16,16,1536]{2,1,0:T(8,128)S(1)} %all_to_all.26.mine_ref, f32[16,16,1536]{2,1,0:T(8,128)S(1)} %copy-done.20, f32[512,512]{1,0:T(8,128)S(1)} %copy-done.6), custom_call_target="tpu_custom_call" | custom-call | flops 20000000000 | bytes 3145728 | tf_op jit(solution)/shard_map/pallas_call | solution.py:161
  200.7 3.1 shard_map.62.p1_ref
  207.9 1.9 collective-permute-start.6
  209.8 6.1 %collective-permute-done.8.refs_7_ = bf16[2,4,16,512]{3,2,1,0:T(8,128)(2,1)S(1)} collective-permute-done((bf16[2,4,16,512]{3,2,1,0:T(8,128)(2,1)S(1)}, bf16[2,4,16,512]{3,2,1,0:T(8,128)(2,1)S(1)}, u32[]{:S(2)}, u32[]{:S(2)}) %collective-permute-start.8) | collective-permute-done | bytes 131104 | tf_op jit(solution)/shard_map/ppermute | solution.py:505
  218.0 2.3 copy-done.4
  220.3 4.2 %all-to-all-done.3 = bf16[16,3,256,256]{3,2,1,0:T(8,128)(2,1)} async-done(((bf16[16,3,256,256]{3,2,1,0:T(8,128)(2,1)}), bf16[16,3,256,256]{3,2,1,0:T(8,128)(2,1)}, u32[]{:S(2)}, u32[]{:S(2)}) %all-to-all-start.3) | async-done | bytes 6291488 | tf_op jit(solution)/shard_map/all_to_all | solution.py:496
  224.5 7.4 %all-to-all-start.4 = ((bf16[16,20,16,512]{3,2,1,0:T(8,128)(2,1)}), bf16[16,20,16,512]{3,2,1,0:T(8,128)(2,1)}, u32[]{:S(2)}, u32[]{:S(2)}) async-start(bf16[16,20,16,512]{3,2,1,0:T(8,128)(2,1)} %copy-done.4), calls=%async_computation.5 | async-start | bytes 10485760 | tf_op jit(solution)/shard_map/all_to_all | solution.py:519
  232.5 1.4 broadcast_select_fusion.1.l_ref
  236.0 3.4 %copy-done.1 = f32[4,1,512,2,1,512]{5,4,3,2,1,0:T(1,128)S(1)} copy-done((f32[4,1,512,2,1,512]{5,4,3,2,1,0:T(1,128)S(1)}, f32[4,1,512,2,1,512]{5,4,3,2,1,0:T(1,128)}, u32[]{:S(2)}) %copy-start.1) | copy-done | bytes 8388632
  239.4 7.7 %shard_map.64.f_ref = f32[16384,128]{1,0:T(8,128)S(1)} custom-call(s32[64]{0:T(128)S(1)} %broadcast_add_fusion.2.slot_ref, f32[16384,128]{1,0:T(8,128)S(1)} %bitcast.64, bf16[48,256,256]{2,1,0:T(8,128)(2,1)} %bitcast.22.refs_0_.refs_1_.refs_2_.refs_3_.refs_4_.refs_5_.refs_6_.refs_7_, ...), custom_call_target="tpu_custom_call" | custom-call | bytes 25165824 | tf_op jit(solution)/shard_map/pallas_call | solution.py:341
  247.1 3.3 copy-done.2
  250.4 40.4 %all-to-all-done.4.row0_ref.row1_ref.mine_ref = bf16[16,20,16,512]{3,2,1,0:T(8,128)(2,1)} async-done(((bf16[16,20,16,512]{3,2,1,0:T(8,128)(2,1)}), bf16[16,20,16,512]{3,2,1,0:T(8,128)(2,1)}, u32[]{:S(2)}, u32[]{:S(2)}) %all-to-all-start.4) | async-done | bytes 5242912 | tf_op jit(solution)/shard_map/all_to_all | solution.py:519
  290.8 2.3 slice.39
  293.1 9.3 %collective-permute-start.9 = (bf16[16,4,16,512]{3,2,1,0:T(8,128)(2,1)}, bf16[16,4,16,512]{3,2,1,0:T(8,128)(2,1)S(1)}, u32[]{:S(2)}, u32[]{:S(2)}) collective-permute-start(bf16[16,4,16,512]{3,2,1,0:T(8,128)(2,1)} %slice.39), channel_id=1, source_target_pairs={{0,16},{16,0},{32,48},{48,32},{64,80},{80,64},{96,112},{112,96},{1... | collective-permute-start | bytes 3145736 | tf_op jit(solution)/shard_map/ppermute | solution.py:524
  304.9 16.8 %shard_map.65 = f32[16384,128]{1,0:T(8,128)} custom-call(s32[49]{0:T(128)S(1)} %pad_add_fusion.flag_ref, f32[16384,128]{1,0:T(8,128)} %copy-done.2, bf16[16,20,16,512]{3,2,1,0:T(8,128)(2,1)} %all-to-all-done.4.row0_ref.row1_ref.mine_ref, bf16[16,20,16,512]{3,2,1,0:T(8,128)(2,1)} %all-to-all-done.4.row0_ref.row1_ref.mine_ref, ...), custom_call_target="tpu_custom_call" | custom-call | flops 5000000000 | bytes 25165824 | tf_op jit(solution)/shard_map/pallas_call | solution.py:413
  (133 shorter events, 32.6 us)
Async XLA Ops:
  6.5 23.6 %copy-start = (s32[8,16,16,3]{2,1,3,0:T(8,128)S(1)}, s32[8,16,16,3]{2,1,3,0:T(8,128)}, u32[]{:S(2)}) copy-start(s32[8,16,16,3]{2,1,3,0:T(8,128)} %param.8) | copy-start | bytes 73732
  6.5 118.2 %reduce-scatter.2.cloned.1.call-start = ((), (), s32[]{:S(2)}) async-start(), calls=%async_computation.6 | async-start | bytes 6684672 | tf_op jit(solution)/shard_map/reduce_scatter | solution.py:468
  14.3 2.8 copy-start.3
  17.1 11.8 %copy-start.23 = (s32[2,60]{1,0:T(2,128)S(1)}, s32[2,60]{1,0:T(2,128)}, u32[]{:S(2)}) copy-start(s32[2,60]{1,0:T(2,128)} %param.7) | copy-start | bytes 1444
  20.3 35.4 %all-to-all-start = ((bf16[16,14,16,256]{3,2,1,0:T(8,128)(2,1)}), bf16[16,14,16,256]{3,2,1,0:T(8,128)(2,1)S(1)}, u32[]{:S(2)}, u32[]{:S(2)}) async-start(bf16[16,14,16,256]{3,2,1,0:T(8,128)(2,1)} %shard_map.56), calls=%async_computation | async-start | bytes 3670016 | tf_op jit(solution)/shard_map/all_to_all | solution.py:472
  55.7 1.3 copy-start.21
  105.7 5.4 %collective-permute-start = (f32[16,16,1536]{2,1,0:T(8,128)S(1)}, f32[16,16,1536]{2,1,0:T(8,128)S(1)}, u32[]{:S(2)}, u32[]{:S(2)}) collective-permute-start(f32[16,16,1536]{2,1,0:T(8,128)S(1)} %all_to_all.26.mine_ref), channel_id=1, source_target_pairs={{0,16},{16,0},{32,48},{48,32},{64,80},{80,64},{96,112},{112,96},{1... | collective-permute-start | bytes 4718600 | tf_op jit(solution)/shard_map/ppermute | solution.py:494
  111.1 1.2 copy-start.18
  124.7 4.9 %copy-start.22 = (s32[64,64]{1,0:T(8,128)S(1)}, s32[64,64]{1,0:T(8,128)}, u32[]{:S(2)}) copy-start(s32[64,64]{1,0:T(8,128)} %param.9) | copy-start | bytes 49156
  124.7 8.9 %copy-start.17 = (s32[3]{0:T(128)S(1)}, s32[3]{0:T(128)}, u32[]{:S(2)}) copy-start(s32[3]{0:T(128)} %pad_add_fusion.1.at_ref) | copy-start | bytes 40
  124.7 99.8 %all-to-all-start.3 = ((bf16[16,3,256,256]{3,2,1,0:T(8,128)(2,1)}), bf16[16,3,256,256]{3,2,1,0:T(8,128)(2,1)}, u32[]{:S(2)}, u32[]{:S(2)}) async-start(bf16[16,3,256,256]{3,2,1,0:T(8,128)(2,1)} %bitcast.65), calls=%async_computation.4 | async-start | bytes 12582912 | tf_op jit(solution)/shard_map/all_to_all | solution.py:496
  133.6 1.4 copy-start.19
  163.4 3.0 collective-permute-start.1
  166.4 49.8 %copy-start.12 = (bf16[8,16,512]{2,1,0:T(8,128)(2,1)S(1)}, bf16[8,16,512]{2,1,0:T(8,128)(2,1)}, u32[]{:S(2)}) copy-start(bf16[8,16,512]{2,1,0:T(8,128)(2,1)} %shard_map.60.p_ref.p0_ref) | copy-start | bytes 393220
  166.4 34.3 %collective-permute-start.4 = (bf16[2,4,16,512]{3,2,1,0:T(8,128)(2,1)S(1)}, bf16[2,4,16,512]{3,2,1,0:T(8,128)(2,1)S(1)}, u32[]{:S(2)}, u32[]{:S(2)}) collective-permute-start(bf16[2,4,16,512]{3,2,1,0:T(8,128)(2,1)S(1)} %maximum_select_fusion.refs_0_), channel_id=1, source_target_pairs={{96,0},{112,16},{0,32},{16,48},{32,64},{48,80},{64,96},{80,112},{9... | collective-permute-start | bytes 393224 | tf_op jit(solution)/shard_map/ppermute | solution.py:505
  167.7 33.0 %collective-permute-start.3 = (bf16[2,4,16,512]{3,2,1,0:T(8,128)(2,1)S(1)}, bf16[2,4,16,512]{3,2,1,0:T(8,128)(2,1)S(1)}, u32[]{:S(2)}, u32[]{:S(2)}) collective-permute-start(bf16[2,4,16,512]{3,2,1,0:T(8,128)(2,1)S(1)} %maximum_select_fusion.refs_0_), channel_id=1, source_target_pairs={{64,0},{80,16},{96,32},{112,48},{0,64},{16,80},{32,96},{48,112},{6... | collective-permute-start | bytes 393224 | tf_op jit(solution)/shard_map/ppermute | solution.py:505
  170.1 30.6 %collective-permute-start.2 = (bf16[2,4,16,512]{3,2,1,0:T(8,128)(2,1)S(1)}, bf16[2,4,16,512]{3,2,1,0:T(8,128)(2,1)S(1)}, u32[]{:S(2)}, u32[]{:S(2)}) collective-permute-start(bf16[2,4,16,512]{3,2,1,0:T(8,128)(2,1)S(1)} %maximum_select_fusion.refs_0_), channel_id=1, source_target_pairs={{32,0},{48,16},{64,32},{80,48},{96,64},{112,80},{0,96},{16,112},{3... | collective-permute-start | bytes 393224 | tf_op jit(solution)/shard_map/ppermute | solution.py:505
  171.2 1.2 copy-start.6
  172.5 1.4 copy-start.20
  204.7 2.2 collective-permute-start.5
  206.9 9.0 %collective-permute-start.8 = (bf16[2,4,16,512]{3,2,1,0:T(8,128)(2,1)S(1)}, bf16[2,4,16,512]{3,2,1,0:T(8,128)(2,1)S(1)}, u32[]{:S(2)}, u32[]{:S(2)}) collective-permute-start(bf16[2,4,16,512]{3,2,1,0:T(8,128)(2,1)S(1)} %maximum_select_fusion.1.refs_4_), channel_id=1, source_target_pairs={{96,0},{112,16},{0,32},{16,48},{32,64},{48,80},{64,96},{80,112},{9... | collective-permute-start | bytes 393224 | tf_op jit(solution)/shard_map/ppermute | solution.py:505
  207.3 8.6 %collective-permute-start.7 = (bf16[2,4,16,512]{3,2,1,0:T(8,128)(2,1)S(1)}, bf16[2,4,16,512]{3,2,1,0:T(8,128)(2,1)S(1)}, u32[]{:S(2)}, u32[]{:S(2)}) collective-permute-start(bf16[2,4,16,512]{3,2,1,0:T(8,128)(2,1)S(1)} %maximum_select_fusion.1.refs_4_), channel_id=1, source_target_pairs={{64,0},{80,16},{96,32},{112,48},{0,64},{16,80},{32,96},{48,112},{6... | collective-permute-start | bytes 393224 | tf_op jit(solution)/shard_map/ppermute | solution.py:505
  207.9 8.3 %collective-permute-start.6 = (bf16[2,4,16,512]{3,2,1,0:T(8,128)(2,1)S(1)}, bf16[2,4,16,512]{3,2,1,0:T(8,128)(2,1)S(1)}, u32[]{:S(2)}, u32[]{:S(2)}) collective-permute-start(bf16[2,4,16,512]{3,2,1,0:T(8,128)(2,1)S(1)} %maximum_select_fusion.1.refs_4_), channel_id=1, source_target_pairs={{32,0},{48,16},{64,32},{80,48},{96,64},{112,80},{0,96},{16,112},{3... | collective-permute-start | bytes 393224 | tf_op jit(solution)/shard_map/ppermute | solution.py:505
  218.0 2.4 copy-start.4
  224.5 9.5 %copy-start.7 = (f32[512,512]{1,0:T(8,128)S(1)}, f32[512,512]{1,0:T(8,128)}, u32[]{:S(2)}) copy-start(f32[512,512]{1,0:T(8,128)} %copy-done.5) | copy-start | bytes 3145732
  224.5 9.5 %copy-start.9 = (f32[512,512]{1,0:T(8,128)S(1)}, f32[512,512]{1,0:T(8,128)}, u32[]{:S(2)}) copy-start(f32[512,512]{1,0:T(8,128)} %copy-done.8) | copy-start | bytes 3145732
  224.5 66.3 %all-to-all-start.4 = ((bf16[16,20,16,512]{3,2,1,0:T(8,128)(2,1)}), bf16[16,20,16,512]{3,2,1,0:T(8,128)(2,1)}, u32[]{:S(2)}, u32[]{:S(2)}) async-start(bf16[16,20,16,512]{3,2,1,0:T(8,128)(2,1)} %copy-done.4), calls=%async_computation.5 | async-start | bytes 10485760 | tf_op jit(solution)/shard_map/all_to_all | solution.py:519
  236.0 3.4 %copy-start.1 = (f32[4,1,512,2,1,512]{5,4,3,2,1,0:T(1,128)S(1)}, f32[4,1,512,2,1,512]{5,4,3,2,1,0:T(1,128)}, u32[]{:S(2)}) copy-start(f32[4,1,512,2,1,512]{5,4,3,2,1,0:T(1,128)} %param.5) | copy-start | bytes 25165828
  239.3 65.5 %copy-start.10 = (bf16[512,512]{1,0:T(8,128)(2,1)S(1)}, bf16[512,512]{1,0:T(8,128)(2,1)}, u32[]{:S(2)}) copy-start(bf16[512,512]{1,0:T(8,128)(2,1)} %subtract_convert_fusion.wl_ref) | copy-start | bytes 1572868
  239.3 65.5 %copy-start.11 = (bf16[512,512]{1,0:T(8,128)(2,1)S(1)}, bf16[512,512]{1,0:T(8,128)(2,1)}, u32[]{:S(2)}) copy-start(bf16[512,512]{1,0:T(8,128)(2,1)} %fusion.wh_ref) | copy-start | bytes 1572868
  247.1 3.3 copy-start.2
  293.1 11.8 %collective-permute-start.9 = (bf16[16,4,16,512]{3,2,1,0:T(8,128)(2,1)}, bf16[16,4,16,512]{3,2,1,0:T(8,128)(2,1)S(1)}, u32[]{:S(2)}, u32[]{:S(2)}) collective-permute-start(bf16[16,4,16,512]{3,2,1,0:T(8,128)(2,1)} %slice.39), channel_id=1, source_target_pairs={{0,16},{16,0},{32,48},{48,32},{64,80},{80,64},{96,112},{112,96},{1... | collective-permute-start | bytes 3145736 | tf_op jit(solution)/shard_map/ppermute | solution.py:524
  (6 other events, 5.7 us)
Sparse Core Ops, SparseCore 0:
  14.4 110.2 reduce-scatter.1

commit v9 on v8

--- a/solution.py
+++ b/solution.py
@@ -352,7 +352,7 @@
     )(slots, front_rows, *([arrived] * 8))
 
 
-def finish_kernel(flag_ref, f_ref, row0_ref, row1_ref, mine_ref, other_ref, l_ref, wh_ref, wl_ref, o_ref, cols_ref):
+def finish_kernel(flag_ref, f_ref, row0_ref, row1_ref, mine_ref, other_ref, l_ref, w_ref, o_ref, cols_ref, wh_ref, wl_ref):
     i = pl.program_id(0)
 
     @pl.when(i == 0)
@@ -363,6 +363,10 @@
                 for lc in range(2):
                     strips = ref[:, panel * 2 + lc].reshape(256, 512)
                     cols_ref[lc * 2 + sub, :, panel * 512 : (panel + 1) * 512] = strips
+
+    @pl.when((i == 0) & (flag_ref[49] > 0))
+    def _():
+        wh_ref[...], wl_ref[...] = split(w_ref[...])
 
     rows = jnp.concatenate([ref[:, 0].reshape(256, 512) for ref in (row0_ref, row1_ref)], axis=1)
     for lc in range(2):
@@ -419,14 +423,14 @@
             + [pl.BlockSpec((16, 1, 16, 512), lambda i, f: (0, i, 0, 0))]
             + [pl.BlockSpec((16, 1, 16, 512), lambda i, f: (0, i + 8, 0, 0))]
             + [whole((16, 4, 16, 512), 0, 4, 0, 0), whole((16, 4, 16, 512), 0, 0, 0, 0)]
-            + [whole((512, 512), 0, 0)] * 3,
+            + [whole((512, 512), 0, 0)] * 2,
             out_specs=pl.BlockSpec((2048, 128), lambda i, f: (i, 0)),
-            scratch_shapes=[pltpu.VMEM((4, 256, 1024), BF16)],
+            scratch_shapes=[pltpu.VMEM((4, 256, 1024), BF16)] + [pltpu.VMEM((512, 512), BF16)] * 2,
         ),
         out_shape=jax.ShapeDtypeStruct(extended.shape, F32),
         cost_estimate=pl.CostEstimate(flops=5_000_000_000, bytes_accessed=24 * MIB, transcendentals=0),
         compiler_params=pltpu.CompilerParams(vmem_limit_bytes=48 * MIB),
-    )(flags, extended, dealt, dealt, dealt, other, L, *W)
+    )(flags, extended, dealt, dealt, dealt, other, L, W)
 
 
 def slot_of_targets(codes, row_map, rows, cols):
@@ -482,7 +486,7 @@
     state = jnp.where(lower, 1, 0)
     owner = (q < 2) & (jnp.arange(2) == 0)
     state = jnp.where(owner[None, :] & lower, jnp.where(row_blocks[:, None] == q, 3, 2), state)
-    flags = jnp.concatenate([mask.reshape(-1), jnp.repeat(state, 2, axis=0).reshape(-1), core.reshape(1)])
+    flags = jnp.concatenate([mask.reshape(-1), jnp.repeat(state, 2, axis=0).reshape(-1), jnp.stack([core, 2 - q])])
     flags = flags.astype(jnp.int32)
     keep0 = (sub_rows >= 2).astype(jnp.int32)
     keep1 = jnp.concatenate([(sub_rows >= 4).astype(jnp.int32), row_mask[:, 2:4].reshape(-1)])
@@ -492,7 +496,7 @@
     half_top = lax.all_to_all(jnp.tile(top, (prow // 2, 1, 1)), "prow", 0, 0, tiled=True)
     first = spread(jnp.concatenate([half_top[0, :, :512], half_top[1]], axis=1), "pcol", pcol)
     diag = (first, lax.ppermute(first, "prow", swap))
-    child, diag, low_front = lax.optimization_barrier((child, diag, low_front))
+    child, diag = lax.optimization_barrier((child, diag))
     arrived = lax.all_to_all(child, "pcol", 0, 0, tiled=True).reshape(48, 256, 256)
 
     def gather_columns(strips):
@@ -505,12 +509,11 @@
         return [chip] + [lax.ppermute(chip, "prow", along(k)) for k in range(1, 4)]
 
     L0, W0 = factor_first(at, *diag)
+    P10, L1, W1 = factor_second(at, struct_mask[2:4, 2:4].reshape(-1), *diag, W0)
+    W1, low_front = lax.optimization_barrier((W1, low_front))
     low = join_strips(join_low_kernel, 6, strip_slots, got, low_front)
     P0 = solve_strips(solve_first_kernel, keep0, top, low, W0)
-    P0, diag = lax.optimization_barrier((P0, diag))
     cols0 = gather_columns(P0)
-    P10, L1, W1 = factor_second(at, struct_mask[2:4, 2:4].reshape(-1), *diag, W0)
-    W1, cols0 = lax.optimization_barrier((W1, cols0))
     P1 = solve_strips(solve_second_kernel, keep1, top, low, P0, P10, W1)
     cols1 = gather_columns(P1)
 
@@ -519,7 +522,7 @@
     dealt = lax.all_to_all(dealt, "pcol", 0, 0, tiled=True)
     extended = extend(slots, front_rows, arrived)
     L = jnp.where(q == 0, L0, L1)
-    W = split(jnp.where(q == 0, W0, W1))
+    W = jnp.where(q == 0, W0, W1)
     dealt, extended, L, W = lax.optimization_barrier((dealt, extended, L, W))
     other = lax.ppermute(dealt[:, 16:], "prow", swap)
     out = finish(flags, extended, dealt, other, L, W)

time: 330 us -> 353 us (1.070)
  waiting for transfers between devices: 93.4 us -> 127 us
  starting transfers between devices: 43.1 us -> 37.6 us
    all_to_all x1, waiting for transfers between devices: 4.15 us -> 27.8 us  [local(): lax.all_to_all(child, 'pcol', 0, 0, tiled=True).reshape(48, 256, 256)]
    all_to_all x1, waiting for transfers between devices: 40.4 us -> 61.6 us  [local(): dealt = lax.all_to_all(dealt, 'pcol', 0, 0, tiled=True)]
    reduce_scatter x1, waiting for transfers between devices: 12.4 us -> 0.01 us  [local(): lax.psum_scatter(low_cut.reshape(96, 16, 1024), 'pcol', scatter_dimension...]
    ppermute x1, starting transfers between devices: 9.28 us -> 2.58 us  [local(): other = lax.ppermute(dealt[:, 16:], 'prow', swap)]
    all_to_all x1, starting transfers between devices: 7.37 us -> 12.4 us  [local(): dealt = lax.all_to_all(dealt, 'pcol', 0, 0, tiled=True)]
    unnamed x48 -> x40, local copies, waits for them, and re-layouts: 24 us -> 21.3 us
  transfers between devices with their start and end apart: 14 -> 14, of which waited for: 10 -> 9; matrix products, arithmetic and copies ran while one was open for 4% -> 3% of each run, Pallas kernels for 21% -> 20%
where the time goes in v9:
time: 353 us; the launch traced here: 351 us
  waiting for transfers between devices  127 us (36%)
  Pallas kernels  93.3 us (26%)
  blocking collectives  45.9 us (13%)
  starting transfers between devices  37.6 us (11%)
  local copies, waits for them, and re-layouts  28.4 us (8%)
  between operations  13.7 us (4%)
  other arithmetic  5.74 us (2%)
    all_to_all x1, waiting for transfers between devices, local(): dealt = lax.all_to_all(dealt, 'pcol', 0, 0, tiled=True)  61.6 us
    all_to_all x1, waiting for transfers between devices, local(): lax.all_to_all(child, 'pcol', 0, 0, tiled=True).reshape(48, 256, 256)  27.8 us
    all_to_all x1, blocking collectives, spread(): lax.all_to_all(jnp.broadcast_to(x[None], (count,) + x.shape), axis, 0, 0,...  26.3 us
    all_to_all x1, waiting for transfers between devices, local(): lax.all_to_all(cut_top(front_top, child.reshape(48, 256, 256)), 'pcol', 0...  24.5 us
    pallas_call x1, Pallas kernels, factor_second(): pl.pallas_call(factor_second_kernel, out_shape=[jax.ShapeDtypeStruct((n,...  23.9 us
    pallas_call x1, Pallas kernels, factor_first(): pl.pallas_call(factor_first_kernel, out_shape=[jax.ShapeDtypeStruct((n, n...  22.7 us
    unnamed x40, local copies, waits for them, and re-layouts  21.3 us
    all_to_all x1, blocking collectives, local(): lax.all_to_all(jnp.tile(top, (prow // 2, 1, 1)), 'prow', 0, 0, tiled=True)  19.5 us
  transfers between devices with their start and end apart: 14, of which 9 were waited for; matrix products, arithmetic and copies ran while one was open for 3% of the time, Pallas kernels for 20%

profile of v9, /device:TPU:1, one launch (start us, length us, event | category | flops | bytes accessed | tf_op | source)
XLA Modules:
  0.0 351.2 jit_solution(14894941987163072919)
XLA Ops:
  7.2 7.1 %shard_map.55 = f32[16,6,16,1024]{3,2,1,0:T(8,128)} custom-call(s32[3]{0:T(128)} %pad_add_fusion.1.at_ref, f32[16384,128]{1,0:T(8,128)} %bitcast.63), custom_call_target="tpu_custom_call" | custom-call | bytes 12582912 | tf_op jit(solution)/shard_map/pallas_call | solution.py:214
  14.3 2.8 copy-done.3
  17.1 3.2 shard_map.56
  20.3 8.2 %all-to-all-start = ((bf16[16,14,16,256]{3,2,1,0:T(8,128)(2,1)}), bf16[16,14,16,256]{3,2,1,0:T(8,128)(2,1)S(1)}, u32[]{:S(2)}, u32[]{:S(2)}) async-start(bf16[16,14,16,256]{3,2,1,0:T(8,128)(2,1)} %shard_map.56), calls=%async_computation | async-start | bytes 3670016 | tf_op jit(solution)/shard_map/all_to_all | solution.py:476
  31.2 24.5 %all-to-all-done.c_ref = bf16[16,14,16,256]{3,2,1,0:T(8,128)(2,1)S(1)} async-done(((bf16[16,14,16,256]{3,2,1,0:T(8,128)(2,1)}), bf16[16,14,16,256]{3,2,1,0:T(8,128)(2,1)S(1)}, u32[]{:S(2)}, u32[]{:S(2)}) %all-to-all-start) | async-done | bytes 1835040 | tf_op jit(solution)/shard_map/all_to_all | solution.py:476
  55.7 1.3 copy-done.17
  57.0 2.3 shard_map.57.d_ref
  60.2 19.5 %all_to_all.25 = f32[8,16,1024]{2,1,0:T(8,128)S(1)} all-to-all(f32[8,16,1024]{2,1,0:T(8,128)S(1)} %bitcast.71), channel_id=1, replica_groups=mesh['prow'=8,'pcol'=16] {'prow'}, dimensions={0} | all-to-all | bytes 1048576 | tf_op jit(solution)/shard_map/all_to_all | solution.py:496
  79.9 26.3 %all_to_all.26.mine_ref = f32[16,16,1536]{2,1,0:T(8,128)S(1)} all-to-all(f32[16,16,1536]{2,1,0:T(8,128)S(1)} %broadcast_in_dim.111), channel_id=1, replica_groups=mesh['prow'=8,'pcol'=16] {'pcol'}, dimensions={0} | all-to-all | bytes 3145728 | tf_op jit(solution)/shard_map/all_to_all | solution.py:453
  106.3 2.0 collective-permute-start
  108.3 3.0 collective-permute-done.other_ref
  112.5 5.0 %all-to-all-start.3 = ((bf16[16,3,256,256]{3,2,1,0:T(8,128)(2,1)}), bf16[16,3,256,256]{3,2,1,0:T(8,128)(2,1)}, u32[]{:S(2)}, u32[]{:S(2)}) async-start(bf16[16,3,256,256]{3,2,1,0:T(8,128)(2,1)} %bitcast.66), calls=%async_computation.4 | async-start | bytes 12582912 | tf_op jit(solution)/shard_map/all_to_all | solution.py:500
  119.7 1.4 copy-done.16
  121.1 22.7 %shard_map.58 = (f32[512,512]{1,0:T(8,128)S(1)}, f32[512,512]{1,0:T(8,128)S(1)}) custom-call(s32[3]{0:T(128)S(1)} %copy-done.14, f32[16,16,1536]{2,1,0:T(8,128)S(1)} %all_to_all.26.mine_ref, f32[16,16,1536]{2,1,0:T(8,128)S(1)} %copy-done.16), custom_call_target="tpu_custom_call" | custom-call | flops 20000000000 | bytes 3145728 | tf_op jit(solution)/shard_map/pallas_call | solution.py:148
  144.8 23.9 %shard_map.59 = (bf16[512,512]{1,0:T(8,128)(2,1)S(1)}, f32[512,512]{1,0:T(8,128)S(1)}, f32[512,512]{1,0:T(8,128)S(1)}) custom-call(s32[3]{0:T(128)S(1)} %copy-done.14, s32[4]{0:T(128)S(1)} %reshape.307.mask_ref, f32[16,16,1536]{2,1,0:T(8,128)S(1)} %all_to_all.26.mine_ref, f32[16,16,1536]{2,1,0:T(8,128)S(1)} %copy-done.16, ...), custom_call_target="tpu_custom_call" | custom-call | flops 20000000000 | bytes 3145728 | tf_op jit(solution)/shard_map/pallas_call | solution.py:161
  171.6 2.6 shard_map.60.r_ref
  174.2 2.7 shard_map.61.p_ref.p0_ref
  176.9 3.1 shard_map.62.p1_ref
  183.1 2.8 collective-permute-start.7
  190.0 2.0 collective-permute-done.7.refs_6_
  192.1 3.9 %collective-permute-done.4.refs_3_ = bf16[2,4,16,512]{3,2,1,0:T(8,128)(2,1)S(1)} collective-permute-done((bf16[2,4,16,512]{3,2,1,0:T(8,128)(2,1)S(1)}, bf16[2,4,16,512]{3,2,1,0:T(8,128)(2,1)S(1)}, u32[]{:S(2)}, u32[]{:S(2)}) %collective-permute-start.4) | collective-permute-done | bytes 131104 | tf_op jit(solution)/shard_map/ppermute | solution.py:509
  196.0 1.7 collective-permute-done.3.refs_2_
  200.4 2.3 copy-done.4
  202.7 27.8 %all-to-all-done.3 = bf16[16,3,256,256]{3,2,1,0:T(8,128)(2,1)} async-done(((bf16[16,3,256,256]{3,2,1,0:T(8,128)(2,1)}), bf16[16,3,256,256]{3,2,1,0:T(8,128)(2,1)}, u32[]{:S(2)}, u32[]{:S(2)}) %all-to-all-start.3) | async-done | bytes 6291488 | tf_op jit(solution)/shard_map/all_to_all | solution.py:500
  230.5 12.4 %all-to-all-start.4 = ((bf16[16,20,16,512]{3,2,1,0:T(8,128)(2,1)}), bf16[16,20,16,512]{3,2,1,0:T(8,128)(2,1)}, u32[]{:S(2)}, u32[]{:S(2)}) async-start(bf16[16,20,16,512]{3,2,1,0:T(8,128)(2,1)} %copy-done.4), calls=%async_computation.5 | async-start | bytes 10485760 | tf_op jit(solution)/shard_map/all_to_all | solution.py:522
  244.1 3.4 copy-done.1
  247.4 7.7 %shard_map.64.f_ref = f32[16384,128]{1,0:T(8,128)S(1)} custom-call(s32[64]{0:T(128)S(1)} %broadcast_add_fusion.2.slot_ref, f32[16384,128]{1,0:T(8,128)S(1)} %bitcast.65, bf16[48,256,256]{2,1,0:T(8,128)(2,1)} %bitcast.23.refs_0_.refs_1_.refs_2_.refs_3_.refs_4_.refs_5_.refs_6_.refs_7_, ...), custom_call_target="tpu_custom_call" | custom-call | bytes 25165824 | tf_op jit(solution)/shard_map/pallas_call | solution.py:341
  255.2 3.3 copy-done.2
  258.4 61.6 %all-to-all-done.4.row0_ref.row1_ref.mine_ref = bf16[16,20,16,512]{3,2,1,0:T(8,128)(2,1)} async-done(((bf16[16,20,16,512]{3,2,1,0:T(8,128)(2,1)}), bf16[16,20,16,512]{3,2,1,0:T(8,128)(2,1)}, u32[]{:S(2)}, u32[]{:S(2)}) %all-to-all-start.4) | async-done | bytes 5242912 | tf_op jit(solution)/shard_map/all_to_all | solution.py:522
  320.0 2.3 slice.39
  322.3 2.6 collective-permute-start.9
  327.4 17.0 %shard_map.65 = f32[16384,128]{1,0:T(8,128)} custom-call(s32[50]{0:T(128)S(1)} %pad_add_fusion.flag_ref, f32[16384,128]{1,0:T(8,128)} %copy-done.2, bf16[16,20,16,512]{3,2,1,0:T(8,128)(2,1)} %all-to-all-done.4.row0_ref.row1_ref.mine_ref, bf16[16,20,16,512]{3,2,1,0:T(8,128)(2,1)} %all-to-all-done.4.row0_ref.row1_ref.mine_ref, ...), custom_call_target="tpu_custom_call" | custom-call | flops 5000000000 | bytes 25165824 | tf_op jit(solution)/shard_map/pallas_call | solution.py:417
  (124 shorter events, 24.9 us)
Async XLA Ops:
  6.5 23.6 %copy-start = (s32[8,16,16,3]{2,1,3,0:T(8,128)S(1)}, s32[8,16,16,3]{2,1,3,0:T(8,128)}, u32[]{:S(2)}) copy-start(s32[8,16,16,3]{2,1,3,0:T(8,128)} %param.8) | copy-start | bytes 73732
  6.5 165.1 %reduce-scatter.2.cloned.1.call-start = ((), (), s32[]{:S(2)}) async-start(), calls=%async_computation.6 | async-start | bytes 6684672 | tf_op jit(solution)/shard_map/reduce_scatter | solution.py:472
  14.3 2.8 copy-start.3
  17.1 11.8 %copy-start.19 = (s32[2,60]{1,0:T(2,128)S(1)}, s32[2,60]{1,0:T(2,128)}, u32[]{:S(2)}) copy-start(s32[2,60]{1,0:T(2,128)} %param.7) | copy-start | bytes 1444
  20.3 35.4 %all-to-all-start = ((bf16[16,14,16,256]{3,2,1,0:T(8,128)(2,1)}), bf16[16,14,16,256]{3,2,1,0:T(8,128)(2,1)S(1)}, u32[]{:S(2)}, u32[]{:S(2)}) async-start(bf16[16,14,16,256]{3,2,1,0:T(8,128)(2,1)} %shard_map.56), calls=%async_computation | async-start | bytes 3670016 | tf_op jit(solution)/shard_map/all_to_all | solution.py:476
  55.7 1.3 copy-start.17
  106.3 5.0 %collective-permute-start = (f32[16,16,1536]{2,1,0:T(8,128)S(1)}, f32[16,16,1536]{2,1,0:T(8,128)S(1)}, u32[]{:S(2)}, u32[]{:S(2)}) collective-permute-start(f32[16,16,1536]{2,1,0:T(8,128)S(1)} %all_to_all.26.mine_ref), channel_id=1, source_target_pairs={{0,16},{16,0},{32,48},{48,32},{64,80},{80,64},{96,112},{112,96},{1... | collective-permute-start | bytes 4718600 | tf_op jit(solution)/shard_map/ppermute | solution.py:498
  111.3 1.2 copy-start.15
  112.5 5.1 %copy-start.18 = (s32[64,64]{1,0:T(8,128)S(1)}, s32[64,64]{1,0:T(8,128)}, u32[]{:S(2)}) copy-start(s32[64,64]{1,0:T(8,128)} %param.9) | copy-start | bytes 49156
  112.5 7.2 %copy-start.14 = (s32[3]{0:T(128)S(1)}, s32[3]{0:T(128)}, u32[]{:S(2)}) copy-start(s32[3]{0:T(128)} %pad_add_fusion.1.at_ref) | copy-start | bytes 40
  112.5 118.0 %all-to-all-start.3 = ((bf16[16,3,256,256]{3,2,1,0:T(8,128)(2,1)}), bf16[16,3,256,256]{3,2,1,0:T(8,128)(2,1)}, u32[]{:S(2)}, u32[]{:S(2)}) async-start(bf16[16,3,256,256]{3,2,1,0:T(8,128)(2,1)} %bitcast.66), calls=%async_computation.4 | async-start | bytes 12582912 | tf_op jit(solution)/shard_map/all_to_all | solution.py:500
  119.7 1.4 copy-start.16
  143.8 1.0 copy-start.10
  144.8 24.0 %copy-start.5 = (f32[512,512]{1,0:T(8,128)}, f32[512,512]{1,0:T(8,128)S(1)}, u32[]{:S(2)}) copy-start(f32[512,512]{1,0:T(8,128)S(1)} %get-tuple-element.25.w0_ref.w_ref) | copy-start | bytes 3145732
  168.8 1.0 copy-start.7
  169.8 1.0 copy-start.12
  181.0 1.6 collective-permute-start.5
  182.3 4.5 %collective-permute-start.1 = (bf16[4,16,512]{2,1,0:T(8,128)(2,1)S(1)}, bf16[4,16,512]{2,1,0:T(8,128)(2,1)S(1)}, u32[]{:S(2)}, u32[]{:S(2)}) collective-permute-start(bf16[4,16,512]{2,1,0:T(8,128)(2,1)S(1)} %get-tuple-element.44), channel_id=1, source_target_pairs={{0,16},{16,0},{32,48},{48,32},{64,80},{80,64},{96,112},{112,96},{1... | collective-permute-start | bytes 196616 | tf_op jit(solution)/shard_map/ppermute | solution.py:505
  182.5 6.3 %collective-permute-start.8 = (bf16[2,4,16,512]{3,2,1,0:T(8,128)(2,1)S(1)}, bf16[2,4,16,512]{3,2,1,0:T(8,128)(2,1)S(1)}, u32[]{:S(2)}, u32[]{:S(2)}) collective-permute-start(bf16[2,4,16,512]{3,2,1,0:T(8,128)(2,1)S(1)} %maximum_select_fusion.1.refs_4_), channel_id=1, source_target_pairs={{96,0},{112,16},{0,32},{16,48},{32,64},{48,80},{64,96},{80,112},{9... | collective-permute-start | bytes 393224 | tf_op jit(solution)/shard_map/ppermute | solution.py:509
  183.1 9.0 %collective-permute-start.7 = (bf16[2,4,16,512]{3,2,1,0:T(8,128)(2,1)S(1)}, bf16[2,4,16,512]{3,2,1,0:T(8,128)(2,1)S(1)}, u32[]{:S(2)}, u32[]{:S(2)}) collective-permute-start(bf16[2,4,16,512]{3,2,1,0:T(8,128)(2,1)S(1)} %maximum_select_fusion.1.refs_4_), channel_id=1, source_target_pairs={{64,0},{80,16},{96,32},{112,48},{0,64},{16,80},{32,96},{48,112},{6... | collective-permute-start | bytes 393224 | tf_op jit(solution)/shard_map/ppermute | solution.py:509
  185.9 6.2 %collective-permute-start.6 = (bf16[2,4,16,512]{3,2,1,0:T(8,128)(2,1)S(1)}, bf16[2,4,16,512]{3,2,1,0:T(8,128)(2,1)S(1)}, u32[]{:S(2)}, u32[]{:S(2)}) collective-permute-start(bf16[2,4,16,512]{3,2,1,0:T(8,128)(2,1)S(1)} %maximum_select_fusion.1.refs_4_), channel_id=1, source_target_pairs={{32,0},{48,16},{64,32},{80,48},{96,64},{112,80},{0,96},{16,112},{3... | collective-permute-start | bytes 393224 | tf_op jit(solution)/shard_map/ppermute | solution.py:509
  186.8 9.1 %collective-permute-start.4 = (bf16[2,4,16,512]{3,2,1,0:T(8,128)(2,1)S(1)}, bf16[2,4,16,512]{3,2,1,0:T(8,128)(2,1)S(1)}, u32[]{:S(2)}, u32[]{:S(2)}) collective-permute-start(bf16[2,4,16,512]{3,2,1,0:T(8,128)(2,1)S(1)} %maximum_select_fusion.refs_0_), channel_id=1, source_target_pairs={{96,0},{112,16},{0,32},{16,48},{32,64},{48,80},{64,96},{80,112},{9... | collective-permute-start | bytes 393224 | tf_op jit(solution)/shard_map/ppermute | solution.py:509
  187.5 10.2 %collective-permute-start.3 = (bf16[2,4,16,512]{3,2,1,0:T(8,128)(2,1)S(1)}, bf16[2,4,16,512]{3,2,1,0:T(8,128)(2,1)S(1)}, u32[]{:S(2)}, u32[]{:S(2)}) collective-permute-start(bf16[2,4,16,512]{3,2,1,0:T(8,128)(2,1)S(1)} %maximum_select_fusion.refs_0_), channel_id=1, source_target_pairs={{64,0},{80,16},{96,32},{112,48},{0,64},{16,80},{32,96},{48,112},{6... | collective-permute-start | bytes 393224 | tf_op jit(solution)/shard_map/ppermute | solution.py:509
  188.8 8.8 %collective-permute-start.2 = (bf16[2,4,16,512]{3,2,1,0:T(8,128)(2,1)S(1)}, bf16[2,4,16,512]{3,2,1,0:T(8,128)(2,1)S(1)}, u32[]{:S(2)}, u32[]{:S(2)}) collective-permute-start(bf16[2,4,16,512]{3,2,1,0:T(8,128)(2,1)S(1)} %maximum_select_fusion.refs_0_), channel_id=1, source_target_pairs={{32,0},{48,16},{64,32},{80,48},{96,64},{112,80},{0,96},{16,112},{3... | collective-permute-start | bytes 393224 | tf_op jit(solution)/shard_map/ppermute | solution.py:509
  197.7 0.9 copy-start.8
  200.4 2.4 copy-start.4
  230.5 13.1 %copy-start.11 = (f32[512,512]{1,0:T(8,128)S(1)}, f32[512,512]{1,0:T(8,128)}, u32[]{:S(2)}) copy-start(f32[512,512]{1,0:T(8,128)} %copy-done.10) | copy-start | bytes 3145732
  230.5 13.3 %copy-start.6 = (f32[512,512]{1,0:T(8,128)S(1)}, f32[512,512]{1,0:T(8,128)}, u32[]{:S(2)}) copy-start(f32[512,512]{1,0:T(8,128)} %copy-done.5) | copy-start | bytes 3145732
  230.5 89.5 %all-to-all-start.4 = ((bf16[16,20,16,512]{3,2,1,0:T(8,128)(2,1)}), bf16[16,20,16,512]{3,2,1,0:T(8,128)(2,1)}, u32[]{:S(2)}, u32[]{:S(2)}) async-start(bf16[16,20,16,512]{3,2,1,0:T(8,128)(2,1)} %copy-done.4), calls=%async_computation.5 | async-start | bytes 10485760 | tf_op jit(solution)/shard_map/all_to_all | solution.py:522
  244.1 3.4 copy-start.1
  255.1 3.3 copy-start.2
  322.3 5.1 %collective-permute-start.9 = (bf16[16,4,16,512]{3,2,1,0:T(8,128)(2,1)}, bf16[16,4,16,512]{3,2,1,0:T(8,128)(2,1)S(1)}, u32[]{:S(2)}, u32[]{:S(2)}) collective-permute-start(bf16[16,4,16,512]{3,2,1,0:T(8,128)(2,1)} %slice.39), channel_id=1, source_target_pairs={{0,16},{16,0},{32,48},{48,32},{64,80},{80,64},{96,112},{112,96},{1... | collective-permute-start | bytes 3145736 | tf_op jit(solution)/shard_map/ppermute | solution.py:527
  (2 other events, 1.7 us)
Sparse Core Ops, SparseCore 0:
  14.4 148.6 reduce-scatter.1

commit v10 on v9

--- a/solution.py
+++ b/solution.py
@@ -496,7 +496,7 @@
     half_top = lax.all_to_all(jnp.tile(top, (prow // 2, 1, 1)), "prow", 0, 0, tiled=True)
     first = spread(jnp.concatenate([half_top[0, :, :512], half_top[1]], axis=1), "pcol", pcol)
     diag = (first, lax.ppermute(first, "prow", swap))
-    child, diag = lax.optimization_barrier((child, diag))
+    child, diag, low_front = lax.optimization_barrier((child, diag, low_front))
     arrived = lax.all_to_all(child, "pcol", 0, 0, tiled=True).reshape(48, 256, 256)
 
     def gather_columns(strips):
@@ -509,11 +509,12 @@
         return [chip] + [lax.ppermute(chip, "prow", along(k)) for k in range(1, 4)]
 
     L0, W0 = factor_first(at, *diag)
-    P10, L1, W1 = factor_second(at, struct_mask[2:4, 2:4].reshape(-1), *diag, W0)
-    W1, low_front = lax.optimization_barrier((W1, low_front))
     low = join_strips(join_low_kernel, 6, strip_slots, got, low_front)
     P0 = solve_strips(solve_first_kernel, keep0, top, low, W0)
+    P0, diag = lax.optimization_barrier((P0, diag))
     cols0 = gather_columns(P0)
+    P10, L1, W1 = factor_second(at, struct_mask[2:4, 2:4].reshape(-1), *diag, W0)
+    W1, cols0 = lax.optimization_barrier((W1, cols0))
     P1 = solve_strips(solve_second_kernel, keep1, top, low, P0, P10, W1)
     cols1 = gather_columns(P1)
 

time: 353 us -> 332 us (0.941)
  waiting for transfers between devices: 127 us -> 97.7 us
  starting transfers between devices: 37.6 us -> 42.7 us
    all_to_all x1, waiting for transfers between devices: 27.8 us -> 4.1 us  [local(): lax.all_to_all(child, 'pcol', 0, 0, tiled=True).reshape(48, 256, 256)]
    all_to_all x1, waiting for transfers between devices: 61.6 us -> 43.4 us  [local(): dealt = lax.all_to_all(dealt, 'pcol', 0, 0, tiled=True)]
    reduce_scatter x1, waiting for transfers between devices: 0.01 us -> 13.8 us  [local(): lax.psum_scatter(low_cut.reshape(96, 16, 1024), 'pcol', scatter_dimension...]
    ppermute x1, starting transfers between devices: 2.58 us -> 9.28 us  [local(): other = lax.ppermute(dealt[:, 16:], 'prow', swap)]
    all_to_all x1, starting transfers between devices: 12.4 us -> 7.37 us  [local(): dealt = lax.all_to_all(dealt, 'pcol', 0, 0, tiled=True)]
    unnamed x40 -> x44, local copies, waits for them, and re-layouts: 21.3 us -> 24 us
  transfers between devices with their start and end apart: 14 -> 14, of which waited for: 9 -> 10; matrix products, arithmetic and copies ran while one was open for 3% -> 3% of each run, Pallas kernels for 20% -> 21%
where the time goes in v10:
time: 332 us; the launch traced here: 330 us
  waiting for transfers between devices  97.7 us (29%)
  Pallas kernels  93.4 us (28%)
  blocking collectives  45.9 us (14%)
  starting transfers between devices  42.7 us (13%)
  local copies, waits for them, and re-layouts  31.1 us (9%)
  between operations  13.7 us (4%)
  other arithmetic  5.69 us (2%)
    all_to_all x1, waiting for transfers between devices, local(): dealt = lax.all_to_all(dealt, 'pcol', 0, 0, tiled=True)  43.4 us
    all_to_all x1, blocking collectives, spread(): lax.all_to_all(jnp.broadcast_to(x[None], (count,) + x.shape), axis, 0, 0,...  26.3 us
    all_to_all x1, waiting for transfers between devices, local(): lax.all_to_all(cut_top(front_top, child.reshape(48, 256, 256)), 'pcol', 0...  24.5 us
    unnamed x44, local copies, waits for them, and re-layouts  24 us
    pallas_call x1, Pallas kernels, factor_second(): pl.pallas_call(factor_second_kernel, out_shape=[jax.ShapeDtypeStruct((n,...  23.9 us
    pallas_call x1, Pallas kernels, factor_first(): pl.pallas_call(factor_first_kernel, out_shape=[jax.ShapeDtypeStruct((n, n...  22.7 us
    all_to_all x1, blocking collectives, local(): lax.all_to_all(jnp.tile(top, (prow // 2, 1, 1)), 'prow', 0, 0, tiled=True)  19.6 us
    pallas_call x1, Pallas kernels, finish(): pl.pallas_call(finish_kernel, grid_spec=pltpu.PrefetchScalarGridSpec(num_...  17 us
  transfers between devices with their start and end apart: 14, of which 10 were waited for; matrix products, arithmetic and copies ran while one was open for 3% of the time, Pallas kernels for 21%

profile of v10, /device:TPU:1, one launch (start us, length us, event | category | flops | bytes accessed | tf_op | source)
XLA Modules:
  0.0 330.2 jit_solution(4470604601887291753)
XLA Ops:
  7.2 7.1 %shard_map.55 = f32[16,6,16,1024]{3,2,1,0:T(8,128)} custom-call(s32[3]{0:T(128)} %pad_add_fusion.1.at_ref, f32[16384,128]{1,0:T(8,128)} %bitcast.63), custom_call_target="tpu_custom_call" | custom-call | bytes 12582912 | tf_op jit(solution)/shard_map/pallas_call | solution.py:214
  14.4 2.8 copy-done.3
  17.1 3.2 shard_map.56
  20.4 8.2 %all-to-all-start = ((bf16[16,14,16,256]{3,2,1,0:T(8,128)(2,1)}), bf16[16,14,16,256]{3,2,1,0:T(8,128)(2,1)S(1)}, u32[]{:S(2)}, u32[]{:S(2)}) async-start(bf16[16,14,16,256]{3,2,1,0:T(8,128)(2,1)} %shard_map.56), calls=%async_computation | async-start | bytes 3670016 | tf_op jit(solution)/shard_map/all_to_all | solution.py:476
  31.2 24.5 %all-to-all-done.c_ref = bf16[16,14,16,256]{3,2,1,0:T(8,128)(2,1)S(1)} async-done(((bf16[16,14,16,256]{3,2,1,0:T(8,128)(2,1)}), bf16[16,14,16,256]{3,2,1,0:T(8,128)(2,1)S(1)}, u32[]{:S(2)}, u32[]{:S(2)}) %all-to-all-start) | async-done | bytes 1835040 | tf_op jit(solution)/shard_map/all_to_all | solution.py:476
  57.0 2.3 shard_map.57.d_ref
  60.2 19.6 %all_to_all.25 = f32[8,16,1024]{2,1,0:T(8,128)S(1)} all-to-all(f32[8,16,1024]{2,1,0:T(8,128)S(1)} %bitcast.71), channel_id=1, replica_groups=mesh['prow'=8,'pcol'=16] {'prow'}, dimensions={0} | all-to-all | bytes 1048576 | tf_op jit(solution)/shard_map/all_to_all | solution.py:496
  80.0 26.3 %all_to_all.26.mine_ref = f32[16,16,1536]{2,1,0:T(8,128)S(1)} all-to-all(f32[16,16,1536]{2,1,0:T(8,128)S(1)} %broadcast_in_dim.111), channel_id=1, replica_groups=mesh['prow'=8,'pcol'=16] {'pcol'}, dimensions={0} | all-to-all | bytes 3145728 | tf_op jit(solution)/shard_map/all_to_all | solution.py:453
  106.3 1.8 collective-permute-start
  108.1 3.0 collective-permute-done.other_ref
  112.4 13.8 %reduce-scatter.2.cloned.1.call-done.f_ref = f32[6,16,1024]{2,1,0:T(8,128)} async-done(((f32[96,16,1024]{2,1,0:T(8,128)}), f32[6,16,1024]{2,1,0:T(8,128)}) %reduce-scatter.2.cloned.1.call-update) | async-done | bytes 393232 | tf_op jit(solution)/shard_map/reduce_scatter | solution.py:472
  126.2 4.8 %all-to-all-start.3 = ((bf16[16,3,256,256]{3,2,1,0:T(8,128)(2,1)}), bf16[16,3,256,256]{3,2,1,0:T(8,128)(2,1)}, u32[]{:S(2)}, u32[]{:S(2)}) async-start(bf16[16,3,256,256]{3,2,1,0:T(8,128)(2,1)} %bitcast.66), calls=%async_computation.4 | async-start | bytes 12582912 | tf_op jit(solution)/shard_map/all_to_all | solution.py:500
  132.5 2.6 shard_map.58.r_ref
  135.1 1.4 copy-done.17
  136.5 22.7 %shard_map.59 = (f32[512,512]{1,0:T(8,128)S(1)}, f32[512,512]{1,0:T(8,128)S(1)}) custom-call(s32[3]{0:T(128)S(1)} %copy-done.15, f32[16,16,1536]{2,1,0:T(8,128)S(1)} %all_to_all.26.mine_ref, f32[16,16,1536]{2,1,0:T(8,128)S(1)} %copy-done.17), custom_call_target="tpu_custom_call" | custom-call | flops 20000000000 | bytes 3145728 | tf_op jit(solution)/shard_map/pallas_call | solution.py:148
  161.2 2.7 shard_map.60.p_ref.p0_ref
  164.8 2.1 collective-permute-start.1
  169.1 2.5 collective-permute-start.3
  175.4 23.9 %shard_map.61 = (bf16[512,512]{1,0:T(8,128)(2,1)S(1)}, f32[512,512]{1,0:T(8,128)S(1)}, f32[512,512]{1,0:T(8,128)S(1)}) custom-call(s32[3]{0:T(128)S(1)} %copy-done.15, s32[4]{0:T(128)S(1)} %reshape.309.mask_ref, f32[16,16,1536]{2,1,0:T(8,128)S(1)} %all_to_all.26.mine_ref, f32[16,16,1536]{2,1,0:T(8,128)S(1)} %copy-done.18, f32[512,512]{1,0:T(8,128)S(1)} %copy-done.6), custom_call_target="tpu_custom_call" | custom-call | flops 20000000000 | bytes 3145728 | tf_op jit(solution)/shard_map/pallas_call | solution.py:161
  202.2 3.1 shard_map.62.p1_ref
  209.4 1.9 collective-permute-start.6
  211.3 6.1 %collective-permute-done.8.refs_7_ = bf16[2,4,16,512]{3,2,1,0:T(8,128)(2,1)S(1)} collective-permute-done((bf16[2,4,16,512]{3,2,1,0:T(8,128)(2,1)S(1)}, bf16[2,4,16,512]{3,2,1,0:T(8,128)(2,1)S(1)}, u32[]{:S(2)}, u32[]{:S(2)}) %collective-permute-start.8) | collective-permute-done | bytes 131104 | tf_op jit(solution)/shard_map/ppermute | solution.py:509
  219.5 2.3 copy-done.4
  221.9 4.1 %all-to-all-done.3 = bf16[16,3,256,256]{3,2,1,0:T(8,128)(2,1)} async-done(((bf16[16,3,256,256]{3,2,1,0:T(8,128)(2,1)}), bf16[16,3,256,256]{3,2,1,0:T(8,128)(2,1)}, u32[]{:S(2)}, u32[]{:S(2)}) %all-to-all-start.3) | async-done | bytes 6291488 | tf_op jit(solution)/shard_map/all_to_all | solution.py:500
  226.0 7.4 %all-to-all-start.4 = ((bf16[16,20,16,512]{3,2,1,0:T(8,128)(2,1)}), bf16[16,20,16,512]{3,2,1,0:T(8,128)(2,1)}, u32[]{:S(2)}, u32[]{:S(2)}) async-start(bf16[16,20,16,512]{3,2,1,0:T(8,128)(2,1)} %copy-done.4), calls=%async_computation.5 | async-start | bytes 10485760 | tf_op jit(solution)/shard_map/all_to_all | solution.py:523
  234.5 3.4 %copy-done.1 = f32[4,1,512,2,1,512]{5,4,3,2,1,0:T(1,128)S(1)} copy-done((f32[4,1,512,2,1,512]{5,4,3,2,1,0:T(1,128)S(1)}, f32[4,1,512,2,1,512]{5,4,3,2,1,0:T(1,128)}, u32[]{:S(2)}) %copy-start.1) | copy-done | bytes 8388632
  237.8 7.8 %shard_map.64.f_ref = f32[16384,128]{1,0:T(8,128)S(1)} custom-call(s32[64]{0:T(128)S(1)} %broadcast_add_fusion.2.slot_ref, f32[16384,128]{1,0:T(8,128)S(1)} %bitcast.65, bf16[48,256,256]{2,1,0:T(8,128)(2,1)} %bitcast.23.refs_0_.refs_1_.refs_2_.refs_3_.refs_4_.refs_5_.refs_6_.refs_7_, ...), custom_call_target="tpu_custom_call" | custom-call | bytes 25165824 | tf_op jit(solution)/shard_map/pallas_call | solution.py:341
  245.7 3.3 copy-done.2
  248.9 43.4 %all-to-all-done.4.row0_ref.row1_ref.mine_ref = bf16[16,20,16,512]{3,2,1,0:T(8,128)(2,1)} async-done(((bf16[16,20,16,512]{3,2,1,0:T(8,128)(2,1)}), bf16[16,20,16,512]{3,2,1,0:T(8,128)(2,1)}, u32[]{:S(2)}, u32[]{:S(2)}) %all-to-all-start.4) | async-done | bytes 5242912 | tf_op jit(solution)/shard_map/all_to_all | solution.py:523
  292.3 2.3 slice.39
  294.6 9.3 %collective-permute-start.9 = (bf16[16,4,16,512]{3,2,1,0:T(8,128)(2,1)}, bf16[16,4,16,512]{3,2,1,0:T(8,128)(2,1)S(1)}, u32[]{:S(2)}, u32[]{:S(2)}) collective-permute-start(bf16[16,4,16,512]{3,2,1,0:T(8,128)(2,1)} %slice.39), channel_id=1, source_target_pairs={{0,16},{16,0},{32,48},{48,32},{64,80},{80,64},{96,112},{112,96},{1... | collective-permute-start | bytes 3145736 | tf_op jit(solution)/shard_map/ppermute | solution.py:528
  306.3 17.0 %shard_map.65 = f32[16384,128]{1,0:T(8,128)} custom-call(s32[50]{0:T(128)S(1)} %pad_add_fusion.flag_ref, f32[16384,128]{1,0:T(8,128)} %copy-done.2, bf16[16,20,16,512]{3,2,1,0:T(8,128)(2,1)} %all-to-all-done.4.row0_ref.row1_ref.mine_ref, bf16[16,20,16,512]{3,2,1,0:T(8,128)(2,1)} %all-to-all-done.4.row0_ref.row1_ref.mine_ref, ...), custom_call_target="tpu_custom_call" | custom-call | flops 5000000000 | bytes 25165824 | tf_op jit(solution)/shard_map/pallas_call | solution.py:417
  (128 shorter events, 29.7 us)
Async XLA Ops:
  6.5 23.6 %copy-start = (s32[8,16,16,3]{2,1,3,0:T(8,128)S(1)}, s32[8,16,16,3]{2,1,3,0:T(8,128)}, u32[]{:S(2)}) copy-start(s32[8,16,16,3]{2,1,3,0:T(8,128)} %param.8) | copy-start | bytes 73732
  6.5 119.7 %reduce-scatter.2.cloned.1.call-start = ((), (), s32[]{:S(2)}) async-start(), calls=%async_computation.6 | async-start | bytes 6684672 | tf_op jit(solution)/shard_map/reduce_scatter | solution.py:472
  14.3 2.8 copy-start.3
  17.1 11.8 %copy-start.21 = (s32[2,60]{1,0:T(2,128)S(1)}, s32[2,60]{1,0:T(2,128)}, u32[]{:S(2)}) copy-start(s32[2,60]{1,0:T(2,128)} %param.7) | copy-start | bytes 1444
  20.4 35.3 %all-to-all-start = ((bf16[16,14,16,256]{3,2,1,0:T(8,128)(2,1)}), bf16[16,14,16,256]{3,2,1,0:T(8,128)(2,1)S(1)}, u32[]{:S(2)}, u32[]{:S(2)}) async-start(bf16[16,14,16,256]{3,2,1,0:T(8,128)(2,1)} %shard_map.56), calls=%async_computation | async-start | bytes 3670016 | tf_op jit(solution)/shard_map/all_to_all | solution.py:476
  55.7 1.3 copy-start.19
  106.3 4.9 %collective-permute-start = (f32[16,16,1536]{2,1,0:T(8,128)S(1)}, f32[16,16,1536]{2,1,0:T(8,128)S(1)}, u32[]{:S(2)}, u32[]{:S(2)}) collective-permute-start(f32[16,16,1536]{2,1,0:T(8,128)S(1)} %all_to_all.26.mine_ref), channel_id=1, source_target_pairs={{0,16},{16,0},{32,48},{48,32},{64,80},{80,64},{96,112},{112,96},{1... | collective-permute-start | bytes 4718600 | tf_op jit(solution)/shard_map/ppermute | solution.py:498
  111.1 1.2 copy-start.16
  126.2 4.9 %copy-start.20 = (s32[64,64]{1,0:T(8,128)S(1)}, s32[64,64]{1,0:T(8,128)}, u32[]{:S(2)}) copy-start(s32[64,64]{1,0:T(8,128)} %param.9) | copy-start | bytes 49156
  126.2 8.9 %copy-start.15 = (s32[3]{0:T(128)S(1)}, s32[3]{0:T(128)}, u32[]{:S(2)}) copy-start(s32[3]{0:T(128)} %pad_add_fusion.1.at_ref) | copy-start | bytes 40
  126.2 99.8 %all-to-all-start.3 = ((bf16[16,3,256,256]{3,2,1,0:T(8,128)(2,1)}), bf16[16,3,256,256]{3,2,1,0:T(8,128)(2,1)}, u32[]{:S(2)}, u32[]{:S(2)}) async-start(bf16[16,3,256,256]{3,2,1,0:T(8,128)(2,1)} %bitcast.66), calls=%async_computation.4 | async-start | bytes 12582912 | tf_op jit(solution)/shard_map/all_to_all | solution.py:500
  135.1 1.4 copy-start.17
  164.8 3.0 collective-permute-start.1
  167.9 49.9 %copy-start.9 = (bf16[8,16,512]{2,1,0:T(8,128)(2,1)S(1)}, bf16[8,16,512]{2,1,0:T(8,128)(2,1)}, u32[]{:S(2)}) copy-start(bf16[8,16,512]{2,1,0:T(8,128)(2,1)} %shard_map.60.p_ref.p0_ref) | copy-start | bytes 393220
  167.9 34.3 %collective-permute-start.4 = (bf16[2,4,16,512]{3,2,1,0:T(8,128)(2,1)S(1)}, bf16[2,4,16,512]{3,2,1,0:T(8,128)(2,1)S(1)}, u32[]{:S(2)}, u32[]{:S(2)}) collective-permute-start(bf16[2,4,16,512]{3,2,1,0:T(8,128)(2,1)S(1)} %maximum_select_fusion.refs_0_), channel_id=1, source_target_pairs={{96,0},{112,16},{0,32},{16,48},{32,64},{48,80},{64,96},{80,112},{9... | collective-permute-start | bytes 393224 | tf_op jit(solution)/shard_map/ppermute | solution.py:509
  169.1 33.1 %collective-permute-start.3 = (bf16[2,4,16,512]{3,2,1,0:T(8,128)(2,1)S(1)}, bf16[2,4,16,512]{3,2,1,0:T(8,128)(2,1)S(1)}, u32[]{:S(2)}, u32[]{:S(2)}) collective-permute-start(bf16[2,4,16,512]{3,2,1,0:T(8,128)(2,1)S(1)} %maximum_select_fusion.refs_0_), channel_id=1, source_target_pairs={{64,0},{80,16},{96,32},{112,48},{0,64},{16,80},{32,96},{48,112},{6... | collective-permute-start | bytes 393224 | tf_op jit(solution)/shard_map/ppermute | solution.py:509
  171.6 30.6 %collective-permute-start.2 = (bf16[2,4,16,512]{3,2,1,0:T(8,128)(2,1)S(1)}, bf16[2,4,16,512]{3,2,1,0:T(8,128)(2,1)S(1)}, u32[]{:S(2)}, u32[]{:S(2)}) collective-permute-start(bf16[2,4,16,512]{3,2,1,0:T(8,128)(2,1)S(1)} %maximum_select_fusion.refs_0_), channel_id=1, source_target_pairs={{32,0},{48,16},{64,32},{80,48},{96,64},{112,80},{0,96},{16,112},{3... | collective-permute-start | bytes 393224 | tf_op jit(solution)/shard_map/ppermute | solution.py:509
  172.8 1.2 copy-start.6
  174.0 1.4 copy-start.18
  199.3 1.1 copy-start.8
  200.4 1.0 copy-start.13
  206.2 2.2 collective-permute-start.5
  208.4 9.0 %collective-permute-start.8 = (bf16[2,4,16,512]{3,2,1,0:T(8,128)(2,1)S(1)}, bf16[2,4,16,512]{3,2,1,0:T(8,128)(2,1)S(1)}, u32[]{:S(2)}, u32[]{:S(2)}) collective-permute-start(bf16[2,4,16,512]{3,2,1,0:T(8,128)(2,1)S(1)} %maximum_select_fusion.1.refs_4_), channel_id=1, source_target_pairs={{96,0},{112,16},{0,32},{16,48},{32,64},{48,80},{64,96},{80,112},{9... | collective-permute-start | bytes 393224 | tf_op jit(solution)/shard_map/ppermute | solution.py:509
  208.8 8.6 %collective-permute-start.7 = (bf16[2,4,16,512]{3,2,1,0:T(8,128)(2,1)S(1)}, bf16[2,4,16,512]{3,2,1,0:T(8,128)(2,1)S(1)}, u32[]{:S(2)}, u32[]{:S(2)}) collective-permute-start(bf16[2,4,16,512]{3,2,1,0:T(8,128)(2,1)S(1)} %maximum_select_fusion.1.refs_4_), channel_id=1, source_target_pairs={{64,0},{80,16},{96,32},{112,48},{0,64},{16,80},{32,96},{48,112},{6... | collective-permute-start | bytes 393224 | tf_op jit(solution)/shard_map/ppermute | solution.py:509
  209.4 8.3 %collective-permute-start.6 = (bf16[2,4,16,512]{3,2,1,0:T(8,128)(2,1)S(1)}, bf16[2,4,16,512]{3,2,1,0:T(8,128)(2,1)S(1)}, u32[]{:S(2)}, u32[]{:S(2)}) collective-permute-start(bf16[2,4,16,512]{3,2,1,0:T(8,128)(2,1)S(1)} %maximum_select_fusion.1.refs_4_), channel_id=1, source_target_pairs={{32,0},{48,16},{64,32},{80,48},{96,64},{112,80},{0,96},{16,112},{3... | collective-permute-start | bytes 393224 | tf_op jit(solution)/shard_map/ppermute | solution.py:509
  219.5 2.4 copy-start.4
  226.0 8.0 %copy-start.12 = (f32[512,512]{1,0:T(8,128)S(1)}, f32[512,512]{1,0:T(8,128)}, u32[]{:S(2)}) copy-start(f32[512,512]{1,0:T(8,128)} %copy-done.11) | copy-start | bytes 3145732
  226.0 8.2 %copy-start.7 = (f32[512,512]{1,0:T(8,128)S(1)}, f32[512,512]{1,0:T(8,128)}, u32[]{:S(2)}) copy-start(f32[512,512]{1,0:T(8,128)} %copy-done.5) | copy-start | bytes 3145732
  226.0 66.3 %all-to-all-start.4 = ((bf16[16,20,16,512]{3,2,1,0:T(8,128)(2,1)}), bf16[16,20,16,512]{3,2,1,0:T(8,128)(2,1)}, u32[]{:S(2)}, u32[]{:S(2)}) async-start(bf16[16,20,16,512]{3,2,1,0:T(8,128)(2,1)} %copy-done.4), calls=%async_computation.5 | async-start | bytes 10485760 | tf_op jit(solution)/shard_map/all_to_all | solution.py:523
  234.5 3.4 %copy-start.1 = (f32[4,1,512,2,1,512]{5,4,3,2,1,0:T(1,128)S(1)}, f32[4,1,512,2,1,512]{5,4,3,2,1,0:T(1,128)}, u32[]{:S(2)}) copy-start(f32[4,1,512,2,1,512]{5,4,3,2,1,0:T(1,128)} %param.5) | copy-start | bytes 25165828
  245.6 3.3 copy-start.2
  294.6 11.8 %collective-permute-start.9 = (bf16[16,4,16,512]{3,2,1,0:T(8,128)(2,1)}, bf16[16,4,16,512]{3,2,1,0:T(8,128)(2,1)S(1)}, u32[]{:S(2)}, u32[]{:S(2)}) collective-permute-start(bf16[16,4,16,512]{3,2,1,0:T(8,128)(2,1)} %slice.39), channel_id=1, source_target_pairs={{0,16},{16,0},{32,48},{48,32},{64,80},{80,64},{96,112},{112,96},{1... | collective-permute-start | bytes 3145736 | tf_op jit(solution)/shard_map/ppermute | solution.py:528
  (4 other events, 3.6 us)
Sparse Core Ops, SparseCore 0:
  14.5 111.6 reduce-scatter.1

commit v11 on v10

--- a/solution.py
+++ b/solution.py
@@ -174,7 +174,7 @@
 def cut_top_kernel(x_ref, c_ref, o_ref):
     for k in range(6):
         o_ref[:, k] = c_ref[k].reshape(16, 16, 256)
-    for i in range(2):
+    for i in range(3):
         for c in range(4):
             high, low = split(x_ref[pl.ds(i * 2048 + c, 256, stride=8), :])
             at = 6 + i * 4 + c // 2 * 2
@@ -187,12 +187,12 @@
     return pl.pallas_call(
         cut_top_kernel,
         grid=(1,),
-        out_shape=jax.ShapeDtypeStruct((16, 14, 16, 256), BF16),
+        out_shape=jax.ShapeDtypeStruct((16, 18, 16, 256), BF16),
         in_specs=[
-            pl.BlockSpec((4096, 128), lambda i: (0, 0)),
+            pl.BlockSpec((6144, 128), lambda i: (0, 0)),
             pl.BlockSpec((6, 256, 256), lambda i: (0, 0, 0)),
         ],
-        out_specs=pl.BlockSpec((16, 14, 16, 256), lambda i: (0, 0, 0, 0)),
+        out_specs=pl.BlockSpec((16, 18, 16, 256), lambda i: (0, 0, 0, 0)),
         cost_estimate=pl.CostEstimate(flops=0, bytes_accessed=5 * MIB, transcendentals=0),
         compiler_params=pltpu.CompilerParams(vmem_limit_bytes=40 * MIB),
     )(front_rows, child)
@@ -213,9 +213,9 @@
 def cut_low(at, front_rows):
     return pl.pallas_call(
         cut_low_kernel,
-        grid=(6,),
-        out_shape=jax.ShapeDtypeStruct((16, 6, 16, 1024), F32),
-        in_specs=[SMEM, pl.BlockSpec((2048, 128), lambda i: (i + 2, 0))],
+        grid=(5,),
+        out_shape=jax.ShapeDtypeStruct((16, 5, 16, 1024), F32),
+        in_specs=[SMEM, pl.BlockSpec((2048, 128), lambda i: (i + 3, 0))],
         out_specs=pl.BlockSpec((16, 1, 16, 1024), lambda i: (0, i, 0, 0)),
         cost_estimate=pl.CostEstimate(flops=0, bytes_accessed=12 * MIB, transcendentals=0),
     )(at, front_rows)
@@ -230,11 +230,15 @@
     return value
 
 
+def whole_piece(c_ref, row, j):
+    at = 6 + row * 4 + j % 2 * 2
+    return c_ref[j // 2, at].astype(F32) + c_ref[j // 2, at + 1].astype(F32)
+
+
 def join_top_kernel(slot_ref, c_ref, o_ref):
     for i in range(2):
         for j in range(4):
-            at = 6 + i * 4 + j % 2 * 2
-            value = c_ref[j // 2, at].astype(F32) + c_ref[j // 2, at + 1].astype(F32)
+            value = whole_piece(c_ref, i, j)
             o_ref[i, :, j * 256 : (j + 1) * 256] = add_pieces(value, slot_ref, c_ref, i, j)
 
 
@@ -242,7 +246,8 @@
     for i in range(6):
         for j in range(4):
             lanes = slice(j * 256, (j + 1) * 256)
-            o_ref[i, :, lanes] = add_pieces(f_ref[i, :, lanes], slot_ref, c_ref, i + 2, j)
+            value = f_ref[i - 1, :, lanes] if i else whole_piece(c_ref, 2, j)
+            o_ref[i, :, lanes] = add_pieces(value, slot_ref, c_ref, i + 2, j)
 
 
 def join_strips(kernel, count, slots, *operands):
@@ -470,7 +475,7 @@
 
     low_cut = cut_low(at, front_rows)
     low_front = lax.psum_scatter(
-        low_cut.reshape(96, 16, 1024), "pcol", scatter_dimension=0, tiled=True
+        low_cut.reshape(80, 16, 1024), "pcol", scatter_dimension=0, tiled=True
     )
     front_top, _ = lax.optimization_barrier((front_rows, low_cut))
     got = lax.all_to_all(cut_top(front_top, child.reshape(48, 256, 256)), "pcol", 0, 0, tiled=True)

time: 332 us -> 331 us (level)
    reduce_scatter x1 -> x0, waiting for transfers between devices: 13.8 us -> none  [local(): lax.psum_scatter(low_cut.reshape(96, 16, 1024), 'pcol', scatter_dimension...]
    all_to_all x1, waiting for transfers between devices: 24.5 us -> 33.3 us  [local(): lax.all_to_all(cut_top(front_top, child.reshape(48, 256, 256)), 'pcol', 0...]
    optimization_barrier x0 -> x1, waiting for transfers between devices: none -> 4.89 us  [local(): child, diag, low_front = lax.optimization_barrier((child, diag, low_front))]
    all_to_all x1, blocking collectives: 19.6 us -> 15.9 us  [local(): lax.all_to_all(jnp.tile(top, (prow // 2, 1, 1)), 'prow', 0, 0, tiled=True)]
where the time goes in v11:
time: 331 us; the launch traced here: 330 us
  waiting for transfers between devices  97.4 us (29%)
  Pallas kernels  94.1 us (28%)
  blocking collectives  44.8 us (14%)
  starting transfers between devices  43 us (13%)
  local copies, waits for them, and re-layouts  31.3 us (9%)
  between operations  13.7 us (4%)
  other arithmetic  5.53 us (2%)
    all_to_all x1, waiting for transfers between devices, local(): dealt = lax.all_to_all(dealt, 'pcol', 0, 0, tiled=True)  43.3 us
    all_to_all x1, waiting for transfers between devices, local(): lax.all_to_all(cut_top(front_top, child.reshape(48, 256, 256)), 'pcol', 0...  33.3 us
    all_to_all x1, blocking collectives, spread(): lax.all_to_all(jnp.broadcast_to(x[None], (count,) + x.shape), axis, 0, 0,...  28.9 us
    unnamed x44, local copies, waits for them, and re-layouts  24.2 us
    pallas_call x1, Pallas kernels, factor_second(): pl.pallas_call(factor_second_kernel, out_shape=[jax.ShapeDtypeStruct((n,...  23.9 us
    pallas_call x1, Pallas kernels, factor_first(): pl.pallas_call(factor_first_kernel, out_shape=[jax.ShapeDtypeStruct((n, n...  22.7 us
    pallas_call x1, Pallas kernels, finish(): pl.pallas_call(finish_kernel, grid_spec=pltpu.PrefetchScalarGridSpec(num_...  17 us
    all_to_all x1, blocking collectives, local(): lax.all_to_all(jnp.tile(top, (prow // 2, 1, 1)), 'prow', 0, 0, tiled=True)  15.9 us
  transfers between devices with their start and end apart: 14, of which 10 were waited for; matrix products, arithmetic and copies ran while one was open for 3% of the time, Pallas kernels for 21%

profile of v11, /device:TPU:1, one launch (start us, length us, event | category | flops | bytes accessed | tf_op | source)
XLA Modules:
  0.0 329.8 jit_solution(12718016441205133706)
XLA Ops:
  7.1 6.8 %shard_map.55 = f32[16,5,16,1024]{3,2,1,0:T(8,128)} custom-call(s32[3]{0:T(128)} %pad_add_fusion.1.at_ref, f32[16384,128]{1,0:T(8,128)} %bitcast.64), custom_call_target="tpu_custom_call" | custom-call | bytes 12582912 | tf_op jit(solution)/shard_map/pallas_call | solution.py:214
  13.9 2.8 copy-done.3
  16.7 3.8 %shard_map.56 = bf16[16,18,16,256]{3,2,1,0:T(8,128)(2,1)} custom-call(f32[16384,128]{1,0:T(8,128)} %bitcast.65, bf16[48,256,256]{2,1,0:T(8,128)(2,1)S(1)} %bitcast.68), custom_call_target="tpu_custom_call" | custom-call | bytes 5242880 | tf_op jit(solution)/shard_map/pallas_call | solution.py:187
  20.5 8.2 %all-to-all-start = ((bf16[16,18,16,256]{3,2,1,0:T(8,128)(2,1)}), bf16[16,18,16,256]{3,2,1,0:T(8,128)(2,1)S(1)}, u32[]{:S(2)}, u32[]{:S(2)}) async-start(bf16[16,18,16,256]{3,2,1,0:T(8,128)(2,1)} %shard_map.56), calls=%async_computation | async-start | bytes 4718592 | tf_op jit(solution)/shard_map/all_to_all | solution.py:481
  31.4 33.3 %all-to-all-done.c_ref = bf16[16,18,16,256]{3,2,1,0:T(8,128)(2,1)S(1)} async-done(((bf16[16,18,16,256]{3,2,1,0:T(8,128)(2,1)}), bf16[16,18,16,256]{3,2,1,0:T(8,128)(2,1)S(1)}, u32[]{:S(2)}, u32[]{:S(2)}) %all-to-all-start) | async-done | bytes 2359328 | tf_op jit(solution)/shard_map/all_to_all | solution.py:481
  64.7 1.5 copy-done.19
  66.2 2.5 shard_map.57.d_ref
  69.6 15.9 %all_to_all.25 = f32[8,16,1024]{2,1,0:T(8,128)S(1)} all-to-all(f32[8,16,1024]{2,1,0:T(8,128)S(1)} %bitcast.72), channel_id=1, replica_groups=mesh['prow'=8,'pcol'=16] {'prow'}, dimensions={0} | all-to-all | bytes 1048576 | tf_op jit(solution)/shard_map/all_to_all | solution.py:501
  85.7 28.9 %all_to_all.26.mine_ref = f32[16,16,1536]{2,1,0:T(8,128)S(1)} all-to-all(f32[16,16,1536]{2,1,0:T(8,128)S(1)} %broadcast_in_dim.111), channel_id=1, replica_groups=mesh['prow'=8,'pcol'=16] {'pcol'}, dimensions={0} | all-to-all | bytes 3145728 | tf_op jit(solution)/shard_map/all_to_all | solution.py:458
  114.6 2.2 collective-permute-start
  116.7 3.0 collective-permute-done.other_ref
  120.9 4.9 %reduce-scatter.4.cloned.1.call-done.f_ref = f32[5,16,1024]{2,1,0:T(8,128)} async-done(((f32[80,16,1024]{2,1,0:T(8,128)}), f32[5,16,1024]{2,1,0:T(8,128)}) %reduce-scatter.4.cloned.1.call-update) | async-done | bytes 327696 | tf_op jit(solution)/shard_map/optimization_barrier | solution.py:504
  125.8 4.9 %all-to-all-start.3 = ((bf16[16,3,256,256]{3,2,1,0:T(8,128)(2,1)}), bf16[16,3,256,256]{3,2,1,0:T(8,128)(2,1)}, u32[]{:S(2)}, u32[]{:S(2)}) async-start(bf16[16,3,256,256]{3,2,1,0:T(8,128)(2,1)} %bitcast.67), calls=%async_computation.3 | async-start | bytes 12582912 | tf_op jit(solution)/shard_map/all_to_all | solution.py:505
  132.2 2.7 shard_map.58.r_ref
  136.3 22.7 %shard_map.59 = (f32[512,512]{1,0:T(8,128)S(1)}, f32[512,512]{1,0:T(8,128)S(1)}) custom-call(s32[3]{0:T(128)S(1)} %copy-done.15, f32[16,16,1536]{2,1,0:T(8,128)S(1)} %all_to_all.26.mine_ref, f32[16,16,1536]{2,1,0:T(8,128)S(1)} %copy-done.17), custom_call_target="tpu_custom_call" | custom-call | flops 20000000000 | bytes 3145728 | tf_op jit(solution)/shard_map/pallas_call | solution.py:148
  161.1 2.7 shard_map.60.p_ref.p0_ref
  164.7 2.1 collective-permute-start.1
  169.0 2.5 collective-permute-start.3
  175.3 23.9 %shard_map.61 = (bf16[512,512]{1,0:T(8,128)(2,1)S(1)}, f32[512,512]{1,0:T(8,128)S(1)}, f32[512,512]{1,0:T(8,128)S(1)}) custom-call(s32[3]{0:T(128)S(1)} %copy-done.15, s32[4]{0:T(128)S(1)} %reshape.309.mask_ref, f32[16,16,1536]{2,1,0:T(8,128)S(1)} %all_to_all.26.mine_ref, f32[16,16,1536]{2,1,0:T(8,128)S(1)} %copy-done.18, f32[512,512]{1,0:T(8,128)S(1)} %copy-done.6), custom_call_target="tpu_custom_call" | custom-call | flops 20000000000 | bytes 3145728 | tf_op jit(solution)/shard_map/pallas_call | solution.py:161
  202.0 3.1 shard_map.62.p1_ref
  209.2 1.9 collective-permute-start.6
  211.1 6.1 %collective-permute-done.8.refs_7_ = bf16[2,4,16,512]{3,2,1,0:T(8,128)(2,1)S(1)} collective-permute-done((bf16[2,4,16,512]{3,2,1,0:T(8,128)(2,1)S(1)}, bf16[2,4,16,512]{3,2,1,0:T(8,128)(2,1)S(1)}, u32[]{:S(2)}, u32[]{:S(2)}) %collective-permute-start.8) | collective-permute-done | bytes 131104 | tf_op jit(solution)/shard_map/ppermute | solution.py:514
  219.3 2.3 copy-done.4
  221.7 4.0 %all-to-all-done.3 = bf16[16,3,256,256]{3,2,1,0:T(8,128)(2,1)} async-done(((bf16[16,3,256,256]{3,2,1,0:T(8,128)(2,1)}), bf16[16,3,256,256]{3,2,1,0:T(8,128)(2,1)}, u32[]{:S(2)}, u32[]{:S(2)}) %all-to-all-start.3) | async-done | bytes 6291488 | tf_op jit(solution)/shard_map/all_to_all | solution.py:505
  225.6 7.4 %all-to-all-start.4 = ((bf16[16,20,16,512]{3,2,1,0:T(8,128)(2,1)}), bf16[16,20,16,512]{3,2,1,0:T(8,128)(2,1)}, u32[]{:S(2)}, u32[]{:S(2)}) async-start(bf16[16,20,16,512]{3,2,1,0:T(8,128)(2,1)} %copy-done.4), calls=%async_computation.4 | async-start | bytes 10485760 | tf_op jit(solution)/shard_map/all_to_all | solution.py:528
  234.1 3.4 %copy-done.1 = f32[4,1,512,2,1,512]{5,4,3,2,1,0:T(1,128)S(1)} copy-done((f32[4,1,512,2,1,512]{5,4,3,2,1,0:T(1,128)S(1)}, f32[4,1,512,2,1,512]{5,4,3,2,1,0:T(1,128)}, u32[]{:S(2)}) %copy-start.1) | copy-done | bytes 8388632
  237.5 7.8 %shard_map.64.f_ref = f32[16384,128]{1,0:T(8,128)S(1)} custom-call(s32[64]{0:T(128)S(1)} %broadcast_add_fusion.2.slot_ref, f32[16384,128]{1,0:T(8,128)S(1)} %bitcast.66, bf16[48,256,256]{2,1,0:T(8,128)(2,1)} %bitcast.24.refs_0_.refs_1_.refs_2_.refs_3_.refs_4_.refs_5_.refs_6_.refs_7_, ...), custom_call_target="tpu_custom_call" | custom-call | bytes 25165824 | tf_op jit(solution)/shard_map/pallas_call | solution.py:346
  245.4 3.3 copy-done.2
  248.6 43.3 %all-to-all-done.4.row0_ref.row1_ref.mine_ref = bf16[16,20,16,512]{3,2,1,0:T(8,128)(2,1)} async-done(((bf16[16,20,16,512]{3,2,1,0:T(8,128)(2,1)}), bf16[16,20,16,512]{3,2,1,0:T(8,128)(2,1)}, u32[]{:S(2)}, u32[]{:S(2)}) %all-to-all-start.4) | async-done | bytes 5242912 | tf_op jit(solution)/shard_map/all_to_all | solution.py:528
  291.9 2.3 slice.39
  294.2 9.3 %collective-permute-start.9 = (bf16[16,4,16,512]{3,2,1,0:T(8,128)(2,1)}, bf16[16,4,16,512]{3,2,1,0:T(8,128)(2,1)S(1)}, u32[]{:S(2)}, u32[]{:S(2)}) collective-permute-start(bf16[16,4,16,512]{3,2,1,0:T(8,128)(2,1)} %slice.39), channel_id=1, source_target_pairs={{0,16},{16,0},{32,48},{48,32},{64,80},{80,64},{96,112},{112,96},{1... | collective-permute-start | bytes 3145736 | tf_op jit(solution)/shard_map/ppermute | solution.py:533
  306.0 17.0 %shard_map.65 = f32[16384,128]{1,0:T(8,128)} custom-call(s32[50]{0:T(128)S(1)} %pad_add_fusion.flag_ref, f32[16384,128]{1,0:T(8,128)} %copy-done.2, bf16[16,20,16,512]{3,2,1,0:T(8,128)(2,1)} %all-to-all-done.4.row0_ref.row1_ref.mine_ref, bf16[16,20,16,512]{3,2,1,0:T(8,128)(2,1)} %all-to-all-done.4.row0_ref.row1_ref.mine_ref, ...), custom_call_target="tpu_custom_call" | custom-call | flops 5000000000 | bytes 25165824 | tf_op jit(solution)/shard_map/pallas_call | solution.py:422
  (128 shorter events, 29.7 us)
Async XLA Ops:
  6.5 23.8 %copy-start = (s32[8,16,16,3]{2,1,3,0:T(8,128)S(1)}, s32[8,16,16,3]{2,1,3,0:T(8,128)}, u32[]{:S(2)}) copy-start(s32[8,16,16,3]{2,1,3,0:T(8,128)} %param.8) | copy-start | bytes 73732
  6.5 119.3 %reduce-scatter.4.cloned.1.call-start = ((), (), s32[]{:S(2)}) async-start(), calls=%async_computation.6 | async-start | bytes 5570560
  13.9 2.8 copy-start.3
  16.7 12.2 %copy-start.21 = (s32[2,60]{1,0:T(2,128)S(1)}, s32[2,60]{1,0:T(2,128)}, u32[]{:S(2)}) copy-start(s32[2,60]{1,0:T(2,128)} %param.7) | copy-start | bytes 1444
  20.5 44.2 %all-to-all-start = ((bf16[16,18,16,256]{3,2,1,0:T(8,128)(2,1)}), bf16[16,18,16,256]{3,2,1,0:T(8,128)(2,1)S(1)}, u32[]{:S(2)}, u32[]{:S(2)}) async-start(bf16[16,18,16,256]{3,2,1,0:T(8,128)(2,1)} %shard_map.56), calls=%async_computation | async-start | bytes 4718592 | tf_op jit(solution)/shard_map/all_to_all | solution.py:481
  64.7 1.5 copy-start.19
  114.6 5.2 %collective-permute-start = (f32[16,16,1536]{2,1,0:T(8,128)S(1)}, f32[16,16,1536]{2,1,0:T(8,128)S(1)}, u32[]{:S(2)}, u32[]{:S(2)}) collective-permute-start(f32[16,16,1536]{2,1,0:T(8,128)S(1)} %all_to_all.26.mine_ref), channel_id=1, source_target_pairs={{0,16},{16,0},{32,48},{48,32},{64,80},{80,64},{96,112},{112,96},{1... | collective-permute-start | bytes 4718600 | tf_op jit(solution)/shard_map/ppermute | solution.py:503
  119.8 1.1 copy-start.16
  125.8 5.0 %copy-start.20 = (s32[64,64]{1,0:T(8,128)S(1)}, s32[64,64]{1,0:T(8,128)}, u32[]{:S(2)}) copy-start(s32[64,64]{1,0:T(8,128)} %param.9) | copy-start | bytes 49156
  125.8 9.1 %copy-start.15 = (s32[3]{0:T(128)S(1)}, s32[3]{0:T(128)}, u32[]{:S(2)}) copy-start(s32[3]{0:T(128)} %pad_add_fusion.1.at_ref) | copy-start | bytes 40
  125.8 99.8 %all-to-all-start.3 = ((bf16[16,3,256,256]{3,2,1,0:T(8,128)(2,1)}), bf16[16,3,256,256]{3,2,1,0:T(8,128)(2,1)}, u32[]{:S(2)}, u32[]{:S(2)}) async-start(bf16[16,3,256,256]{3,2,1,0:T(8,128)(2,1)} %bitcast.67), calls=%async_computation.3 | async-start | bytes 12582912 | tf_op jit(solution)/shard_map/all_to_all | solution.py:505
  134.9 1.4 copy-start.17
  160.0 1.1 copy-start.11
  164.7 3.0 collective-permute-start.1
  167.7 49.8 %copy-start.9 = (bf16[8,16,512]{2,1,0:T(8,128)(2,1)S(1)}, bf16[8,16,512]{2,1,0:T(8,128)(2,1)}, u32[]{:S(2)}) copy-start(bf16[8,16,512]{2,1,0:T(8,128)(2,1)} %shard_map.60.p_ref.p0_ref) | copy-start | bytes 393220
  167.7 34.3 %collective-permute-start.4 = (bf16[2,4,16,512]{3,2,1,0:T(8,128)(2,1)S(1)}, bf16[2,4,16,512]{3,2,1,0:T(8,128)(2,1)S(1)}, u32[]{:S(2)}, u32[]{:S(2)}) collective-permute-start(bf16[2,4,16,512]{3,2,1,0:T(8,128)(2,1)S(1)} %maximum_select_fusion.refs_0_), channel_id=1, source_target_pairs={{96,0},{112,16},{0,32},{16,48},{32,64},{48,80},{64,96},{80,112},{9... | collective-permute-start | bytes 393224 | tf_op jit(solution)/shard_map/ppermute | solution.py:514
  169.0 33.0 %collective-permute-start.3 = (bf16[2,4,16,512]{3,2,1,0:T(8,128)(2,1)S(1)}, bf16[2,4,16,512]{3,2,1,0:T(8,128)(2,1)S(1)}, u32[]{:S(2)}, u32[]{:S(2)}) collective-permute-start(bf16[2,4,16,512]{3,2,1,0:T(8,128)(2,1)S(1)} %maximum_select_fusion.refs_0_), channel_id=1, source_target_pairs={{64,0},{80,16},{96,32},{112,48},{0,64},{16,80},{32,96},{48,112},{6... | collective-permute-start | bytes 393224 | tf_op jit(solution)/shard_map/ppermute | solution.py:514
  171.5 30.5 %collective-permute-start.2 = (bf16[2,4,16,512]{3,2,1,0:T(8,128)(2,1)S(1)}, bf16[2,4,16,512]{3,2,1,0:T(8,128)(2,1)S(1)}, u32[]{:S(2)}, u32[]{:S(2)}) collective-permute-start(bf16[2,4,16,512]{3,2,1,0:T(8,128)(2,1)S(1)} %maximum_select_fusion.refs_0_), channel_id=1, source_target_pairs={{32,0},{48,16},{64,32},{80,48},{96,64},{112,80},{0,96},{16,112},{3... | collective-permute-start | bytes 393224 | tf_op jit(solution)/shard_map/ppermute | solution.py:514
  172.6 1.2 copy-start.6
  173.9 1.4 copy-start.18
  200.2 1.0 copy-start.13
  206.0 2.2 collective-permute-start.5
  208.2 9.0 %collective-permute-start.8 = (bf16[2,4,16,512]{3,2,1,0:T(8,128)(2,1)S(1)}, bf16[2,4,16,512]{3,2,1,0:T(8,128)(2,1)S(1)}, u32[]{:S(2)}, u32[]{:S(2)}) collective-permute-start(bf16[2,4,16,512]{3,2,1,0:T(8,128)(2,1)S(1)} %maximum_select_fusion.1.refs_4_), channel_id=1, source_target_pairs={{96,0},{112,16},{0,32},{16,48},{32,64},{48,80},{64,96},{80,112},{9... | collective-permute-start | bytes 393224 | tf_op jit(solution)/shard_map/ppermute | solution.py:514
  208.6 8.6 %collective-permute-start.7 = (bf16[2,4,16,512]{3,2,1,0:T(8,128)(2,1)S(1)}, bf16[2,4,16,512]{3,2,1,0:T(8,128)(2,1)S(1)}, u32[]{:S(2)}, u32[]{:S(2)}) collective-permute-start(bf16[2,4,16,512]{3,2,1,0:T(8,128)(2,1)S(1)} %maximum_select_fusion.1.refs_4_), channel_id=1, source_target_pairs={{64,0},{80,16},{96,32},{112,48},{0,64},{16,80},{32,96},{48,112},{6... | collective-permute-start | bytes 393224 | tf_op jit(solution)/shard_map/ppermute | solution.py:514
  209.2 8.3 %collective-permute-start.6 = (bf16[2,4,16,512]{3,2,1,0:T(8,128)(2,1)S(1)}, bf16[2,4,16,512]{3,2,1,0:T(8,128)(2,1)S(1)}, u32[]{:S(2)}, u32[]{:S(2)}) collective-permute-start(bf16[2,4,16,512]{3,2,1,0:T(8,128)(2,1)S(1)} %maximum_select_fusion.1.refs_4_), channel_id=1, source_target_pairs={{32,0},{48,16},{64,32},{80,48},{96,64},{112,80},{0,96},{16,112},{3... | collective-permute-start | bytes 393224 | tf_op jit(solution)/shard_map/ppermute | solution.py:514
  219.3 2.4 copy-start.4
  225.6 8.0 %copy-start.12 = (f32[512,512]{1,0:T(8,128)S(1)}, f32[512,512]{1,0:T(8,128)}, u32[]{:S(2)}) copy-start(f32[512,512]{1,0:T(8,128)} %copy-done.11) | copy-start | bytes 3145732
  225.6 8.2 %copy-start.7 = (f32[512,512]{1,0:T(8,128)S(1)}, f32[512,512]{1,0:T(8,128)}, u32[]{:S(2)}) copy-start(f32[512,512]{1,0:T(8,128)} %copy-done.5) | copy-start | bytes 3145732
  225.6 66.3 %all-to-all-start.4 = ((bf16[16,20,16,512]{3,2,1,0:T(8,128)(2,1)}), bf16[16,20,16,512]{3,2,1,0:T(8,128)(2,1)}, u32[]{:S(2)}, u32[]{:S(2)}) async-start(bf16[16,20,16,512]{3,2,1,0:T(8,128)(2,1)} %copy-done.4), calls=%async_computation.4 | async-start | bytes 10485760 | tf_op jit(solution)/shard_map/all_to_all | solution.py:528
  234.1 3.4 %copy-start.1 = (f32[4,1,512,2,1,512]{5,4,3,2,1,0:T(1,128)S(1)}, f32[4,1,512,2,1,512]{5,4,3,2,1,0:T(1,128)}, u32[]{:S(2)}) copy-start(f32[4,1,512,2,1,512]{5,4,3,2,1,0:T(1,128)} %param.5) | copy-start | bytes 25165828
  245.4 3.3 copy-start.2
  294.2 11.8 %collective-permute-start.9 = (bf16[16,4,16,512]{3,2,1,0:T(8,128)(2,1)}, bf16[16,4,16,512]{3,2,1,0:T(8,128)(2,1)S(1)}, u32[]{:S(2)}, u32[]{:S(2)}) collective-permute-start(bf16[16,4,16,512]{3,2,1,0:T(8,128)(2,1)} %slice.39), channel_id=1, source_target_pairs={{0,16},{16,0},{32,48},{48,32},{64,80},{80,64},{96,112},{112,96},{1... | collective-permute-start | bytes 3145736 | tf_op jit(solution)/shard_map/ppermute | solution.py:533
  (4 other events, 3.7 us)
Sparse Core Ops, SparseCore 0:
  14.0 111.7 reduce-scatter.3

commit v12 on v11

--- a/solution.py
+++ b/solution.py
@@ -325,8 +325,13 @@
 
 
 def extend_kernel(slot_ref, f_ref, *refs):
-    child, o_ref = refs[:8], refs[8]
+    child, (w_ref, o_ref, wh_ref, wl_ref) = refs[:8], refs[8:]
     i = pl.program_id(0)
+
+    @pl.when(i == 0)
+    def _():
+        wh_ref[...], wl_ref[...] = split(w_ref[...])
+
     for j in range(4):
         live = [slot_ref[(i * 4 + j) * 2 + ch] >= 0 for ch in range(2)]
         pieces = [child[j * 2 + ch] for ch in range(2)]
@@ -339,25 +344,29 @@
             o_ref[rows, :] = value
 
 
-def extend(slots, front_rows, arrived):
+def extend(slots, front_rows, arrived, W):
     def child_spec(k):
         return pl.BlockSpec((1, 256, 256), lambda i, s: (jnp.maximum(s[i * 8 + k], 0), 0, 0))
+
+    whole = pl.BlockSpec((512, 512), lambda i, s: (0, 0))
 
     return pl.pallas_call(
         extend_kernel,
         grid_spec=pltpu.PrefetchScalarGridSpec(
             num_scalar_prefetch=1,
             grid=(8,),
-            in_specs=[pl.BlockSpec((2048, 128), lambda i, s: (i, 0))] + [child_spec(k) for k in range(8)],
-            out_specs=pl.BlockSpec((2048, 128), lambda i, s: (i, 0)),
+            in_specs=[pl.BlockSpec((2048, 128), lambda i, s: (i, 0))] + [child_spec(k) for k in range(8)]
+            + [whole],
+            out_specs=[pl.BlockSpec((2048, 128), lambda i, s: (i, 0)), whole, whole],
         ),
-        out_shape=jax.ShapeDtypeStruct(front_rows.shape, F32),
+        out_shape=[jax.ShapeDtypeStruct(front_rows.shape, F32)]
+        + [jax.ShapeDtypeStruct((512, 512), BF16)] * 2,
         cost_estimate=pl.CostEstimate(flops=0, bytes_accessed=24 * MIB, transcendentals=0),
         compiler_params=pltpu.CompilerParams(vmem_limit_bytes=24 * MIB),
-    )(slots, front_rows, *([arrived] * 8))
-
-
-def finish_kernel(flag_ref, f_ref, row0_ref, row1_ref, mine_ref, other_ref, l_ref, w_ref, o_ref, cols_ref, wh_ref, wl_ref):
+    )(slots, front_rows, *([arrived] * 8), W)
+
+
+def finish_kernel(flag_ref, f_ref, row0_ref, row1_ref, mine_ref, other_ref, l_ref, wh_ref, wl_ref, o_ref, cols_ref):
     i = pl.program_id(0)
 
     @pl.when(i == 0)
@@ -368,10 +377,6 @@
                 for lc in range(2):
                     strips = ref[:, panel * 2 + lc].reshape(256, 512)
                     cols_ref[lc * 2 + sub, :, panel * 512 : (panel + 1) * 512] = strips
-
-    @pl.when((i == 0) & (flag_ref[49] > 0))
-    def _():
-        wh_ref[...], wl_ref[...] = split(w_ref[...])
 
     rows = jnp.concatenate([ref[:, 0].reshape(256, 512) for ref in (row0_ref, row1_ref)], axis=1)
     for lc in range(2):
@@ -415,7 +420,7 @@
                 o_ref[pl.ds(lc * 4 + c, 256, stride=8), :] = jnp.zeros((256, 128), F32)
 
 
-def finish(flags, extended, dealt, other, L, W):
+def finish(flags, extended, dealt, other, L, high, low):
     def whole(shape, *at):
         return pl.BlockSpec(shape, lambda i, f: at)
 
@@ -428,14 +433,14 @@
             + [pl.BlockSpec((16, 1, 16, 512), lambda i, f: (0, i, 0, 0))]
             + [pl.BlockSpec((16, 1, 16, 512), lambda i, f: (0, i + 8, 0, 0))]
             + [whole((16, 4, 16, 512), 0, 4, 0, 0), whole((16, 4, 16, 512), 0, 0, 0, 0)]
-            + [whole((512, 512), 0, 0)] * 2,
+            + [whole((512, 512), 0, 0)] * 3,
             out_specs=pl.BlockSpec((2048, 128), lambda i, f: (i, 0)),
-            scratch_shapes=[pltpu.VMEM((4, 256, 1024), BF16)] + [pltpu.VMEM((512, 512), BF16)] * 2,
+            scratch_shapes=[pltpu.VMEM((4, 256, 1024), BF16)],
         ),
         out_shape=jax.ShapeDtypeStruct(extended.shape, F32),
         cost_estimate=pl.CostEstimate(flops=5_000_000_000, bytes_accessed=24 * MIB, transcendentals=0),
         compiler_params=pltpu.CompilerParams(vmem_limit_bytes=48 * MIB),
-    )(flags, extended, dealt, dealt, dealt, other, L, W)
+    )(flags, extended, dealt, dealt, dealt, other, L, high, low)
 
 
 def slot_of_targets(codes, row_map, rows, cols):
@@ -526,12 +531,12 @@
     dealt = deal(at, P0, P1, cols0, cols1)
     dealt, arrived = lax.optimization_barrier((dealt, arrived))
     dealt = lax.all_to_all(dealt, "pcol", 0, 0, tiled=True)
-    extended = extend(slots, front_rows, arrived)
     L = jnp.where(q == 0, L0, L1)
-    W = jnp.where(q == 0, W0, W1)
-    dealt, extended, L, W = lax.optimization_barrier((dealt, extended, L, W))
+    extended = extend(slots, front_rows, arrived, jnp.where(q == 0, W0, W1))
+    dealt, extended, L = lax.optimization_barrier((dealt, extended, L))
+    extended, high, low_part = extended
     other = lax.ppermute(dealt[:, 16:], "prow", swap)
-    out = finish(flags, extended, dealt, other, L, W)
+    out = finish(flags, extended, dealt, other, L, high, low_part)
     return out.reshape(front.shape)
 
 

time: 331 us -> 334 us (level)
  no operation moved by 1% of the time
where the time goes in v12:
time: 334 us; the launch traced here: 333 us
  waiting for transfers between devices  99.3 us (30%)
  Pallas kernels  94 us (28%)
  blocking collectives  44.7 us (13%)
  starting transfers between devices  42.9 us (13%)
  local copies, waits for them, and re-layouts  31.3 us (9%)
  between operations  13.7 us (4%)
  other arithmetic  6.77 us (2%)
    all_to_all x1, waiting for transfers between devices, local(): dealt = lax.all_to_all(dealt, 'pcol', 0, 0, tiled=True)  42 us
    all_to_all x1, waiting for transfers between devices, local(): lax.all_to_all(cut_top(front_top, child.reshape(48, 256, 256)), 'pcol', 0...  33.3 us
    all_to_all x1, blocking collectives, spread(): lax.all_to_all(jnp.broadcast_to(x[None], (count,) + x.shape), axis, 0, 0,...  28.9 us
    unnamed x44, local copies, waits for them, and re-layouts  24.2 us
    pallas_call x1, Pallas kernels, factor_second(): pl.pallas_call(factor_second_kernel, out_shape=[jax.ShapeDtypeStruct((n,...  23.9 us
    pallas_call x1, Pallas kernels, factor_first(): pl.pallas_call(factor_first_kernel, out_shape=[jax.ShapeDtypeStruct((n, n...  22.7 us
    pallas_call x1, Pallas kernels, finish(): pl.pallas_call(finish_kernel, grid_spec=pltpu.PrefetchScalarGridSpec(num_...  16.8 us
    all_to_all x1, blocking collectives, local(): lax.all_to_all(jnp.tile(top, (prow // 2, 1, 1)), 'prow', 0, 0, tiled=True)  15.8 us
  transfers between devices with their start and end apart: 14, of which 10 were waited for; matrix products, arithmetic and copies ran while one was open for 3% of the time, Pallas kernels for 21%

profile of v12, /device:TPU:1, one launch (start us, length us, event | category | flops | bytes accessed | tf_op | source)
XLA Modules:
  0.0 332.6 jit_solution(14622674648617372971)
XLA Ops:
  7.1 6.8 %shard_map.55 = f32[16,5,16,1024]{3,2,1,0:T(8,128)} custom-call(s32[3]{0:T(128)} %pad_add_fusion.1.at_ref, f32[16384,128]{1,0:T(8,128)} %bitcast.64), custom_call_target="tpu_custom_call" | custom-call | bytes 12582912 | tf_op jit(solution)/shard_map/pallas_call | solution.py:214
  13.9 2.8 copy-done.2
  16.7 3.8 %shard_map.56 = bf16[16,18,16,256]{3,2,1,0:T(8,128)(2,1)} custom-call(f32[16384,128]{1,0:T(8,128)} %bitcast.65, bf16[48,256,256]{2,1,0:T(8,128)(2,1)S(1)} %bitcast.68), custom_call_target="tpu_custom_call" | custom-call | bytes 5242880 | tf_op jit(solution)/shard_map/pallas_call | solution.py:187
  20.5 8.2 %all-to-all-start = ((bf16[16,18,16,256]{3,2,1,0:T(8,128)(2,1)}), bf16[16,18,16,256]{3,2,1,0:T(8,128)(2,1)S(1)}, u32[]{:S(2)}, u32[]{:S(2)}) async-start(bf16[16,18,16,256]{3,2,1,0:T(8,128)(2,1)} %shard_map.56), calls=%async_computation | async-start | bytes 4718592 | tf_op jit(solution)/shard_map/all_to_all | solution.py:486
  31.4 33.3 %all-to-all-done.c_ref = bf16[16,18,16,256]{3,2,1,0:T(8,128)(2,1)S(1)} async-done(((bf16[16,18,16,256]{3,2,1,0:T(8,128)(2,1)}), bf16[16,18,16,256]{3,2,1,0:T(8,128)(2,1)S(1)}, u32[]{:S(2)}, u32[]{:S(2)}) %all-to-all-start) | async-done | bytes 2359328 | tf_op jit(solution)/shard_map/all_to_all | solution.py:486
  64.7 1.5 copy-done.19
  66.2 2.5 shard_map.57.d_ref
  69.6 15.8 %all_to_all.25 = f32[8,16,1024]{2,1,0:T(8,128)S(1)} all-to-all(f32[8,16,1024]{2,1,0:T(8,128)S(1)} %bitcast.72), channel_id=1, replica_groups=mesh['prow'=8,'pcol'=16] {'prow'}, dimensions={0} | all-to-all | bytes 1048576 | tf_op jit(solution)/shard_map/all_to_all | solution.py:506
  85.6 28.9 %all_to_all.26.mine_ref = f32[16,16,1536]{2,1,0:T(8,128)S(1)} all-to-all(f32[16,16,1536]{2,1,0:T(8,128)S(1)} %broadcast_in_dim.111), channel_id=1, replica_groups=mesh['prow'=8,'pcol'=16] {'pcol'}, dimensions={0} | all-to-all | bytes 3145728 | tf_op jit(solution)/shard_map/all_to_all | solution.py:463
  114.5 2.2 collective-permute-start
  116.6 3.0 collective-permute-done.other_ref
  120.8 8.1 %reduce-scatter.4.cloned.1.call-done.f_ref = f32[5,16,1024]{2,1,0:T(8,128)} async-done(((f32[80,16,1024]{2,1,0:T(8,128)}), f32[5,16,1024]{2,1,0:T(8,128)}) %reduce-scatter.4.cloned.1.call-update) | async-done | bytes 327696 | tf_op jit(solution)/shard_map/optimization_barrier | solution.py:509
  128.9 4.8 %all-to-all-start.3 = ((bf16[16,3,256,256]{3,2,1,0:T(8,128)(2,1)}), bf16[16,3,256,256]{3,2,1,0:T(8,128)(2,1)}, u32[]{:S(2)}, u32[]{:S(2)}) async-start(bf16[16,3,256,256]{3,2,1,0:T(8,128)(2,1)} %bitcast.67), calls=%async_computation.3 | async-start | bytes 12582912 | tf_op jit(solution)/shard_map/all_to_all | solution.py:510
  135.2 2.7 shard_map.58.r_ref
  139.3 22.7 %shard_map.59 = (f32[512,512]{1,0:T(8,128)S(1)}, f32[512,512]{1,0:T(8,128)S(1)}) custom-call(s32[3]{0:T(128)S(1)} %copy-done.15, f32[16,16,1536]{2,1,0:T(8,128)S(1)} %all_to_all.26.mine_ref, f32[16,16,1536]{2,1,0:T(8,128)S(1)} %copy-done.17), custom_call_target="tpu_custom_call" | custom-call | flops 20000000000 | bytes 3145728 | tf_op jit(solution)/shard_map/pallas_call | solution.py:148
  164.1 2.7 shard_map.60.p_ref.p0_ref
  167.7 2.1 collective-permute-start.1
  172.0 2.5 collective-permute-start.3
  178.2 23.9 %shard_map.61 = (bf16[512,512]{1,0:T(8,128)(2,1)S(1)}, f32[512,512]{1,0:T(8,128)S(1)}, f32[512,512]{1,0:T(8,128)S(1)}) custom-call(s32[3]{0:T(128)S(1)} %copy-done.15, s32[4]{0:T(128)S(1)} %reshape.309.mask_ref, f32[16,16,1536]{2,1,0:T(8,128)S(1)} %all_to_all.26.mine_ref, f32[16,16,1536]{2,1,0:T(8,128)S(1)} %copy-done.18, f32[512,512]{1,0:T(8,128)S(1)} %copy-done.6), custom_call_target="tpu_custom_call" | custom-call | flops 20000000000 | bytes 3145728 | tf_op jit(solution)/shard_map/pallas_call | solution.py:161
  205.0 3.1 shard_map.62.p1_ref
  212.2 1.9 collective-permute-start.6
  214.0 6.2 %collective-permute-done.8.refs_7_ = bf16[2,4,16,512]{3,2,1,0:T(8,128)(2,1)S(1)} collective-permute-done((bf16[2,4,16,512]{3,2,1,0:T(8,128)(2,1)S(1)}, bf16[2,4,16,512]{3,2,1,0:T(8,128)(2,1)S(1)}, u32[]{:S(2)}, u32[]{:S(2)}) %collective-permute-start.8) | collective-permute-done | bytes 131104 | tf_op jit(solution)/shard_map/ppermute | solution.py:519
  222.3 2.3 copy-done.3
  224.6 4.0 %all-to-all-done.3 = bf16[16,3,256,256]{3,2,1,0:T(8,128)(2,1)} async-done(((bf16[16,3,256,256]{3,2,1,0:T(8,128)(2,1)}), bf16[16,3,256,256]{3,2,1,0:T(8,128)(2,1)}, u32[]{:S(2)}, u32[]{:S(2)}) %all-to-all-start.3) | async-done | bytes 6291488 | tf_op jit(solution)/shard_map/all_to_all | solution.py:510
  228.6 7.4 %all-to-all-start.4 = ((bf16[16,20,16,512]{3,2,1,0:T(8,128)(2,1)}), bf16[16,20,16,512]{3,2,1,0:T(8,128)(2,1)}, u32[]{:S(2)}, u32[]{:S(2)}) async-start(bf16[16,20,16,512]{3,2,1,0:T(8,128)(2,1)} %copy-done.3), calls=%async_computation.4 | async-start | bytes 10485760 | tf_op jit(solution)/shard_map/all_to_all | solution.py:533
  238.3 3.4 %copy-done.1 = f32[4,1,512,2,1,512]{5,4,3,2,1,0:T(1,128)S(1)} copy-done((f32[4,1,512,2,1,512]{5,4,3,2,1,0:T(1,128)S(1)}, f32[4,1,512,2,1,512]{5,4,3,2,1,0:T(1,128)}, u32[]{:S(2)}) %copy-start.1) | copy-done | bytes 8388632
  241.7 7.9 %shard_map.64 = (f32[16384,128]{1,0:T(8,128)S(1)}, bf16[512,512]{1,0:T(8,128)(2,1)S(1)}, bf16[512,512]{1,0:T(8,128)(2,1)S(1)}) custom-call(s32[64]{0:T(128)S(1)} %broadcast_add_fusion.2.slot_ref, f32[16384,128]{1,0:T(8,128)S(1)} %bitcast.66, bf16[48,256,256]{2,1,0:T(8,128)(2,1)} %bitcast.24.refs_0_.refs_1_.refs_2_.refs_3_.refs_4_.refs_5_.refs_6_.refs_7_, ...), custom_call_target="tpu_custom_call" | custom-call | bytes 25165824 | tf_op jit(solution)/shard_map/pallas_call | solution.py:353
  249.6 3.3 copy-done.4
  252.9 42.0 %all-to-all-done.4.row0_ref.row1_ref.mine_ref = bf16[16,20,16,512]{3,2,1,0:T(8,128)(2,1)} async-done(((bf16[16,20,16,512]{3,2,1,0:T(8,128)(2,1)}), bf16[16,20,16,512]{3,2,1,0:T(8,128)(2,1)}, u32[]{:S(2)}, u32[]{:S(2)}) %all-to-all-start.4) | async-done | bytes 5242912 | tf_op jit(solution)/shard_map/all_to_all | solution.py:533
  294.9 2.3 slice.39
  297.2 9.3 %collective-permute-start.9 = (bf16[16,4,16,512]{3,2,1,0:T(8,128)(2,1)}, bf16[16,4,16,512]{3,2,1,0:T(8,128)(2,1)S(1)}, u32[]{:S(2)}, u32[]{:S(2)}) collective-permute-start(bf16[16,4,16,512]{3,2,1,0:T(8,128)(2,1)} %slice.39), channel_id=1, source_target_pairs={{0,16},{16,0},{32,48},{48,32},{64,80},{80,64},{96,112},{112,96},{1... | collective-permute-start | bytes 3145736 | tf_op jit(solution)/shard_map/ppermute | solution.py:538
  309.0 16.8 %shard_map.65 = f32[16384,128]{1,0:T(8,128)} custom-call(s32[50]{0:T(128)S(1)} %pad_add_fusion.flag_ref, f32[16384,128]{1,0:T(8,128)} %copy-done.4, bf16[16,20,16,512]{3,2,1,0:T(8,128)(2,1)} %all-to-all-done.4.row0_ref.row1_ref.mine_ref, bf16[16,20,16,512]{3,2,1,0:T(8,128)(2,1)} %all-to-all-done.4.row0_ref.row1_ref.mine_ref, ...), custom_call_target="tpu_custom_call" | custom-call | flops 5000000000 | bytes 25165824 | tf_op jit(solution)/shard_map/pallas_call | solution.py:427
  (128 shorter events, 30.9 us)
Async XLA Ops:
  6.5 23.8 %copy-start = (s32[8,16,16,3]{2,1,3,0:T(8,128)S(1)}, s32[8,16,16,3]{2,1,3,0:T(8,128)}, u32[]{:S(2)}) copy-start(s32[8,16,16,3]{2,1,3,0:T(8,128)} %param.8) | copy-start | bytes 73732
  6.5 122.3 %reduce-scatter.4.cloned.1.call-start = ((), (), s32[]{:S(2)}) async-start(), calls=%async_computation.6 | async-start | bytes 5570560
  13.9 2.8 copy-start.2
  16.7 12.2 %copy-start.21 = (s32[2,60]{1,0:T(2,128)S(1)}, s32[2,60]{1,0:T(2,128)}, u32[]{:S(2)}) copy-start(s32[2,60]{1,0:T(2,128)} %param.7) | copy-start | bytes 1444
  20.5 44.1 %all-to-all-start = ((bf16[16,18,16,256]{3,2,1,0:T(8,128)(2,1)}), bf16[16,18,16,256]{3,2,1,0:T(8,128)(2,1)S(1)}, u32[]{:S(2)}, u32[]{:S(2)}) async-start(bf16[16,18,16,256]{3,2,1,0:T(8,128)(2,1)} %shard_map.56), calls=%async_computation | async-start | bytes 4718592 | tf_op jit(solution)/shard_map/all_to_all | solution.py:486
  64.7 1.5 copy-start.19
  114.5 5.2 %collective-permute-start = (f32[16,16,1536]{2,1,0:T(8,128)S(1)}, f32[16,16,1536]{2,1,0:T(8,128)S(1)}, u32[]{:S(2)}, u32[]{:S(2)}) collective-permute-start(f32[16,16,1536]{2,1,0:T(8,128)S(1)} %all_to_all.26.mine_ref), channel_id=1, source_target_pairs={{0,16},{16,0},{32,48},{48,32},{64,80},{80,64},{96,112},{112,96},{1... | collective-permute-start | bytes 4718600 | tf_op jit(solution)/shard_map/ppermute | solution.py:508
  119.6 1.1 copy-start.16
  128.9 4.9 %copy-start.20 = (s32[64,64]{1,0:T(8,128)S(1)}, s32[64,64]{1,0:T(8,128)}, u32[]{:S(2)}) copy-start(s32[64,64]{1,0:T(8,128)} %param.9) | copy-start | bytes 49156
  128.9 9.0 %copy-start.15 = (s32[3]{0:T(128)S(1)}, s32[3]{0:T(128)}, u32[]{:S(2)}) copy-start(s32[3]{0:T(128)} %pad_add_fusion.1.at_ref) | copy-start | bytes 40
  128.9 99.8 %all-to-all-start.3 = ((bf16[16,3,256,256]{3,2,1,0:T(8,128)(2,1)}), bf16[16,3,256,256]{3,2,1,0:T(8,128)(2,1)}, u32[]{:S(2)}, u32[]{:S(2)}) async-start(bf16[16,3,256,256]{3,2,1,0:T(8,128)(2,1)} %bitcast.67), calls=%async_computation.3 | async-start | bytes 12582912 | tf_op jit(solution)/shard_map/all_to_all | solution.py:510
  137.9 1.4 copy-start.17
  163.0 1.1 copy-start.12
  167.7 3.0 collective-permute-start.1
  170.7 49.8 %copy-start.10 = (bf16[8,16,512]{2,1,0:T(8,128)(2,1)S(1)}, bf16[8,16,512]{2,1,0:T(8,128)(2,1)}, u32[]{:S(2)}) copy-start(bf16[8,16,512]{2,1,0:T(8,128)(2,1)} %shard_map.60.p_ref.p0_ref) | copy-start | bytes 393220
  170.7 34.3 %collective-permute-start.4 = (bf16[2,4,16,512]{3,2,1,0:T(8,128)(2,1)S(1)}, bf16[2,4,16,512]{3,2,1,0:T(8,128)(2,1)S(1)}, u32[]{:S(2)}, u32[]{:S(2)}) collective-permute-start(bf16[2,4,16,512]{3,2,1,0:T(8,128)(2,1)S(1)} %maximum_select_fusion.refs_0_), channel_id=1, source_target_pairs={{96,0},{112,16},{0,32},{16,48},{32,64},{48,80},{64,96},{80,112},{9... | collective-permute-start | bytes 393224 | tf_op jit(solution)/shard_map/ppermute | solution.py:519
  172.0 33.0 %collective-permute-start.3 = (bf16[2,4,16,512]{3,2,1,0:T(8,128)(2,1)S(1)}, bf16[2,4,16,512]{3,2,1,0:T(8,128)(2,1)S(1)}, u32[]{:S(2)}, u32[]{:S(2)}) collective-permute-start(bf16[2,4,16,512]{3,2,1,0:T(8,128)(2,1)S(1)} %maximum_select_fusion.refs_0_), channel_id=1, source_target_pairs={{64,0},{80,16},{96,32},{112,48},{0,64},{16,80},{32,96},{48,112},{6... | collective-permute-start | bytes 393224 | tf_op jit(solution)/shard_map/ppermute | solution.py:519
  174.4 30.5 %collective-permute-start.2 = (bf16[2,4,16,512]{3,2,1,0:T(8,128)(2,1)S(1)}, bf16[2,4,16,512]{3,2,1,0:T(8,128)(2,1)S(1)}, u32[]{:S(2)}, u32[]{:S(2)}) collective-permute-start(bf16[2,4,16,512]{3,2,1,0:T(8,128)(2,1)S(1)} %maximum_select_fusion.refs_0_), channel_id=1, source_target_pairs={{32,0},{48,16},{64,32},{80,48},{96,64},{112,80},{0,96},{16,112},{3... | collective-permute-start | bytes 393224 | tf_op jit(solution)/shard_map/ppermute | solution.py:519
  175.6 1.2 copy-start.6
  176.8 1.4 copy-start.18
  203.2 1.0 copy-start.13
  209.0 2.2 collective-permute-start.5
  211.2 9.0 %collective-permute-start.8 = (bf16[2,4,16,512]{3,2,1,0:T(8,128)(2,1)S(1)}, bf16[2,4,16,512]{3,2,1,0:T(8,128)(2,1)S(1)}, u32[]{:S(2)}, u32[]{:S(2)}) collective-permute-start(bf16[2,4,16,512]{3,2,1,0:T(8,128)(2,1)S(1)} %maximum_select_fusion.1.refs_4_), channel_id=1, source_target_pairs={{96,0},{112,16},{0,32},{16,48},{32,64},{48,80},{64,96},{80,112},{9... | collective-permute-start | bytes 393224 | tf_op jit(solution)/shard_map/ppermute | solution.py:519
  211.6 8.6 %collective-permute-start.7 = (bf16[2,4,16,512]{3,2,1,0:T(8,128)(2,1)S(1)}, bf16[2,4,16,512]{3,2,1,0:T(8,128)(2,1)S(1)}, u32[]{:S(2)}, u32[]{:S(2)}) collective-permute-start(bf16[2,4,16,512]{3,2,1,0:T(8,128)(2,1)S(1)} %maximum_select_fusion.1.refs_4_), channel_id=1, source_target_pairs={{64,0},{80,16},{96,32},{112,48},{0,64},{16,80},{32,96},{48,112},{6... | collective-permute-start | bytes 393224 | tf_op jit(solution)/shard_map/ppermute | solution.py:519
  212.2 8.3 %collective-permute-start.6 = (bf16[2,4,16,512]{3,2,1,0:T(8,128)(2,1)S(1)}, bf16[2,4,16,512]{3,2,1,0:T(8,128)(2,1)S(1)}, u32[]{:S(2)}, u32[]{:S(2)}) collective-permute-start(bf16[2,4,16,512]{3,2,1,0:T(8,128)(2,1)S(1)} %maximum_select_fusion.1.refs_4_), channel_id=1, source_target_pairs={{32,0},{48,16},{64,32},{80,48},{96,64},{112,80},{0,96},{16,112},{3... | collective-permute-start | bytes 393224 | tf_op jit(solution)/shard_map/ppermute | solution.py:519
  222.3 2.4 copy-start.3
  228.6 9.5 %copy-start.7 = (f32[512,512]{1,0:T(8,128)S(1)}, f32[512,512]{1,0:T(8,128)}, u32[]{:S(2)}) copy-start(f32[512,512]{1,0:T(8,128)} %copy-done.5) | copy-start | bytes 3145732
  228.6 9.5 %copy-start.9 = (f32[512,512]{1,0:T(8,128)S(1)}, f32[512,512]{1,0:T(8,128)}, u32[]{:S(2)}) copy-start(f32[512,512]{1,0:T(8,128)} %copy-done.8) | copy-start | bytes 3145732
  228.6 66.3 %all-to-all-start.4 = ((bf16[16,20,16,512]{3,2,1,0:T(8,128)(2,1)}), bf16[16,20,16,512]{3,2,1,0:T(8,128)(2,1)}, u32[]{:S(2)}, u32[]{:S(2)}) async-start(bf16[16,20,16,512]{3,2,1,0:T(8,128)(2,1)} %copy-done.3), calls=%async_computation.4 | async-start | bytes 10485760 | tf_op jit(solution)/shard_map/all_to_all | solution.py:533
  238.3 3.4 %copy-start.1 = (f32[4,1,512,2,1,512]{5,4,3,2,1,0:T(1,128)S(1)}, f32[4,1,512,2,1,512]{5,4,3,2,1,0:T(1,128)}, u32[]{:S(2)}) copy-start(f32[4,1,512,2,1,512]{5,4,3,2,1,0:T(1,128)} %param.5) | copy-start | bytes 25165828
  249.6 3.3 copy-start.4
  297.2 11.8 %collective-permute-start.9 = (bf16[16,4,16,512]{3,2,1,0:T(8,128)(2,1)}, bf16[16,4,16,512]{3,2,1,0:T(8,128)(2,1)S(1)}, u32[]{:S(2)}, u32[]{:S(2)}) collective-permute-start(bf16[16,4,16,512]{3,2,1,0:T(8,128)(2,1)} %slice.39), channel_id=1, source_target_pairs={{0,16},{16,0},{32,48},{48,32},{64,80},{80,64},{96,112},{112,96},{1... | collective-permute-start | bytes 3145736 | tf_op jit(solution)/shard_map/ppermute | solution.py:538
  (4 other events, 3.6 us)
Sparse Core Ops, SparseCore 0:
  14.0 114.7 reduce-scatter.3
